TPU v7x, 32 devices: a whole 2x2x4 slice. The times are simulated.
32 devices in a mesh: dp: 4 (over z), seq: 2 (over core), tensor: 4 (over y, x).
Axes of the slice: x: 2, y: 2, z: 4, core: 2. Of those that a mesh axis runs over, the one named last changes fastest.
Arguments:
- source: bfloat16 [16, 1024, 1024], P('dp', ('seq', 'tensor')), may hold values from -61 to 61
- target: bfloat16 [16, 1024, 1024], P('dp', ('seq', 'tensor')), may hold values from -61 to 61
- out_grad: bfloat16 [16, 1024, 1024], P('dp', ('seq', 'tensor')), may hold values from -6 to 6
- source_segments: int32 [16, 1024], P('dp'), may hold values from 0 to 8, as said below
- target_segments: int32 [16, 1024], P('dp'), may hold values from 0 to 8, as said below
- enc_gain: float32 [3, 1024], replicated, may hold values from 0.5 to 1.5
- enc_shift: float32 [3, 1024], replicated, may hold values from -1.2 to 1.2
- enc_qkv: bfloat16 [1024, 3, 1024], P(None, None, 'tensor'), may hold values from -0.1875 to 0.1875
- enc_proj: bfloat16 [1024, 1024], P('tensor'), may hold values from -0.5 to 0.5
- enc_up: bfloat16 [1024, 4096], P(None, 'tensor'), may hold values from -0.1875 to 0.1875
- enc_down: bfloat16 [4096, 1024], P('tensor'), may hold values from -0.09375 to 0.09375
- dec_gain: float32 [4, 1024], replicated, may hold values from 0.5 to 1.5
- dec_shift: float32 [4, 1024], replicated, may hold values from -1.2 to 1.2
- dec_self_qkv: bfloat16 [1024, 3, 1024], P(None, None, 'tensor'), may hold values from -0.1875 to 0.1875
- dec_self_proj: bfloat16 [1024, 1024], P('tensor'), may hold values from -0.5 to 0.5
- dec_cross_q: bfloat16 [1024, 1024], P(None, 'tensor'), may hold values from -0.1875 to 0.1875
- dec_cross_kv: bfloat16 [1024, 2, 1024], P(None, None, 'tensor'), may hold values from -0.1875 to 0.1875
- dec_cross_proj: bfloat16 [1024, 1024], P('tensor'), may hold values from -0.5 to 0.5
- dec_up: bfloat16 [1024, 4096], P(None, 'tensor'), may hold values from -0.1875 to 0.1875
- dec_down: bfloat16 [4096, 1024], P('tensor'), may hold values from -0.09375 to 0.09375
Outputs:
- decoded: bfloat16 [16, 1024, 1024], P('dp', ('seq', 'tensor'))
- source_grad: float32 [16, 1024, 1024], P('dp', ('seq', 'tensor'))
- target_grad: float32 [16, 1024, 1024], P('dp', ('seq', 'tensor'))
- enc_gain_grad: float32 [3, 1024], P(None, 'seq')
- enc_shift_grad: float32 [3, 1024], P(None, 'seq')
- enc_qkv_grad: float32 [1024, 3, 1024], P('seq', None, 'tensor')
- enc_proj_grad: float32 [1024, 1024], P('tensor', 'seq')
- enc_up_grad: float32 [1024, 4096], P('seq', 'tensor')
- enc_down_grad: float32 [4096, 1024], P('tensor', 'seq')
- dec_gain_grad: float32 [4, 1024], P(None, 'seq')
- dec_shift_grad: float32 [4, 1024], P(None, 'seq')
- dec_self_qkv_grad: float32 [1024, 3, 1024], P('seq', None, 'tensor')
- dec_self_proj_grad: float32 [1024, 1024], P('tensor', 'seq')
- dec_cross_q_grad: float32 [1024, 1024], P('seq', 'tensor')
- dec_cross_kv_grad: float32 [1024, 2, 1024], P('seq', None, 'tensor')
- dec_cross_proj_grad: float32 [1024, 1024], P('tensor', 'seq')
- dec_up_grad: float32 [1024, 4096], P('seq', 'tensor')
- dec_down_grad: float32 [4096, 1024], P('tensor', 'seq')
Inputs may be any that keep to these rules, and one draw needn't show every extreme that they name: `source_segments`: 0 marks padding and k the k-th sentence pair of a slot; a slot holds either one pair (id 1) or eight pairs, pair k in rows (k - 1) * 128 to k * 128 - 1; every slot has a padding source row; of each 4 slots of one dp index, one holds a single pair whose source and target rows run past 7 / 8 of the slot and another holds eight pairs. `target_segments`: same slot layout as the source of the slot; every id in a slot's target occurs in its source.
All inputs are finite; a program needn't handle non-finite values.
Results may differ from a plain program's by a relative error of at most 0.038.
Values may be sent and summed in bfloat16 or wider, within the bound.
No kernel may reach another device: no remote copies, remote signals or barrier semaphores. Data moves between devices by JAX's collectives and lax.ppermute only.
A program may use at most 576 MiB of HBM per device.

v0:
```python
import jax
import jax.numpy as jnp
from jax import lax
from jax.sharding import PartitionSpec as P

HEAD_DIM = 64


EPS = 1e-05
NEG = -1e30


def layer_norm(inputs, norm_gain, norm_shift):
    row_mean = jnp.mean(inputs, -1, keepdims=True)
    centred = inputs - row_mean
    spread = jnp.mean(centred * centred, -1, keepdims=True)
    return centred * lax.rsqrt(spread + EPS) * norm_gain + norm_shift


def exact_gelu(inputs):
    return jax.nn.gelu(inputs, approximate=False)


def norm_back(inputs, norm_gain, norm_shift, cotangent):
    _, pullback = jax.vjp(layer_norm, inputs, norm_gain, norm_shift)
    return pullback(cotangent)


def gather_rows(row_block):
    return lax.all_gather(row_block, "tensor", axis=1, tiled=True)


def scatter_rows(term_block):
    return lax.psum_scatter(
        term_block.astype(jnp.bfloat16), "tensor", scatter_dimension=1, tiled=True
    ).astype(jnp.float32)


def gather_keys(row_block):
    return lax.all_gather(row_block, "seq", axis=1, tiled=True)


def scatter_keys(term_block):
    return lax.psum_scatter(
        term_block.astype(jnp.bfloat16), "seq", scatter_dimension=1, tiled=True
    ).astype(jnp.float32)


def project(row_block, weight):
    return jnp.einsum("sra,ab->srb", row_block, weight, preferred_element_type=jnp.float32)


def weight_grad(row_block, grad_block):
    return jnp.einsum("sra,srb->ab", row_block, grad_block, preferred_element_type=jnp.float32)


def back_project(grad_block, weight):
    return jnp.einsum("srb,ab->sra", grad_block, weight, preferred_element_type=jnp.float32)


def split_heads(row_block, groups):
    head_count = row_block.shape[2] // groups // HEAD_DIM
    return row_block.reshape(row_block.shape[0], row_block.shape[1], groups, head_count, HEAD_DIM)


def masked_scores(queries, key_rows, allowed):
    raw_scores = jnp.einsum(
        "sqhd,skhd->shqk", queries, key_rows, preferred_element_type=jnp.float32
    )
    return jnp.where(allowed[:, None], raw_scores * HEAD_DIM ** (-0.5), NEG)


def attend(queries, key_values, allowed):
    query_heads = split_heads(queries, 1)[:, :, 0]
    pair_heads = split_heads(key_values, 2)
    raw_scores = masked_scores(query_heads, pair_heads[:, :, 0], allowed)
    row_max = jnp.max(raw_scores, -1, keepdims=True)
    weights = jnp.exp(raw_scores - row_max)
    row_total = jnp.sum(weights, -1, keepdims=True)
    probs_low = (weights / row_total).astype(jnp.bfloat16)
    mixed_rows = jnp.einsum(
        "shqk,skhd->sqhd", probs_low, pair_heads[:, :, 1], preferred_element_type=jnp.float32
    )
    return (mixed_rows.astype(jnp.bfloat16).reshape(queries.shape), row_max + jnp.log(row_total))


def attend_back(queries, key_values, allowed, log_total, d_mixed):
    query_heads = split_heads(queries, 1)[:, :, 0]
    pair_heads = split_heads(key_values, 2)
    d_heads = split_heads(d_mixed, 1)[:, :, 0]
    probs = jnp.exp(masked_scores(query_heads, pair_heads[:, :, 0], allowed) - log_total)
    d_probs = jnp.einsum(
        "sqhd,skhd->shqk", d_heads, pair_heads[:, :, 1], preferred_element_type=jnp.float32
    )
    d_scores = (probs * (d_probs - jnp.sum(probs * d_probs, -1, keepdims=True))).astype(
        jnp.bfloat16
    )
    scale_factor = HEAD_DIM ** (-0.5)
    d_query = (
        jnp.einsum(
            "shqk,skhd->sqhd", d_scores, pair_heads[:, :, 0], preferred_element_type=jnp.float32
        )
        * scale_factor
    )
    d_keys = (
        jnp.einsum("shqk,sqhd->skhd", d_scores, query_heads, preferred_element_type=jnp.float32)
        * scale_factor
    )
    d_values = jnp.einsum(
        "shqk,sqhd->skhd", probs.astype(jnp.bfloat16), d_heads, preferred_element_type=jnp.float32
    )
    d_pairs = jnp.stack([d_keys, d_values], 2).reshape(key_values.shape)
    return (d_query.astype(jnp.bfloat16).reshape(queries.shape), d_pairs)


def self_forward(normed, weight_qkv, allowed):
    model_width = weight_qkv.shape[0]
    head_width = weight_qkv.shape[2]
    row_block = gather_rows(normed.astype(jnp.bfloat16))
    qkv_rows = project(row_block, weight_qkv.reshape(model_width, 3 * head_width)).astype(
        jnp.bfloat16
    )
    key_values = gather_keys(qkv_rows[:, :, head_width:])
    mixed_rows, log_total = attend(qkv_rows[:, :, :head_width], key_values, allowed)
    return (row_block, qkv_rows, key_values, mixed_rows, log_total)


def self_back(
    d_out, row_block, qkv_rows, key_values, allowed, log_total, mixed_rows, weight_qkv, weight_proj
):
    head_width = weight_proj.shape[0]
    d_rows = gather_rows(d_out.astype(jnp.bfloat16))
    grad_proj = weight_grad(mixed_rows, d_rows)
    d_mixed = back_project(d_rows, weight_proj).astype(jnp.bfloat16)
    d_query, d_pairs = attend_back(
        qkv_rows[:, :, :head_width], key_values, allowed, log_total, d_mixed
    )
    d_own = scatter_keys(d_pairs).astype(jnp.bfloat16)
    d_qkv = jnp.concatenate([d_query, d_own], 2)
    flat_weight = weight_qkv.reshape(weight_qkv.shape[0], 3 * head_width)
    grad_qkv = weight_grad(row_block, d_qkv).reshape(weight_qkv.shape)
    d_normed = scatter_rows(back_project(d_qkv, flat_weight))
    return (d_normed, grad_qkv, grad_proj)


def ffn_forward(normed, weight_up, weight_down):
    row_block = gather_rows(normed.astype(jnp.bfloat16))
    inner = project(row_block, weight_up)
    active = exact_gelu(inner).astype(jnp.bfloat16)
    return (row_block, inner, active, scatter_rows(project(active, weight_down)))


def ffn_back(d_out, row_block, inner, active, weight_up, weight_down):
    d_rows = gather_rows(d_out.astype(jnp.bfloat16))
    grad_down = weight_grad(active, d_rows)
    d_active = back_project(d_rows, weight_down)
    _, gelu_back = jax.vjp(exact_gelu, inner)
    d_inner = gelu_back(d_active)[0].astype(jnp.bfloat16)
    grad_up = weight_grad(row_block, d_inner)
    d_normed = scatter_rows(back_project(d_inner, weight_up))
    return (d_normed, grad_up, grad_down)


def local(
    source,
    target,
    out_grad,
    source_segments,
    target_segments,
    enc_gain,
    enc_shift,
    enc_qkv,
    enc_proj,
    enc_up,
    enc_down,
    dec_gain,
    dec_shift,
    dec_self_qkv,
    dec_self_proj,
    dec_cross_q,
    dec_cross_kv,
    dec_cross_proj,
    dec_up,
    dec_down,
):
    head_width = enc_proj.shape[0]
    model_width = enc_proj.shape[1]
    half_rows = source.shape[1] * lax.axis_size("tensor")
    first_row = lax.axis_index("seq") * half_rows
    own_source = lax.dynamic_slice_in_dim(source_segments, first_row, half_rows, 1)
    own_target = lax.dynamic_slice_in_dim(target_segments, first_row, half_rows, 1)
    enc_mask = own_source[:, :, None] == source_segments[:, None, :]
    cross_mask = own_target[:, :, None] == source_segments[:, None, :]
    row_place = first_row + jnp.arange(half_rows, dtype=jnp.int32)
    key_place = jnp.arange(target_segments.shape[1], dtype=jnp.int32)
    self_mask = (own_target[:, :, None] == target_segments[:, None, :]) & (
        key_place[None, None, :] <= row_place[None, :, None]
    )
    x_source = source.astype(jnp.float32)
    rows_a, qkv_a, pairs_a, mixed_a, total_a = self_forward(
        layer_norm(x_source, enc_gain[0], enc_shift[0]), enc_qkv, enc_mask
    )
    hidden = x_source + scatter_rows(project(mixed_a, enc_proj))
    rows_b, inner_b, active_b, branch_b = ffn_forward(
        layer_norm(hidden, enc_gain[1], enc_shift[1]), enc_up, enc_down
    )
    encoded = hidden + branch_b
    rows_m = gather_rows(layer_norm(encoded, enc_gain[2], enc_shift[2]).astype(jnp.bfloat16))
    memory_pairs = project(rows_m, dec_cross_kv.reshape(model_width, 2 * head_width)).astype(
        jnp.bfloat16
    )
    pairs_m = gather_keys(memory_pairs)
    x_target = target.astype(jnp.float32)
    rows_c, qkv_c, pairs_c, mixed_c, total_c = self_forward(
        layer_norm(x_target, dec_gain[0], dec_shift[0]), dec_self_qkv, self_mask
    )
    after_self = x_target + scatter_rows(project(mixed_c, dec_self_proj))
    rows_e = gather_rows(layer_norm(after_self, dec_gain[1], dec_shift[1]).astype(jnp.bfloat16))
    query_e = project(rows_e, dec_cross_q).astype(jnp.bfloat16)
    mixed_e, total_e = attend(query_e, pairs_m, cross_mask)
    after_cross = after_self + scatter_rows(project(mixed_e, dec_cross_proj))
    rows_f, inner_f, active_f, branch_f = ffn_forward(
        layer_norm(after_cross, dec_gain[2], dec_shift[2]), dec_up, dec_down
    )
    final_rows = after_cross + branch_f
    decoded, final_back = jax.vjp(layer_norm, final_rows, dec_gain[3], dec_shift[3])
    d_final, dec_gain_three, dec_shift_three = final_back(out_grad.astype(jnp.float32))
    d_normed, grad_dec_up, grad_dec_down = ffn_back(
        d_final, rows_f, inner_f, active_f, dec_up, dec_down
    )
    d_input, dec_gain_two, dec_shift_two = norm_back(
        after_cross, dec_gain[2], dec_shift[2], d_normed
    )
    d_cross = d_final + d_input
    d_rows = gather_rows(d_cross.astype(jnp.bfloat16))
    grad_cross_proj = weight_grad(mixed_e, d_rows)
    d_mixed = back_project(d_rows, dec_cross_proj).astype(jnp.bfloat16)
    d_query, d_pairs = attend_back(query_e, pairs_m, cross_mask, total_e, d_mixed)
    grad_cross_q = weight_grad(rows_e, d_query)
    d_normed = scatter_rows(back_project(d_query, dec_cross_q))
    d_memory_pairs = scatter_keys(d_pairs).astype(jnp.bfloat16)
    grad_cross_kv = weight_grad(rows_m, d_memory_pairs).reshape(dec_cross_kv.shape)
    d_memory = scatter_rows(
        back_project(d_memory_pairs, dec_cross_kv.reshape(model_width, 2 * head_width))
    )
    d_input, dec_gain_one, dec_shift_one = norm_back(
        after_self, dec_gain[1], dec_shift[1], d_normed
    )
    d_self = d_cross + d_input
    d_normed, grad_self_qkv, grad_self_proj = self_back(
        d_self, rows_c, qkv_c, pairs_c, self_mask, total_c, mixed_c, dec_self_qkv, dec_self_proj
    )
    d_input, dec_gain_zero, dec_shift_zero = norm_back(
        x_target, dec_gain[0], dec_shift[0], d_normed
    )
    target_grad = d_self + d_input
    d_encoded, enc_gain_two, enc_shift_two = norm_back(encoded, enc_gain[2], enc_shift[2], d_memory)
    d_normed, grad_enc_up, grad_enc_down = ffn_back(
        d_encoded, rows_b, inner_b, active_b, enc_up, enc_down
    )
    d_input, enc_gain_one, enc_shift_one = norm_back(hidden, enc_gain[1], enc_shift[1], d_normed)
    d_hidden = d_encoded + d_input
    d_normed, grad_enc_qkv, grad_enc_proj = self_back(
        d_hidden, rows_a, qkv_a, pairs_a, enc_mask, total_a, mixed_a, enc_qkv, enc_proj
    )
    d_input, enc_gain_zero, enc_shift_zero = norm_back(
        x_source, enc_gain[0], enc_shift[0], d_normed
    )
    source_grad = d_hidden + d_input
    norm_grads = (
        lax.psum(
            jnp.stack([enc_gain_zero, enc_gain_one, enc_gain_two]).astype(jnp.bfloat16), "tensor"
        ).astype(jnp.float32),
        lax.psum(
            jnp.stack([enc_shift_zero, enc_shift_one, enc_shift_two]).astype(jnp.bfloat16), "tensor"
        ).astype(jnp.float32),
        lax.psum(
            jnp.stack([dec_gain_zero, dec_gain_one, dec_gain_two, dec_gain_three]).astype(
                jnp.bfloat16
            ),
            "tensor",
        ).astype(jnp.float32),
        lax.psum(
            jnp.stack([dec_shift_zero, dec_shift_one, dec_shift_two, dec_shift_three]).astype(
                jnp.bfloat16
            ),
            "tensor",
        ).astype(jnp.float32),
    )
    pieces = [
        (norm_grads[0], 1),
        (norm_grads[1], 1),
        (grad_enc_qkv, 0),
        (grad_enc_proj, 1),
        (grad_enc_up, 0),
        (grad_enc_down, 1),
        (norm_grads[2], 1),
        (norm_grads[3], 1),
        (grad_self_qkv, 0),
        (grad_self_proj, 1),
        (grad_cross_q, 0),
        (grad_cross_kv, 0),
        (grad_cross_proj, 1),
        (grad_dec_up, 0),
        (grad_dec_down, 1),
    ]
    leading = [jnp.moveaxis(gradient, split_axis, 0) for gradient, split_axis in pieces]
    seq_count = lax.axis_size("seq")
    data_count = lax.axis_size("dp")
    packed = jnp.concatenate(
        [gradient.reshape(seq_count, data_count, -1).swapaxes(0, 1) for gradient in leading], 2
    )
    packed = packed.reshape(seq_count * data_count, -1)
    collected = lax.all_gather(
        lax.psum_scatter(
            packed.astype(jnp.bfloat16), ("dp", "seq"), scatter_dimension=0, tiled=True
        ),
        "dp",
        axis=0,
        tiled=True,
    ).astype(jnp.float32)
    results = []
    offset = 0
    for gradient, (initial, split_axis) in zip(leading, pieces):
        length = gradient.size // seq_count // collected.shape[0]
        segment_piece = collected[:, offset : offset + length].reshape(
            (gradient.shape[0] // seq_count,) + gradient.shape[1:]
        )
        results.append(jnp.moveaxis(segment_piece, 0, split_axis))
        offset = offset + length
    return (decoded.astype(jnp.bfloat16), source_grad, target_grad) + tuple(results)


def solution(mesh):
    placed = (
        P("dp", ("seq", "tensor"), None),
        P("dp", ("seq", "tensor"), None),
        P("dp", ("seq", "tensor"), None),
        P("dp", None),
        P("dp", None),
        P(),
        P(),
        P(None, None, "tensor"),
        P("tensor", None),
        P(None, "tensor"),
        P("tensor", None),
        P(),
        P(),
        P(None, None, "tensor"),
        P("tensor", None),
        P(None, "tensor"),
        P(None, None, "tensor"),
        P("tensor", None),
        P(None, "tensor"),
        P("tensor", None),
    )
    return jax.shard_map(
        local,
        mesh=mesh,
        in_specs=placed,
        out_specs=(
            P("dp", ("seq", "tensor"), None),
            P("dp", ("seq", "tensor"), None),
            P("dp", ("seq", "tensor"), None),
            P(None, "seq"),
            P(None, "seq"),
            P("seq", None, "tensor"),
            P("tensor", "seq"),
            P("seq", "tensor"),
            P("tensor", "seq"),
            P(None, "seq"),
            P(None, "seq"),
            P("seq", None, "tensor"),
            P("tensor", "seq"),
            P("seq", "tensor"),
            P("seq", None, "tensor"),
            P("tensor", "seq"),
            P("seq", "tensor"),
            P("tensor", "seq"),
        ),
        check_vma=False,
    )
```

profile of v0, /device:TPU:9, one launch (start us, length us, event | category | flops | bytes accessed | tf_op | source)
XLA Modules:
  0.0 2442.3 jit_solution(670846785400597645)
XLA Ops:
  19.3 51.4 %all-gather.21.cloned.1.call-done = bf16[4,512,1024]{2,1,0:T(8,128)(2,1)} async-done(((bf16[4,128,1024]{2,1,0:T(8,128)(2,1)}), bf16[4,512,1024]{2,1,0:T(8,128)(2,1)}) %all-gather.21.cloned.1.call-update) | async-done | bytes 4194320 | tf_op jit(solution)/shard_map/all_gather | solution.py:30
  100.9 16.0 fusion.158
  116.9 14.4 fusion.1
  131.4 12.9 fusion.108
  156.5 45.5 %reduce-scatter.17.cloned.1.call-done = bf16[4,128,1024]{2,1,0:T(8,128)(2,1)} async-done(((bf16[4,512,1024]{2,1,0:T(8,128)(2,1)}), bf16[4,128,1024]{2,1,0:T(8,128)(2,1)}) %reduce-scatter.17.cloned.1.call-update) | async-done | bytes 1048592 | tf_op jit(solution)/shard_map/reduce_scatter | solution.py:34
  211.0 46.1 %all-gather.17.cloned.1.call-done = bf16[4,512,1024]{2,1,0:T(8,128)(2,1)} async-done(((bf16[4,128,1024]{2,1,0:T(8,128)(2,1)}), bf16[4,512,1024]{2,1,0:T(8,128)(2,1)}) %all-gather.17.cloned.1.call-update) | async-done | bytes 4194320 | tf_op jit(solution)/shard_map/all_gather | solution.py:30
  266.7 45.7 %all-gather.25.cloned.1.call-done = bf16[4,512,1024]{2,1,0:T(8,128)(2,1)} async-done(((bf16[4,128,1024]{2,1,0:T(8,128)(2,1)}), bf16[4,512,1024]{2,1,0:T(8,128)(2,1)}) %all-gather.25.cloned.1.call-update) | async-done | bytes 4194320 | tf_op jit(solution)/shard_map/all_gather | solution.py:30
  321.8 19.7 multiply_convert_fusion.4
  361.2 17.0 fusion.157
  378.2 14.6 fusion
  392.9 13.2 fusion.109
  416.3 47.3 %reduce-scatter.15.cloned.1.call-done = bf16[4,128,1024]{2,1,0:T(8,128)(2,1)} async-done(((bf16[4,512,1024]{2,1,0:T(8,128)(2,1)}), bf16[4,128,1024]{2,1,0:T(8,128)(2,1)}) %reduce-scatter.15.cloned.1.call-update) | async-done | bytes 1048592 | tf_op jit(solution)/shard_map/reduce_scatter | solution.py:34
  472.8 46.1 %all-gather.27.cloned.1.call-done = bf16[4,512,1024]{2,1,0:T(8,128)(2,1)} async-done(((bf16[4,128,1024]{2,1,0:T(8,128)(2,1)}), bf16[4,512,1024]{2,1,0:T(8,128)(2,1)}) %all-gather.27.cloned.1.call-update) | async-done | bytes 4194320 | tf_op jit(solution)/shard_map/all_gather | solution.py:30
  525.1 48.9 %all-gather.31.cloned.1.call-done = bf16[4,512,1024]{2,1,0:T(8,128)(2,1)} async-done(((bf16[4,128,1024]{2,1,0:T(8,128)(2,1)}), bf16[4,512,1024]{2,1,0:T(8,128)(2,1)}) %all-gather.31.cloned.1.call-update) | async-done | bytes 4194320 | tf_op jit(solution)/shard_map/all_gather | solution.py:30
  578.6 12.1 all-gather.29.cloned.1.call-done
  597.0 16.3 fusion.159
  613.4 14.4 fusion.2
  627.8 12.9 fusion.107
  645.4 53.0 %reduce-scatter.21.cloned.1.call-done = bf16[4,128,1024]{2,1,0:T(8,128)(2,1)} async-done(((bf16[4,512,1024]{2,1,0:T(8,128)(2,1)}), bf16[4,128,1024]{2,1,0:T(8,128)(2,1)}) %reduce-scatter.21.cloned.1.call-update) | async-done | bytes 1048592 | tf_op jit(solution)/shard_map/reduce_scatter | solution.py:34
  703.2 52.8 %all-gather.33.cloned.1.call-done = bf16[4,512,1024]{2,1,0:T(8,128)(2,1)} async-done(((bf16[4,128,1024]{2,1,0:T(8,128)(2,1)}), bf16[4,512,1024]{2,1,0:T(8,128)(2,1)}) %all-gather.33.cloned.1.call-update) | async-done | bytes 4194320 | tf_op jit(solution)/shard_map/all_gather | solution.py:30
  764.8 19.7 multiply_convert_fusion.3
  792.8 52.8 %reduce-scatter.23.cloned.1.call-done = bf16[4,128,1024]{2,1,0:T(8,128)(2,1)} async-done(((bf16[4,512,1024]{2,1,0:T(8,128)(2,1)}), bf16[4,128,1024]{2,1,0:T(8,128)(2,1)}) %reduce-scatter.23.cloned.1.call-update) | async-done | bytes 1048592 | tf_op jit(solution)/shard_map/reduce_scatter | solution.py:34
  852.2 52.4 %all-gather.35.cloned.1.call-done = bf16[4,512,1024]{2,1,0:T(8,128)(2,1)} async-done(((bf16[4,128,1024]{2,1,0:T(8,128)(2,1)}), bf16[4,512,1024]{2,1,0:T(8,128)(2,1)}) %all-gather.35.cloned.1.call-update) | async-done | bytes 4194320 | tf_op jit(solution)/shard_map/all_gather | solution.py:30
  904.6 11.5 add_convert_fusion.1
  924.5 52.8 %reduce-scatter.25.cloned.1.call-done = bf16[4,128,1024]{2,1,0:T(8,128)(2,1)} async-done(((bf16[4,512,1024]{2,1,0:T(8,128)(2,1)}), bf16[4,128,1024]{2,1,0:T(8,128)(2,1)}) %reduce-scatter.25.cloned.1.call-update) | async-done | bytes 1048592 | tf_op jit(solution)/shard_map/reduce_scatter | solution.py:34
  985.5 52.6 %all-gather.37.cloned.1.call-done = bf16[4,512,1024]{2,1,0:T(8,128)(2,1)} async-done(((bf16[4,128,1024]{2,1,0:T(8,128)(2,1)}), bf16[4,512,1024]{2,1,0:T(8,128)(2,1)}) %all-gather.37.cloned.1.call-update) | async-done | bytes 4194320 | tf_op jit(solution)/shard_map/all_gather | solution.py:30
  1041.7 14.8 convert_bitcast_fusion.2
  1056.5 23.2 multiply_reduce_fusion.2
  1079.7 27.7 %multiply_convert_fusion.2 = bf16[4,4,512,1024]{3,2,1,0:T(8,128)(2,1)} fusion(f32[4,4,512,1024]{3,2,1,0:T(8,128)} %get-tuple-element.131, f32[4,4,512,1024]{3,2,1,0:T(8,128)} %get-tuple-element.128, f32[4,4,512]{2,1,0:T(4,128)S(1)} %get-tuple-element.130, f32[4,4,512]{2,1,0:T(4,128)S(1)} %bitcast.397), kind=kLoop, calls=%fused_computation.6 | loop fusion | flops 33554432 | bytes 83951616 | tf_op jit(solution)/shard_map/convert_element_type | solution.py:95
  1119.9 11.6 multiply_convert_fusion.9
  1142.2 46.8 %reduce-scatter.37.cloned.1.call-done = bf16[4,128,1024]{2,1,0:T(8,128)(2,1)} async-done(((bf16[4,512,1024]{2,1,0:T(8,128)(2,1)}), bf16[4,128,1024]{2,1,0:T(8,128)(2,1)}) %reduce-scatter.37.cloned.1.call-update) | async-done | bytes 1048592 | tf_op jit(solution)/shard_map/reduce_scatter | solution.py:34
  1191.3 53.3 %reduce-scatter.29.cloned.1.call-done = bf16[4,128,1024]{2,1,0:T(8,128)(2,1)} async-done(((bf16[4,512,1024]{2,1,0:T(8,128)(2,1)}), bf16[4,128,1024]{2,1,0:T(8,128)(2,1)}) %reduce-scatter.29.cloned.1.call-update) | async-done | bytes 1048592 | tf_op jit(solution)/shard_map/reduce_scatter | solution.py:34
  1257.2 48.2 %all-gather.39.cloned.1.call-done = bf16[4,512,1024]{2,1,0:T(8,128)(2,1)} async-done(((bf16[4,128,1024]{2,1,0:T(8,128)(2,1)}), bf16[4,512,1024]{2,1,0:T(8,128)(2,1)}) %all-gather.39.cloned.1.call-update) | async-done | bytes 4194320 | tf_op jit(solution)/shard_map/all_gather | solution.py:30
  1305.4 11.6 add_convert_fusion
  1326.3 34.5 %all-gather.43.cloned.1.call-done = bf16[4,512,1024]{2,1,0:T(8,128)(2,1)} async-done(((bf16[4,128,1024]{2,1,0:T(8,128)(2,1)}), bf16[4,512,1024]{2,1,0:T(8,128)(2,1)}) %all-gather.43.cloned.1.call-update) | async-done | bytes 4194320 | tf_op jit(solution)/shard_map/all_gather | solution.py:30
  1365.2 51.5 %reduce-scatter.31.cloned.1.call-done = bf16[4,128,1024]{2,1,0:T(8,128)(2,1)} async-done(((bf16[4,512,1024]{2,1,0:T(8,128)(2,1)}), bf16[4,128,1024]{2,1,0:T(8,128)(2,1)}) %reduce-scatter.31.cloned.1.call-update) | async-done | bytes 1048592 | tf_op jit(solution)/shard_map/reduce_scatter | solution.py:34
  1424.0 23.7 multiply_reduce_fusion
  1447.7 28.1 %multiply_convert_fusion = bf16[4,4,512,1024]{3,2,1,0:T(8,128)(2,1)} fusion(f32[4,4,512,1024]{3,2,1,0:T(8,128)} %get-tuple-element.135, f32[4,4,512,1024]{3,2,1,0:T(8,128)} %get-tuple-element.123, f32[4,4,512]{2,1,0:T(4,128)S(1)} %get-tuple-element.134, f32[4,4,512]{2,1,0:T(4,128)S(1)} %bitcast.393), kind=kLoop, calls=%fused_computation | loop fusion | flops 33554432 | bytes 83951616 | tf_op jit(solution)/shard_map/convert_element_type | solution.py:95
  1484.6 13.9 convert_bitcast_fusion
  1512.3 24.6 %multiply_reduce_fusion.1 = (f32[4,4,512]{2,1,0:T(4,128)S(1)}, f32[4,4,512,1024]{3,2,1,0:T(8,128)}) fusion(f32[4,4,512,1024]{3,2,1,0:T(8,128)} %get-tuple-element.125, f32[4,4,512]{2,1,0:T(4,128)S(1)} %bitcast.389, bf16[4,512,4,64]{1,3,2,0:T(8,128)(2,1)S(1)} %bitcast.364, bf16[4,1024,2,4,64]{1,4,3,2,0:T(8,128)(2,1)S(1)} %bitcast.342), kind=kOutput, calls=%fused_computation.4 | convolution fusion | flops 1098899456 | bytes 70320128 | tf_op jit(solution)/shard_map/sqhd,skhd->shqk/dot_general | solution.py:92
  1536.9 27.8 %multiply_convert_fusion.1 = bf16[4,4,512,1024]{3,2,1,0:T(8,128)(2,1)} fusion(f32[4,4,512,1024]{3,2,1,0:T(8,128)} %get-tuple-element.133, f32[4,4,512,1024]{3,2,1,0:T(8,128)} %get-tuple-element.125, f32[4,4,512]{2,1,0:T(4,128)S(1)} %get-tuple-element.132, f32[4,4,512]{2,1,0:T(4,128)S(1)} %bitcast.390), kind=kLoop, calls=%fused_computation.3 | loop fusion | flops 33554432 | bytes 83951616 | tf_op jit(solution)/shard_map/convert_element_type | solution.py:95
  1573.6 13.9 convert_bitcast_fusion.1
  1597.1 11.9 multiply_convert_fusion.8
  1618.9 12.2 multiply_convert_fusion.10
  1793.7 25.3 %convert_element_type.312 = bf16[8,919296]{1,0:T(8,128)(2,1)} reshape(bf16[4,2,919296]{2,1,0:T(2,128)(2,1)} %bitcast_dynamic-update-slice_fusion) | data formatting | bytes 29417472 | tf_op jit(solution)/shard_map/convert_element_type | solution.py:316
  1820.2 298.1 %all-reduce.4.cloned.1.call-done = bf16[8,919296]{1,0:T(8,128)(2,1)} async-done(((bf16[8,919296]{1,0:T(8,128)(2,1)}), bf16[8,919296]{1,0:T(8,128)(2,1)}) %all-reduce.4.cloned.1.call-update) | async-done | bytes 14708752
  2136.6 241.5 %all-gather.45.cloned.1.call-done = bf16[4,1,919296]{2,1,0:T(2,128)(2,1)} async-done(((bf16[1,1,919296]{2,1,0:T(2,128)(2,1)}), bf16[4,1,919296]{2,1,0:T(2,128)(2,1)}) %all-gather.45.cloned.1.call-update) | async-done | bytes 7354384 | tf_op jit(solution)/shard_map/all_gather | solution.py:314
  2378.1 12.2 copy.276
  (633 shorter events, 526.6 us)
Async XLA Ops:
  7.2 748.8 %copy-start = (bf16[1024,1024]{1,0:T(8,128)(2,1)S(1)}, bf16[1024,1024]{1,0:T(8,128)(2,1)}, u32[]{:S(2)}) copy-start(bf16[1024,1024]{1,0:T(8,128)(2,1)} %param.38) | copy-start | bytes 6291460
  7.2 63.4 %all-gather.21.cloned.1.call-start = ((), (), s32[]{:S(2)}) async-start(), calls=%async_computation.17 | async-start | bytes 5242880 | tf_op jit(solution)/shard_map/all_gather | solution.py:30
  12.5 193.5 %copy-start.89 = (f32[1,1024]{1,0:T(1,128)}, f32[1,1024]{1,0:T(1,128)S(1)}, u32[]{:S(2)}) copy-start(f32[1,1024]{1,0:T(1,128)S(1)} %get-tuple-element.111) | copy-start | bytes 12292
  16.6 77.9 %all-gather.23.cloned.1.call-start = ((), (), s32[]{:S(2)}) async-start(), calls=%async_computation.18 | async-start | bytes 6291456 | tf_op jit(solution)/shard_map/all_gather | solution.py:40
  80.0 122.0 %reduce-scatter.17.cloned.1.call-start = ((), (), s32[]{:S(2)}) async-start(), calls=%async_computation.19 | async-start | bytes 5242880 | tf_op jit(solution)/shard_map/reduce_scatter | solution.py:34
  148.7 108.4 %all-gather.17.cloned.1.call-start = ((), (), s32[]{:S(2)}) async-start(), calls=%async_computation.14 | async-start | bytes 5242880 | tf_op jit(solution)/shard_map/all_gather | solution.py:30
  153.2 314.8 %copy-start.86 = (f32[1,1024]{1,0:T(1,128)}, f32[1,1024]{1,0:T(1,128)S(1)}, u32[]{:S(2)}) copy-start(f32[1,1024]{1,0:T(1,128)S(1)} %get-tuple-element.104) | copy-start | bytes 12292
  156.5 155.9 %all-gather.25.cloned.1.call-start = ((), (), s32[]{:S(2)}) async-start(), calls=%async_computation.20 | async-start | bytes 5242880 | tf_op jit(solution)/shard_map/all_gather | solution.py:30
  208.2 146.5 %all-gather.19.cloned.1.call-start = ((), (), s32[]{:S(2)}) async-start(), calls=%async_computation.15 | async-start | bytes 6291456 | tf_op jit(solution)/shard_map/all_gather | solution.py:40
  266.6 144.0 %reduce-scatter.19.cloned.1.call-start = ((), (), s32[]{:S(2)}) async-start(), calls=%async_computation.21 | async-start | bytes 5242880 | tf_op jit(solution)/shard_map/reduce_scatter | solution.py:34
  349.6 114.0 %reduce-scatter.15.cloned.1.call-start = ((), (), s32[]{:S(2)}) async-start(), calls=%async_computation.16 | async-start | bytes 5242880 | tf_op jit(solution)/shard_map/reduce_scatter | solution.py:34
  410.5 108.4 %all-gather.27.cloned.1.call-start = ((), (), s32[]{:S(2)}) async-start(), calls=%async_computation.22 | async-start | bytes 5242880 | tf_op jit(solution)/shard_map/all_gather | solution.py:30
  416.3 157.8 %all-gather.31.cloned.1.call-start = ((), (), s32[]{:S(2)}) async-start(), calls=%async_computation.24 | async-start | bytes 5242880 | tf_op jit(solution)/shard_map/all_gather | solution.py:30
  470.1 120.6 %all-gather.29.cloned.1.call-start = ((), (), s32[]{:S(2)}) async-start(), calls=%async_computation.23 | async-start | bytes 6291456 | tf_op jit(solution)/shard_map/all_gather | solution.py:40
  525.1 173.3 %reduce-scatter.21.cloned.1.call-start = ((), (), s32[]{:S(2)}) async-start(), calls=%async_computation.25 | async-start | bytes 5242880 | tf_op jit(solution)/shard_map/reduce_scatter | solution.py:34
  645.1 56.7 %copy-start.104 = (f32[1,1024]{1,0:T(1,128)S(1)}, f32[1,1024]{1,0:T(1,128)}, u32[]{:S(2)}) copy-start(f32[1,1024]{1,0:T(1,128)} %get-tuple-element.106) | copy-start | bytes 12292
  645.1 56.6 %copy-start.154 = (f32[1,1024]{1,0:T(1,128)S(1)}, f32[1,1024]{1,0:T(1,128)}, u32[]{:S(2)}) copy-start(f32[1,1024]{1,0:T(1,128)} %get-tuple-element.110) | copy-start | bytes 12292
  645.1 110.9 %all-gather.33.cloned.1.call-start = ((), (), s32[]{:S(2)}) async-start(), calls=%async_computation.26 | async-start | bytes 5242880 | tf_op jit(solution)/shard_map/all_gather | solution.py:30
  703.1 142.4 %reduce-scatter.23.cloned.1.call-start = ((), (), s32[]{:S(2)}) async-start(), calls=%async_computation.27 | async-start | bytes 5242880 | tf_op jit(solution)/shard_map/reduce_scatter | solution.py:34
  792.7 111.9 %all-gather.35.cloned.1.call-start = ((), (), s32[]{:S(2)}) async-start(), calls=%async_computation.28 | async-start | bytes 5242880 | tf_op jit(solution)/shard_map/all_gather | solution.py:30
  851.8 125.5 %reduce-scatter.25.cloned.1.call-start = ((), (), s32[]{:S(2)}) async-start(), calls=%async_computation.29 | async-start | bytes 5242880 | tf_op jit(solution)/shard_map/reduce_scatter | solution.py:34
  924.5 57.6 %copy-start.153 = (f32[1,1024]{1,0:T(1,128)S(1)}, f32[1,1024]{1,0:T(1,128)}, u32[]{:S(2)}) copy-start(f32[1,1024]{1,0:T(1,128)} %get-tuple-element.107) | copy-start | bytes 12292
  924.5 113.6 %all-gather.37.cloned.1.call-start = ((), (), s32[]{:S(2)}) async-start(), calls=%async_computation.30 | async-start | bytes 5242880 | tf_op jit(solution)/shard_map/all_gather | solution.py:30
  985.2 149.7 %reduce-scatter.27.cloned.1.call-start = ((), (), s32[]{:S(2)}) async-start(), calls=%async_computation.31 | async-start | bytes 6291456 | tf_op jit(solution)/shard_map/reduce_scatter | solution.py:44
  1119.6 69.4 %reduce-scatter.37.cloned.1.call-start = ((), (), s32[]{:S(2)}) async-start(), calls=%async_computation.38 | async-start | bytes 5242880 | tf_op jit(solution)/shard_map/reduce_scatter | solution.py:34
  1134.9 109.7 %reduce-scatter.29.cloned.1.call-start = ((), (), s32[]{:S(2)}) async-start(), calls=%async_computation.32 | async-start | bytes 5242880 | tf_op jit(solution)/shard_map/reduce_scatter | solution.py:34
  1142.1 102.5 %copy-start.3 = (bf16[4,128,1024]{2,1,0:T(8,128)(2,1)S(1)}, bf16[4,128,1024]{2,1,0:T(8,128)(2,1)}, u32[]{:S(2)}) copy-start(bf16[4,128,1024]{2,1,0:T(8,128)(2,1)} %param.20) | copy-start | bytes 3145732
  1142.1 102.5 %copy-start.9 = (bf16[4,128,1024]{2,1,0:T(8,128)(2,1)S(1)}, bf16[4,128,1024]{2,1,0:T(8,128)(2,1)}, u32[]{:S(2)}) copy-start(bf16[4,128,1024]{2,1,0:T(8,128)(2,1)} %reduce-scatter.17.cloned.1.call-done) | copy-start | bytes 3145732
  1142.1 102.5 %copy-start.84 = (f32[1,1024]{1,0:T(1,128)S(1)}, f32[1,1024]{1,0:T(1,128)}, u32[]{:S(2)}) copy-start(f32[1,1024]{1,0:T(1,128)} %get-tuple-element.113) | copy-start | bytes 12292
  1142.1 102.5 %copy-start.97 = (f32[4,128]{1,0:T(4,128)S(1)}, f32[4,128]{1,0:T(4,128)}, u32[]{:S(2)}) copy-start(f32[4,128]{1,0:T(4,128)} %copy-done.96) | copy-start | bytes 6148
  1142.1 105.0 %copy-start.145 = (f32[4,128]{1,0:T(4,128)S(1)}, f32[4,128]{1,0:T(4,128)}, u32[]{:S(2)}) copy-start(f32[4,128]{1,0:T(4,128)} %copy-done.144) | copy-start | bytes 6148
  1142.1 105.0 %copy-start.116 = (f32[4,128]{1,0:T(4,128)S(1)}, f32[4,128]{1,0:T(4,128)}, u32[]{:S(2)}) copy-start(f32[4,128]{1,0:T(4,128)} %copy-done.115) | copy-start | bytes 6148
  1142.1 105.0 %copy-start.119 = (f32[4,128]{1,0:T(4,128)S(1)}, f32[4,128]{1,0:T(4,128)}, u32[]{:S(2)}) copy-start(f32[4,128]{1,0:T(4,128)} %copy-done.118) | copy-start | bytes 6148
  1142.2 163.3 %all-gather.39.cloned.1.call-start = ((), (), s32[]{:S(2)}) async-start(), calls=%async_computation.33 | async-start | bytes 5242880 | tf_op jit(solution)/shard_map/all_gather | solution.py:30
  1191.3 61.8 %copy-start.130 = (f32[4,128]{1,0:T(4,128)}, f32[4,128]{1,0:T(4,128)S(1)}, u32[]{:S(2)}) copy-start(f32[4,128]{1,0:T(4,128)S(1)} %multiply_multiply_fusion.11) | copy-start | bytes 6148
  1247.4 173.3 %copy-start.124 = (f32[4,128]{1,0:T(4,128)}, f32[4,128]{1,0:T(4,128)S(1)}, u32[]{:S(2)}) copy-start(f32[4,128]{1,0:T(4,128)S(1)} %multiply_multiply_fusion.14) | copy-start | bytes 6148
  1250.6 170.1 %copy-start.132 = (f32[4,128]{1,0:T(4,128)}, f32[4,128]{1,0:T(4,128)S(1)}, u32[]{:S(2)}) copy-start(f32[4,128]{1,0:T(4,128)S(1)} %negate_multiply_fusion.6) | copy-start | bytes 6148
  1252.6 108.1 %all-gather.43.cloned.1.call-start = ((), (), s32[]{:S(2)}) async-start(), calls=%async_computation.39 | async-start | bytes 5242880 | tf_op jit(solution)/shard_map/all_gather | solution.py:30
  1257.1 159.6 %reduce-scatter.31.cloned.1.call-start = ((), (), s32[]{:S(2)}) async-start(), calls=%async_computation.34 | async-start | bytes 5242880 | tf_op jit(solution)/shard_map/reduce_scatter | solution.py:34
  1325.5 182.4 %all-gather.41.cloned.1.call-start = ((), (), s32[]{:S(2)}) async-start(), calls=%async_computation.35 | async-start | bytes 5242880 | tf_op jit(solution)/shard_map/all_gather | solution.py:30
  1326.2 90.5 %copy-start.90 = (f32[1,1024]{1,0:T(1,128)S(1)}, f32[1,1024]{1,0:T(1,128)}, u32[]{:S(2)}) copy-start(f32[1,1024]{1,0:T(1,128)} %copy-done.89) | copy-start | bytes 12292
  1326.3 90.5 %copy-start.109 = (f32[4,128]{1,0:T(4,128)S(1)}, f32[4,128]{1,0:T(4,128)}, u32[]{:S(2)}) copy-start(f32[4,128]{1,0:T(4,128)} %copy-done.108) | copy-start | bytes 6148
  1423.8 185.8 %reduce-scatter.39.cloned.1.call-start = ((), (), s32[]{:S(2)}) async-start(), calls=%async_computation.40 | async-start | bytes 6291456 | tf_op jit(solution)/shard_map/reduce_scatter | solution.py:44
  1507.6 124.0 %reduce-scatter.33.cloned.1.call-start = ((), (), s32[]{:S(2)}) async-start(), calls=%async_computation.36 | async-start | bytes 6291456 | tf_op jit(solution)/shard_map/reduce_scatter | solution.py:44
  1596.7 132.2 %reduce-scatter.41.cloned.1.call-start = ((), (), s32[]{:S(2)}) async-start(), calls=%async_computation.41 | async-start | bytes 5242880 | tf_op jit(solution)/shard_map/reduce_scatter | solution.py:34
  1617.5 128.1 %reduce-scatter.35.cloned.1.call-start = ((), (), s32[]{:S(2)}) async-start(), calls=%async_computation.37 | async-start | bytes 5242880 | tf_op jit(solution)/shard_map/reduce_scatter | solution.py:34
  1639.3 478.9 %all-reduce.4.cloned.1.call-start = ((), (), s32[]{:S(2)}) async-start(), calls=%async_computation.43 | async-start | bytes 29417472
  1818.9 559.2 %all-gather.45.cloned.1.call-start = ((), (), s32[]{:S(2)}) async-start(), calls=%async_computation.42 | async-start | bytes 18385920 | tf_op jit(solution)/shard_map/all_gather | solution.py:314
  (150 other events, 1309.9 us)
Sparse Core Ops, SparseCore 0:
  16.7 53.8 all-gather.20
  80.1 14.3 all-gather.22
  148.8 53.1 reduce-scatter.16
  204.5 52.6 all-gather.16
  259.6 52.6 all-gather.24
  314.4 14.3 all-gather.18
  349.8 52.6 reduce-scatter.18
  410.6 52.9 reduce-scatter.14
  466.2 52.6 all-gather.26
  521.3 52.6 all-gather.30
  576.3 14.3 all-gather.28
  645.2 53.1 reduce-scatter.20
  703.2 52.6 all-gather.32
  792.8 52.6 reduce-scatter.22
  851.9 52.6 all-gather.34
  924.6 52.6 reduce-scatter.24
  985.4 52.6 all-gather.36
  1119.7 12.7 reduce-scatter.26
  1135.7 53.2 reduce-scatter.36
  1191.9 52.6 reduce-scatter.28
  1252.7 52.6 all-gather.38
  1308.0 52.6 all-gather.42
  1364.0 52.6 reduce-scatter.30
  1423.9 52.6 all-gather.40
  1507.7 12.8 reduce-scatter.38
  1596.8 12.4 reduce-scatter.32
  1617.6 52.4 reduce-scatter.40
  1673.3 52.6 reduce-scatter.34
  1819.1 299.1 all-reduce.3
  2127.4 250.6 all-gather.44
where the time goes:
time: 2450 us; the launch traced here: 2440 us
  waiting for transfers between devices  1440 us (59%)
  matrix products  472 us (19%)
  other arithmetic  255 us (10%)
  local copies, waits for them, and re-layouts  243 us (10%)
    all_gather x11, waiting for transfers between devices, gather_rows(): return lax.all_gather(row_block, 'tensor', axis=1, tiled=True)  479 us
    reduce_scatter x11, waiting for transfers between devices, scatter_rows(): lax.psum_scatter(term_block.astype(jnp.bfloat16), 'tensor', scatter_dimen...  403 us
    unnamed x31, waiting for transfers between devices  299 us
    all_gather x1, waiting for transfers between devices, local(): lax.all_gather(lax.psum_scatter(packed.astype(jnp.bfloat16), ('dp', 'seq'...  242 us
    unnamed x366, local copies, waits for them, and re-layouts  95.2 us
    convert_element_type x3, other arithmetic, attend_back(): (probs * (d_probs - jnp.sum(probs * d_probs, -1, keepdims=True))).astype(...  83.7 us
    dot_general x11, matrix products, back_project(): jnp.einsum('srb,ab->sra', grad_block, weight, preferred_element_type=jnp....  72.2 us
    dot_general x11, matrix products, weight_grad(): jnp.einsum('sra,srb->ab', row_block, grad_block, preferred_element_type=j...  71.6 us
  transfers between devices with their start and end apart: 30, of which 22 were waited for; matrix products, arithmetic and copies ran while one was open for 22% of the time, Pallas kernels for 0%

commit v1 on v0

v1 whole, which is shorter than its diff:
```python
import functools

import jax
import jax.numpy as jnp
from jax import lax
from jax.experimental import pallas as pl
from jax.experimental.pallas import tpu as pltpu
from jax.sharding import PartitionSpec as P

HEAD_DIM = 64
LANES = 128
IDS = 9
EPS = 1e-05
NEG = -1e30
SCALE = HEAD_DIM ** (-0.5)
F32 = jnp.float32
BF16 = jnp.bfloat16
NT = (((1,), (1,)), ((), ()))
NN = (((1,), (0,)), ((), ()))
TN = (((0,), (0,)), ((), ()))


def mxu(left, right, dims):
    return lax.dot_general(left, right, dims, preferred_element_type=F32)


def layer_norm(inputs, norm_gain, norm_shift):
    row_mean = jnp.mean(inputs, -1, keepdims=True)
    centred = inputs - row_mean
    spread = jnp.mean(centred * centred, -1, keepdims=True)
    return centred * lax.rsqrt(spread + EPS) * norm_gain + norm_shift


def exact_gelu(inputs):
    return jax.nn.gelu(inputs, approximate=False)


def norm_back(inputs, norm_gain, norm_shift, cotangent):
    _, pullback = jax.vjp(layer_norm, inputs, norm_gain, norm_shift)
    return pullback(cotangent)


def project(rows, weight):
    return mxu(rows, weight, NN)


def back_project(grad, weight):
    return mxu(grad, weight, NT)


def weight_grad(rows, grad):
    return mxu(rows, grad, TN).astype(BF16)


def attend_kernel(causal, first_ref, q_ref, k_ref, v_ref, qa_ref, ka_ref, o_ref, lse_ref):
    rows = q_ref.shape[0]
    keys = k_ref.shape[0]
    block = min(rows, 256)
    low_half = lax.broadcasted_iota(jnp.int32, (1, LANES), 1) < HEAD_DIM
    key_block = k_ref[...]
    key_mark = ka_ref[...]
    values = v_ref[...]
    for start in range(0, rows, block):
        query = q_ref[pl.ds(start, block), :] * BF16(SCALE)
        query_mark = qa_ref[pl.ds(start, block), :]
        halves = []
        lses = []
        for head in range(2):
            keep = low_half if head == 0 else jnp.logical_not(low_half)
            scores = mxu(
                jnp.where(keep, query, query_mark), jnp.where(keep, key_block, key_mark), NT
            )
            if causal:
                place = (
                    first_ref[0] + start + lax.broadcasted_iota(jnp.int32, (block, keys), 0)
                )
                scores = jnp.where(
                    lax.broadcasted_iota(jnp.int32, (block, keys), 1) <= place, scores, NEG
                )
            top = jnp.max(scores, -1, keepdims=True)
            weights = jnp.exp(scores - top)
            total = jnp.sum(weights, -1, keepdims=True)
            mixed = mxu(weights.astype(BF16), values, NN)
            halves.append(mixed / total)
            lses.append(top + jnp.log(total))
        o_ref[pl.ds(start, block), :] = jnp.where(low_half, halves[0], halves[1]).astype(BF16)
        both = jnp.where(low_half, lses[0], lses[1])
        turned = both.T
        lse_ref[0, 0:1, pl.ds(start, block)] = turned[0:1]
        lse_ref[0, 1:2, pl.ds(start, block)] = turned[HEAD_DIM : HEAD_DIM + 1]


def attend(queries, keys, values, query_mark, key_mark, first_row, causal):
    rows, width = queries.shape
    key_rows = keys.shape[0]
    pairs = width // LANES
    return pl.pallas_call(
        functools.partial(attend_kernel, causal),
        grid_spec=pltpu.PrefetchScalarGridSpec(
            num_scalar_prefetch=1,
            grid=(pairs,),
            in_specs=[
                pl.BlockSpec((rows, LANES), lambda p, first: (0, p)),
                pl.BlockSpec((key_rows, LANES), lambda p, first: (0, p)),
                pl.BlockSpec((key_rows, LANES), lambda p, first: (0, p)),
                pl.BlockSpec((rows, LANES), lambda p, first: (0, 0)),
                pl.BlockSpec((key_rows, LANES), lambda p, first: (0, 0)),
            ],
            out_specs=[
                pl.BlockSpec((rows, LANES), lambda p, first: (0, p)),
                pl.BlockSpec((1, 2, rows), lambda p, first: (p, 0, 0)),
            ],
        ),
        out_shape=[
            jax.ShapeDtypeStruct((rows, width), BF16),
            jax.ShapeDtypeStruct((pairs, 2, rows), F32),
        ],
        compiler_params=pltpu.CompilerParams(vmem_limit_bytes=40 << 20),
        cost_estimate=pl.CostEstimate(
            flops=4 * rows * key_rows * width * 2,
            bytes_accessed=4 * rows * width + 4 * key_rows * width,
            transcendentals=rows * key_rows * width // HEAD_DIM,
        ),
        name="attend",
    )(first_row, queries, keys, values, query_mark, key_mark)


def attend_back_kernel(
    causal,
    first_ref,
    q_ref,
    k_ref,
    v_ref,
    qa_ref,
    ka_ref,
    lse_ref,
    o_ref,
    do_ref,
    dq_ref,
    dk_ref,
    dv_ref,
    dk_acc,
    dv_acc,
):
    rows = q_ref.shape[0]
    keys = k_ref.shape[0]
    block = min(rows, 256)
    low_half = lax.broadcasted_iota(jnp.int32, (1, LANES), 1) < HEAD_DIM
    key_block = k_ref[...]
    key_mark = ka_ref[...]
    values = v_ref[...]
    zero = jnp.zeros((), BF16)
    dk_acc[...] = jnp.zeros_like(dk_acc)
    dv_acc[...] = jnp.zeros_like(dv_acc)
    for start in range(0, rows, block):
        span = pl.ds(start, block)
        query = q_ref[span, :] * BF16(SCALE)
        query_mark = qa_ref[span, :]
        d_out = do_ref[span, :]
        inner = (d_out.astype(F32) * o_ref[span, :].astype(F32)).T
        d_query = None
        for head in range(2):
            keep = low_half if head == 0 else jnp.logical_not(low_half)
            delta = jnp.sum(
                inner[head * HEAD_DIM : (head + 1) * HEAD_DIM], axis=0, keepdims=True
            )
            scores = mxu(
                jnp.where(keep, key_block, key_mark), jnp.where(keep, query, query_mark), NT
            )
            if causal:
                place = (
                    first_ref[0] + start + lax.broadcasted_iota(jnp.int32, (keys, block), 1)
                )
                scores = jnp.where(
                    lax.broadcasted_iota(jnp.int32, (keys, block), 0) <= place, scores, NEG
                )
            probs = jnp.exp(scores - lse_ref[0, head : head + 1, span])
            own_out = jnp.where(keep, d_out, zero)
            d_probs = mxu(values, own_out, NT)
            d_scores = (probs * (d_probs - delta)).astype(BF16)
            dv_acc[...] += mxu(probs.astype(BF16), own_out, NN)
            dk_acc[...] += mxu(d_scores, jnp.where(keep, query, zero), NN)
            term = mxu(jnp.where(keep, key_block, zero), d_scores, TN)
            d_query = term if d_query is None else d_query + term
        dq_ref[span, :] = (d_query * SCALE).T.astype(BF16)
    dk_ref[...] = dk_acc[...].astype(BF16)
    dv_ref[...] = dv_acc[...].astype(BF16)


def attend_back(
    queries, keys, values, query_mark, key_mark, first_row, causal, log_total, mixed, d_mixed
):
    rows, width = queries.shape
    key_rows = keys.shape[0]
    pairs = width // LANES
    row_spec = pl.BlockSpec((rows, LANES), lambda p, first: (0, p))
    key_spec = pl.BlockSpec((key_rows, LANES), lambda p, first: (0, p))
    return pl.pallas_call(
        functools.partial(attend_back_kernel, causal),
        grid_spec=pltpu.PrefetchScalarGridSpec(
            num_scalar_prefetch=1,
            grid=(pairs,),
            in_specs=[
                row_spec,
                key_spec,
                key_spec,
                pl.BlockSpec((rows, LANES), lambda p, first: (0, 0)),
                pl.BlockSpec((key_rows, LANES), lambda p, first: (0, 0)),
                pl.BlockSpec((1, 2, rows), lambda p, first: (p, 0, 0)),
                row_spec,
                row_spec,
            ],
            out_specs=[row_spec, key_spec, key_spec],
            scratch_shapes=[
                pltpu.VMEM((key_rows, LANES), F32),
                pltpu.VMEM((key_rows, LANES), F32),
            ],
        ),
        out_shape=[
            jax.ShapeDtypeStruct((rows, width), BF16),
            jax.ShapeDtypeStruct((key_rows, width), BF16),
            jax.ShapeDtypeStruct((key_rows, width), BF16),
        ],
        compiler_params=pltpu.CompilerParams(vmem_limit_bytes=40 << 20),
        cost_estimate=pl.CostEstimate(
            flops=10 * rows * key_rows * width * 2,
            bytes_accessed=8 * rows * width + 8 * key_rows * width,
            transcendentals=rows * key_rows * width // HEAD_DIM,
        ),
        name="attend_back",
    )(first_row, queries, keys, values, query_mark, key_mark, log_total, mixed, d_mixed)


class Layout:
    def __init__(self, slots):
        self.tensor = lax.axis_size("tensor")
        self.seq = lax.axis_size("seq")
        self.slots = slots
        self.spread = self.tensor // slots
        self.place = lax.axis_index("tensor")
        self.half = lax.axis_index("seq")
        self.row_groups = [
            [j * slots + u for u in range(slots)] for j in range(self.spread)
        ]
        self.slot_groups = [
            [j * slots + u for j in range(self.spread)] for u in range(slots)
        ]

    def to_slots(self, block):
        rows = lax.all_to_all(
            block, "tensor", 0, 1, axis_index_groups=self.row_groups, tiled=True
        )
        return rows.reshape(-1, block.shape[2])

    def from_slots(self, rows):
        block = rows.reshape(1, rows.shape[0], rows.shape[1])
        return lax.all_to_all(
            block, "tensor", 1, 0, axis_index_groups=self.row_groups, tiled=True
        )

    def gather_keys(self, rows):
        if self.spread > 1:
            rows = lax.all_gather(
                rows, "tensor", axis=0, axis_index_groups=self.slot_groups, tiled=True
            )
        return lax.all_gather(rows, "seq", axis=0, tiled=True)

    def scatter_keys(self, rows):
        rows = lax.psum_scatter(rows, "seq", scatter_dimension=0, tiled=True)
        if self.spread > 1:
            rows = lax.psum_scatter(
                rows,
                "tensor",
                scatter_dimension=0,
                axis_index_groups=self.slot_groups,
                tiled=True,
            )
        return rows

    def gather_weight(self, shard):
        part = shard.shape[0] // self.seq
        own = lax.dynamic_slice_in_dim(shard, self.half * part, part, 0)
        return lax.all_gather(own, ("tensor", "seq"), axis=0, tiled=True)

    def gather_columns(self, shard):
        depth, blocks, own = shard.shape
        whole = self.gather_weight(shard.reshape(depth, blocks * own))
        whole = whole.reshape(self.tensor, depth, blocks, own)
        return jnp.transpose(whole, (1, 2, 0, 3)).reshape(depth, blocks * self.tensor * own)

    def reduce_rows(self, gradient):
        rows, width = gradient.shape
        parts = gradient.reshape(self.tensor, rows // self.tensor, self.seq, width // self.seq)
        parts = jnp.transpose(parts, (2, 0, 1, 3)).reshape(
            self.seq * rows, width // self.seq
        )
        return self.reduce(parts)

    def reduce_columns(self, gradient, blocks):
        depth, width = gradient.shape
        own = width // blocks // self.tensor
        parts = gradient.reshape(self.seq, depth // self.seq, blocks, self.tensor, own)
        parts = jnp.transpose(parts, (0, 3, 1, 2, 4)).reshape(
            self.seq * self.tensor * depth // self.seq, blocks * own
        )
        return self.reduce(parts).reshape(depth // self.seq, blocks, own)

    def reduce(self, parts):
        own = lax.psum_scatter(parts, ("seq", "tensor"), scatter_dimension=0, tiled=True)
        return lax.psum(own, "dp").astype(F32)


def local(
    source,
    target,
    out_grad,
    source_segments,
    target_segments,
    enc_gain,
    enc_shift,
    enc_qkv,
    enc_proj,
    enc_up,
    enc_down,
    dec_gain,
    dec_shift,
    dec_self_qkv,
    dec_self_proj,
    dec_cross_q,
    dec_cross_kv,
    dec_cross_proj,
    dec_up,
    dec_down,
):
    width = source.shape[2]
    lay = Layout(source.shape[0])
    w_enc_qkv = lay.gather_columns(enc_qkv)
    w_self_qkv = lay.gather_columns(dec_self_qkv)
    w_enc_proj = lay.gather_weight(enc_proj)
    w_self_proj = lay.gather_weight(dec_self_proj)
    w_enc_up = lay.gather_columns(enc_up[:, None])
    w_enc_down = lay.gather_weight(enc_down)
    w_cross_q = lay.gather_columns(dec_cross_q[:, None])
    w_cross_kv = lay.gather_columns(dec_cross_kv)
    w_cross_proj = lay.gather_weight(dec_cross_proj)
    w_dec_up = lay.gather_columns(dec_up[:, None])
    w_dec_down = lay.gather_weight(dec_down)
    slot = lax.rem(lay.place, lay.slots)
    rows = source.shape[1] * lay.slots
    first_row = (lay.half * lay.spread + lay.place // lay.slots) * rows
    source_ids = lax.dynamic_index_in_dim(source_segments, slot, 0, keepdims=False)
    target_ids = lax.dynamic_index_in_dim(target_segments, slot, 0, keepdims=False)
    ids = jnp.arange(LANES, dtype=jnp.int32) % HEAD_DIM
    own_source = lax.dynamic_slice_in_dim(source_ids, first_row, rows, 0)
    own_target = lax.dynamic_slice_in_dim(target_ids, first_row, rows, 0)
    source_query = jnp.where(own_source[:, None] == ids[None], NEG, 0.0).astype(BF16)
    target_query = jnp.where(own_target[:, None] == ids[None], NEG, 0.0).astype(BF16)
    counted = ids[None] < IDS
    source_key = ((source_ids[:, None] != ids[None]) & counted).astype(BF16)
    target_key = ((target_ids[:, None] != ids[None]) & counted).astype(BF16)
    first = first_row[None].astype(jnp.int32)

    x_source = lay.to_slots(source).astype(F32)
    x_target = lay.to_slots(target).astype(F32)
    cotangent = lay.to_slots(out_grad).astype(F32)

    rows_a = layer_norm(x_source, enc_gain[0], enc_shift[0]).astype(BF16)
    qkv_a = project(rows_a, w_enc_qkv).astype(BF16)
    query_a = qkv_a[:, :width]
    pairs_a = lay.gather_keys(qkv_a[:, width:])
    mixed_a, total_a = attend(
        query_a, pairs_a[:, :width], pairs_a[:, width:], source_query, source_key, first, False
    )
    hidden = x_source + project(mixed_a, w_enc_proj)
    rows_c = layer_norm(x_target, dec_gain[0], dec_shift[0]).astype(BF16)
    qkv_c = project(rows_c, w_self_qkv).astype(BF16)
    query_c = qkv_c[:, :width]
    pairs_c = lay.gather_keys(qkv_c[:, width:])
    mixed_c, total_c = attend(
        query_c, pairs_c[:, :width], pairs_c[:, width:], target_query, target_key, first, True
    )
    after_self = x_target + project(mixed_c, w_self_proj)
    rows_b = layer_norm(hidden, enc_gain[1], enc_shift[1]).astype(BF16)
    inner_b = project(rows_b, w_enc_up)
    active_b = exact_gelu(inner_b).astype(BF16)
    encoded = hidden + project(active_b, w_enc_down)
    rows_m = layer_norm(encoded, enc_gain[2], enc_shift[2]).astype(BF16)
    pairs_m = lay.gather_keys(project(rows_m, w_cross_kv).astype(BF16))
    rows_e = layer_norm(after_self, dec_gain[1], dec_shift[1]).astype(BF16)
    query_e = project(rows_e, w_cross_q).astype(BF16)
    mixed_e, total_e = attend(
        query_e, pairs_m[:, :width], pairs_m[:, width:], target_query, source_key, first, False
    )
    after_cross = after_self + project(mixed_e, w_cross_proj)
    rows_f = layer_norm(after_cross, dec_gain[2], dec_shift[2]).astype(BF16)
    inner_f = project(rows_f, w_dec_up)
    active_f = exact_gelu(inner_f).astype(BF16)
    final_rows = after_cross + project(active_f, w_dec_down)
    decoded, final_back = jax.vjp(layer_norm, final_rows, dec_gain[3], dec_shift[3])

    d_final, dec_gain_three, dec_shift_three = final_back(cotangent)

    def ffn_back(d_out, rows_in, inner, active, weight_up, weight_down):
        d_low = d_out.astype(BF16)
        grad_down = lay.reduce_rows(weight_grad(active, d_low))
        d_active = back_project(d_low, weight_down)
        _, gelu_back = jax.vjp(exact_gelu, inner)
        d_inner = gelu_back(d_active)[0].astype(BF16)
        grad_up = lay.reduce_columns(weight_grad(rows_in, d_inner), 1)[:, 0]
        return back_project(d_inner, weight_up), grad_up, grad_down

    d_normed, grad_dec_up, grad_dec_down = ffn_back(
        d_final, rows_f, inner_f, active_f, w_dec_up, w_dec_down
    )
    d_input, dec_gain_two, dec_shift_two = norm_back(
        after_cross, dec_gain[2], dec_shift[2], d_normed
    )
    d_cross = d_final + d_input
    d_low = d_cross.astype(BF16)
    grad_cross_proj = lay.reduce_rows(weight_grad(mixed_e, d_low))
    d_mixed = back_project(d_low, w_cross_proj).astype(BF16)
    d_query, d_keys, d_values = attend_back(
        query_e,
        pairs_m[:, :width],
        pairs_m[:, width:],
        target_query,
        source_key,
        first,
        False,
        total_e,
        mixed_e,
        d_mixed,
    )
    d_pairs = lay.scatter_keys(jnp.concatenate([d_keys, d_values], 1))
    grad_cross_q = lay.reduce_columns(weight_grad(rows_e, d_query), 1)[:, 0]
    grad_cross_kv = lay.reduce_columns(weight_grad(rows_m, d_pairs), 2)
    d_normed = back_project(d_query, w_cross_q)
    d_memory = back_project(d_pairs, w_cross_kv)
    d_input, dec_gain_one, dec_shift_one = norm_back(
        after_self, dec_gain[1], dec_shift[1], d_normed
    )
    d_self = d_cross + d_input
    d_encoded, enc_gain_two, enc_shift_two = norm_back(encoded, enc_gain[2], enc_shift[2], d_memory)
    d_normed, grad_enc_up, grad_enc_down = ffn_back(
        d_encoded, rows_b, inner_b, active_b, w_enc_up, w_enc_down
    )
    d_input, enc_gain_one, enc_shift_one = norm_back(hidden, enc_gain[1], enc_shift[1], d_normed)
    d_hidden = d_encoded + d_input

    def self_back(d_out, rows_in, query, pairs, marks, causal, totals, mixed, w_qkv, w_proj):
        d_low = d_out.astype(BF16)
        grad_proj = lay.reduce_rows(weight_grad(mixed, d_low))
        d_mixed = back_project(d_low, w_proj).astype(BF16)
        d_query, d_keys, d_values = attend_back(
            query,
            pairs[:, :width],
            pairs[:, width:],
            marks[0],
            marks[1],
            first,
            causal,
            totals,
            mixed,
            d_mixed,
        )
        d_pairs = lay.scatter_keys(jnp.concatenate([d_keys, d_values], 1))
        d_qkv = jnp.concatenate([d_query, d_pairs], 1)
        grad_qkv = lay.reduce_columns(weight_grad(rows_in, d_qkv), 3)
        return back_project(d_qkv, w_qkv), grad_qkv, grad_proj

    d_normed, grad_self_qkv, grad_self_proj = self_back(
        d_self,
        rows_c,
        query_c,
        pairs_c,
        (target_query, target_key),
        True,
        total_c,
        mixed_c,
        w_self_qkv,
        w_self_proj,
    )
    d_input, dec_gain_zero, dec_shift_zero = norm_back(
        x_target, dec_gain[0], dec_shift[0], d_normed
    )
    target_grad = d_self + d_input
    d_normed, grad_enc_qkv, grad_enc_proj = self_back(
        d_hidden,
        rows_a,
        query_a,
        pairs_a,
        (source_query, source_key),
        False,
        total_a,
        mixed_a,
        w_enc_qkv,
        w_enc_proj,
    )
    d_input, enc_gain_zero, enc_shift_zero = norm_back(
        x_source, enc_gain[0], enc_shift[0], d_normed
    )
    source_grad = d_hidden + d_input
    norms = jnp.stack(
        [
            enc_gain_zero,
            enc_gain_one,
            enc_gain_two,
            enc_shift_zero,
            enc_shift_one,
            enc_shift_two,
            dec_gain_zero,
            dec_gain_one,
            dec_gain_two,
            dec_gain_three,
            dec_shift_zero,
            dec_shift_one,
            dec_shift_two,
            dec_shift_three,
        ]
    )
    part = width // lay.seq
    norms = lax.dynamic_slice_in_dim(
        lax.psum(norms, ("dp", "seq", "tensor")), lay.half * part, part, 1
    )
    return (
        lay.from_slots(decoded.astype(BF16)),
        lay.from_slots(source_grad.astype(BF16)).astype(F32),
        lay.from_slots(target_grad.astype(BF16)).astype(F32),
        norms[0:3],
        norms[3:6],
        grad_enc_qkv,
        grad_enc_proj,
        grad_enc_up,
        grad_enc_down,
        norms[6:10],
        norms[10:14],
        grad_self_qkv,
        grad_self_proj,
        grad_cross_q,
        grad_cross_kv,
        grad_cross_proj,
        grad_dec_up,
        grad_dec_down,
    )


def swap_pairs(count, bit):
    return [(i, i ^ bit) for i in range(count)]


def norm_parts(inputs):
    centred = inputs - jnp.mean(inputs, -1, keepdims=True)
    scale = lax.rsqrt(jnp.mean(centred * centred, -1, keepdims=True) + EPS)
    return centred * scale, scale


def norm_pull(hat, scale, gain, cotangent):
    tilted = cotangent * gain
    return scale * (
        tilted
        - jnp.mean(tilted, -1, keepdims=True)
        - hat * jnp.mean(tilted * hat, -1, keepdims=True)
    )


ROW_BLOCK = 256
VMEM = 56 << 20


def row_call(kernel, inputs, vectors, outs, sums, name):
    rows, width = inputs[0].shape
    block = pl.BlockSpec((ROW_BLOCK, width), lambda i: (i, 0))
    whole = pl.BlockSpec((1, width), lambda i: (0, 0))
    return pl.pallas_call(
        kernel,
        grid=(rows // ROW_BLOCK,),
        in_specs=[block] * len(inputs) + [whole] * len(vectors),
        out_specs=[block] * len(outs) + [whole] * sums,
        out_shape=[jax.ShapeDtypeStruct((rows, width), kind) for kind in outs]
        + [jax.ShapeDtypeStruct((1, width), F32)] * sums,
        compiler_params=pltpu.CompilerParams(vmem_limit_bytes=VMEM),
        cost_estimate=pl.CostEstimate(
            flops=20 * rows * width,
            bytes_accessed=4 * rows * width * (len(inputs) + len(outs)),
            transcendentals=rows,
        ),
        name=name,
    )(*inputs, *vectors)


def norm_kernel(x_ref, gain_ref, shift_ref, low_ref):
    hat, _ = norm_parts(x_ref[...].astype(F32))
    low_ref[...] = (hat * gain_ref[...] + shift_ref[...]).astype(BF16)


def norm_rows(inputs, gain, shift):
    return row_call(norm_kernel, [inputs], [gain, shift], [BF16], 0, "norm_rows")[0]


def add_norm_kernel(x_ref, own_ref, other_ref, gain_ref, shift_ref, sum_ref, low_ref):
    total = (
        x_ref[...].astype(F32) + own_ref[...].astype(F32) + other_ref[...].astype(F32)
    )
    sum_ref[...] = total
    hat, _ = norm_parts(total)
    low_ref[...] = (hat * gain_ref[...] + shift_ref[...]).astype(BF16)


def add_norm(inputs, own, other, gain, shift):
    return row_call(
        add_norm_kernel, [inputs, own, other], [gain, shift], [F32, BF16], 0, "add_norm"
    )


def add_sums(first, gain_out, shift_out, cotangent, hat):
    @pl.when(first)
    def _():
        gain_out[...] = jnp.zeros_like(gain_out)
        shift_out[...] = jnp.zeros_like(shift_out)

    gain_out[...] += jnp.sum(cotangent * hat, 0, keepdims=True)
    shift_out[...] += jnp.sum(cotangent, 0, keepdims=True)


def last_norm_kernel(
    x_ref, own_ref, other_ref, cot_ref, gain_ref, shift_ref, y_ref, d_ref, low_ref, dg_ref, ds_ref
):
    total = (
        x_ref[...].astype(F32) + own_ref[...].astype(F32) + other_ref[...].astype(F32)
    )
    hat, scale = norm_parts(total)
    y_ref[...] = (hat * gain_ref[...] + shift_ref[...]).astype(BF16)
    cotangent = cot_ref[...].astype(F32)
    d_total = norm_pull(hat, scale, gain_ref[...], cotangent)
    d_ref[...] = d_total
    low_ref[...] = d_total.astype(BF16)
    add_sums(pl.program_id(0) == 0, dg_ref, ds_ref, cotangent, hat)


def last_norm(inputs, own, other, cotangent, gain, shift):
    return row_call(
        last_norm_kernel,
        [inputs, own, other, cotangent],
        [gain, shift],
        [BF16, F32, BF16],
        2,
        "last_norm",
    )


def norm_back_kernel(residual, low, *refs):
    x_ref, own_ref, other_ref = refs[:3]
    refs = refs[3:]
    if residual:
        res_ref, refs = refs[0], refs[1:]
    gain_ref, refs = refs[0], refs[1:]
    hat, scale = norm_parts(x_ref[...].astype(F32))
    cotangent = own_ref[...].astype(F32) + other_ref[...].astype(F32)
    d_total = norm_pull(hat, scale, gain_ref[...], cotangent)
    if residual:
        d_total = d_total + res_ref[...]
    refs[0][...] = d_total.astype(refs[0].dtype)
    if low:
        refs[1][...] = d_total.astype(BF16)
    add_sums(pl.program_id(0) == 0, refs[-2], refs[-1], cotangent, hat)


def norm_back_rows(inputs, own, other, gain, residual, kinds):
    return row_call(
        functools.partial(norm_back_kernel, residual is not None, len(kinds) > 1),
        [inputs, own, other] + ([] if residual is None else [residual]),
        [gain],
        kinds,
        2,
        "norm_back",
    )


def chip_attend_kernel(causal, q_ref, k_ref, v_ref, qa_ref, ka_ref, o_ref, lse_ref):
    rows = q_ref.shape[0]
    block = 256
    low_half = lax.broadcasted_iota(jnp.int32, (1, LANES), 1) < HEAD_DIM
    for start in range(0, rows, block):
        keys = start + block if causal else k_ref.shape[0]
        query = q_ref[pl.ds(start, block), :] * BF16(SCALE)
        query_mark = qa_ref[pl.ds(start, block), :]
        key_block = k_ref[:keys, :]
        key_mark = ka_ref[:keys, :]
        values = v_ref[:keys, :]
        halves = []
        lses = []
        for head in range(2):
            keep = low_half if head == 0 else jnp.logical_not(low_half)
            scores = mxu(
                jnp.where(keep, query, query_mark), jnp.where(keep, key_block, key_mark), NT
            )
            if causal:
                scores = jnp.where(
                    lax.broadcasted_iota(jnp.int32, (block, keys), 1)
                    <= start + lax.broadcasted_iota(jnp.int32, (block, keys), 0),
                    scores,
                    NEG,
                )
            top = jnp.max(scores, -1, keepdims=True)
            weights = jnp.exp(scores - top)
            total = jnp.sum(weights, -1, keepdims=True)
            mixed = mxu(weights.astype(BF16), values, NN)
            halves.append(mixed / total)
            lses.append(top + jnp.log(total))
        o_ref[pl.ds(start, block), :] = jnp.where(low_half, halves[0], halves[1]).astype(BF16)
        turned = jnp.where(low_half, lses[0], lses[1]).T
        lse_ref[0, 0:1, pl.ds(start, block)] = turned[0:1]
        lse_ref[0, 1:2, pl.ds(start, block)] = turned[HEAD_DIM : HEAD_DIM + 1]


def pair_spec(rows, stride, offset):
    return pl.BlockSpec((rows, LANES), lambda p: (0, stride * p + offset))


def chip_attend(queries, q_at, pairs, k_at, v_at, query_mark, key_mark, causal):
    rows = queries.shape[0]
    keys = pairs.shape[0]
    count = queries.shape[1] // LANES // q_at[0]
    return pl.pallas_call(
        functools.partial(chip_attend_kernel, causal),
        grid=(count,),
        in_specs=[
            pair_spec(rows, *q_at),
            pair_spec(keys, *k_at),
            pair_spec(keys, *v_at),
            pl.BlockSpec((rows, LANES), lambda p: (0, 0)),
            pl.BlockSpec((keys, LANES), lambda p: (0, 0)),
        ],
        out_specs=[
            pair_spec(rows, 1, 0),
            pl.BlockSpec((1, 2, rows), lambda p: (p, 0, 0)),
        ],
        out_shape=[
            jax.ShapeDtypeStruct((rows, count * LANES), BF16),
            jax.ShapeDtypeStruct((count, 2, rows), F32),
        ],
        compiler_params=pltpu.CompilerParams(vmem_limit_bytes=VMEM),
        cost_estimate=pl.CostEstimate(
            flops=8 * rows * keys * count * LANES,
            bytes_accessed=16 * rows * count * LANES,
            transcendentals=2 * rows * keys * count,
        ),
        name="attend",
    )(queries, pairs, pairs, query_mark, key_mark)


def chip_attend_back_kernel(causal, fused, *refs):
    q_ref, k_ref, v_ref, qa_ref, ka_ref, lse_ref, o_ref, do_ref = refs[:8]
    outs, (dk_acc, dv_acc) = refs[8:-2], refs[-2:]
    rows = q_ref.shape[0]
    block = 256
    low_half = lax.broadcasted_iota(jnp.int32, (1, LANES), 1) < HEAD_DIM
    zero = jnp.zeros((), BF16)
    dk_acc[...] = jnp.zeros_like(dk_acc)
    dv_acc[...] = jnp.zeros_like(dv_acc)
    for start in range(0, rows, block):
        keys = start + block if causal else k_ref.shape[0]
        span = pl.ds(start, block)
        query = q_ref[span, :] * BF16(SCALE)
        query_mark = qa_ref[span, :]
        key_block = k_ref[:keys, :]
        key_mark = ka_ref[:keys, :]
        values = v_ref[:keys, :]
        d_out = do_ref[span, :]
        inner = (d_out.astype(F32) * o_ref[span, :].astype(F32)).T
        d_query = None
        for head in range(2):
            keep = low_half if head == 0 else jnp.logical_not(low_half)
            delta = jnp.sum(
                inner[head * HEAD_DIM : (head + 1) * HEAD_DIM], axis=0, keepdims=True
            )
            scores = mxu(
                jnp.where(keep, key_block, key_mark), jnp.where(keep, query, query_mark), NT
            )
            if causal:
                scores = jnp.where(
                    lax.broadcasted_iota(jnp.int32, (keys, block), 0)
                    <= start + lax.broadcasted_iota(jnp.int32, (keys, block), 1),
                    scores,
                    NEG,
                )
            probs = jnp.exp(scores - lse_ref[0, head : head + 1, span])
            own_out = jnp.where(keep, d_out, zero)
            d_probs = mxu(values, own_out, NT)
            d_scores = (probs * (d_probs - delta)).astype(BF16)
            dv_acc[:keys, :] += mxu(probs.astype(BF16), own_out, NN)
            dk_acc[:keys, :] += mxu(d_scores, jnp.where(keep, query, zero), NN)
            term = mxu(jnp.where(keep, key_block, zero), d_scores, TN)
            d_query = term if d_query is None else d_query + term
        outs[0][span, :LANES] = (d_query * SCALE).T.astype(BF16)
    if fused:
        outs[0][:, LANES : 2 * LANES] = dk_acc[...].astype(BF16)
        outs[0][:, 2 * LANES :] = dv_acc[...].astype(BF16)
    else:
        outs[1][:, :LANES] = dk_acc[...].astype(BF16)
        outs[1][:, LANES:] = dv_acc[...].astype(BF16)


def chip_attend_back(
    queries, q_at, pairs, k_at, v_at, query_mark, key_mark, causal, log_total, mixed, d_mixed, fused
):
    rows = queries.shape[0]
    keys = pairs.shape[0]
    count = mixed.shape[1] // LANES

    def out(rows, blocks):
        return (
            pl.BlockSpec((rows, blocks * LANES), lambda p: (0, p)),
            jax.ShapeDtypeStruct((rows, count * blocks * LANES), BF16),
        )

    outs = [out(rows, 3)] if fused else [out(rows, 1), out(keys, 2)]
    return pl.pallas_call(
        functools.partial(chip_attend_back_kernel, causal, fused),
        grid=(count,),
        in_specs=[
            pair_spec(rows, *q_at),
            pair_spec(keys, *k_at),
            pair_spec(keys, *v_at),
            pl.BlockSpec((rows, LANES), lambda p: (0, 0)),
            pl.BlockSpec((keys, LANES), lambda p: (0, 0)),
            pl.BlockSpec((1, 2, rows), lambda p: (p, 0, 0)),
            pair_spec(rows, 1, 0),
            pair_spec(rows, 1, 0),
        ],
        out_specs=[spec for spec, _ in outs],
        out_shape=[shape for _, shape in outs],
        scratch_shapes=[pltpu.VMEM((keys, LANES), F32), pltpu.VMEM((keys, LANES), F32)],
        compiler_params=pltpu.CompilerParams(vmem_limit_bytes=VMEM),
        cost_estimate=pl.CostEstimate(
            flops=20 * rows * keys * count * LANES,
            bytes_accessed=32 * rows * count * LANES,
            transcendentals=2 * rows * keys * count,
        ),
        name="attend_back",
    )(queries, pairs, pairs, query_mark, key_mark, log_total, mixed, d_mixed)


def gelu_kernel(x_ref, w_ref, act_ref, slope_ref):
    inner = mxu(x_ref[...], w_ref[...], NN)
    below = 0.5 + 0.5 * lax.erf(inner * (0.5**0.5))
    act_ref[...] = (inner * below).astype(BF16)
    bell = jnp.exp(inner * inner * (-0.5)) * (0.5 / jnp.pi) ** 0.5
    slope_ref[...] = (below + inner * bell).astype(BF16)


def up_gelu(rows_in, weight):
    rows, depth = rows_in.shape
    width = weight.shape[1]
    step = 256
    return pl.pallas_call(
        gelu_kernel,
        grid=(width // step,),
        in_specs=[
            pl.BlockSpec((rows, depth), lambda j: (0, 0)),
            pl.BlockSpec((depth, step), lambda j: (0, j)),
        ],
        out_specs=[pl.BlockSpec((rows, step), lambda j: (0, j))] * 2,
        out_shape=[jax.ShapeDtypeStruct((rows, width), BF16)] * 2,
        compiler_params=pltpu.CompilerParams(vmem_limit_bytes=VMEM),
        cost_estimate=pl.CostEstimate(
            flops=2 * rows * depth * width,
            bytes_accessed=2 * (rows + width) * depth + 4 * rows * width,
            transcendentals=2 * rows * width,
        ),
        name="up_gelu",
    )(rows_in, weight)


def weight_kernel(count, *refs):
    out_ref = refs[-1]
    at = 0
    for i in range(count):
        own = refs[i].shape[1]
        out_ref[pl.ds(at, own), :] = mxu(refs[i][...], refs[count + i][...], TN).astype(BF16)
        at += own


def weight_grads(pairs, part):
    rows, width = pairs[0][1].shape
    owns = [hidden.shape[1] // 4 for hidden, _ in pairs]
    return pl.pallas_call(
        functools.partial(weight_kernel, len(pairs)),
        grid=(2,),
        in_specs=[
            pl.BlockSpec((rows, own), lambda i: (0, 2 * part + i)) for own in owns
        ]
        + [pl.BlockSpec((rows, width), lambda i: (0, 0)) for _ in pairs],
        out_specs=pl.BlockSpec((sum(owns), width), lambda i: (i, 0)),
        out_shape=jax.ShapeDtypeStruct((2 * sum(owns), width), BF16),
        compiler_params=pltpu.CompilerParams(vmem_limit_bytes=VMEM),
        cost_estimate=pl.CostEstimate(
            flops=4 * sum(owns) * width * rows,
            bytes_accessed=4 * sum(owns) * (width + rows) + 2 * len(pairs) * rows * width,
            transcendentals=0,
        ),
        name="weight_grads",
    )(*[hidden for hidden, _ in pairs], *[wide for _, wide in pairs])


CROSS = ("seq", "tensor")


class Chip:
    def __init__(self):
        self.core = lax.axis_index("seq")
        self.place = lax.axis_index("tensor")
        self.line = lax.axis_index("dp")
        self.first = [(i, i ^ 1) for i in range(4)] + [(4 + i, 4 + (i ^ 2)) for i in range(4)]
        self.second = [(i, i ^ 2) for i in range(4)] + [(4 + i, 4 + (i ^ 1)) for i in range(4)]

    def other(self, block):
        return lax.ppermute(block, "seq", swap_pairs(2, 1))

    def gather(self, block):
        near = lax.ppermute(block, CROSS, self.first)
        side = lax.ppermute(block, CROSS, self.second)
        far = lax.ppermute(side, CROSS, self.first)
        return [block, side, near, far]

    def ordered(self, own, other, index):
        first = index == 0
        return jnp.concatenate([jnp.where(first, own, other), jnp.where(first, other, own)], 0)

    def to_slot(self, block):
        rows = lax.all_to_all(block, "tensor", 0, 0, tiled=True)
        rows = rows.reshape(-1, block.shape[2])
        return self.ordered(rows, self.other(rows), self.core)

    def from_slot(self, rows):
        half = rows.shape[0] // 2
        own = lax.dynamic_slice_in_dim(rows, self.core * half, half, 0)
        return lax.all_to_all(own.reshape(4, half // 4, -1), "tensor", 0, 0, tiled=True)

    def send_near(self, block):
        return lax.ppermute(block, CROSS, self.first)

    def send_side(self, block):
        return lax.ppermute(block, CROSS, self.second)

    def split(self, block, index):
        half = block.shape[0] // 2
        return (
            lax.dynamic_slice_in_dim(block, index * half, half, 0),
            lax.dynamic_slice_in_dim(block, (1 - index) * half, half, 0),
        )

    def along(self, block, bit):
        return lax.ppermute(block, "dp", swap_pairs(4, bit))


def add_low(left, right):
    return (left.astype(F32) + right.astype(F32)).astype(BF16)


def chip_local(
    source,
    target,
    out_grad,
    source_segments,
    target_segments,
    enc_gain,
    enc_shift,
    enc_qkv,
    enc_proj,
    enc_up,
    enc_down,
    dec_gain,
    dec_shift,
    dec_self_qkv,
    dec_self_proj,
    dec_cross_q,
    dec_cross_kv,
    dec_cross_proj,
    dec_up,
    dec_down,
):
    chip = Chip()
    core = chip.core
    tie = lax.optimization_barrier

    def own_columns(weight):
        part = weight.shape[-1] // 2
        cut = lax.dynamic_slice_in_dim(weight, core * part, part, weight.ndim - 1)
        return cut.reshape(weight.shape[0], -1)

    def own_rows(weight):
        part = weight.shape[0] // 2
        return lax.dynamic_slice_in_dim(weight, core * part, part, 0)

    def columns(pieces, low, high):
        return jnp.concatenate([piece[:, low:high] for piece in pieces], 1)

    def rows_of(pieces, low, high):
        return jnp.concatenate([piece[low:high] for piece in pieces], 0)

    x_source = chip.to_slot(source)
    x_target = chip.to_slot(target)
    source_ids = lax.dynamic_index_in_dim(source_segments, chip.place, 0, keepdims=False)
    target_ids = lax.dynamic_index_in_dim(target_segments, chip.place, 0, keepdims=False)
    ids = jnp.arange(LANES, dtype=jnp.int32)[None] % HEAD_DIM
    counted = ids < IDS
    source_query = jnp.where(source_ids[:, None] == ids, NEG, 0.0).astype(BF16)
    target_query = jnp.where(target_ids[:, None] == ids, NEG, 0.0).astype(BF16)
    source_key = ((source_ids[:, None] != ids) & counted).astype(BF16)
    target_key = ((target_ids[:, None] != ids) & counted).astype(BF16)

    bundles = [
        jnp.concatenate([own_columns(enc_qkv), own_columns(dec_self_qkv)], 1),
        jnp.concatenate([own_rows(enc_proj), own_rows(dec_self_proj), own_rows(dec_cross_proj)], 0),
        own_columns(enc_up),
        own_rows(enc_down),
        jnp.concatenate(
            [own_columns(dec_cross_q), own_columns(dec_cross_kv), own_columns(dec_up)], 1
        ),
        own_rows(dec_down),
    ]
    gathered = []
    for index, bundle in enumerate(bundles):
        if index >= 2:
            bundle, _ = tie((bundle, gathered[index - 2][1]))
        gathered.append(chip.gather(bundle))
    qkv_width = bundles[0].shape[1] // 2
    proj_rows = bundles[1].shape[0] // 3
    head_width = dec_cross_q.shape[1] // 2
    w_enc_qkv = columns(gathered[0], 0, qkv_width)
    w_self_qkv = columns(gathered[0], qkv_width, 2 * qkv_width)
    w_enc_proj = rows_of(gathered[1], 0, proj_rows)
    w_self_proj = rows_of(gathered[1], proj_rows, 2 * proj_rows)
    w_cross_proj = rows_of(gathered[1], 2 * proj_rows, 3 * proj_rows)
    w_enc_up = jnp.concatenate(gathered[2], 1)
    w_enc_down = jnp.concatenate(gathered[3], 0)
    w_cross_q = columns(gathered[4], 0, head_width)
    w_cross_kv = columns(gathered[4], head_width, 3 * head_width)
    w_dec_up = columns(gathered[4], 3 * head_width, bundles[4].shape[1])
    w_dec_down = jnp.concatenate(gathered[5], 0)

    def enc(index):
        return enc_gain[index : index + 1], enc_shift[index : index + 1]

    def dec(index):
        return dec_gain[index : index + 1], dec_shift[index : index + 1]

    def partial(rows_in, weight):
        own = project(rows_in, weight).astype(BF16)
        return own, chip.other(own)

    def back_partial(grad, weight):
        own = back_project(grad, weight).astype(BF16)
        return own, chip.other(own)

    fused_at = ((3, 0), (3, 1), (3, 2))

    def attend_self(rows_in, weight, marks, causal):
        qkv = project(rows_in, weight).astype(BF16)
        mixed, totals = chip_attend(
            qkv, fused_at[0], qkv, fused_at[1], fused_at[2], marks[0], marks[1], causal
        )
        return qkv, mixed, totals

    rows_a = norm_rows(x_source, *enc(0))
    rows_c = norm_rows(x_target, *dec(0))
    qkv_a, mixed_a, total_a = attend_self(rows_a, w_enc_qkv, (source_query, source_key), False)
    hidden, rows_b = add_norm(x_source, *partial(mixed_a, w_enc_proj), *enc(1))
    qkv_c, mixed_c, total_c = attend_self(rows_c, w_self_qkv, (target_query, target_key), True)
    after_self, rows_e = add_norm(x_target, *partial(mixed_c, w_self_proj), *dec(1))
    cotangent = chip.to_slot(out_grad)
    active_b, slope_b = up_gelu(rows_b, w_enc_up)
    encoded, rows_m = add_norm(hidden, *partial(active_b, w_enc_down), *enc(2))
    query_e = project(rows_e, w_cross_q).astype(BF16)
    pairs_m = project(rows_m, w_cross_kv).astype(BF16)
    mixed_e, total_e = chip_attend(
        query_e, (1, 0), pairs_m, (2, 0), (2, 1), target_query, source_key, False
    )
    after_cross, rows_f = add_norm(after_self, *partial(mixed_e, w_cross_proj), *dec(2))
    active_f, slope_f = up_gelu(rows_f, w_dec_up)
    decoded, d_final, low_final, gain_d3, shift_d3 = last_norm(
        after_cross, *partial(active_f, w_dec_down), cotangent, *dec(3)
    )
    decoded = chip.from_slot(decoded)


    def stage_one(pairs):
        sent = weight_grads(pairs, 1)
        return chip.send_near(sent), weight_grads(pairs, 0)

    def stage_two(state):
        came, kept = state
        half = kept.shape[0] // 2
        sent = add_low(kept[half:], came[half:])
        return chip.send_side(sent), add_low(kept[:half], came[:half])

    low_bit = lax.rem(chip.line, 2)
    high_bit = chip.line // 2

    def stage_three(state):
        came, kept = state
        kept_own, kept_other = chip.split(kept, low_bit)
        came_own, came_other = chip.split(came, low_bit)
        return chip.along(add_low(kept_other, came_other), 1), add_low(kept_own, came_own)

    def stage_four(state):
        came, kept = state
        kept_own, kept_other = chip.split(kept, high_bit)
        came_own, came_other = chip.split(came, high_bit)
        return chip.along(add_low(kept_other, came_other), 2), add_low(kept_own, came_own)

    def stage_five(state):
        own = add_low(*state)
        return chip.along(own, 2), own

    def stage_six(state):
        came, own = state
        half = chip.ordered(own, came, high_bit)
        return chip.along(half, 1), half

    def stage_seven(state):
        came, own = state
        whole = chip.ordered(own, came, low_bit)
        width = whole.shape[1] // 2
        sent = lax.dynamic_slice_in_dim(whole, (1 - core) * width, width, 1)
        own = lax.dynamic_slice_in_dim(whole, core * width, width, 1)
        return chip.other(sent), own

    def stage_eight(state):
        came, own = state
        return chip.ordered(own[None], came[None], core).astype(F32)

    stages = [stage_two, stage_three, stage_four, stage_five, stage_six, stage_seven, stage_eight]

    class Reduction:
        def __init__(self, pairs):
            self.state = stage_one(pairs)
            self.at = 0

        def step(self):
            if self.at < len(stages):
                self.state = stages[self.at](self.state)
                self.at += 1

        def finish(self):
            while self.at < len(stages):
                self.step()
            return self.state

    def ffn_back(low_out, rows_in, slope, weight_up, weight_down):
        d_inner = (back_project(low_out, weight_down) * slope.astype(F32)).astype(BF16)
        return d_inner, back_partial(d_inner, weight_up)

    d_inner_f, (own, other) = ffn_back(low_final, rows_f, slope_f, w_dec_up, w_dec_down)
    red_f = Reduction([(d_inner_f, rows_f), (active_f, low_final)])
    other, _ = tie((other, red_f.state[1]))
    d_cross, low_cross, gain_d2, shift_d2 = norm_back_rows(
        after_cross, own, other, dec(2)[0], d_final, [F32, BF16]
    )
    d_mixed = back_project(low_cross, w_cross_proj).astype(BF16)
    d_query_e, d_pairs_m = chip_attend_back(
        query_e,
        (1, 0),
        pairs_m,
        (2, 0),
        (2, 1),
        target_query,
        source_key,
        False,
        total_e,
        mixed_e,
        d_mixed,
        False,
    )
    own_m, other_m = back_partial(d_pairs_m, w_cross_kv)
    own_e, other_e = back_partial(d_query_e, w_cross_q)
    red_f.step()
    red_x = Reduction([(mixed_e, low_cross), (d_query_e, rows_e), (d_pairs_m, rows_m)])
    other_m, other_e, _, _ = tie((other_m, other_e, red_x.state[1], red_f.state[1]))
    low_encoded_pair = norm_back_rows(encoded, own_m, other_m, enc(2)[0], None, [F32, BF16])
    d_encoded, low_encoded, gain_e2, shift_e2 = low_encoded_pair
    d_self, low_self, gain_d1, shift_d1 = norm_back_rows(
        after_self, own_e, other_e, dec(1)[0], d_cross, [F32, BF16]
    )
    d_inner_b, (own, other) = ffn_back(low_encoded, rows_b, slope_b, w_enc_up, w_enc_down)
    red_f.step()
    red_b = Reduction([(d_inner_b, rows_b), (active_b, low_encoded)])
    red_x.step()
    other, _, _, _ = tie((other, red_b.state[1], red_x.state[1], red_f.state[1]))
    d_hidden, low_hidden, gain_e1, shift_e1 = norm_back_rows(
        hidden, own, other, enc(1)[0], d_encoded, [F32, BF16]
    )

    def self_back(low_out, qkv, marks, causal, totals, mixed, w_qkv, w_proj):
        d_mixed = back_project(low_out, w_proj).astype(BF16)
        (d_qkv,) = chip_attend_back(
            qkv,
            fused_at[0],
            qkv,
            fused_at[1],
            fused_at[2],
            marks[0],
            marks[1],
            causal,
            totals,
            mixed,
            d_mixed,
            True,
        )
        return d_qkv

    d_qkv_c = self_back(
        low_self, qkv_c, (target_query, target_key), True, total_c, mixed_c, w_self_qkv, w_self_proj
    )
    red_c = Reduction([(mixed_c, low_self), (d_qkv_c, rows_c)])
    red_f.step()
    red_x.step()
    red_b.step()
    low_hidden, _, _, _, _ = tie(
        (low_hidden, red_c.state[1], red_f.state[1], red_x.state[1], red_b.state[1])
    )
    d_qkv_a = self_back(
        low_hidden, qkv_a, (source_query, source_key), False, total_a, mixed_a, w_enc_qkv, w_enc_proj
    )
    own_a, other_a = back_partial(d_qkv_a, w_enc_qkv)
    red_a = Reduction([(mixed_a, low_hidden), (d_qkv_a, rows_a)])
    own_c, other_c = back_partial(d_qkv_c, w_self_qkv)
    source_grad, gain_e0, shift_e0 = norm_back_rows(
        x_source, own_a, other_a, enc(0)[0], d_hidden, [BF16]
    )
    target_grad, gain_d0, shift_d0 = norm_back_rows(
        x_target, own_c, other_c, dec(0)[0], d_self, [BF16]
    )
    source_grad = chip.from_slot(source_grad).astype(F32)
    target_grad = chip.from_slot(target_grad).astype(F32)

    norms = jnp.concatenate(
        [
            gain_e0,
            gain_e1,
            gain_e2,
            shift_e0,
            shift_e1,
            shift_e2,
            gain_d0,
            gain_d1,
            gain_d2,
            gain_d3,
            shift_d0,
            shift_d1,
            shift_d2,
            shift_d3,
        ],
        0,
    )
    part = norms.shape[1] // 2
    norms = lax.dynamic_slice_in_dim(norms, core * part, part, 1)
    norms = lax.psum(norms, ("dp", "tensor"))

    def wide(block, blocks):
        cores, rows, width = block.shape
        block = block.reshape(cores, blocks, rows // blocks, width)
        return jnp.transpose(block, (3, 1, 0, 2)).reshape(width, blocks, -1)

    def tall(block):
        return block.reshape(-1, block.shape[2])

    done_f, done_x, done_b, done_c, done_a = (
        red.finish() for red in (red_f, red_x, red_b, red_c, red_a)
    )
    hid = done_f.shape[1] // 2
    n = proj_rows
    return (
        decoded,
        source_grad,
        target_grad,
        norms[0:3],
        norms[3:6],
        wide(done_a[:, n:], 3),
        tall(done_a[:, :n]),
        wide(done_b[:, :hid], 1)[:, 0],
        tall(done_b[:, hid:]),
        norms[6:10],
        norms[10:14],
        wide(done_c[:, n:], 3),
        tall(done_c[:, :n]),
        wide(done_x[:, n : n + head_width], 1)[:, 0],
        wide(done_x[:, n + head_width :], 2),
        tall(done_x[:, :n]),
        wide(done_f[:, :hid], 1)[:, 0],
        tall(done_f[:, hid:]),
    )


def solution(mesh):
    rows = P("dp", ("seq", "tensor"), None)
    segments = P("dp", None)
    shape = dict(mesh.shape)
    chips = shape["dp"] == 4 and shape["seq"] == 2 and shape["tensor"] == 4
    return jax.shard_map(
        chip_local if chips else local,
        mesh=mesh,
        in_specs=(
            rows,
            rows,
            rows,
            segments,
            segments,
            P(),
            P(),
            P(None, None, "tensor"),
            P("tensor", None),
            P(None, "tensor"),
            P("tensor", None),
            P(),
            P(),
            P(None, None, "tensor"),
            P("tensor", None),
            P(None, "tensor"),
            P(None, None, "tensor"),
            P("tensor", None),
            P(None, "tensor"),
            P("tensor", None),
        ),
        out_specs=(
            rows,
            rows,
            rows,
            P(None, "seq"),
            P(None, "seq"),
            P("seq", None, "tensor"),
            P("tensor", "seq"),
            P("seq", "tensor"),
            P("tensor", "seq"),
            P(None, "seq"),
            P(None, "seq"),
            P("seq", None, "tensor"),
            P("tensor", "seq"),
            P("seq", "tensor"),
            P("seq", None, "tensor"),
            P("tensor", "seq"),
            P("seq", "tensor"),
            P("tensor", "seq"),
        ),
        check_vma=False,
    )
```

time: 2450 us -> 1030 us (0.42)
  waiting for transfers between devices: 1440 us -> 187 us
  matrix products: 472 us -> 106 us
  Pallas kernels: 0 us -> 311 us
  other arithmetic: 255 us -> 95.2 us
  starting transfers between devices: 4.59 us -> 150 us
  local copies, waits for them, and re-layouts: 243 us -> 110 us
  blocking collectives: 10.8 us -> 60.8 us
    all_gather x15 -> x0, waiting for transfers between devices: 737 us -> none  [the longest x11 479 us: gather_rows(): return lax.all_gather(row_block, 'tensor', axis=1, tiled=True)]
    reduce_scatter x14 -> x0, waiting for transfers between devices: 403 us -> none  [the longest x11 403 us: scatter_rows(): lax.psum_scatter(term_block.astype(jnp.bfloat16), 'tensor', scatter_dimen...]
    dot_general x51 -> x20, matrix products: 472 us -> 106 us  [mxu(): return lax.dot_general(left, right, dims, preferred_element_type=F32)]
    pallas_call x0 -> x31, Pallas kernels: none -> 311 us  [the longest x13 92.3 us: row_call(): pl.pallas_call(kernel, grid=(rows // ROW_BLOCK,), in_specs=[block] * len(...]
    unnamed x31 -> x0, waiting for transfers between devices: 299 us -> none
    ppermute x0 -> x67, starting transfers between devices: none -> 128 us  [the longest x19 62.9 us: other(): return lax.ppermute(block, 'seq', swap_pairs(2, 1))]
    ppermute x0 -> x67, waiting for transfers between devices: none -> 125 us  [the longest x6 53.5 us: gather(): near = lax.ppermute(block, CROSS, self.first)]
    reduce_sum x36 -> x0, other arithmetic: 93 us -> none  [the longest x3 43.5 us: attend(): row_total = jnp.sum(weights, -1, keepdims=True)]
  transfers between devices with their start and end apart: 30 -> 73, of which waited for: 22 -> 16; matrix products, arithmetic and copies ran while one was open for 22% -> 26% of each run, Pallas kernels for 0% -> 28%
where the time goes in v1:
time: 1030 us; the launch traced here: 1020 us
  Pallas kernels  311 us (30%)
  waiting for transfers between devices  187 us (18%)
  starting transfers between devices  150 us (15%)
  local copies, waits for them, and re-layouts  110 us (11%)
  matrix products  106 us (10%)
  other arithmetic  95.2 us (9%)
  blocking collectives  60.8 us (6%)
    dot_general x20, matrix products, mxu(): return lax.dot_general(left, right, dims, preferred_element_type=F32)  106 us
    pallas_call x13, Pallas kernels, row_call(): pl.pallas_call(kernel, grid=(rows // ROW_BLOCK,), in_specs=[block] * len(...  92.3 us
    pallas_call x10, Pallas kernels, weight_grads(): pl.pallas_call(functools.partial(weight_kernel, len(pairs)), grid=(2,), i...  76.2 us
    pallas_call x3, Pallas kernels, chip_attend_back(): pl.pallas_call(functools.partial(chip_attend_back_kernel, causal, fused),...  65.1 us
    ppermute x19, starting transfers between devices, other(): return lax.ppermute(block, 'seq', swap_pairs(2, 1))  62.9 us
    all_to_all x3, waiting for transfers between devices, to_slot(): rows = lax.all_to_all(block, 'tensor', 0, 0, tiled=True)  62.2 us
    psum x1, blocking collectives, chip_local(): norms = lax.psum(norms, ('dp', 'tensor'))  60.8 us
    ppermute x6, waiting for transfers between devices, gather(): near = lax.ppermute(block, CROSS, self.first)  53.5 us
  transfers between devices with their start and end apart: 73, of which 16 were waited for; matrix products, arithmetic and copies ran while one was open for 26% of the time, Pallas kernels for 28%

profile of v1, /device:TPU:9, one launch (start us, length us, event | category | flops | bytes accessed | tf_op | source)
XLA Modules:
  0.0 1023.3 jit_solution(17033892295747610507)
XLA Ops:
  23.2 51.1 %all-to-all-done.1 = bf16[4,128,1024]{2,1,0:T(8,128)(2,1)S(1)} async-done(((bf16[4,128,1024]{2,1,0:T(8,128)(2,1)}), bf16[4,128,1024]{2,1,0:T(8,128)(2,1)S(1)}, u32[]{:S(2)}, u32[]{:S(2)}) %all-to-all-start.1) | async-done | bytes 1048608 | tf_op jit(solution)/shard_map/all_to_all | solution.py:931
  84.4 6.8 all-to-all-done.2
  151.6 41.6 %collective-permute-done.14 = bf16[1024,512]{1,0:T(8,128)(2,1)S(1)} collective-permute-done((bf16[1024,512]{1,0:T(8,128)(2,1)S(1)}, bf16[1024,512]{1,0:T(8,128)(2,1)S(1)}, u32[]{:S(2)}, u32[]{:S(2)}) %collective-permute-start.14) | collective-permute-done | bytes 1048608 | tf_op jit(solution)/shard_map/ppermute | solution.py:921
  196.8 6.9 convolution_convert_fusion.q_ref.k_ref.v_ref.refs_0_.refs_1_.refs_2_
  203.7 18.9 %attend.4 = (bf16[1024,512]{1,0:T(8,128)(2,1)}, f32[4,2,1024]{2,1,0:T(2,128)}) custom-call(bf16[1024,1536]{1,0:T(8,128)(2,1)} %convolution_convert_fusion.q_ref.k_ref.v_ref.refs_0_.refs_1_.refs_2_, bf16[1024,1536]{1,0:T(8,128)(2,1)} %convolution_convert_fusion.q_ref.k_ref.v_ref.refs_0_.refs_1_.refs_2_, ...), custom_call_target="tpu_custom_call" | custom-call | flops 4294967296 | bytes 8388608 | tf_op jit(solution)/shard_map/attend/pallas_call | solution.py:724
  229.1 7.1 convolution_convert_fusion.1.q_ref.k_ref.v_ref.refs_0_.refs_1_.refs_2_
  236.1 15.6 %attend.3 = (bf16[1024,512]{1,0:T(8,128)(2,1)}, f32[4,2,1024]{2,1,0:T(2,128)}) custom-call(bf16[1024,1536]{1,0:T(8,128)(2,1)} %convolution_convert_fusion.1.q_ref.k_ref.v_ref.refs_0_.refs_1_.refs_2_, bf16[1024,1536]{1,0:T(8,128)(2,1)} %convolution_convert_fusion.1.q_ref.k_ref.v_ref.refs_0_.refs_1_.refs_2_, ...), custom_call_target="tpu_custom_call" | custom-call | flops 4294967296 | bytes 8388608 | tf_op jit(solution)/shard_map/attend/pallas_call | solution.py:724
  264.3 12.0 %up_gelu.2 = (bf16[1024,2048]{1,0:T(8,128)(2,1)}, bf16[1024,2048]{1,0:T(8,128)(2,1)}) custom-call(bf16[1024,1024]{1,0:T(8,128)(2,1)} %get-tuple-element.81.x_ref.refs_2_, bf16[1024,2048]{1,0:T(8,128)(2,1)} %constant_dynamic-update-slice_fusion.w_ref), custom_call_target="tpu_custom_call" | custom-call | flops 4294967296 | bytes 14680064 | tf_op jit(solution)/shard_map/up_gelu/pallas_call | solution.py:856
  276.3 8.1 convolution_convert_fusion.11.own_ref
  307.8 6.4 add_norm.6
  319.4 18.9 %attend.5 = (bf16[1024,512]{1,0:T(8,128)(2,1)}, f32[4,2,1024]{2,1,0:T(2,128)}) custom-call(bf16[1024,512]{1,0:T(8,128)(2,1)} %convolution_convert_fusion.17.q_ref.refs_0_, bf16[1024,1024]{1,0:T(8,128)(2,1)} %convolution_convert_fusion.10.k_ref.v_ref.refs_1_.refs_2_, bf16[1024,1024]{1,0:T(8,128)(2,1)} %convolution_convert_fusion.10.k_ref.v_ref.refs_1_.refs_2_, ...), custom_call_target="tpu_custom_call" | custom-call | flops 4294967296 | bytes 8388608 | tf_op jit(solution)/shard_map/attend/pallas_call | solution.py:724
  344.7 11.0 %collective-permute-done.22 = bf16[512,1024]{1,0:T(8,128)(2,1)S(1)} collective-permute-done((bf16[512,1024]{1,0:T(8,128)(2,1)S(1)}, bf16[512,1024]{1,0:T(8,128)(2,1)S(1)}, u32[]{:S(2)}, u32[]{:S(2)}) %collective-permute-start.22) | collective-permute-done | bytes 1048608 | tf_op jit(solution)/shard_map/ppermute | solution.py:921
  355.8 11.2 %collective-permute-done.23 = bf16[512,1024]{1,0:T(8,128)(2,1)S(1)} collective-permute-done((bf16[512,1024]{1,0:T(8,128)(2,1)S(1)}, bf16[512,1024]{1,0:T(8,128)(2,1)S(1)}, u32[]{:S(2)}, u32[]{:S(2)}) %collective-permute-start.23) | collective-permute-done | bytes 1048608 | tf_op jit(solution)/shard_map/ppermute | solution.py:923
  375.4 6.4 add_norm.7
  381.8 12.4 %up_gelu.3 = (bf16[1024,2048]{1,0:T(8,128)(2,1)}, bf16[1024,2048]{1,0:T(8,128)(2,1)}) custom-call(bf16[1024,1024]{1,0:T(8,128)(2,1)} %get-tuple-element.87.x_ref.refs_2_, bf16[1024,2048]{1,0:T(8,128)(2,1)} %pad_maximum_fusion.w_ref), custom_call_target="tpu_custom_call" | custom-call | flops 4294967296 | bytes 14680064 | tf_op jit(solution)/shard_map/up_gelu/pallas_call | solution.py:856
  394.2 8.0 convolution_convert_fusion.8.own_ref
  408.3 9.1 last_norm.1
  417.4 8.6 multiply_convert_fusion.1.refs_0_
  431.3 9.3 weight_grads.12
  440.9 9.1 weight_grads.10
  451.4 8.5 norm_back.6
  463.8 23.9 %attend_back.3 = (bf16[1024,512]{1,0:T(8,128)(2,1)}, bf16[1024,1024]{1,0:T(8,128)(2,1)}) custom-call(bf16[1024,512]{1,0:T(8,128)(2,1)} %convolution_convert_fusion.17.q_ref.refs_0_, bf16[1024,1024]{1,0:T(8,128)(2,1)} %convolution_convert_fusion.10.k_ref.v_ref.refs_1_.refs_2_, bf16[1024,1024]{1,0:T(8,128)(2,1)} %convolution_convert_fusion.10.k_ref.v_ref.refs_1_.refs_2_, ...), custom_call_target="tpu_custom_call" | custom-call | flops 10737418240 | bytes 16777216 | tf_op jit(solution)/shard_map/attend_back/pallas_call | solution.py:818
  487.7 7.0 weight_grads.14
  509.4 7.0 weight_grads.11
  516.4 9.5 collective-permute-done.31
  536.5 9.3 norm_back.9
  549.7 17.0 %attend_back.4.refs_1_ = bf16[1024,1536]{1,0:T(8,128)(2,1)} custom-call(bf16[1024,1536]{1,0:T(8,128)(2,1)} %convolution_convert_fusion.1.q_ref.k_ref.v_ref.refs_0_.refs_1_.refs_2_, bf16[1024,1536]{1,0:T(8,128)(2,1)} %convolution_convert_fusion.1.q_ref.k_ref.v_ref.refs_0_.refs_1_.refs_2_, ...), custom_call_target="tpu_custom_call" | custom-call | flops 10737418240 | bytes 16777216 | tf_op jit(solution)/shard_map/attend_back/pallas_call | solution.py:818
  574.1 8.4 norm_back.7
  582.6 6.3 convolution_convert_fusion.2.refs_1_
  590.8 8.3 multiply_convert_fusion.refs_0_
  605.0 9.0 weight_grads.16
  618.8 7.9 convolution_convert_fusion.4.refs_1_
  631.0 6.7 weight_grads.15
  651.6 7.3 norm_back.11
  667.6 9.0 weight_grads.13
  676.6 8.5 norm_back.8
  697.8 9.7 collective-permute-done.53
  713.1 17.5 %collective-permute-done.54 = bf16[128,1024]{1,0:T(8,128)(2,1)S(1)} collective-permute-done((bf16[128,1024]{1,0:T(8,128)(2,1)S(1)}, bf16[128,1024]{1,0:T(8,128)(2,1)S(1)}, u32[]{:S(2)}, u32[]{:S(2)}) %collective-permute-start.54) | collective-permute-done | bytes 262176 | tf_op jit(solution)/shard_map/ppermute | solution.py:954
  744.3 24.2 %attend_back.5.refs_1_ = bf16[1024,1536]{1,0:T(8,128)(2,1)} custom-call(bf16[1024,1536]{1,0:T(8,128)(2,1)} %convolution_convert_fusion.q_ref.k_ref.v_ref.refs_0_.refs_1_.refs_2_, bf16[1024,1536]{1,0:T(8,128)(2,1)} %convolution_convert_fusion.q_ref.k_ref.v_ref.refs_0_.refs_1_.refs_2_, ...), custom_call_target="tpu_custom_call" | custom-call | flops 10737418240 | bytes 16777216 | tf_op jit(solution)/shard_map/attend_back/pallas_call | solution.py:818
  768.5 6.3 weight_grads.18
  783.5 7.6 collective-permute-start.56
  793.0 6.5 weight_grads.17
  799.6 10.0 collective-permute-start.36
  830.0 8.7 collective-permute-start.66
  857.8 7.3 norm_back.10
  878.4 60.8 %psum.7 = f32[14,512]{1,0:T(8,128)S(1)} all-reduce(f32[14,512]{1,0:T(8,128)S(1)} %constant_dynamic-slice_fusion), channel_id=1, replica_groups=mesh['dp'=4,'seq'=2,'tensor'=4] {'dp','tensor'}, use_global_device_ids=true, to_apply=%region_0.1 | all-reduce | flops 7168 | bytes 57344 | tf_op jit(solution)/shard_map/psum | solution.py:1259
  955.1 12.4 %collective-permute-done.43 = bf16[256,1024]{1,0:T(8,128)(2,1)S(1)} collective-permute-done((bf16[256,1024]{1,0:T(8,128)(2,1)S(1)}, bf16[256,1024]{1,0:T(8,128)(2,1)S(1)}, u32[]{:S(2)}, u32[]{:S(2)}) %collective-permute-start.43) | collective-permute-done | bytes 524320 | tf_op jit(solution)/shard_map/ppermute | solution.py:954
  968.6 25.4 %collective-permute-start.44 = (bf16[512,512]{1,0:T(8,128)(2,1)}, bf16[512,512]{1,0:T(8,128)(2,1)}, u32[]{:S(2)}, u32[]{:S(2)}) collective-permute-start(bf16[512,512]{1,0:T(8,128)(2,1)} %fusion.8), channel_id=1, source_target_pairs={{0,4},{4,0},{1,5},{5,1},{2,6},{6,2},{3,7},{7,3},{8,12},{12,8},{9,1... | collective-permute-start | bytes 1572872 | tf_op jit(solution)/shard_map/ppermute | solution.py:918
  (546 shorter events, 392.3 us)
Async XLA Ops:
  8.6 95.1 %collective-permute-start.1 = (bf16[1024,768]{0,1:T(8,128)(2,1)}, bf16[1024,768]{0,1:T(8,128)(2,1)}, u32[]{:S(2)}, u32[]{:S(2)}) collective-permute-start(bf16[1024,768]{0,1:T(8,128)(2,1)} %pad_maximum_fusion.8), channel_id=1, source_target_pairs={{0,2},{1,3},{2,0},{3,1},{4,5},{5,4},{6,7},{7,6},{8,10},{9,11},{10,... | collective-permute-start | bytes 4718600 | tf_op jit(solution)/shard_map/ppermute | solution.py:922
  9.8 107.7 %collective-permute-start.2 = (bf16[1024,768]{0,1:T(8,128)(2,1)}, bf16[1024,768]{0,1:T(8,128)(2,1)}, u32[]{:S(2)}, u32[]{:S(2)}) collective-permute-start(bf16[1024,768]{0,1:T(8,128)(2,1)} %pad_maximum_fusion.8), channel_id=1, source_target_pairs={{0,1},{1,0},{2,3},{3,2},{4,6},{5,7},{6,4},{7,5},{8,9},{9,8},{10,11... | collective-permute-start | bytes 4718600 | tf_op jit(solution)/shard_map/ppermute | solution.py:921
  12.7 70.0 %collective-permute-start.4 = (bf16[384,1024]{1,0:T(8,128)(2,1)}, bf16[384,1024]{1,0:T(8,128)(2,1)}, u32[]{:S(2)}, u32[]{:S(2)}) collective-permute-start(bf16[384,1024]{1,0:T(8,128)(2,1)} %pad_maximum_fusion.15), channel_id=1, source_target_pairs={{0,2},{1,3},{2,0},{3,1},{4,5},{5,4},{6,7},{7,6},{8,10},{9,11},{10,... | collective-permute-start | bytes 2359304 | tf_op jit(solution)/shard_map/ppermute | solution.py:922
  13.0 84.3 %collective-permute-start.5 = (bf16[384,1024]{1,0:T(8,128)(2,1)}, bf16[384,1024]{1,0:T(8,128)(2,1)}, u32[]{:S(2)}, u32[]{:S(2)}) collective-permute-start(bf16[384,1024]{1,0:T(8,128)(2,1)} %pad_maximum_fusion.15), channel_id=1, source_target_pairs={{0,1},{1,0},{2,3},{3,2},{4,6},{5,7},{6,4},{7,5},{8,9},{9,8},{10,11... | collective-permute-start | bytes 2359304 | tf_op jit(solution)/shard_map/ppermute | solution.py:921
  13.2 61.1 %all-to-all-start.1 = ((bf16[4,128,1024]{2,1,0:T(8,128)(2,1)}), bf16[4,128,1024]{2,1,0:T(8,128)(2,1)S(1)}, u32[]{:S(2)}, u32[]{:S(2)}) async-start(bf16[4,128,1024]{2,1,0:T(8,128)(2,1)} %param.20), calls=%async_computation.1 | async-start | bytes 2097152 | tf_op jit(solution)/shard_map/all_to_all | solution.py:931
  82.4 39.0 %collective-permute-start.12 = (bf16[512,1024]{1,0:T(8,128)(2,1)S(1)}, bf16[512,1024]{1,0:T(8,128)(2,1)}, u32[]{:S(2)}, u32[]{:S(2)}) collective-permute-start(bf16[512,1024]{1,0:T(8,128)(2,1)S(1)} %bitcast.102), channel_id=1, source_target_pairs={{0,4},{4,0},{1,5},{5,1},{2,6},{6,2},{3,7},{7,3},{8,12},{12,8},{9,1... | collective-permute-start | bytes 3145736 | tf_op jit(solution)/shard_map/ppermute | solution.py:918
  82.8 29.5 %collective-permute-start.6 = (bf16[384,1024]{1,0:T(8,128)(2,1)}, bf16[384,1024]{1,0:T(8,128)(2,1)}, u32[]{:S(2)}, u32[]{:S(2)}) collective-permute-start(bf16[384,1024]{1,0:T(8,128)(2,1)} %collective-permute-done.4), channel_id=1, source_target_pairs={{0,1},{1,0},{2,3},{3,2},{4,6},{5,7},{6,4},{7,5},{8,9},{9,8},{10,11... | collective-permute-start | bytes 2359304 | tf_op jit(solution)/shard_map/ppermute | solution.py:923
  121.3 26.1 %collective-permute-start.8 = (bf16[1024,512]{1,0:T(8,128)(2,1)S(1)}, bf16[1024,512]{1,0:T(8,128)(2,1)}, u32[]{:S(2)}, u32[]{:S(2)}) collective-permute-start(bf16[1024,512]{1,0:T(8,128)(2,1)S(1)} %copy-done.30), channel_id=1, source_target_pairs={{0,2},{1,3},{2,0},{3,1},{4,5},{5,4},{6,7},{7,6},{8,10},{9,11},{10,... | collective-permute-start | bytes 3145736 | tf_op jit(solution)/shard_map/ppermute | solution.py:922
  121.4 72.9 %collective-permute-start.3 = (bf16[1024,768]{0,1:T(8,128)(2,1)}, bf16[1024,768]{0,1:T(8,128)(2,1)}, u32[]{:S(2)}, u32[]{:S(2)}) collective-permute-start(bf16[1024,768]{0,1:T(8,128)(2,1)} %collective-permute-done.1), channel_id=1, source_target_pairs={{0,1},{1,0},{2,3},{3,2},{4,6},{5,7},{6,4},{7,5},{8,9},{9,8},{10,11... | collective-permute-start | bytes 4718600 | tf_op jit(solution)/shard_map/ppermute | solution.py:923
  125.0 68.1 %collective-permute-start.14 = (bf16[1024,512]{1,0:T(8,128)(2,1)S(1)}, bf16[1024,512]{1,0:T(8,128)(2,1)S(1)}, u32[]{:S(2)}, u32[]{:S(2)}) collective-permute-start(bf16[1024,512]{1,0:T(8,128)(2,1)S(1)} %copy-done.30), channel_id=1, source_target_pairs={{0,1},{1,0},{2,3},{3,2},{4,6},{5,7},{6,4},{7,5},{8,9},{9,8},{10,11... | collective-permute-start | bytes 3145736 | tf_op jit(solution)/shard_map/ppermute | solution.py:921
  132.2 93.9 %collective-permute-start.18 = (bf16[512,1024]{1,0:T(8,128)(2,1)}, bf16[512,1024]{1,0:T(8,128)(2,1)}, u32[]{:S(2)}, u32[]{:S(2)}) collective-permute-start(bf16[512,1024]{1,0:T(8,128)(2,1)} %collective-permute-done.16), channel_id=1, source_target_pairs={{0,1},{1,0},{2,3},{3,2},{4,6},{5,7},{6,4},{7,5},{8,9},{9,8},{10,11... | collective-permute-start | bytes 3145736 | tf_op jit(solution)/shard_map/ppermute | solution.py:923
  147.5 109.5 %collective-permute-start.9 = (bf16[1024,896]{1,0:T(8,128)(2,1)}, bf16[1024,896]{1,0:T(8,128)(2,1)}, u32[]{:S(2)}, u32[]{:S(2)}) collective-permute-start(bf16[1024,896]{1,0:T(8,128)(2,1)} %pad_maximum_fusion.7), channel_id=1, source_target_pairs={{0,2},{1,3},{2,0},{3,1},{4,5},{5,4},{6,7},{7,6},{8,10},{9,11},{10,... | collective-permute-start | bytes 5505032 | tf_op jit(solution)/shard_map/ppermute | solution.py:922
  147.5 144.3 %collective-permute-start.10 = (bf16[1024,896]{1,0:T(8,128)(2,1)}, bf16[1024,896]{1,0:T(8,128)(2,1)}, u32[]{:S(2)}, u32[]{:S(2)}) collective-permute-start(bf16[1024,896]{1,0:T(8,128)(2,1)} %pad_maximum_fusion.7), channel_id=1, source_target_pairs={{0,1},{1,0},{2,3},{3,2},{4,6},{5,7},{6,4},{7,5},{8,9},{9,8},{10,11... | collective-permute-start | bytes 5505032 | tf_op jit(solution)/shard_map/ppermute | solution.py:921
  193.1 62.7 %collective-permute-start.15 = (bf16[1024,512]{1,0:T(8,128)(2,1)}, bf16[1024,512]{1,0:T(8,128)(2,1)S(1)}, u32[]{:S(2)}, u32[]{:S(2)}) collective-permute-start(bf16[1024,512]{1,0:T(8,128)(2,1)} %collective-permute-done.8), channel_id=1, source_target_pairs={{0,1},{1,0},{2,3},{3,2},{4,6},{5,7},{6,4},{7,5},{8,9},{9,8},{10,11... | collective-permute-start | bytes 3145736 | tf_op jit(solution)/shard_map/ppermute | solution.py:923
  225.3 33.1 %collective-permute-start.13 = (bf16[1024,1024]{1,0:T(8,128)(2,1)S(1)}, bf16[1024,1024]{1,0:T(8,128)(2,1)}, u32[]{:S(2)}, u32[]{:S(2)}) collective-permute-start(bf16[1024,1024]{1,0:T(8,128)(2,1)S(1)} %convolution_convert_fusion.12.own_ref), channel_id=1, source_target_pairs={{0,4},{4,0},{1,5},{5,1},{2,6},{6,2},{3,7},{7,3},{8,12},{12,8},{9,1... | collective-permute-start | bytes 6291464 | tf_op jit(solution)/shard_map/ppermute | solution.py:918
  255.6 39.1 %collective-permute-start.7 = (bf16[1024,1024]{1,0:T(8,128)(2,1)}, bf16[1024,1024]{1,0:T(8,128)(2,1)}, u32[]{:S(2)}, u32[]{:S(2)}) collective-permute-start(bf16[1024,1024]{1,0:T(8,128)(2,1)} %convolution_convert_fusion.13.own_ref), channel_id=1, source_target_pairs={{0,4},{4,0},{1,5},{5,1},{2,6},{6,2},{3,7},{7,3},{8,12},{12,8},{9,1... | collective-permute-start | bytes 6291464 | tf_op jit(solution)/shard_map/ppermute | solution.py:918
  256.9 43.9 %collective-permute-start.11 = (bf16[1024,896]{1,0:T(8,128)(2,1)}, bf16[1024,896]{1,0:T(8,128)(2,1)}, u32[]{:S(2)}, u32[]{:S(2)}) collective-permute-start(bf16[1024,896]{1,0:T(8,128)(2,1)} %collective-permute-done.9), channel_id=1, source_target_pairs={{0,1},{1,0},{2,3},{3,2},{4,6},{5,7},{6,4},{7,5},{8,9},{9,8},{10,11... | collective-permute-start | bytes 5505032 | tf_op jit(solution)/shard_map/ppermute | solution.py:923
  285.0 57.0 %collective-permute-start.21 = (bf16[512,1024]{1,0:T(8,128)(2,1)S(1)}, bf16[512,1024]{1,0:T(8,128)(2,1)S(1)}, u32[]{:S(2)}, u32[]{:S(2)}) collective-permute-start(bf16[512,1024]{1,0:T(8,128)(2,1)S(1)} %constant_dynamic-slice_fusion.4), channel_id=1, source_target_pairs={{0,2},{1,3},{2,0},{3,1},{4,5},{5,4},{6,7},{7,6},{8,10},{9,11},{10,... | collective-permute-start | bytes 3145736 | tf_op jit(solution)/shard_map/ppermute | solution.py:922
  340.9 33.2 %collective-permute-start.20 = (bf16[1024,1024]{1,0:T(8,128)(2,1)S(1)}, bf16[1024,1024]{1,0:T(8,128)(2,1)S(1)}, u32[]{:S(2)}, u32[]{:S(2)}) collective-permute-start(bf16[1024,1024]{1,0:T(8,128)(2,1)S(1)} %convolution_convert_fusion.9.own_ref), channel_id=1, source_target_pairs={{0,4},{4,0},{1,5},{5,1},{2,6},{6,2},{3,7},{7,3},{8,12},{12,8},{9,1... | collective-permute-start | bytes 6291464 | tf_op jit(solution)/shard_map/ppermute | solution.py:918
  440.6 90.8 %collective-permute-start.29 = (bf16[2048,1024]{1,0:T(8,128)(2,1)}, bf16[2048,1024]{1,0:T(8,128)(2,1)}, u32[]{:S(2)}, u32[]{:S(2)}) collective-permute-start(bf16[2048,1024]{1,0:T(8,128)(2,1)} %weight_grads.12), channel_id=1, source_target_pairs={{0,1},{1,0},{2,3},{3,2},{4,6},{5,7},{6,4},{7,5},{8,9},{9,8},{10,11... | collective-permute-start | bytes 12582920 | tf_op jit(solution)/shard_map/ppermute | solution.py:941
  494.8 31.2 %collective-permute-start.31 = (bf16[1024,1024]{1,0:T(8,128)(2,1)}, bf16[1024,1024]{1,0:T(8,128)(2,1)}, u32[]{:S(2)}, u32[]{:S(2)}) collective-permute-start(bf16[1024,1024]{1,0:T(8,128)(2,1)} %weight_grads.14), channel_id=1, source_target_pairs={{0,1},{1,0},{2,3},{3,2},{4,6},{5,7},{6,4},{7,5},{8,9},{9,8},{10,11... | collective-permute-start | bytes 6291464 | tf_op jit(solution)/shard_map/ppermute | solution.py:941
  502.4 34.0 %collective-permute-start.28 = (bf16[1024,1024]{1,0:T(8,128)(2,1)}, bf16[1024,1024]{1,0:T(8,128)(2,1)}, u32[]{:S(2)}, u32[]{:S(2)}) collective-permute-start(bf16[1024,1024]{1,0:T(8,128)(2,1)} %convolution_convert_fusion.5.refs_1_), channel_id=1, source_target_pairs={{0,4},{4,0},{1,5},{5,1},{2,6},{6,2},{3,7},{7,3},{8,12},{12,8},{9,1... | collective-permute-start | bytes 6291464 | tf_op jit(solution)/shard_map/ppermute | solution.py:918
  503.4 33.1 %collective-permute-start.27 = (bf16[1024,1024]{1,0:T(8,128)(2,1)}, bf16[1024,1024]{1,0:T(8,128)(2,1)S(1)}, u32[]{:S(2)}, u32[]{:S(2)}) collective-permute-start(bf16[1024,1024]{1,0:T(8,128)(2,1)} %convolution_convert_fusion.6.refs_1_), channel_id=1, source_target_pairs={{0,4},{4,0},{1,5},{5,1},{2,6},{6,2},{3,7},{7,3},{8,12},{12,8},{9,1... | collective-permute-start | bytes 6291464 | tf_op jit(solution)/shard_map/ppermute | solution.py:918
  505.7 125.4 %all-to-all-start.3 = ((bf16[4,128,1024]{2,1,0:T(8,128)(2,1)}), bf16[4,128,1024]{2,1,0:T(8,128)(2,1)S(1)}, u32[]{:S(2)}, u32[]{:S(2)}) async-start(bf16[4,128,1024]{2,1,0:T(8,128)(2,1)} %bitcast.7), calls=%async_computation.3 | async-start | bytes 2097152 | tf_op jit(solution)/shard_map/all_to_all | solution.py:938
  530.1 58.8 %collective-permute-start.34 = (bf16[512,1024]{1,0:T(8,128)(2,1)}, bf16[512,1024]{1,0:T(8,128)(2,1)}, u32[]{:S(2)}, u32[]{:S(2)}) collective-permute-start(bf16[512,1024]{1,0:T(8,128)(2,1)} %get-tuple-element.182), channel_id=1, source_target_pairs={{0,2},{1,3},{2,0},{3,1},{4,5},{5,4},{6,7},{7,6},{8,10},{9,11},{10,... | collective-permute-start | bytes 3145736 | tf_op jit(solution)/shard_map/ppermute | solution.py:944
  536.3 110.4 %collective-permute-start.32 = (bf16[1024,1024]{1,0:T(8,128)(2,1)}, bf16[1024,1024]{1,0:T(8,128)(2,1)}, u32[]{:S(2)}, u32[]{:S(2)}) collective-permute-start(bf16[1024,1024]{1,0:T(8,128)(2,1)} %get-tuple-element.170), channel_id=1, source_target_pairs={{0,2},{1,3},{2,0},{3,1},{4,5},{5,4},{6,7},{7,6},{8,10},{9,11},{10,... | collective-permute-start | bytes 6291464 | tf_op jit(solution)/shard_map/ppermute | solution.py:944
  572.9 66.5 %collective-permute-start.51 = (bf16[1024,1024]{1,0:T(8,128)(2,1)}, bf16[1024,1024]{1,0:T(8,128)(2,1)}, u32[]{:S(2)}, u32[]{:S(2)}) collective-permute-start(bf16[1024,1024]{1,0:T(8,128)(2,1)} %weight_grads.19), channel_id=1, source_target_pairs={{0,1},{1,0},{2,3},{3,2},{4,6},{5,7},{6,4},{7,5},{8,9},{9,8},{10,11... | collective-permute-start | bytes 6291464 | tf_op jit(solution)/shard_map/ppermute | solution.py:941
  613.9 121.0 %collective-permute-start.35 = (bf16[2048,1024]{1,0:T(8,128)(2,1)}, bf16[2048,1024]{1,0:T(8,128)(2,1)}, u32[]{:S(2)}, u32[]{:S(2)}) collective-permute-start(bf16[2048,1024]{1,0:T(8,128)(2,1)} %weight_grads.16), channel_id=1, source_target_pairs={{0,1},{1,0},{2,3},{3,2},{4,6},{5,7},{6,4},{7,5},{8,9},{9,8},{10,11... | collective-permute-start | bytes 12582920 | tf_op jit(solution)/shard_map/ppermute | solution.py:941
  614.3 37.0 %collective-permute-start.37 = (bf16[1024,1024]{1,0:T(8,128)(2,1)}, bf16[1024,1024]{1,0:T(8,128)(2,1)}, u32[]{:S(2)}, u32[]{:S(2)}) collective-permute-start(bf16[1024,1024]{1,0:T(8,128)(2,1)} %convolution_convert_fusion.2.refs_1_), channel_id=1, source_target_pairs={{0,4},{4,0},{1,5},{5,1},{2,6},{6,2},{3,7},{7,3},{8,12},{12,8},{9,1... | collective-permute-start | bytes 6291464 | tf_op jit(solution)/shard_map/ppermute | solution.py:918
  630.5 46.0 %collective-permute-start.30 = (bf16[1024,1024]{1,0:T(8,128)(2,1)}, bf16[1024,1024]{1,0:T(8,128)(2,1)}, u32[]{:S(2)}, u32[]{:S(2)}) collective-permute-start(bf16[1024,1024]{1,0:T(8,128)(2,1)} %convolution_convert_fusion.4.refs_1_), channel_id=1, source_target_pairs={{0,4},{4,0},{1,5},{5,1},{2,6},{6,2},{3,7},{7,3},{8,12},{12,8},{9,1... | collective-permute-start | bytes 6291464 | tf_op jit(solution)/shard_map/ppermute | solution.py:918
  646.6 40.0 %collective-permute-start.52 = (bf16[512,1024]{1,0:T(8,128)(2,1)}, bf16[512,1024]{1,0:T(8,128)(2,1)}, u32[]{:S(2)}, u32[]{:S(2)}) collective-permute-start(bf16[512,1024]{1,0:T(8,128)(2,1)} %get-tuple-element.175), channel_id=1, source_target_pairs={{0,2},{1,3},{2,0},{3,1},{4,5},{5,4},{6,7},{7,6},{8,10},{9,11},{10,... | collective-permute-start | bytes 3145736 | tf_op jit(solution)/shard_map/ppermute | solution.py:944
  651.3 39.3 %collective-permute-start.33 = (bf16[512,1024]{1,0:T(8,128)(2,1)}, bf16[512,1024]{1,0:T(8,128)(2,1)}, u32[]{:S(2)}, u32[]{:S(2)}) collective-permute-start(bf16[512,1024]{1,0:T(8,128)(2,1)} %get-tuple-element.184), channel_id=1, source_target_pairs={{0,8},{8,0},{16,24},{24,16},{1,9},{9,1},{17,25},{25,17},{2,10},{10... | collective-permute-start | bytes 3145736 | tf_op jit(solution)/shard_map/ppermute | solution.py:954
  666.9 25.8 %collective-permute-start.62 = (bf16[512,512]{1,0:T(8,128)(2,1)}, bf16[512,512]{1,0:T(8,128)(2,1)}, u32[]{:S(2)}, u32[]{:S(2)}) collective-permute-start(bf16[512,512]{1,0:T(8,128)(2,1)} %fusion.4), channel_id=1, source_target_pairs={{0,4},{4,0},{1,5},{5,1},{2,6},{6,2},{3,7},{7,3},{8,12},{12,8},{9,1... | collective-permute-start | bytes 1572872 | tf_op jit(solution)/shard_map/ppermute | solution.py:918
  713.0 78.1 %collective-permute-start.64 = (bf16[256,1024]{1,0:T(8,128)(2,1)S(1)}, bf16[256,1024]{1,0:T(8,128)(2,1)S(1)}, u32[]{:S(2)}, u32[]{:S(2)}) collective-permute-start(bf16[256,1024]{1,0:T(8,128)(2,1)S(1)} %add_convert_fusion.14), channel_id=1, source_target_pairs={{0,16},{8,24},{16,0},{24,8},{1,17},{9,25},{17,1},{25,9},{2,18},{10... | collective-permute-start | bytes 1572872 | tf_op jit(solution)/shard_map/ppermute | solution.py:954
  731.7 50.7 %collective-permute-start.55 = (bf16[128,1024]{1,0:T(8,128)(2,1)S(1)}, bf16[128,1024]{1,0:T(8,128)(2,1)}, u32[]{:S(2)}, u32[]{:S(2)}) collective-permute-start(bf16[128,1024]{1,0:T(8,128)(2,1)S(1)} %add_convert_fusion.29), channel_id=1, source_target_pairs={{0,16},{8,24},{16,0},{24,8},{1,17},{9,25},{17,1},{25,9},{2,18},{10... | collective-permute-start | bytes 786440 | tf_op jit(solution)/shard_map/ppermute | solution.py:954
  740.3 69.5 %collective-permute-start.45 = (bf16[1024,1024]{1,0:T(8,128)(2,1)}, bf16[1024,1024]{1,0:T(8,128)(2,1)}, u32[]{:S(2)}, u32[]{:S(2)}) collective-permute-start(bf16[1024,1024]{1,0:T(8,128)(2,1)} %get-tuple-element.168), channel_id=1, source_target_pairs={{0,2},{1,3},{2,0},{3,1},{4,5},{5,4},{6,7},{7,6},{8,10},{9,11},{10,... | collective-permute-start | bytes 6291464 | tf_op jit(solution)/shard_map/ppermute | solution.py:944
  774.8 40.8 %collective-permute-start.38 = (bf16[1024,1024]{1,0:T(8,128)(2,1)}, bf16[1024,1024]{1,0:T(8,128)(2,1)}, u32[]{:S(2)}, u32[]{:S(2)}) collective-permute-start(bf16[1024,1024]{1,0:T(8,128)(2,1)} %weight_grads.18), channel_id=1, source_target_pairs={{0,1},{1,0},{2,3},{3,2},{4,6},{5,7},{6,4},{7,5},{8,9},{9,8},{10,11... | collective-permute-start | bytes 6291464 | tf_op jit(solution)/shard_map/ppermute | solution.py:941
  783.5 26.0 %collective-permute-start.56 = (bf16[256,1024]{1,0:T(8,128)(2,1)S(1)}, bf16[256,1024]{1,0:T(8,128)(2,1)S(1)}, u32[]{:S(2)}, u32[]{:S(2)}) collective-permute-start(bf16[256,1024]{1,0:T(8,128)(2,1)S(1)} %pad_maximum_fusion.21), channel_id=1, source_target_pairs={{0,8},{8,0},{16,24},{24,16},{1,9},{9,1},{17,25},{25,17},{2,10},{10... | collective-permute-start | bytes 1572872 | tf_op jit(solution)/shard_map/ppermute | solution.py:954
  793.0 33.8 %collective-permute-start.65 = (bf16[512,1024]{1,0:T(8,128)(2,1)}, bf16[512,1024]{1,0:T(8,128)(2,1)}, u32[]{:S(2)}, u32[]{:S(2)}) collective-permute-start(bf16[512,1024]{1,0:T(8,128)(2,1)} %pad_maximum_fusion.14), channel_id=1, source_target_pairs={{0,8},{8,0},{16,24},{24,16},{1,9},{9,1},{17,25},{25,17},{2,10},{10... | collective-permute-start | bytes 3145736 | tf_op jit(solution)/shard_map/ppermute | solution.py:954
  799.6 58.1 %collective-permute-start.36 = (bf16[1024,1024]{1,0:T(8,128)(2,1)}, bf16[1024,1024]{1,0:T(8,128)(2,1)}, u32[]{:S(2)}, u32[]{:S(2)}) collective-permute-start(bf16[1024,1024]{1,0:T(8,128)(2,1)} %convolution_convert_fusion.3.refs_1_), channel_id=1, source_target_pairs={{0,4},{4,0},{1,5},{5,1},{2,6},{6,2},{3,7},{7,3},{8,12},{12,8},{9,1... | collective-permute-start | bytes 6291464 | tf_op jit(solution)/shard_map/ppermute | solution.py:918
  813.8 26.1 %collective-permute-start.46 = (bf16[512,1024]{1,0:T(8,128)(2,1)}, bf16[512,1024]{1,0:T(8,128)(2,1)}, u32[]{:S(2)}, u32[]{:S(2)}) collective-permute-start(bf16[512,1024]{1,0:T(8,128)(2,1)} %get-tuple-element.179), channel_id=1, source_target_pairs={{0,8},{8,0},{16,24},{24,16},{1,9},{9,1},{17,25},{25,17},{2,10},{10... | collective-permute-start | bytes 3145736 | tf_op jit(solution)/shard_map/ppermute | solution.py:954
  830.0 123.4 %collective-permute-start.66 = (bf16[1024,512]{1,0:T(8,128)(2,1)}, bf16[1024,512]{1,0:T(8,128)(2,1)}, u32[]{:S(2)}, u32[]{:S(2)}) collective-permute-start(bf16[1024,512]{1,0:T(8,128)(2,1)} %fusion), channel_id=1, source_target_pairs={{0,4},{4,0},{1,5},{5,1},{2,6},{6,2},{3,7},{7,3},{8,12},{12,8},{9,1... | collective-permute-start | bytes 3145736 | tf_op jit(solution)/shard_map/ppermute | solution.py:918
  842.4 26.0 %collective-permute-start.47 = (bf16[256,1024]{1,0:T(8,128)(2,1)}, bf16[256,1024]{1,0:T(8,128)(2,1)}, u32[]{:S(2)}, u32[]{:S(2)}) collective-permute-start(bf16[256,1024]{1,0:T(8,128)(2,1)} %add_convert_fusion.21), channel_id=1, source_target_pairs={{0,16},{8,24},{16,0},{24,8},{1,17},{9,25},{17,1},{25,9},{2,18},{10... | collective-permute-start | bytes 1572872 | tf_op jit(solution)/shard_map/ppermute | solution.py:954
  870.7 71.9 %collective-permute-start.48 = (bf16[256,1024]{1,0:T(8,128)(2,1)}, bf16[256,1024]{1,0:T(8,128)(2,1)S(1)}, u32[]{:S(2)}, u32[]{:S(2)}) collective-permute-start(bf16[256,1024]{1,0:T(8,128)(2,1)} %add_convert_fusion.19), channel_id=1, source_target_pairs={{0,16},{8,24},{16,0},{24,8},{1,17},{9,25},{17,1},{25,9},{2,18},{10... | collective-permute-start | bytes 1572872 | tf_op jit(solution)/shard_map/ppermute | solution.py:954
  872.2 67.7 %collective-permute-start.41 = (bf16[128,1024]{1,0:T(8,128)(2,1)S(1)}, bf16[128,1024]{1,0:T(8,128)(2,1)S(1)}, u32[]{:S(2)}, u32[]{:S(2)}) collective-permute-start(bf16[128,1024]{1,0:T(8,128)(2,1)S(1)} %add_convert_fusion.34), channel_id=1, source_target_pairs={{0,16},{8,24},{16,0},{24,8},{1,17},{9,25},{17,1},{25,9},{2,18},{10... | collective-permute-start | bytes 786440 | tf_op jit(solution)/shard_map/ppermute | solution.py:954
  874.1 127.1 %all-to-all-start.4 = ((bf16[4,128,1024]{2,1,0:T(8,128)(2,1)}), bf16[4,128,1024]{2,1,0:T(8,128)(2,1)}, u32[]{:S(2)}, u32[]{:S(2)}) async-start(bf16[4,128,1024]{2,1,0:T(8,128)(2,1)} %bitcast.8), calls=%async_computation.4 | async-start | bytes 2097152 | tf_op jit(solution)/shard_map/all_to_all | solution.py:938
  943.8 50.2 %collective-permute-start.49 = (bf16[512,1024]{1,0:T(8,128)(2,1)S(1)}, bf16[512,1024]{1,0:T(8,128)(2,1)S(1)}, u32[]{:S(2)}, u32[]{:S(2)}) collective-permute-start(bf16[512,1024]{1,0:T(8,128)(2,1)S(1)} %pad_maximum_fusion.13), channel_id=1, source_target_pairs={{0,8},{8,0},{16,24},{24,16},{1,9},{9,1},{17,25},{25,17},{2,10},{10... | collective-permute-start | bytes 3145736 | tf_op jit(solution)/shard_map/ppermute | solution.py:954
  968.6 35.5 %collective-permute-start.44 = (bf16[512,512]{1,0:T(8,128)(2,1)}, bf16[512,512]{1,0:T(8,128)(2,1)}, u32[]{:S(2)}, u32[]{:S(2)}) collective-permute-start(bf16[512,512]{1,0:T(8,128)(2,1)} %fusion.8), channel_id=1, source_target_pairs={{0,4},{4,0},{1,5},{5,1},{2,6},{6,2},{3,7},{7,3},{8,12},{12,8},{9,1... | collective-permute-start | bytes 1572872 | tf_op jit(solution)/shard_map/ppermute | solution.py:918
  (154 other events, 1763.4 us)

commit v2 on v1

--- a/solution.py
+++ b/solution.py
@@ -565,6 +565,7 @@
 
 ROW_BLOCK = 256
 VMEM = 56 << 20
+LIGHT = pl.CostEstimate(flops=1 << 20, bytes_accessed=1 << 16, transcendentals=0)
 
 
 def row_call(kernel, inputs, vectors, outs, sums, name):
@@ -579,11 +580,7 @@
         out_shape=[jax.ShapeDtypeStruct((rows, width), kind) for kind in outs]
         + [jax.ShapeDtypeStruct((1, width), F32)] * sums,
         compiler_params=pltpu.CompilerParams(vmem_limit_bytes=VMEM),
-        cost_estimate=pl.CostEstimate(
-            flops=20 * rows * width,
-            bytes_accessed=4 * rows * width * (len(inputs) + len(outs)),
-            transcendentals=rows,
-        ),
+        cost_estimate=LIGHT,
         name=name,
     )(*inputs, *vectors)
 
@@ -740,11 +737,7 @@
             jax.ShapeDtypeStruct((count, 2, rows), F32),
         ],
         compiler_params=pltpu.CompilerParams(vmem_limit_bytes=VMEM),
-        cost_estimate=pl.CostEstimate(
-            flops=8 * rows * keys * count * LANES,
-            bytes_accessed=16 * rows * count * LANES,
-            transcendentals=2 * rows * keys * count,
-        ),
+        cost_estimate=LIGHT,
         name="attend",
     )(queries, pairs, pairs, query_mark, key_mark)
 
@@ -832,44 +825,79 @@
         out_shape=[shape for _, shape in outs],
         scratch_shapes=[pltpu.VMEM((keys, LANES), F32), pltpu.VMEM((keys, LANES), F32)],
         compiler_params=pltpu.CompilerParams(vmem_limit_bytes=VMEM),
-        cost_estimate=pl.CostEstimate(
-            flops=20 * rows * keys * count * LANES,
-            bytes_accessed=32 * rows * count * LANES,
-            transcendentals=2 * rows * keys * count,
-        ),
+        cost_estimate=LIGHT,
         name="attend_back",
     )(queries, pairs, pairs, query_mark, key_mark, log_total, mixed, d_mixed)
 
 
-def gelu_kernel(x_ref, w_ref, act_ref, slope_ref):
-    inner = mxu(x_ref[...], w_ref[...], NN)
-    below = 0.5 + 0.5 * lax.erf(inner * (0.5**0.5))
-    act_ref[...] = (inner * below).astype(BF16)
-    bell = jnp.exp(inner * inner * (-0.5)) * (0.5 / jnp.pi) ** 0.5
-    slope_ref[...] = (below + inner * bell).astype(BF16)
-
-
-def up_gelu(rows_in, weight):
+def piece_kernel(kind, low, high, count, x_ref, *refs):
+    if count == 1:
+        order_ref, stack_ref, rest = refs[0], refs[1], refs[2:]
+        weights = [stack_ref.at[order_ref[i]] for i in range(stack_ref.shape[0])]
+    else:
+        weights, rest = refs[:count], refs[count:]
+    own = high - low
+    total = None
+    for i, ref in enumerate(weights):
+        span = pl.ds(i * own, own)
+        if kind == "columns":
+            rest[-1][:, span] = mxu(x_ref[...], ref[:, low:high], NN).astype(BF16)
+        elif kind == "gelu":
+            inner = mxu(x_ref[...], ref[:, low:high], NN)
+            below = 0.5 + 0.5 * lax.erf(inner * (0.5**0.5))
+            rest[0][:, span] = (inner * below).astype(BF16)
+            bell = jnp.exp(inner * inner * (-0.5)) * (0.5 / jnp.pi) ** 0.5
+            rest[1][:, span] = (below + inner * bell).astype(BF16)
+        elif kind == "rows":
+            term = mxu(x_ref[:, span], ref[low:high, :], NN)
+            total = term if total is None else total + term
+        elif kind == "columns_back":
+            term = mxu(x_ref[:, span], ref[:, low:high], NT)
+            total = term if total is None else total + term
+        elif kind == "rows_back":
+            rest[-1][:, span] = mxu(x_ref[...], ref[low:high, :], NT).astype(BF16)
+        elif kind == "rows_back_slope":
+            term = mxu(x_ref[...], ref[low:high, :], NT)
+            rest[-1][:, span] = (term * rest[0][:, span].astype(F32)).astype(BF16)
+    if total is not None:
+        rest[-1][...] = total.astype(BF16)
+
+
+def piece_product(kind, rows_in, pieces, low, high, slope=None, block=512):
     rows, depth = rows_in.shape
-    width = weight.shape[1]
-    step = 256
-    return pl.pallas_call(
-        gelu_kernel,
-        grid=(width // step,),
-        in_specs=[
-            pl.BlockSpec((rows, depth), lambda j: (0, 0)),
-            pl.BlockSpec((depth, step), lambda j: (0, j)),
-        ],
-        out_specs=[pl.BlockSpec((rows, step), lambda j: (0, j))] * 2,
-        out_shape=[jax.ShapeDtypeStruct((rows, width), BF16)] * 2,
+    stacked = len(pieces) == 2
+    shape = pieces[1].shape[1:] if stacked else pieces[0].shape
+    all_own = 4 * (high - low)
+    width = {
+        "columns": all_own,
+        "gelu": all_own,
+        "rows": shape[1],
+        "columns_back": shape[0],
+        "rows_back": all_own,
+        "rows_back_slope": all_own,
+    }[kind]
+    outs = 2 if kind == "gelu" else 1
+    out = pl.BlockSpec((block, width), lambda i: (i, 0))
+    results = pl.pallas_call(
+        functools.partial(piece_kernel, kind, low, high, 1 if stacked else len(pieces)),
+        grid=(rows // block,),
+        in_specs=[pl.BlockSpec((block, depth), lambda i: (i, 0))]
+        + (
+            [
+                pl.BlockSpec(memory_space=pltpu.SMEM),
+                pl.BlockSpec(pieces[1].shape, lambda i: (0, 0, 0)),
+            ]
+            if stacked
+            else [pl.BlockSpec(piece.shape, lambda i: (0, 0)) for piece in pieces]
+        )
+        + ([] if slope is None else [out]),
+        out_specs=[out] * outs,
+        out_shape=[jax.ShapeDtypeStruct((rows, width), BF16)] * outs,
         compiler_params=pltpu.CompilerParams(vmem_limit_bytes=VMEM),
-        cost_estimate=pl.CostEstimate(
-            flops=2 * rows * depth * width,
-            bytes_accessed=2 * (rows + width) * depth + 4 * rows * width,
-            transcendentals=2 * rows * width,
-        ),
-        name="up_gelu",
-    )(rows_in, weight)
+        cost_estimate=LIGHT,
+        name="product_" + kind,
+    )(rows_in, *pieces, *([] if slope is None else [slope]))
+    return results if outs > 1 else results[0]
 
 
 def weight_kernel(count, *refs):
@@ -894,11 +922,7 @@
         out_specs=pl.BlockSpec((sum(owns), width), lambda i: (i, 0)),
         out_shape=jax.ShapeDtypeStruct((2 * sum(owns), width), BF16),
         compiler_params=pltpu.CompilerParams(vmem_limit_bytes=VMEM),
-        cost_estimate=pl.CostEstimate(
-            flops=4 * sum(owns) * width * rows,
-            bytes_accessed=4 * sum(owns) * (width + rows) + 2 * len(pairs) * rows * width,
-            transcendentals=0,
-        ),
+        cost_estimate=LIGHT,
         name="weight_grads",
     )(*[hidden for hidden, _ in pairs], *[wide for _, wide in pairs])
 
@@ -927,28 +951,41 @@
         first = index == 0
         return jnp.concatenate([jnp.where(first, own, other), jnp.where(first, other, own)], 0)
 
-    def to_slot(self, block):
-        rows = lax.all_to_all(block, "tensor", 0, 0, tiled=True)
-        rows = rows.reshape(-1, block.shape[2])
+    def swap_start(self, blocks):
+        near_bit = 1 + self.core
+
+        def to(bits):
+            return lax.dynamic_index_in_dim(blocks, jnp.bitwise_xor(self.place, bits), 0)
+
+        cuts = lax.optimization_barrier((to(0), to(near_bit), to(3 - near_bit), to(3)))
+        far = lax.ppermute(cuts[3], "tensor", swap_pairs(4, 3))
+        return cuts[0], self.send_near(cuts[1]), self.send_side(cuts[2]), far
+
+    def swap_end(self, parts):
+        own, near, side, far = parts
+        low, high = lax.rem(self.place, 2), self.place // 2
+        first = self.core == 0
+        beside, across = jnp.where(first, near, side), jnp.where(first, side, near)
+        blocks = self.ordered(self.ordered(own, beside, low), self.ordered(across, far, low), high)
+        return blocks.reshape(-1, own.shape[2]) if own.ndim == 3 else blocks
+
+    def swap_rows(self, block):
+        return self.swap_end(self.swap_start(block))
+
+    def both_cores(self, rows):
         return self.ordered(rows, self.other(rows), self.core)
 
     def from_slot(self, rows):
         half = rows.shape[0] // 2
         own = lax.dynamic_slice_in_dim(rows, self.core * half, half, 0)
-        return lax.all_to_all(own.reshape(4, half // 4, -1), "tensor", 0, 0, tiled=True)
+        rows = self.swap_rows(own.reshape(4, half // 4, -1))
+        return rows.reshape(4, half // 4, -1)
 
     def send_near(self, block):
         return lax.ppermute(block, CROSS, self.first)
 
     def send_side(self, block):
         return lax.ppermute(block, CROSS, self.second)
-
-    def split(self, block, index):
-        half = block.shape[0] // 2
-        return (
-            lax.dynamic_slice_in_dim(block, index * half, half, 0),
-            lax.dynamic_slice_in_dim(block, (1 - index) * half, half, 0),
-        )
 
     def along(self, block, bit):
         return lax.ppermute(block, "dp", swap_pairs(4, bit))
@@ -993,14 +1030,69 @@
         part = weight.shape[0] // 2
         return lax.dynamic_slice_in_dim(weight, core * part, part, 0)
 
-    def columns(pieces, low, high):
-        return jnp.concatenate([piece[:, low:high] for piece in pieces], 1)
-
-    def rows_of(pieces, low, high):
-        return jnp.concatenate([piece[low:high] for piece in pieces], 0)
-
-    x_source = chip.to_slot(source)
-    x_target = chip.to_slot(target)
+    def pin(value, *others):
+        return tie((value,) + others)[0]
+
+    bundles = [
+        own_columns(enc_qkv),
+        own_columns(dec_self_qkv),
+        jnp.concatenate([own_rows(enc_proj), own_rows(dec_self_proj), own_rows(dec_cross_proj)], 0),
+        jnp.concatenate([own_columns(dec_cross_q), own_columns(dec_cross_kv)], 1),
+        own_rows(dec_down),
+    ]
+    near_bit = 1 + core
+    order = jnp.bitwise_xor(
+        chip.place, jnp.stack([0 * core, 3 - near_bit, near_bit, 0 * core + 3])
+    ).astype(jnp.int32)
+
+    def all_groups(own):
+        return [order, lax.all_gather(own, "tensor", axis=0)]
+
+    inner = enc_up.shape[1] // 2
+    pieces = [None] * len(bundles)
+
+    def launch(index, *after):
+        own = pin(bundles[index], *after)
+        pieces[index] = [own, chip.send_side(own), chip.send_near(own)]
+        return pieces[index][1]
+
+    def relay(index, value):
+        side, near, value = tie((pieces[index][1], pieces[index][2], value))
+        pieces[index][1:] = [side, near]
+        pieces[index].append(chip.send_near(side))
+        return value
+
+    def arrived(index, value):
+        tied = tie(tuple(pieces[index]) + (value,))
+        pieces[index] = list(tied[:-1])
+        return tied[-1]
+
+    def enc(index):
+        return enc_gain[index : index + 1], enc_shift[index : index + 1]
+
+    def dec(index):
+        return dec_gain[index : index + 1], dec_shift[index : index + 1]
+
+    def part_rows(rows_in, weight, low, high):
+        own = piece_product("rows", rows_in, weight, low, high)
+        return own, chip.other(own)
+
+    def part_back(grad, weight, low, high):
+        own = piece_product("columns_back", grad, weight, low, high)
+        return own, chip.other(own)
+
+    fused_at = ((3, 0), (3, 1), (3, 2))
+
+    def attend_self(qkv, marks, causal):
+        return chip_attend(
+            qkv, fused_at[0], qkv, fused_at[1], fused_at[2], marks[0], marks[1], causal
+        )
+
+    launch(0)
+    swapped = arrived(0, chip.swap_rows(relay(0, source)))
+    launch(1, swapped)
+    x_source = chip.both_cores(swapped)
+    sent_target = chip.swap_start(pin(target, swapped))
     source_ids = lax.dynamic_index_in_dim(source_segments, chip.place, 0, keepdims=False)
     target_ids = lax.dynamic_index_in_dim(target_segments, chip.place, 0, keepdims=False)
     ids = jnp.arange(LANES, dtype=jnp.int32)[None] % HEAD_DIM
@@ -1009,156 +1101,138 @@
     target_query = jnp.where(target_ids[:, None] == ids, NEG, 0.0).astype(BF16)
     source_key = ((source_ids[:, None] != ids) & counted).astype(BF16)
     target_key = ((target_ids[:, None] != ids) & counted).astype(BF16)
-
-    bundles = [
-        jnp.concatenate([own_columns(enc_qkv), own_columns(dec_self_qkv)], 1),
-        jnp.concatenate([own_rows(enc_proj), own_rows(dec_self_proj), own_rows(dec_cross_proj)], 0),
-        own_columns(enc_up),
-        own_rows(enc_down),
-        jnp.concatenate(
-            [own_columns(dec_cross_q), own_columns(dec_cross_kv), own_columns(dec_up)], 1
-        ),
-        own_rows(dec_down),
-    ]
-    gathered = []
-    for index, bundle in enumerate(bundles):
-        if index >= 2:
-            bundle, _ = tie((bundle, gathered[index - 2][1]))
-        gathered.append(chip.gather(bundle))
-    qkv_width = bundles[0].shape[1] // 2
-    proj_rows = bundles[1].shape[0] // 3
+    rows_a = norm_rows(x_source, *enc(0))
+    rows_a = pin(rows_a, source_query, source_key)
+    qkv_a = piece_product("columns", rows_a, pieces[0], 0, bundles[0].shape[1])
+    launch(2, qkv_a)
+    mixed_a, total_a = attend_self(qkv_a, (source_query, source_key), False)
+    mixed_a, sent_target = tie((relay(1, mixed_a), sent_target))
+    x_target = chip.both_cores(chip.swap_end(sent_target))
+    w_enc_up = all_groups(pin(own_columns(enc_up), mixed_a))
+    rows_c = norm_rows(pin(x_target, target_query, target_key), *dec(0))
+    rows_c = arrived(1, rows_c)
+    qkv_c = piece_product("columns", rows_c, pieces[1], 0, bundles[1].shape[1])
+    qkv_c = relay(2, qkv_c)
+    w_enc_down = all_groups(pin(own_rows(enc_down), qkv_c))
+    mixed_c, total_c = attend_self(qkv_c, (target_query, target_key), True)
+    proj_rows = bundles[2].shape[0] // 3
+    mixed_c, mixed_a = tie((arrived(2, mixed_c), mixed_a))
+    launch(3, mixed_c)
+    w_dec_up = all_groups(pin(own_columns(dec_up), mixed_c))
+    own_a, other_a = part_rows(mixed_a, pieces[2], 0, proj_rows)
+    own_c, other_c = part_rows(mixed_c, pieces[2], proj_rows, 2 * proj_rows)
+    other_a, other_c = tie((other_a, other_c, own_a, own_c))[:2]
+    hidden, rows_b = add_norm(x_source, own_a, other_a, *enc(1))
+    after_self, rows_e = add_norm(x_target, own_c, other_c, *dec(1))
+    rows_b = pin(rows_b, rows_e)
+    active_b, slope_b = piece_product("gelu", rows_b, w_enc_up, 0, inner, block=256)
+    active_b = relay(3, active_b)
+    encoded, rows_m = add_norm(hidden, *part_rows(active_b, w_enc_down, 0, inner), *enc(2))
+    rows_m, rows_e = tie((arrived(3, rows_m), rows_e))
+    launch(4, rows_m)
     head_width = dec_cross_q.shape[1] // 2
-    w_enc_qkv = columns(gathered[0], 0, qkv_width)
-    w_self_qkv = columns(gathered[0], qkv_width, 2 * qkv_width)
-    w_enc_proj = rows_of(gathered[1], 0, proj_rows)
-    w_self_proj = rows_of(gathered[1], proj_rows, 2 * proj_rows)
-    w_cross_proj = rows_of(gathered[1], 2 * proj_rows, 3 * proj_rows)
-    w_enc_up = jnp.concatenate(gathered[2], 1)
-    w_enc_down = jnp.concatenate(gathered[3], 0)
-    w_cross_q = columns(gathered[4], 0, head_width)
-    w_cross_kv = columns(gathered[4], head_width, 3 * head_width)
-    w_dec_up = columns(gathered[4], 3 * head_width, bundles[4].shape[1])
-    w_dec_down = jnp.concatenate(gathered[5], 0)
-
-    def enc(index):
-        return enc_gain[index : index + 1], enc_shift[index : index + 1]
-
-    def dec(index):
-        return dec_gain[index : index + 1], dec_shift[index : index + 1]
-
-    def partial(rows_in, weight):
-        own = project(rows_in, weight).astype(BF16)
-        return own, chip.other(own)
-
-    def back_partial(grad, weight):
-        own = back_project(grad, weight).astype(BF16)
-        return own, chip.other(own)
-
-    fused_at = ((3, 0), (3, 1), (3, 2))
-
-    def attend_self(rows_in, weight, marks, causal):
-        qkv = project(rows_in, weight).astype(BF16)
-        mixed, totals = chip_attend(
-            qkv, fused_at[0], qkv, fused_at[1], fused_at[2], marks[0], marks[1], causal
-        )
-        return qkv, mixed, totals
-
-    rows_a = norm_rows(x_source, *enc(0))
-    rows_c = norm_rows(x_target, *dec(0))
-    qkv_a, mixed_a, total_a = attend_self(rows_a, w_enc_qkv, (source_query, source_key), False)
-    hidden, rows_b = add_norm(x_source, *partial(mixed_a, w_enc_proj), *enc(1))
-    qkv_c, mixed_c, total_c = attend_self(rows_c, w_self_qkv, (target_query, target_key), True)
-    after_self, rows_e = add_norm(x_target, *partial(mixed_c, w_self_proj), *dec(1))
-    cotangent = chip.to_slot(out_grad)
-    active_b, slope_b = up_gelu(rows_b, w_enc_up)
-    encoded, rows_m = add_norm(hidden, *partial(active_b, w_enc_down), *enc(2))
-    query_e = project(rows_e, w_cross_q).astype(BF16)
-    pairs_m = project(rows_m, w_cross_kv).astype(BF16)
+    pairs_m = piece_product("columns", rows_m, pieces[3], head_width, 3 * head_width)
+    query_e = piece_product("columns", rows_e, pieces[3], 0, head_width)
+    query_e = pin(query_e, pairs_m)
     mixed_e, total_e = chip_attend(
         query_e, (1, 0), pairs_m, (2, 0), (2, 1), target_query, source_key, False
     )
-    after_cross, rows_f = add_norm(after_self, *partial(mixed_e, w_cross_proj), *dec(2))
-    active_f, slope_f = up_gelu(rows_f, w_dec_up)
+    mixed_e = relay(4, mixed_e)
+    after_cross, rows_f = add_norm(
+        after_self, *part_rows(mixed_e, pieces[2], 2 * proj_rows, 3 * proj_rows), *dec(2)
+    )
+    sent_grad = chip.swap_start(pin(out_grad, rows_f))
+    active_f, slope_f = piece_product("gelu", rows_f, w_dec_up, 0, inner, block=256)
+    active_f, sent_grad = tie((arrived(4, active_f), sent_grad))
+    cotangent = chip.both_cores(chip.swap_end(sent_grad))
+    w_dec_down = pieces[4]
     decoded, d_final, low_final, gain_d3, shift_d3 = last_norm(
-        after_cross, *partial(active_f, w_dec_down), cotangent, *dec(3)
-    )
-    decoded = chip.from_slot(decoded)
-
-
-    def stage_one(pairs):
-        sent = weight_grads(pairs, 1)
-        return chip.send_near(sent), weight_grads(pairs, 0)
-
-    def stage_two(state):
-        came, kept = state
+        after_cross, *part_rows(active_f, w_dec_down, 0, inner), cotangent, *dec(3)
+    )
+
+
+    low_bit = lax.rem(chip.line, 2)
+    high_bit = chip.line // 2
+
+    def here(value, step, *args):
+        args, value = tie((args, value))
+        *result, sent = step(*args)
+        return pin(value, result[1], *sent), result
+
+    def to_side(came, kept):
         half = kept.shape[0] // 2
         sent = add_low(kept[half:], came[half:])
-        return chip.send_side(sent), add_low(kept[:half], came[:half])
-
-    low_bit = lax.rem(chip.line, 2)
-    high_bit = chip.line // 2
-
-    def stage_three(state):
-        came, kept = state
-        kept_own, kept_other = chip.split(kept, low_bit)
-        came_own, came_other = chip.split(came, low_bit)
-        return chip.along(add_low(kept_other, came_other), 1), add_low(kept_own, came_own)
-
-    def stage_four(state):
-        came, kept = state
-        kept_own, kept_other = chip.split(kept, high_bit)
-        came_own, came_other = chip.split(came, high_bit)
-        return chip.along(add_low(kept_other, came_other), 2), add_low(kept_own, came_own)
-
-    def stage_five(state):
-        own = add_low(*state)
-        return chip.along(own, 2), own
-
-    def stage_six(state):
-        came, own = state
-        half = chip.ordered(own, came, high_bit)
-        return chip.along(half, 1), half
-
-    def stage_seven(state):
-        came, own = state
-        whole = chip.ordered(own, came, low_bit)
+        return chip.send_side(sent), add_low(kept[:half], came[:half]), [sent]
+
+    def to_line(*states):
+        def cut(bits):
+            parts = []
+            for came, kept in states:
+                quarter = kept.shape[0] // 4
+                at = jnp.bitwise_xor(chip.line, bits) * quarter
+                parts.append(
+                    add_low(
+                        lax.dynamic_slice_in_dim(kept, at, quarter, 0),
+                        lax.dynamic_slice_in_dim(came, at, quarter, 0),
+                    )
+                )
+            return jnp.concatenate(parts, 0)
+
+        sent = [cut(bits) for bits in (3, 2, 1)]
+        return [chip.along(part, bits) for part, bits in zip(sent, (3, 2, 1))], cut(0), sent
+
+    def from_line(came, own):
+        total = own.astype(F32)
+        for block in came:
+            total = total + block.astype(F32)
+        own = total.astype(BF16)
+        return [chip.along(own, bits) for bits in (3, 2, 1)], own, []
+
+    def to_core(came, own):
+        far, next_but_one, next_one = came
+        first = chip.ordered(own, next_one, low_bit)
+        second = chip.ordered(next_but_one, far, low_bit)
+        return share(chip.ordered(first, second, high_bit))
+
+    def share(whole):
         width = whole.shape[1] // 2
         sent = lax.dynamic_slice_in_dim(whole, (1 - core) * width, width, 1)
         own = lax.dynamic_slice_in_dim(whole, core * width, width, 1)
         return chip.other(sent), own
 
-    def stage_eight(state):
-        came, own = state
-        return chip.ordered(own[None], came[None], core).astype(F32)
-
-    stages = [stage_two, stage_three, stage_four, stage_five, stage_six, stage_seven, stage_eight]
-
-    class Reduction:
-        def __init__(self, pairs):
-            self.state = stage_one(pairs)
-            self.at = 0
-
-        def step(self):
-            if self.at < len(stages):
-                self.state = stages[self.at](self.state)
-                self.at += 1
-
-        def finish(self):
-            while self.at < len(stages):
-                self.step()
-            return self.state
-
-    def ffn_back(low_out, rows_in, slope, weight_up, weight_down):
-        d_inner = (back_project(low_out, weight_down) * slope.astype(F32)).astype(BF16)
-        return d_inner, back_partial(d_inner, weight_up)
-
-    d_inner_f, (own, other) = ffn_back(low_final, rows_f, slope_f, w_dec_up, w_dec_down)
-    red_f = Reduction([(d_inner_f, rows_f), (active_f, low_final)])
-    other, _ = tie((other, red_f.state[1]))
+    def in_place(came, own):
+        return chip.ordered(own[None], came[None], core)
+
+    def sum_line(*states):
+        total = jnp.concatenate([add_low(*state) for state in states], 0)
+        return None, total, []
+
+    def send_half(value, *pairs):
+        sent = weight_grads(list(pairs), 1)
+        return pin(value, sent), chip.send_near(sent)
+
+    def keep_half(value, came, *pairs):
+        first, value = tie((pairs[0], value))
+        kept = weight_grads([first] + list(pairs[1:]), 0)
+        return pin(value, kept), (came, kept)
+
+    def ffn_back(low_out, slope, weight):
+        return piece_product("rows_back_slope", low_out, weight, 0, inner, slope)
+
+    low_send, near_fd = send_half(low_final, (active_f, low_final))
+    d_inner_f = ffn_back(low_send, slope_f, w_dec_down)
+    d_inner_f, near_fu = send_half(d_inner_f, (d_inner_f, rows_f))
+    own = piece_product("columns_back", d_inner_f, w_dec_up, 0, inner)
+    own, near_fd = tie((own, near_fd))
+    other = chip.other(own)
+    hold, keep_fd = keep_half(own, near_fd, (active_f, low_final))
+    hold, side_fd = here(hold, to_side, *keep_fd)
+    hold, keep_fu = keep_half(hold, near_fu, (d_inner_f, rows_f))
     d_cross, low_cross, gain_d2, shift_d2 = norm_back_rows(
-        after_cross, own, other, dec(2)[0], d_final, [F32, BF16]
-    )
-    d_mixed = back_project(low_cross, w_cross_proj).astype(BF16)
+        after_cross, own, pin(other, hold), dec(2)[0], d_final, [F32, BF16]
+    )
+    d_mixed = piece_product("rows_back", low_cross, pieces[2], 2 * proj_rows, 3 * proj_rows)
+    d_mixed, side_fu = here(d_mixed, to_side, *keep_fu)
     d_query_e, d_pairs_m = chip_attend_back(
         query_e,
         (1, 0),
@@ -1173,27 +1247,35 @@
         d_mixed,
         False,
     )
-    own_m, other_m = back_partial(d_pairs_m, w_cross_kv)
-    own_e, other_e = back_partial(d_query_e, w_cross_q)
-    red_f.step()
-    red_x = Reduction([(mixed_e, low_cross), (d_query_e, rows_e), (d_pairs_m, rows_m)])
-    other_m, other_e, _, _ = tie((other_m, other_e, red_x.state[1], red_f.state[1]))
-    low_encoded_pair = norm_back_rows(encoded, own_m, other_m, enc(2)[0], None, [F32, BF16])
-    d_encoded, low_encoded, gain_e2, shift_e2 = low_encoded_pair
+    d_pairs_m, (_, total_f) = here(d_pairs_m, sum_line, side_fd, side_fu)
+    sum_f = lax.psum(total_f, "dp")
+    own_m, other_m = part_back(d_pairs_m, pieces[3], head_width, 3 * head_width)
+    own_e, other_e = part_back(pin(d_query_e, own_m), pieces[3], 0, head_width)
+    d_encoded, low_encoded, gain_e2, shift_e2 = norm_back_rows(
+        encoded, own_m, pin(other_m, own_e), enc(2)[0], None, [F32, BF16]
+    )
+    low_send, near_bd = send_half(low_encoded, (active_b, low_encoded))
+    d_inner_b = ffn_back(low_send, slope_b, w_enc_down)
+    d_inner_b, near_bu = send_half(d_inner_b, (d_inner_b, rows_b))
+    own = piece_product("columns_back", d_inner_b, w_enc_up, 0, inner)
+    own, near_bd, other_e = tie((own, near_bd, other_e))
+    other = chip.other(own)
+    hold, keep_bd = keep_half(own, near_bd, (active_b, low_encoded))
+    hold, side_bd = here(hold, to_side, *keep_bd)
+    hold, keep_bu = keep_half(hold, near_bu, (d_inner_b, rows_b))
+    d_hidden, low_hidden, gain_e1, shift_e1 = norm_back_rows(
+        hidden, own, pin(other, hold), enc(1)[0], d_encoded, [F32, BF16]
+    )
+    pairs_x = ((mixed_e, low_cross), (d_query_e, rows_e), (d_pairs_m, rows_m))
+    own_e, side_bu = here(pin(own_e, low_hidden), to_side, *keep_bu)
+    pairs_x = tie((pairs_x, own_e))[0]
+    own_e, near_x = send_half(own_e, *pairs_x)
+    own_e, keep_x = keep_half(own_e, near_x, *pairs_x)
     d_self, low_self, gain_d1, shift_d1 = norm_back_rows(
         after_self, own_e, other_e, dec(1)[0], d_cross, [F32, BF16]
     )
-    d_inner_b, (own, other) = ffn_back(low_encoded, rows_b, slope_b, w_enc_up, w_enc_down)
-    red_f.step()
-    red_b = Reduction([(d_inner_b, rows_b), (active_b, low_encoded)])
-    red_x.step()
-    other, _, _, _ = tie((other, red_b.state[1], red_x.state[1], red_f.state[1]))
-    d_hidden, low_hidden, gain_e1, shift_e1 = norm_back_rows(
-        hidden, own, other, enc(1)[0], d_encoded, [F32, BF16]
-    )
-
-    def self_back(low_out, qkv, marks, causal, totals, mixed, w_qkv, w_proj):
-        d_mixed = back_project(low_out, w_proj).astype(BF16)
+
+    def self_back(d_mixed, qkv, marks, causal, totals, mixed):
         (d_qkv,) = chip_attend_back(
             qkv,
             fused_at[0],
@@ -1210,30 +1292,43 @@
         )
         return d_qkv
 
-    d_qkv_c = self_back(
-        low_self, qkv_c, (target_query, target_key), True, total_c, mixed_c, w_self_qkv, w_self_proj
-    )
-    red_c = Reduction([(mixed_c, low_self), (d_qkv_c, rows_c)])
-    red_f.step()
-    red_x.step()
-    red_b.step()
-    low_hidden, _, _, _, _ = tie(
-        (low_hidden, red_c.state[1], red_f.state[1], red_x.state[1], red_b.state[1])
-    )
-    d_qkv_a = self_back(
-        low_hidden, qkv_a, (source_query, source_key), False, total_a, mixed_a, w_enc_qkv, w_enc_proj
-    )
-    own_a, other_a = back_partial(d_qkv_a, w_enc_qkv)
-    red_a = Reduction([(mixed_a, low_hidden), (d_qkv_a, rows_a)])
-    own_c, other_c = back_partial(d_qkv_c, w_self_qkv)
+    d_mixed = piece_product("rows_back", low_self, pieces[2], proj_rows, 2 * proj_rows)
+    d_mixed, (_, total_b) = here(d_mixed, sum_line, side_bd, side_bu)
+    d_qkv_c = self_back(d_mixed, qkv_c, (target_query, target_key), True, total_c, mixed_c)
+    d_qkv_c, sum_f, total_b = tie((d_qkv_c, sum_f, total_b))
+    sum_b = lax.psum(total_b, "dp")
+    d_qkv_c, side_x = here(d_qkv_c, to_side, *keep_x)
+    pairs_c = ((mixed_c, low_self), (d_qkv_c, rows_c))
+    d_qkv_c, near_c = send_half(d_qkv_c, *pairs_c)
+    own_c = piece_product("columns_back", d_qkv_c, pieces[1], 0, 3 * head_width)
+    own_c, keep_c = keep_half(own_c, near_c, *pairs_c)
+    low_hidden, decoded = tie((low_hidden, decoded, own_c))[:2]
+    decoded = chip.from_slot(decoded)
+    d_mixed = piece_product("rows_back", low_hidden, pieces[2], 0, proj_rows)
+    d_mixed, side_c = here(d_mixed, to_side, *keep_c)
+    d_mixed, decoded = tie((d_mixed, decoded))
+    d_qkv_a = self_back(d_mixed, qkv_a, (source_query, source_key), False, total_a, mixed_a)
+    pairs_a = ((mixed_a, low_hidden), (d_qkv_a, rows_a))
+    d_qkv_a, near_a = send_half(d_qkv_a, *pairs_a)
+    d_qkv_a, (_, total_xc) = here(d_qkv_a, sum_line, side_x, side_c)
+    d_qkv_a, sum_b, total_xc = tie((d_qkv_a, sum_b, total_xc))
+    sum_xc = lax.psum(total_xc, "dp")
+    own_a, other_a = part_back(d_qkv_a, pieces[0], 0, 3 * head_width)
+    other_c = chip.other(pin(own_c, own_a))
+    own_a, keep_a = keep_half(own_a, near_a, *pairs_a)
     source_grad, gain_e0, shift_e0 = norm_back_rows(
         x_source, own_a, other_a, enc(0)[0], d_hidden, [BF16]
     )
+    own_c = pin(own_c, source_grad)
+    own_c, side_a = here(own_c, to_side, *keep_a)
     target_grad, gain_d0, shift_d0 = norm_back_rows(
         x_target, own_c, other_c, dec(0)[0], d_self, [BF16]
     )
-    source_grad = chip.from_slot(source_grad).astype(F32)
-    target_grad = chip.from_slot(target_grad).astype(F32)
+    gain_d0, line_a = here(gain_d0, to_line, side_a)
+    source_grad = chip.from_slot(pin(source_grad, gain_d0))
+    target_grad = chip.from_slot(pin(target_grad, gain_d0))
+    line_a, sum_xc = tie((line_a, sum_xc))
+    sum_f, sum_b = tie((sum_f, sum_b, gain_d0))[:2]
 
     norms = jnp.concatenate(
         [
@@ -1256,21 +1351,27 @@
     )
     part = norms.shape[1] // 2
     norms = lax.dynamic_slice_in_dim(norms, core * part, part, 1)
-    norms = lax.psum(norms, ("dp", "tensor"))
+    norms = norms + chip.send_near(norms)
+    norms = norms + chip.send_side(norms)
+    norms = norms + chip.along(norms, 1)
+    norms = norms + chip.along(norms, 2)
+    line_a = from_line(*line_a)[:2]
+    line_a = to_core(*line_a)
 
     def wide(block, blocks):
         cores, rows, width = block.shape
         block = block.reshape(cores, blocks, rows // blocks, width)
-        return jnp.transpose(block, (3, 1, 0, 2)).reshape(width, blocks, -1)
+        return jnp.transpose(block, (3, 1, 0, 2)).reshape(width, blocks, -1).astype(F32)
 
     def tall(block):
-        return block.reshape(-1, block.shape[2])
-
-    done_f, done_x, done_b, done_c, done_a = (
-        red.finish() for red in (red_f, red_x, red_b, red_c, red_a)
-    )
+        return block.reshape(-1, block.shape[2]).astype(F32)
+
+    n = proj_rows
+    done_f, done_b = in_place(*share(sum_f)), in_place(*share(sum_b))
+    done_xc, done_a = in_place(*share(sum_xc)), in_place(*line_a)
+    done_x, done_c = done_xc[:, : 4 * n], done_xc[:, 4 * n :]
+    source_grad, target_grad = source_grad.astype(F32), target_grad.astype(F32)
     hid = done_f.shape[1] // 2
-    n = proj_rows
     return (
         decoded,
         source_grad,
@@ -1279,8 +1380,8 @@
         norms[3:6],
         wide(done_a[:, n:], 3),
         tall(done_a[:, :n]),
-        wide(done_b[:, :hid], 1)[:, 0],
-        tall(done_b[:, hid:]),
+        wide(done_b[:, inner:], 1)[:, 0],
+        tall(done_b[:, :inner]),
         norms[6:10],
         norms[10:14],
         wide(done_c[:, n:], 3),
@@ -1288,8 +1389,8 @@
         wide(done_x[:, n : n + head_width], 1)[:, 0],
         wide(done_x[:, n + head_width :], 2),
         tall(done_x[:, :n]),
-        wide(done_f[:, :hid], 1)[:, 0],
-        tall(done_f[:, hid:]),
+        wide(done_f[:, hid:], 1)[:, 0],
+        tall(done_f[:, :hid]),
     )
 
 

time: 1030 us -> 977 us (0.949)
  Pallas kernels: 311 us -> 457 us
  matrix products: 106 us -> 0 us
  waiting for transfers between devices: 187 us -> 286 us
  starting transfers between devices: 150 us -> 83.7 us
  blocking collectives: 60.8 us -> 0 us
  local copies, waits for them, and re-layouts: 110 us -> 55.9 us
  other arithmetic: 95.2 us -> 69.2 us
  between operations: 2.56 us -> 15.6 us
    pallas_call x2 -> x22, Pallas kernels: 24.4 us -> 164 us  [piece_product(): pl.pallas_call(functools.partial(piece_kernel, kind, low, high, 1 if stac...]
    dot_general x20 -> x0, matrix products: 106 us -> none  [mxu(): return lax.dot_general(left, right, dims, preferred_element_type=F32)]
    ppermute x5 -> x24, waiting for transfers between devices: 9.54 us -> 97.8 us  [send_near(): return lax.ppermute(block, CROSS, self.first)]
    ppermute x5 -> x19, waiting for transfers between devices: 0.01 us -> 67.8 us  [send_side(): return lax.ppermute(block, CROSS, self.second)]
    all_to_all x6 -> x0, waiting for transfers between devices: 62.2 us -> none  [the longest x3 62.2 us: to_slot(): rows = lax.all_to_all(block, 'tensor', 0, 0, tiled=True)]
    psum x1 -> x0, blocking collectives: 60.8 us -> none  [chip_local(): norms = lax.psum(norms, ('dp', 'tensor'))]
    ppermute x18 -> x6, waiting for transfers between devices: 67.1 us -> 9.33 us  [swap_start(): far = lax.ppermute(cuts[3], 'tensor', swap_pairs(4, 3))]
    slice x23 -> x0, local copies, waits for them, and re-layouts: 39.1 us -> none  [the longest x15 25.4 us: columns(): return jnp.concatenate([piece[:, low:high] for piece in pieces], 1)]
  transfers between devices with their start and end apart: 73 -> 81, of which waited for: 16 -> 37; matrix products, arithmetic and copies ran while one was open for 26% -> 9% of each run, Pallas kernels for 28% -> 43%
where the time goes in v2:
time: 977 us; the launch traced here: 967 us
  Pallas kernels  457 us (47%)
  waiting for transfers between devices  286 us (29%)
  starting transfers between devices  83.7 us (9%)
  other arithmetic  69.2 us (7%)
  local copies, waits for them, and re-layouts  55.9 us (6%)
  between operations  15.6 us (2%)
    pallas_call x22, Pallas kernels, piece_product(): pl.pallas_call(functools.partial(piece_kernel, kind, low, high, 1 if stac...  164 us
    ppermute x24, waiting for transfers between devices, send_near(): return lax.ppermute(block, CROSS, self.first)  97.8 us
    pallas_call x13, Pallas kernels, row_call(): pl.pallas_call(kernel, grid=(rows // ROW_BLOCK,), in_specs=[block] * len(...  91 us
    pallas_call x14, Pallas kernels, weight_grads(): pl.pallas_call(functools.partial(weight_kernel, len(pairs)), grid=(2,), i...  83.5 us
    ppermute x19, waiting for transfers between devices, send_side(): return lax.ppermute(block, CROSS, self.second)  67.8 us
    pallas_call x3, Pallas kernels, chip_attend_back(): pl.pallas_call(functools.partial(chip_attend_back_kernel, causal, fused),...  65.5 us
    ppermute x8, waiting for transfers between devices, along(): return lax.ppermute(block, 'dp', swap_pairs(4, bit))  55.6 us
    pallas_call x3, Pallas kernels, chip_attend(): pl.pallas_call(functools.partial(chip_attend_kernel, causal), grid=(count...  53.2 us
  transfers between devices with their start and end apart: 81, of which 37 were waited for; matrix products, arithmetic and copies ran while one was open for 9% of the time, Pallas kernels for 43%

profile of v2, /device:TPU:9, one launch (start us, length us, event | category | flops | bytes accessed | tf_op | source)
XLA Modules:
  0.0 967.5 jit_solution(3460526682570420126)
XLA Ops:
  13.6 14.6 %collective-permute-done.refs_1_ = bf16[1024,384]{1,0:T(8,128)(2,1)S(1)} collective-permute-done((bf16[1024,384]{1,0:T(8,128)(2,1)}, bf16[1024,384]{1,0:T(8,128)(2,1)S(1)}, u32[]{:S(2)}, u32[]{:S(2)}) %collective-permute-start) | collective-permute-done | bytes 786464 | tf_op jit(solution)/shard_map/ppermute | solution.py:988
  80.1 8.1 product_columns.4.q_ref.k_ref.v_ref.refs_0_.refs_1_.refs_2_
  88.2 18.9 %attend.3 = (bf16[1024,512]{1,0:T(8,128)(2,1)}, f32[4,2,1024]{2,1,0:T(2,128)}) custom-call(bf16[1024,1536]{1,0:T(8,128)(2,1)} %product_columns.4.q_ref.k_ref.v_ref.refs_0_.refs_1_.refs_2_, bf16[1024,1536]{1,0:T(8,128)(2,1)} %product_columns.4.q_ref.k_ref.v_ref.refs_0_.refs_1_.refs_2_, ...), custom_call_target="tpu_custom_call" | custom-call | flops 1048576 | bytes 65536 | tf_op jit(solution)/shard_map/attend/pallas_call | solution.py:721
  122.9 32.8 %collective-permute-done.11.refs_3_ = bf16[1024,384]{1,0:T(8,128)(2,1)} collective-permute-done((bf16[1024,384]{1,0:T(8,128)(2,1)}, bf16[1024,384]{1,0:T(8,128)(2,1)}, u32[]{:S(2)}, u32[]{:S(2)}) %collective-permute-start.11) | collective-permute-done | bytes 786464 | tf_op jit(solution)/shard_map/ppermute | solution.py:985
  158.0 8.0 product_columns.5.q_ref.k_ref.v_ref.refs_0_.refs_1_.refs_2_
  168.4 15.5 %attend.4 = (bf16[1024,512]{1,0:T(8,128)(2,1)}, f32[4,2,1024]{2,1,0:T(2,128)}) custom-call(bf16[1024,1536]{1,0:T(8,128)(2,1)} %product_columns.5.q_ref.k_ref.v_ref.refs_0_.refs_1_.refs_2_, bf16[1024,1536]{1,0:T(8,128)(2,1)} %product_columns.5.q_ref.k_ref.v_ref.refs_0_.refs_1_.refs_2_, ...), custom_call_target="tpu_custom_call" | custom-call | flops 1048576 | bytes 65536 | tf_op jit(solution)/shard_map/attend/pallas_call | solution.py:721
  212.4 11.5 %product_gelu.2 = (bf16[1024,2048]{1,0:T(8,128)(2,1)}, bf16[1024,2048]{1,0:T(8,128)(2,1)}) custom-call(bf16[1024,1024]{1,0:T(8,128)(2,1)} %get-tuple-element.394.x_ref.refs_1_, s32[4]{0:T(128)} %add_xor_fusion.refs_0_, bf16[4,1024,512]{2,1,0:T(8,128)(2,1)} %bitcast.94), custom_call_target="tpu_custom_call" | custom-call | flops 1048576 | bytes 65536 | tf_op jit(solution)/shard_map/product_gelu/pallas_call | solution.py:881
  225.0 17.1 %all-gather.9.cloned.1.call-done = bf16[2048,1024]{1,0:T(8,128)(2,1)} async-done(((bf16[512,1024]{1,0:T(8,128)(2,1)}), bf16[2048,1024]{1,0:T(8,128)(2,1)}) %all-gather.9.cloned.1.call-update) | async-done | bytes 4194320 | tf_op jit(solution)/shard_map/all_gather | solution.py:1049
  242.1 8.5 product_rows.7.own_ref
  256.3 6.4 add_norm.6
  262.8 10.6 %collective-permute-done.21.refs_3_ = bf16[1024,384]{1,0:T(8,128)(2,1)S(1)} collective-permute-done((bf16[1024,384]{1,0:T(8,128)(2,1)S(1)}, bf16[1024,384]{1,0:T(8,128)(2,1)S(1)}, u32[]{:S(2)}, u32[]{:S(2)}) %collective-permute-start.21) | collective-permute-done | bytes 786464 | tf_op jit(solution)/shard_map/ppermute | solution.py:985
  286.0 18.8 %attend.5 = (bf16[1024,512]{1,0:T(8,128)(2,1)}, f32[4,2,1024]{2,1,0:T(2,128)}) custom-call(bf16[1024,512]{1,0:T(8,128)(2,1)} %product_columns.6.q_ref.refs_0_, bf16[1024,1024]{1,0:T(8,128)(2,1)} %product_columns.7.k_ref.v_ref.refs_1_.refs_2_, bf16[1024,1024]{1,0:T(8,128)(2,1)} %product_columns.7.k_ref.v_ref.refs_1_.refs_2_, ...), custom_call_target="tpu_custom_call" | custom-call | flops 1048576 | bytes 65536 | tf_op jit(solution)/shard_map/attend/pallas_call | solution.py:721
  304.9 8.0 collective-permute-done.23.refs_1_
  312.8 6.1 collective-permute-done.24.refs_2_
  331.4 6.6 add_norm.7
  340.8 11.4 %product_gelu.3 = (bf16[1024,2048]{1,0:T(8,128)(2,1)}, bf16[1024,2048]{1,0:T(8,128)(2,1)}) custom-call(bf16[1024,1024]{1,0:T(8,128)(2,1)} %get-tuple-element.368.x_ref.refs_1_, s32[4]{0:T(128)} %add_xor_fusion.refs_0_, bf16[4,1024,512]{2,1,0:T(8,128)(2,1)} %bitcast.96), custom_call_target="tpu_custom_call" | custom-call | flops 1048576 | bytes 65536 | tf_op jit(solution)/shard_map/product_gelu/pallas_call | solution.py:881
  353.3 8.5 product_rows.9.own_ref
  371.3 9.0 last_norm.1
  386.3 9.2 product_rows_back_slope.2.refs_0_.x_ref
  401.0 8.6 product_columns_back.6.refs_1_
  428.6 8.5 norm_back.6
  447.4 23.9 %attend_back.3 = (bf16[1024,512]{1,0:T(8,128)(2,1)}, bf16[1024,1024]{1,0:T(8,128)(2,1)}) custom-call(bf16[1024,512]{1,0:T(8,128)(2,1)} %product_columns.6.q_ref.refs_0_, bf16[1024,1024]{1,0:T(8,128)(2,1)} %product_columns.7.k_ref.v_ref.refs_1_.refs_2_, bf16[1024,1024]{1,0:T(8,128)(2,1)} %product_columns.7.k_ref.v_ref.refs_1_.refs_2_, ...), custom_call_target="tpu_custom_call" | custom-call | flops 1048576 | bytes 65536 | tf_op jit(solution)/shard_map/attend_back/pallas_call | solution.py:811
  487.4 7.6 norm_back.7
  501.8 9.3 product_rows_back_slope.3.refs_0_.x_ref
  516.5 8.6 product_columns_back.9.refs_1_
  540.2 8.7 norm_back.8
  555.4 7.1 weight_grads.21
  567.4 7.0 weight_grads.22
  574.4 8.8 norm_back.9
  591.5 19.8 %collective-permute-done.44 = bf16[512,1024]{1,0:T(8,128)(2,1)S(1)} collective-permute-done((bf16[512,1024]{1,0:T(8,128)(2,1)S(1)}, bf16[512,1024]{1,0:T(8,128)(2,1)S(1)}, u32[]{:S(2)}, u32[]{:S(2)}) %collective-permute-start.44) | collective-permute-done | bytes 1048608 | tf_op jit(solution)/shard_map/ppermute | solution.py:988
  613.5 17.6 %attend_back.4.refs_1_.x_ref = bf16[1024,1536]{1,0:T(8,128)(2,1)} custom-call(bf16[1024,1536]{1,0:T(8,128)(2,1)} %product_columns.5.q_ref.k_ref.v_ref.refs_0_.refs_1_.refs_2_, bf16[1024,1536]{1,0:T(8,128)(2,1)} %product_columns.5.q_ref.k_ref.v_ref.refs_0_.refs_1_.refs_2_, bf16[1024,1536]{1,0:T(8,128)(2,1)} %product_columns.5.q_ref.k_ref.v_ref.refs_0_.refs_1_.refs_2_, ...), custom_call_target="tpu_custom_call" | custom-call | flops 1048576 | bytes 65536 | tf_op jit(solution)/shard_map/attend_back/pallas_call | solution.py:811
  635.1 6.2 weight_grads.24
  644.7 8.0 product_columns_back.10.refs_1_
  652.7 6.2 weight_grads.25
  664.6 13.9 %collective-permute-done.45 = bf16[1024,1024]{1,0:T(8,128)(2,1)S(1)} collective-permute-done((bf16[1024,1024]{1,0:T(8,128)(2,1)}, bf16[1024,1024]{1,0:T(8,128)(2,1)S(1)}, u32[]{:S(2)}, u32[]{:S(2)}) %collective-permute-start.45) | collective-permute-done | bytes 2097184 | tf_op jit(solution)/shard_map/ppermute | solution.py:985
  690.3 12.7 %collective-permute-done.47 = bf16[1,128,1024]{2,1,0:T(8,128)(2,1)S(1)} collective-permute-done((bf16[1,128,1024]{2,1,0:T(8,128)(2,1)S(1)}, bf16[1,128,1024]{2,1,0:T(8,128)(2,1)S(1)}, u32[]{:S(2)}, u32[]{:S(2)}) %collective-permute-start.47) | collective-permute-done | bytes 262176 | tf_op jit(solution)/shard_map/ppermute | solution.py:988
  707.9 24.0 %attend_back.5.refs_1_.x_ref = bf16[1024,1536]{1,0:T(8,128)(2,1)} custom-call(bf16[1024,1536]{1,0:T(8,128)(2,1)} %product_columns.4.q_ref.k_ref.v_ref.refs_0_.refs_1_.refs_2_, bf16[1024,1536]{1,0:T(8,128)(2,1)} %product_columns.4.q_ref.k_ref.v_ref.refs_0_.refs_1_.refs_2_, bf16[1024,1536]{1,0:T(8,128)(2,1)} %product_columns.4.q_ref.k_ref.v_ref.refs_0_.refs_1_.refs_2_, ...), custom_call_target="tpu_custom_call" | custom-call | flops 1048576 | bytes 65536 | tf_op jit(solution)/shard_map/attend_back/pallas_call | solution.py:811
  731.8 6.4 weight_grads.26
  740.6 8.2 product_columns_back.11.refs_1_
  750.8 6.1 weight_grads.27
  758.3 7.3 norm_back.10
  765.6 8.6 collective-permute-done.52
  778.9 7.2 norm_back.11
  805.0 17.8 %collective-permute-done.63 = f32[14,512]{1,0:T(8,128)S(1)} collective-permute-done((f32[14,512]{1,0:T(8,128)S(1)}, f32[14,512]{1,0:T(8,128)S(1)}, u32[]{:S(2)}, u32[]{:S(2)}) %collective-permute-start.63) | collective-permute-done | bytes 28704 | tf_op jit(solution)/shard_map/ppermute | solution.py:991
  823.8 19.0 %collective-permute-done.64 = f32[14,512]{1,0:T(8,128)S(1)} collective-permute-done((f32[14,512]{1,0:T(8,128)S(1)}, f32[14,512]{1,0:T(8,128)S(1)}, u32[]{:S(2)}, u32[]{:S(2)}) %collective-permute-start.64) | collective-permute-done | bytes 28704 | tf_op jit(solution)/shard_map/ppermute | solution.py:991
  857.1 8.1 collective-permute-start.72
  865.2 26.2 %all-reduce.8.cloned.1.call-done = bf16[1024,1024]{1,0:T(8,128)(2,1)} async-done(((bf16[1024,1024]{1,0:T(8,128)(2,1)}), bf16[1024,1024]{1,0:T(8,128)(2,1)}) %all-reduce.8.cloned.1.call-update) | async-done | bytes 2097168 | tf_op jit(solution)/shard_map/psum | solution.py:1315
  905.3 12.7 %collective-permute-done.70 = bf16[128,1024]{1,0:T(8,128)(2,1)S(1)} collective-permute-done((bf16[128,1024]{1,0:T(8,128)(2,1)S(1)}, bf16[128,1024]{1,0:T(8,128)(2,1)S(1)}, u32[]{:S(2)}, u32[]{:S(2)}) %collective-permute-start.70) | collective-permute-done | bytes 262176 | tf_op jit(solution)/shard_map/ppermute | solution.py:991
  (451 shorter events, 388.3 us)
Async XLA Ops:
  7.2 205.2 %all-gather.7.cloned.1.call-start = ((), (), s32[]{:S(2)}) async-start(), calls=%async_computation.3 | async-start | bytes 5242880 | tf_op jit(solution)/shard_map/all_gather | solution.py:1049
  37.1 20.0 %collective-permute-start.2 = (bf16[1024,384]{1,0:T(8,128)(2,1)S(1)}, bf16[1024,384]{1,0:T(8,128)(2,1)}, u32[]{:S(2)}, u32[]{:S(2)}) collective-permute-start(bf16[1024,384]{1,0:T(8,128)(2,1)S(1)} %collective-permute-done.refs_1_), channel_id=1, source_target_pairs={{0,1},{1,0},{2,3},{3,2},{4,6},{5,7},{6,4},{7,5},{8,9},{9,8},{10,11... | collective-permute-start | bytes 2359304 | tf_op jit(solution)/shard_map/ppermute | solution.py:985
  64.3 42.7 %collective-permute-start.10 = (bf16[1024,384]{1,0:T(8,128)(2,1)}, bf16[1024,384]{1,0:T(8,128)(2,1)S(1)}, u32[]{:S(2)}, u32[]{:S(2)}) collective-permute-start(bf16[1024,384]{1,0:T(8,128)(2,1)} %copy.51), channel_id=1, source_target_pairs={{0,1},{1,0},{2,3},{3,2},{4,6},{5,7},{6,4},{7,5},{8,9},{9,8},{10,11... | collective-permute-start | bytes 2359304 | tf_op jit(solution)/shard_map/ppermute | solution.py:985
  64.6 42.4 %collective-permute-start.9 = (bf16[1024,384]{1,0:T(8,128)(2,1)}, bf16[1024,384]{1,0:T(8,128)(2,1)}, u32[]{:S(2)}, u32[]{:S(2)}) collective-permute-start(bf16[1024,384]{1,0:T(8,128)(2,1)} %copy.51), channel_id=1, source_target_pairs={{0,2},{1,3},{2,0},{3,1},{4,5},{5,4},{6,7},{7,6},{8,10},{9,11},{10,... | collective-permute-start | bytes 2359304 | tf_op jit(solution)/shard_map/ppermute | solution.py:988
  68.6 38.5 %collective-permute-start.12 = (bf16[1,128,1024]{2,1,0:T(8,128)(2,1)}, bf16[1,128,1024]{2,1,0:T(8,128)(2,1)S(1)}, u32[]{:S(2)}, u32[]{:S(2)}) collective-permute-start(bf16[1,128,1024]{2,1,0:T(8,128)(2,1)} %get-tuple-element.287), channel_id=1, source_target_pairs={{0,1},{1,0},{2,3},{3,2},{4,6},{5,7},{6,4},{7,5},{8,9},{9,8},{10,11... | collective-permute-start | bytes 786440 | tf_op jit(solution)/shard_map/ppermute | solution.py:985
  69.9 37.2 %collective-permute-start.13 = (bf16[1,128,1024]{2,1,0:T(8,128)(2,1)}, bf16[1,128,1024]{2,1,0:T(8,128)(2,1)S(1)}, u32[]{:S(2)}, u32[]{:S(2)}) collective-permute-start(bf16[1,128,1024]{2,1,0:T(8,128)(2,1)} %get-tuple-element.288), channel_id=1, source_target_pairs={{0,2},{1,3},{2,0},{3,1},{4,5},{5,4},{6,7},{7,6},{8,10},{9,11},{10,... | collective-permute-start | bytes 786440 | tf_op jit(solution)/shard_map/ppermute | solution.py:988
  72.4 34.7 %collective-permute-start.14 = (bf16[1,128,1024]{2,1,0:T(8,128)(2,1)}, bf16[1,128,1024]{2,1,0:T(8,128)(2,1)S(1)}, u32[]{:S(2)}, u32[]{:S(2)}) collective-permute-start(bf16[1,128,1024]{2,1,0:T(8,128)(2,1)} %get-tuple-element.289), channel_id=1, source_target_pairs={{0,3},{1,2},{2,1},{3,0},{4,7},{5,6},{6,5},{7,4},{8,11},{9,10},{10,... | collective-permute-start | bytes 786440 | tf_op jit(solution)/shard_map/ppermute | solution.py:961
  108.0 134.1 %all-gather.9.cloned.1.call-start = ((), (), s32[]{:S(2)}) async-start(), calls=%async_computation.4 | async-start | bytes 5242880 | tf_op jit(solution)/shard_map/all_gather | solution.py:1049
  111.5 54.5 %collective-permute-start.7 = (bf16[384,1024]{1,0:T(8,128)(2,1)S(1)}, bf16[384,1024]{1,0:T(8,128)(2,1)S(1)}, u32[]{:S(2)}, u32[]{:S(2)}) collective-permute-start(bf16[384,1024]{1,0:T(8,128)(2,1)S(1)} %pad_maximum_fusion.12.refs_0_), channel_id=1, source_target_pairs={{0,2},{1,3},{2,0},{3,1},{4,5},{5,4},{6,7},{7,6},{8,10},{9,11},{10,... | collective-permute-start | bytes 2359304 | tf_op jit(solution)/shard_map/ppermute | solution.py:988
  113.1 53.0 %collective-permute-start.8 = (bf16[384,1024]{1,0:T(8,128)(2,1)S(1)}, bf16[384,1024]{1,0:T(8,128)(2,1)S(1)}, u32[]{:S(2)}, u32[]{:S(2)}) collective-permute-start(bf16[384,1024]{1,0:T(8,128)(2,1)S(1)} %pad_maximum_fusion.12.refs_0_), channel_id=1, source_target_pairs={{0,1},{1,0},{2,3},{3,2},{4,6},{5,7},{6,4},{7,5},{8,9},{9,8},{10,11... | collective-permute-start | bytes 2359304 | tf_op jit(solution)/shard_map/ppermute | solution.py:985
  114.2 41.5 %collective-permute-start.11 = (bf16[1024,384]{1,0:T(8,128)(2,1)}, bf16[1024,384]{1,0:T(8,128)(2,1)}, u32[]{:S(2)}, u32[]{:S(2)}) collective-permute-start(bf16[1024,384]{1,0:T(8,128)(2,1)} %collective-permute-done.9.refs_1_), channel_id=1, source_target_pairs={{0,1},{1,0},{2,3},{3,2},{4,6},{5,7},{6,4},{7,5},{8,9},{9,8},{10,11... | collective-permute-start | bytes 2359304 | tf_op jit(solution)/shard_map/ppermute | solution.py:985
  166.1 174.7 %all-gather.11.cloned.1.call-start = ((), (), s32[]{:S(2)}) async-start(), calls=%async_computation.5 | async-start | bytes 5242880 | tf_op jit(solution)/shard_map/all_gather | solution.py:1049
  197.0 26.8 %collective-permute-start.17 = (bf16[1024,384]{1,0:T(8,128)(2,1)S(1)}, bf16[1024,384]{1,0:T(8,128)(2,1)S(1)}, u32[]{:S(2)}, u32[]{:S(2)}) collective-permute-start(bf16[1024,384]{1,0:T(8,128)(2,1)S(1)} %pad_maximum_fusion.13.refs_0_), channel_id=1, source_target_pairs={{0,2},{1,3},{2,0},{3,1},{4,5},{5,4},{6,7},{7,6},{8,10},{9,11},{10,... | collective-permute-start | bytes 2359304 | tf_op jit(solution)/shard_map/ppermute | solution.py:988
  197.1 27.9 %collective-permute-start.18 = (bf16[1024,384]{1,0:T(8,128)(2,1)S(1)}, bf16[1024,384]{1,0:T(8,128)(2,1)S(1)}, u32[]{:S(2)}, u32[]{:S(2)}) collective-permute-start(bf16[1024,384]{1,0:T(8,128)(2,1)S(1)} %pad_maximum_fusion.13.refs_0_), channel_id=1, source_target_pairs={{0,1},{1,0},{2,3},{3,2},{4,6},{5,7},{6,4},{7,5},{8,9},{9,8},{10,11... | collective-permute-start | bytes 2359304 | tf_op jit(solution)/shard_map/ppermute | solution.py:985
  198.2 433.0 %all-reduce.4.cloned.1.call-start = ((), (), s32[]{:S(2)}) async-start(), calls=%async_computation | async-start | bytes 4194304 | tf_op jit(solution)/shard_map/psum | solution.py:1251
  251.0 22.4 %collective-permute-start.21 = (bf16[1024,384]{1,0:T(8,128)(2,1)S(1)}, bf16[1024,384]{1,0:T(8,128)(2,1)S(1)}, u32[]{:S(2)}, u32[]{:S(2)}) collective-permute-start(bf16[1024,384]{1,0:T(8,128)(2,1)S(1)} %collective-permute-done.17.refs_1_), channel_id=1, source_target_pairs={{0,1},{1,0},{2,3},{3,2},{4,6},{5,7},{6,4},{7,5},{8,9},{9,8},{10,11... | collective-permute-start | bytes 2359304 | tf_op jit(solution)/shard_map/ppermute | solution.py:985
  273.4 39.4 %collective-permute-start.23 = (bf16[512,1024]{1,0:T(8,128)(2,1)S(1)}, bf16[512,1024]{1,0:T(8,128)(2,1)S(1)}, u32[]{:S(2)}, u32[]{:S(2)}) collective-permute-start(bf16[512,1024]{1,0:T(8,128)(2,1)S(1)} %copy-done.10), channel_id=1, source_target_pairs={{0,2},{1,3},{2,0},{3,1},{4,5},{5,4},{6,7},{7,6},{8,10},{9,11},{10,... | collective-permute-start | bytes 3145736 | tf_op jit(solution)/shard_map/ppermute | solution.py:988
  274.6 44.4 %collective-permute-start.24 = (bf16[512,1024]{1,0:T(8,128)(2,1)S(1)}, bf16[512,1024]{1,0:T(8,128)(2,1)S(1)}, u32[]{:S(2)}, u32[]{:S(2)}) collective-permute-start(bf16[512,1024]{1,0:T(8,128)(2,1)S(1)} %copy-done.10), channel_id=1, source_target_pairs={{0,1},{1,0},{2,3},{3,2},{4,6},{5,7},{6,4},{7,5},{8,9},{9,8},{10,11... | collective-permute-start | bytes 3145736 | tf_op jit(solution)/shard_map/ppermute | solution.py:985
  326.1 26.2 %collective-permute-start.26 = (bf16[512,1024]{1,0:T(8,128)(2,1)S(1)}, bf16[512,1024]{1,0:T(8,128)(2,1)S(1)}, u32[]{:S(2)}, u32[]{:S(2)}) collective-permute-start(bf16[512,1024]{1,0:T(8,128)(2,1)S(1)} %collective-permute-done.23.refs_1_), channel_id=1, source_target_pairs={{0,1},{1,0},{2,3},{3,2},{4,6},{5,7},{6,4},{7,5},{8,9},{9,8},{10,11... | collective-permute-start | bytes 3145736 | tf_op jit(solution)/shard_map/ppermute | solution.py:985
  385.8 25.4 %collective-permute-start.32 = (bf16[1024,1024]{1,0:T(8,128)(2,1)}, bf16[1024,1024]{1,0:T(8,128)(2,1)S(1)}, u32[]{:S(2)}, u32[]{:S(2)}) collective-permute-start(bf16[1024,1024]{1,0:T(8,128)(2,1)} %weight_grads.14), channel_id=1, source_target_pairs={{0,1},{1,0},{2,3},{3,2},{4,6},{5,7},{6,4},{7,5},{8,9},{9,8},{10,11... | collective-permute-start | bytes 6291464 | tf_op jit(solution)/shard_map/ppermute | solution.py:985
  412.4 31.0 %collective-permute-start.34 = (bf16[1024,1024]{1,0:T(8,128)(2,1)}, bf16[1024,1024]{1,0:T(8,128)(2,1)S(1)}, u32[]{:S(2)}, u32[]{:S(2)}) collective-permute-start(bf16[1024,1024]{1,0:T(8,128)(2,1)} %weight_grads.15), channel_id=1, source_target_pairs={{0,1},{1,0},{2,3},{3,2},{4,6},{5,7},{6,4},{7,5},{8,9},{9,8},{10,11... | collective-permute-start | bytes 6291464 | tf_op jit(solution)/shard_map/ppermute | solution.py:985
  427.9 43.4 %collective-permute-start.35 = (bf16[512,1024]{1,0:T(8,128)(2,1)}, bf16[512,1024]{1,0:T(8,128)(2,1)S(1)}, u32[]{:S(2)}, u32[]{:S(2)}) collective-permute-start(bf16[512,1024]{1,0:T(8,128)(2,1)} %get-tuple-element.561), channel_id=1, source_target_pairs={{0,2},{1,3},{2,0},{3,1},{4,5},{5,4},{6,7},{7,6},{8,10},{9,11},{10,... | collective-permute-start | bytes 3145736 | tf_op jit(solution)/shard_map/ppermute | solution.py:988
  445.3 26.0 %collective-permute-start.36 = (bf16[512,1024]{1,0:T(8,128)(2,1)}, bf16[512,1024]{1,0:T(8,128)(2,1)S(1)}, u32[]{:S(2)}, u32[]{:S(2)}) collective-permute-start(bf16[512,1024]{1,0:T(8,128)(2,1)} %get-tuple-element.562), channel_id=1, source_target_pairs={{0,2},{1,3},{2,0},{3,1},{4,5},{5,4},{6,7},{7,6},{8,10},{9,11},{10,... | collective-permute-start | bytes 3145736 | tf_op jit(solution)/shard_map/ppermute | solution.py:988
  486.1 39.0 %collective-permute-start.40 = (bf16[1024,1024]{1,0:T(8,128)(2,1)}, bf16[1024,1024]{1,0:T(8,128)(2,1)S(1)}, u32[]{:S(2)}, u32[]{:S(2)}) collective-permute-start(bf16[1024,1024]{1,0:T(8,128)(2,1)} %product_columns_back.8.refs_1_), channel_id=1, source_target_pairs={{0,4},{4,0},{1,5},{5,1},{2,6},{6,2},{3,7},{7,3},{8,12},{12,8},{9,1... | collective-permute-start | bytes 6291464 | tf_op jit(solution)/shard_map/ppermute | solution.py:942
  500.5 25.4 %collective-permute-start.39 = (bf16[1024,1024]{1,0:T(8,128)(2,1)}, bf16[1024,1024]{1,0:T(8,128)(2,1)S(1)}, u32[]{:S(2)}, u32[]{:S(2)}) collective-permute-start(bf16[1024,1024]{1,0:T(8,128)(2,1)} %weight_grads.18), channel_id=1, source_target_pairs={{0,1},{1,0},{2,3},{3,2},{4,6},{5,7},{6,4},{7,5},{8,9},{9,8},{10,11... | collective-permute-start | bytes 6291464 | tf_op jit(solution)/shard_map/ppermute | solution.py:985
  527.3 25.6 %collective-permute-start.38 = (bf16[1024,1024]{1,0:T(8,128)(2,1)}, bf16[1024,1024]{1,0:T(8,128)(2,1)}, u32[]{:S(2)}, u32[]{:S(2)}) collective-permute-start(bf16[1024,1024]{1,0:T(8,128)(2,1)} %weight_grads.19), channel_id=1, source_target_pairs={{0,1},{1,0},{2,3},{3,2},{4,6},{5,7},{6,4},{7,5},{8,9},{9,8},{10,11... | collective-permute-start | bytes 6291464 | tf_op jit(solution)/shard_map/ppermute | solution.py:985
  528.9 211.7 %all-reduce.6.cloned.1.call-start = ((), (), s32[]{:S(2)}) async-start(), calls=%async_computation.1 | async-start | bytes 4194304 | tf_op jit(solution)/shard_map/psum | solution.py:1299
  562.5 68.7 %collective-permute-start.42 = (bf16[1024,1024]{1,0:T(8,128)(2,1)}, bf16[1024,1024]{1,0:T(8,128)(2,1)}, u32[]{:S(2)}, u32[]{:S(2)}) collective-permute-start(bf16[1024,1024]{1,0:T(8,128)(2,1)} %weight_grads.21), channel_id=1, source_target_pairs={{0,1},{1,0},{2,3},{3,2},{4,6},{5,7},{6,4},{7,5},{8,9},{9,8},{10,11... | collective-permute-start | bytes 6291464 | tf_op jit(solution)/shard_map/ppermute | solution.py:985
  565.9 25.6 %collective-permute-start.43 = (bf16[512,1024]{1,0:T(8,128)(2,1)}, bf16[512,1024]{1,0:T(8,128)(2,1)S(1)}, u32[]{:S(2)}, u32[]{:S(2)}) collective-permute-start(bf16[512,1024]{1,0:T(8,128)(2,1)} %get-tuple-element.557), channel_id=1, source_target_pairs={{0,2},{1,3},{2,0},{3,1},{4,5},{5,4},{6,7},{7,6},{8,10},{9,11},{10,... | collective-permute-start | bytes 3145736 | tf_op jit(solution)/shard_map/ppermute | solution.py:988
  567.2 44.1 %collective-permute-start.44 = (bf16[512,1024]{1,0:T(8,128)(2,1)S(1)}, bf16[512,1024]{1,0:T(8,128)(2,1)S(1)}, u32[]{:S(2)}, u32[]{:S(2)}) collective-permute-start(bf16[512,1024]{1,0:T(8,128)(2,1)S(1)} %get-tuple-element.558), channel_id=1, source_target_pairs={{0,2},{1,3},{2,0},{3,1},{4,5},{5,4},{6,7},{7,6},{8,10},{9,11},{10,... | collective-permute-start | bytes 3145736 | tf_op jit(solution)/shard_map/ppermute | solution.py:988
  641.2 37.2 %collective-permute-start.45 = (bf16[1024,1024]{1,0:T(8,128)(2,1)}, bf16[1024,1024]{1,0:T(8,128)(2,1)S(1)}, u32[]{:S(2)}, u32[]{:S(2)}) collective-permute-start(bf16[1024,1024]{1,0:T(8,128)(2,1)} %weight_grads.24), channel_id=1, source_target_pairs={{0,1},{1,0},{2,3},{3,2},{4,6},{5,7},{6,4},{7,5},{8,9},{9,8},{10,11... | collective-permute-start | bytes 6291464 | tf_op jit(solution)/shard_map/ppermute | solution.py:985
  643.2 248.1 %all-reduce.8.cloned.1.call-start = ((), (), s32[]{:S(2)}) async-start(), calls=%async_computation.2 | async-start | bytes 4194304 | tf_op jit(solution)/shard_map/psum | solution.py:1315
  643.3 95.0 %collective-permute-start.49 = (bf16[512,1024]{1,0:T(8,128)(2,1)}, bf16[512,1024]{1,0:T(8,128)(2,1)S(1)}, u32[]{:S(2)}, u32[]{:S(2)}) collective-permute-start(bf16[512,1024]{1,0:T(8,128)(2,1)} %get-tuple-element.554), channel_id=1, source_target_pairs={{0,2},{1,3},{2,0},{3,1},{4,5},{5,4},{6,7},{7,6},{8,10},{9,11},{10,... | collective-permute-start | bytes 3145736 | tf_op jit(solution)/shard_map/ppermute | solution.py:988
  680.4 57.8 %collective-permute-start.50 = (bf16[512,1024]{1,0:T(8,128)(2,1)}, bf16[512,1024]{1,0:T(8,128)(2,1)S(1)}, u32[]{:S(2)}, u32[]{:S(2)}) collective-permute-start(bf16[512,1024]{1,0:T(8,128)(2,1)} %get-tuple-element.552), channel_id=1, source_target_pairs={{0,2},{1,3},{2,0},{3,1},{4,5},{5,4},{6,7},{7,6},{8,10},{9,11},{10,... | collective-permute-start | bytes 3145736 | tf_op jit(solution)/shard_map/ppermute | solution.py:988
  683.5 23.2 %collective-permute-start.48 = (bf16[1,128,1024]{2,1,0:T(8,128)(2,1)S(1)}, bf16[1,128,1024]{2,1,0:T(8,128)(2,1)S(1)}, u32[]{:S(2)}, u32[]{:S(2)}) collective-permute-start(bf16[1,128,1024]{2,1,0:T(8,128)(2,1)S(1)} %get-tuple-element.449), channel_id=1, source_target_pairs={{0,3},{1,2},{2,1},{3,0},{4,7},{5,6},{6,5},{7,4},{8,11},{9,10},{10,... | collective-permute-start | bytes 786440 | tf_op jit(solution)/shard_map/ppermute | solution.py:961
  748.8 25.4 %collective-permute-start.52 = (bf16[1024,1024]{1,0:T(8,128)(2,1)S(1)}, bf16[1024,1024]{1,0:T(8,128)(2,1)}, u32[]{:S(2)}, u32[]{:S(2)}) collective-permute-start(bf16[1024,1024]{1,0:T(8,128)(2,1)S(1)} %copy-done.37), channel_id=1, source_target_pairs={{0,1},{1,0},{2,3},{3,2},{4,6},{5,7},{6,4},{7,5},{8,9},{9,8},{10,11... | collective-permute-start | bytes 6291464 | tf_op jit(solution)/shard_map/ppermute | solution.py:985
  750.1 28.9 %collective-permute-start.54 = (bf16[1024,1024]{1,0:T(8,128)(2,1)S(1)}, bf16[1024,1024]{1,0:T(8,128)(2,1)}, u32[]{:S(2)}, u32[]{:S(2)}) collective-permute-start(bf16[1024,1024]{1,0:T(8,128)(2,1)S(1)} %copy-done.13), channel_id=1, source_target_pairs={{0,4},{4,0},{1,5},{5,1},{2,6},{6,2},{3,7},{7,3},{8,12},{12,8},{9,1... | collective-permute-start | bytes 6291464 | tf_op jit(solution)/shard_map/ppermute | solution.py:942
  794.3 57.1 %collective-permute-start.65 = (bf16[128,1024]{1,0:T(8,128)(2,1)}, bf16[128,1024]{1,0:T(8,128)(2,1)}, u32[]{:S(2)}, u32[]{:S(2)}) collective-permute-start(bf16[128,1024]{1,0:T(8,128)(2,1)} %get-tuple-element.579), channel_id=1, source_target_pairs={{0,24},{8,16},{16,8},{24,0},{1,25},{9,17},{17,9},{25,1},{2,26},{10... | collective-permute-start | bytes 786440 | tf_op jit(solution)/shard_map/ppermute | solution.py:991
  795.5 58.9 %collective-permute-start.66 = (bf16[128,1024]{1,0:T(8,128)(2,1)}, bf16[128,1024]{1,0:T(8,128)(2,1)}, u32[]{:S(2)}, u32[]{:S(2)}) collective-permute-start(bf16[128,1024]{1,0:T(8,128)(2,1)} %get-tuple-element.578), channel_id=1, source_target_pairs={{0,16},{8,24},{16,0},{24,8},{1,17},{9,25},{17,1},{25,9},{2,18},{10... | collective-permute-start | bytes 786440 | tf_op jit(solution)/shard_map/ppermute | solution.py:991
  802.4 43.8 %collective-permute-start.58 = (bf16[1,128,1024]{2,1,0:T(8,128)(2,1)S(1)}, bf16[1,128,1024]{2,1,0:T(8,128)(2,1)S(1)}, u32[]{:S(2)}, u32[]{:S(2)}) collective-permute-start(bf16[1,128,1024]{2,1,0:T(8,128)(2,1)S(1)} %get-tuple-element.488), channel_id=1, source_target_pairs={{0,1},{1,0},{2,3},{3,2},{4,6},{5,7},{6,4},{7,5},{8,9},{9,8},{10,11... | collective-permute-start | bytes 786440 | tf_op jit(solution)/shard_map/ppermute | solution.py:985
  803.2 46.9 %collective-permute-start.59 = (bf16[1,128,1024]{2,1,0:T(8,128)(2,1)S(1)}, bf16[1,128,1024]{2,1,0:T(8,128)(2,1)S(1)}, u32[]{:S(2)}, u32[]{:S(2)}) collective-permute-start(bf16[1,128,1024]{2,1,0:T(8,128)(2,1)S(1)} %get-tuple-element.489), channel_id=1, source_target_pairs={{0,2},{1,3},{2,0},{3,1},{4,5},{5,4},{6,7},{7,6},{8,10},{9,11},{10,... | collective-permute-start | bytes 786440 | tf_op jit(solution)/shard_map/ppermute | solution.py:988
  850.0 42.7 %collective-permute-start.55 = (bf16[1,128,1024]{2,1,0:T(8,128)(2,1)}, bf16[1,128,1024]{2,1,0:T(8,128)(2,1)}, u32[]{:S(2)}, u32[]{:S(2)}) collective-permute-start(bf16[1,128,1024]{2,1,0:T(8,128)(2,1)} %get-tuple-element.482), channel_id=1, source_target_pairs={{0,1},{1,0},{2,3},{3,2},{4,6},{5,7},{6,4},{7,5},{8,9},{9,8},{10,11... | collective-permute-start | bytes 786440 | tf_op jit(solution)/shard_map/ppermute | solution.py:985
  850.2 43.7 %collective-permute-start.56 = (bf16[1,128,1024]{2,1,0:T(8,128)(2,1)}, bf16[1,128,1024]{2,1,0:T(8,128)(2,1)}, u32[]{:S(2)}, u32[]{:S(2)}) collective-permute-start(bf16[1,128,1024]{2,1,0:T(8,128)(2,1)} %get-tuple-element.483), channel_id=1, source_target_pairs={{0,2},{1,3},{2,0},{3,1},{4,5},{5,4},{6,7},{7,6},{8,10},{9,11},{10,... | collective-permute-start | bytes 786440 | tf_op jit(solution)/shard_map/ppermute | solution.py:988
  851.4 42.5 %collective-permute-start.57 = (bf16[1,128,1024]{2,1,0:T(8,128)(2,1)}, bf16[1,128,1024]{2,1,0:T(8,128)(2,1)}, u32[]{:S(2)}, u32[]{:S(2)}) collective-permute-start(bf16[1,128,1024]{2,1,0:T(8,128)(2,1)} %get-tuple-element.484), channel_id=1, source_target_pairs={{0,3},{1,2},{2,1},{3,0},{4,7},{5,6},{6,5},{7,4},{8,11},{9,10},{10,... | collective-permute-start | bytes 786440 | tf_op jit(solution)/shard_map/ppermute | solution.py:961
  854.4 67.8 %collective-permute-start.74 = (bf16[1024,512]{1,0:T(8,128)(2,1)}, bf16[1024,512]{1,0:T(8,128)(2,1)}, u32[]{:S(2)}, u32[]{:S(2)}) collective-permute-start(bf16[1024,512]{1,0:T(8,128)(2,1)} %constant_dynamic-slice_fusion), channel_id=1, source_target_pairs={{0,4},{4,0},{1,5},{5,1},{2,6},{6,2},{3,7},{7,3},{8,12},{12,8},{9,1... | collective-permute-start | bytes 3145736 | tf_op jit(solution)/shard_map/ppermute | solution.py:942
  857.1 73.0 %collective-permute-start.72 = (bf16[1024,512]{1,0:T(8,128)(2,1)}, bf16[1024,512]{1,0:T(8,128)(2,1)}, u32[]{:S(2)}, u32[]{:S(2)}) collective-permute-start(bf16[1024,512]{1,0:T(8,128)(2,1)} %constant_dynamic-slice_fusion.2), channel_id=1, source_target_pairs={{0,4},{4,0},{1,5},{5,1},{2,6},{6,2},{3,7},{7,3},{8,12},{12,8},{9,1... | collective-permute-start | bytes 3145736 | tf_op jit(solution)/shard_map/ppermute | solution.py:942
  893.9 24.1 %collective-permute-start.70 = (bf16[128,1024]{1,0:T(8,128)(2,1)S(1)}, bf16[128,1024]{1,0:T(8,128)(2,1)S(1)}, u32[]{:S(2)}, u32[]{:S(2)}) collective-permute-start(bf16[128,1024]{1,0:T(8,128)(2,1)S(1)} %add_convert_fusion.20), channel_id=1, source_target_pairs={{0,24},{8,16},{16,8},{24,0},{1,25},{9,17},{17,9},{25,1},{2,26},{10... | collective-permute-start | bytes 786440 | tf_op jit(solution)/shard_map/ppermute | solution.py:991
  903.1 42.6 %collective-permute-start.73 = (bf16[1024,512]{1,0:T(8,128)(2,1)}, bf16[1024,512]{1,0:T(8,128)(2,1)}, u32[]{:S(2)}, u32[]{:S(2)}) collective-permute-start(bf16[1024,512]{1,0:T(8,128)(2,1)} %constant_dynamic-slice_fusion.1), channel_id=1, source_target_pairs={{0,4},{4,0},{1,5},{5,1},{2,6},{6,2},{3,7},{7,3},{8,12},{12,8},{9,1... | collective-permute-start | bytes 3145736 | tf_op jit(solution)/shard_map/ppermute | solution.py:942
  (112 other events, 1205.8 us)
Sparse Core Ops, SparseCore 0:
  107.3 70.1 all-gather.6
  179.4 62.6 all-gather.8
  244.5 77.9 all-gather.10
  529.0 84.5 all-reduce.3
  643.4 84.4 all-reduce.5
  779.0 112.2 all-reduce.7

commit v3 on v2

--- a/solution.py
+++ b/solution.py
@@ -1093,6 +1093,7 @@
     launch(1, swapped)
     x_source = chip.both_cores(swapped)
     sent_target = chip.swap_start(pin(target, swapped))
+    w_enc_up = all_groups(pin(own_columns(enc_up), swapped))
     source_ids = lax.dynamic_index_in_dim(source_segments, chip.place, 0, keepdims=False)
     target_ids = lax.dynamic_index_in_dim(target_segments, chip.place, 0, keepdims=False)
     ids = jnp.arange(LANES, dtype=jnp.int32)[None] % HEAD_DIM
@@ -1108,27 +1109,27 @@
     mixed_a, total_a = attend_self(qkv_a, (source_query, source_key), False)
     mixed_a, sent_target = tie((relay(1, mixed_a), sent_target))
     x_target = chip.both_cores(chip.swap_end(sent_target))
-    w_enc_up = all_groups(pin(own_columns(enc_up), mixed_a))
+    w_enc_down = all_groups(pin(own_rows(enc_down), mixed_a))
     rows_c = norm_rows(pin(x_target, target_query, target_key), *dec(0))
     rows_c = arrived(1, rows_c)
     qkv_c = piece_product("columns", rows_c, pieces[1], 0, bundles[1].shape[1])
     qkv_c = relay(2, qkv_c)
-    w_enc_down = all_groups(pin(own_rows(enc_down), qkv_c))
+    launch(3, qkv_c)
+    w_dec_up = all_groups(pin(own_columns(dec_up), qkv_c))
     mixed_c, total_c = attend_self(qkv_c, (target_query, target_key), True)
     proj_rows = bundles[2].shape[0] // 3
     mixed_c, mixed_a = tie((arrived(2, mixed_c), mixed_a))
-    launch(3, mixed_c)
-    w_dec_up = all_groups(pin(own_columns(dec_up), mixed_c))
-    own_a, other_a = part_rows(mixed_a, pieces[2], 0, proj_rows)
-    own_c, other_c = part_rows(mixed_c, pieces[2], proj_rows, 2 * proj_rows)
-    other_a, other_c = tie((other_a, other_c, own_a, own_c))[:2]
+    own_a = piece_product("rows", mixed_a, pieces[2], 0, proj_rows)
+    own_c = piece_product("rows", mixed_c, pieces[2], proj_rows, 2 * proj_rows)
+    own_a, own_c = tie((relay(3, own_a), own_c))
+    other_a, other_c = chip.other(own_a), chip.other(own_c)
     hidden, rows_b = add_norm(x_source, own_a, other_a, *enc(1))
     after_self, rows_e = add_norm(x_target, own_c, other_c, *dec(1))
     rows_b = pin(rows_b, rows_e)
     active_b, slope_b = piece_product("gelu", rows_b, w_enc_up, 0, inner, block=256)
-    active_b = relay(3, active_b)
-    encoded, rows_m = add_norm(hidden, *part_rows(active_b, w_enc_down, 0, inner), *enc(2))
-    rows_m, rows_e = tie((arrived(3, rows_m), rows_e))
+    own_b = arrived(3, piece_product("rows", active_b, w_enc_down, 0, inner))
+    encoded, rows_m = add_norm(hidden, own_b, chip.other(own_b), *enc(2))
+    rows_m, rows_e = tie((rows_m, rows_e))
     launch(4, rows_m)
     head_width = dec_cross_q.shape[1] // 2
     pairs_m = piece_product("columns", rows_m, pieces[3], head_width, 3 * head_width)
@@ -1328,7 +1329,6 @@
     source_grad = chip.from_slot(pin(source_grad, gain_d0))
     target_grad = chip.from_slot(pin(target_grad, gain_d0))
     line_a, sum_xc = tie((line_a, sum_xc))
-    sum_f, sum_b = tie((sum_f, sum_b, gain_d0))[:2]
 
     norms = jnp.concatenate(
         [

time: 977 us -> 955 us (0.977)
  starting transfers between devices: 83.7 us -> 65.7 us
    all_gather x3, waiting for transfers between devices: 17.1 us -> 0.01 us  [all_groups(): return [order, lax.all_gather(own, 'tensor', axis=0)]]
    ppermute x19, waiting for transfers between devices: 67.8 us -> 55.3 us  [send_side(): return lax.ppermute(block, CROSS, self.second)]
    psum x1, waiting for transfers between devices: 26.2 us -> 38.4 us  [chip_local(): sum_xc = lax.psum(total_xc, 'dp')]
    ppermute x18, starting transfers between devices: 24.1 us -> 13.9 us  [other(): return lax.ppermute(block, 'seq', swap_pairs(2, 1))]
  transfers between devices with their start and end apart: 81 -> 81, of which waited for: 37 -> 33; matrix products, arithmetic and copies ran while one was open for 9% -> 10% of each run, Pallas kernels for 43% -> 44%
where the time goes in v3:
time: 955 us; the launch traced here: 946 us
  Pallas kernels  459 us (48%)
  waiting for transfers between devices  279 us (29%)
  other arithmetic  66.8 us (7%)
  starting transfers between devices  65.7 us (7%)
  local copies, waits for them, and re-layouts  59.4 us (6%)
  between operations  15.6 us (2%)
    pallas_call x22, Pallas kernels, piece_product(): pl.pallas_call(functools.partial(piece_kernel, kind, low, high, 1 if stac...  165 us
    ppermute x24, waiting for transfers between devices, send_near(): return lax.ppermute(block, CROSS, self.first)  97.9 us
    pallas_call x13, Pallas kernels, row_call(): pl.pallas_call(kernel, grid=(rows // ROW_BLOCK,), in_specs=[block] * len(...  91.6 us
    pallas_call x14, Pallas kernels, weight_grads(): pl.pallas_call(functools.partial(weight_kernel, len(pairs)), grid=(2,), i...  84 us
    pallas_call x3, Pallas kernels, chip_attend_back(): pl.pallas_call(functools.partial(chip_attend_back_kernel, causal, fused),...  65.5 us
    ppermute x19, waiting for transfers between devices, send_side(): return lax.ppermute(block, CROSS, self.second)  55.3 us
    ppermute x8, waiting for transfers between devices, along(): return lax.ppermute(block, 'dp', swap_pairs(4, bit))  54.1 us
    pallas_call x3, Pallas kernels, chip_attend(): pl.pallas_call(functools.partial(chip_attend_kernel, causal), grid=(count...  53.2 us
  transfers between devices with their start and end apart: 81, of which 33 were waited for; matrix products, arithmetic and copies ran while one was open for 10% of the time, Pallas kernels for 44%

profile of v3, /device:TPU:9, one launch (start us, length us, event | category | flops | bytes accessed | tf_op | source)
XLA Modules:
  0.0 945.7 jit_solution(6082731436636742221)
XLA Ops:
  13.6 14.6 %collective-permute-done.refs_1_ = bf16[1024,384]{1,0:T(8,128)(2,1)S(1)} collective-permute-done((bf16[1024,384]{1,0:T(8,128)(2,1)}, bf16[1024,384]{1,0:T(8,128)(2,1)S(1)}, u32[]{:S(2)}, u32[]{:S(2)}) %collective-permute-start) | collective-permute-done | bytes 786464 | tf_op jit(solution)/shard_map/ppermute | solution.py:988
  81.3 8.1 product_columns.4.q_ref.k_ref.v_ref.refs_0_.refs_1_.refs_2_
  89.3 18.9 %attend.3 = (bf16[1024,512]{1,0:T(8,128)(2,1)}, f32[4,2,1024]{2,1,0:T(2,128)}) custom-call(bf16[1024,1536]{1,0:T(8,128)(2,1)} %product_columns.4.q_ref.k_ref.v_ref.refs_0_.refs_1_.refs_2_, bf16[1024,1536]{1,0:T(8,128)(2,1)} %product_columns.4.q_ref.k_ref.v_ref.refs_0_.refs_1_.refs_2_, ...), custom_call_target="tpu_custom_call" | custom-call | flops 1048576 | bytes 65536 | tf_op jit(solution)/shard_map/attend/pallas_call | solution.py:721
  108.2 7.8 collective-permute-done.14
  128.9 37.6 %collective-permute-done.11.refs_3_ = bf16[1024,384]{1,0:T(8,128)(2,1)} collective-permute-done((bf16[1024,384]{1,0:T(8,128)(2,1)}, bf16[1024,384]{1,0:T(8,128)(2,1)}, u32[]{:S(2)}, u32[]{:S(2)}) %collective-permute-start.11) | collective-permute-done | bytes 786464 | tf_op jit(solution)/shard_map/ppermute | solution.py:985
  167.6 8.1 product_columns.5.q_ref.k_ref.v_ref.refs_0_.refs_1_.refs_2_
  177.6 15.5 %attend.4 = (bf16[1024,512]{1,0:T(8,128)(2,1)}, f32[4,2,1024]{2,1,0:T(2,128)}) custom-call(bf16[1024,1536]{1,0:T(8,128)(2,1)} %product_columns.5.q_ref.k_ref.v_ref.refs_0_.refs_1_.refs_2_, bf16[1024,1536]{1,0:T(8,128)(2,1)} %product_columns.5.q_ref.k_ref.v_ref.refs_0_.refs_1_.refs_2_, ...), custom_call_target="tpu_custom_call" | custom-call | flops 1048576 | bytes 65536 | tf_op jit(solution)/shard_map/attend/pallas_call | solution.py:721
  193.1 18.6 %collective-permute-done.16.refs_3_ = bf16[384,1024]{1,0:T(8,128)(2,1)S(1)} collective-permute-done((bf16[384,1024]{1,0:T(8,128)(2,1)S(1)}, bf16[384,1024]{1,0:T(8,128)(2,1)S(1)}, u32[]{:S(2)}, u32[]{:S(2)}) %collective-permute-start.16) | collective-permute-done | bytes 786464 | tf_op jit(solution)/shard_map/ppermute | solution.py:985
  233.0 6.4 add_norm.5
  239.4 5.9 add_norm.4
  245.4 11.5 %product_gelu.2 = (bf16[1024,2048]{1,0:T(8,128)(2,1)}, bf16[1024,2048]{1,0:T(8,128)(2,1)}) custom-call(bf16[1024,1024]{1,0:T(8,128)(2,1)} %get-tuple-element.392.x_ref.refs_1_, s32[4]{0:T(128)} %add_xor_fusion.refs_0_, bf16[4,1024,512]{2,1,0:T(8,128)(2,1)} %bitcast.94), custom_call_target="tpu_custom_call" | custom-call | flops 1048576 | bytes 65536 | tf_op jit(solution)/shard_map/product_gelu/pallas_call | solution.py:881
  256.9 8.9 product_rows.7.own_ref
  271.5 6.4 add_norm.6
  290.9 18.9 %attend.5 = (bf16[1024,512]{1,0:T(8,128)(2,1)}, f32[4,2,1024]{2,1,0:T(2,128)}) custom-call(bf16[1024,512]{1,0:T(8,128)(2,1)} %product_columns.6.q_ref.refs_0_, bf16[1024,1024]{1,0:T(8,128)(2,1)} %product_columns.7.k_ref.v_ref.refs_1_.refs_2_, bf16[1024,1024]{1,0:T(8,128)(2,1)} %product_columns.7.k_ref.v_ref.refs_1_.refs_2_, ...), custom_call_target="tpu_custom_call" | custom-call | flops 1048576 | bytes 65536 | tf_op jit(solution)/shard_map/attend/pallas_call | solution.py:721
  309.8 6.2 product_rows.8.own_ref
  322.3 6.4 add_norm.7
  331.5 11.6 %product_gelu.3 = (bf16[1024,2048]{1,0:T(8,128)(2,1)}, bf16[1024,2048]{1,0:T(8,128)(2,1)}) custom-call(bf16[1024,1024]{1,0:T(8,128)(2,1)} %get-tuple-element.366.x_ref.refs_1_, s32[4]{0:T(128)} %add_xor_fusion.refs_0_, bf16[4,1024,512]{2,1,0:T(8,128)(2,1)} %bitcast.96), custom_call_target="tpu_custom_call" | custom-call | flops 1048576 | bytes 65536 | tf_op jit(solution)/shard_map/product_gelu/pallas_call | solution.py:881
  344.1 8.5 product_rows.9.own_ref
  362.2 9.0 last_norm.1
  377.5 9.2 product_rows_back_slope.2.refs_0_.x_ref
  392.2 8.6 product_columns_back.6.refs_1_
  409.7 5.9 weight_grads.17
  419.6 8.5 norm_back.6
  437.9 23.9 %attend_back.3 = (bf16[1024,512]{1,0:T(8,128)(2,1)}, bf16[1024,1024]{1,0:T(8,128)(2,1)}) custom-call(bf16[1024,512]{1,0:T(8,128)(2,1)} %product_columns.6.q_ref.refs_0_, bf16[1024,1024]{1,0:T(8,128)(2,1)} %product_columns.7.k_ref.v_ref.refs_1_.refs_2_, bf16[1024,1024]{1,0:T(8,128)(2,1)} %product_columns.7.k_ref.v_ref.refs_1_.refs_2_, ...), custom_call_target="tpu_custom_call" | custom-call | flops 1048576 | bytes 65536 | tf_op jit(solution)/shard_map/attend_back/pallas_call | solution.py:811
  478.7 7.6 norm_back.7
  492.5 9.3 product_rows_back_slope.3.refs_0_.x_ref
  507.3 8.6 product_columns_back.9.refs_1_
  530.9 8.7 norm_back.8
  546.6 7.1 weight_grads.21
  558.2 7.0 weight_grads.22
  565.2 8.8 norm_back.9
  582.3 20.8 %collective-permute-done.44 = bf16[512,1024]{1,0:T(8,128)(2,1)S(1)} collective-permute-done((bf16[512,1024]{1,0:T(8,128)(2,1)S(1)}, bf16[512,1024]{1,0:T(8,128)(2,1)S(1)}, u32[]{:S(2)}, u32[]{:S(2)}) %collective-permute-start.44) | collective-permute-done | bytes 1048608 | tf_op jit(solution)/shard_map/ppermute | solution.py:988
  605.3 17.6 %attend_back.4.refs_1_.x_ref = bf16[1024,1536]{1,0:T(8,128)(2,1)} custom-call(bf16[1024,1536]{1,0:T(8,128)(2,1)} %product_columns.5.q_ref.k_ref.v_ref.refs_0_.refs_1_.refs_2_, bf16[1024,1536]{1,0:T(8,128)(2,1)} %product_columns.5.q_ref.k_ref.v_ref.refs_0_.refs_1_.refs_2_, bf16[1024,1536]{1,0:T(8,128)(2,1)} %product_columns.5.q_ref.k_ref.v_ref.refs_0_.refs_1_.refs_2_, ...), custom_call_target="tpu_custom_call" | custom-call | flops 1048576 | bytes 65536 | tf_op jit(solution)/shard_map/attend_back/pallas_call | solution.py:811
  626.8 6.1 weight_grads.24
  635.3 8.0 product_columns_back.10.refs_1_
  643.3 6.2 weight_grads.25
  655.2 14.0 %collective-permute-done.45 = bf16[1024,1024]{1,0:T(8,128)(2,1)S(1)} collective-permute-done((bf16[1024,1024]{1,0:T(8,128)(2,1)}, bf16[1024,1024]{1,0:T(8,128)(2,1)S(1)}, u32[]{:S(2)}, u32[]{:S(2)}) %collective-permute-start.45) | collective-permute-done | bytes 2097184 | tf_op jit(solution)/shard_map/ppermute | solution.py:985
  680.8 13.0 %collective-permute-done.47 = bf16[1,128,1024]{2,1,0:T(8,128)(2,1)S(1)} collective-permute-done((bf16[1,128,1024]{2,1,0:T(8,128)(2,1)S(1)}, bf16[1,128,1024]{2,1,0:T(8,128)(2,1)S(1)}, u32[]{:S(2)}, u32[]{:S(2)}) %collective-permute-start.47) | collective-permute-done | bytes 262176 | tf_op jit(solution)/shard_map/ppermute | solution.py:988
  698.5 24.0 %attend_back.5.refs_1_.x_ref = bf16[1024,1536]{1,0:T(8,128)(2,1)} custom-call(bf16[1024,1536]{1,0:T(8,128)(2,1)} %product_columns.4.q_ref.k_ref.v_ref.refs_0_.refs_1_.refs_2_, bf16[1024,1536]{1,0:T(8,128)(2,1)} %product_columns.4.q_ref.k_ref.v_ref.refs_0_.refs_1_.refs_2_, bf16[1024,1536]{1,0:T(8,128)(2,1)} %product_columns.4.q_ref.k_ref.v_ref.refs_0_.refs_1_.refs_2_, ...), custom_call_target="tpu_custom_call" | custom-call | flops 1048576 | bytes 65536 | tf_op jit(solution)/shard_map/attend_back/pallas_call | solution.py:811
  722.5 6.4 weight_grads.26
  731.2 8.0 product_columns_back.11.refs_1_
  752.6 6.2 weight_grads.27
  758.8 7.3 norm_back.10
  781.1 7.5 norm_back.11
  801.8 28.4 %collective-permute-done.63 = f32[14,512]{1,0:T(8,128)S(1)} collective-permute-done((f32[14,512]{1,0:T(8,128)S(1)}, f32[14,512]{1,0:T(8,128)S(1)}, u32[]{:S(2)}, u32[]{:S(2)}) %collective-permute-start.63) | collective-permute-done | bytes 28704 | tf_op jit(solution)/shard_map/ppermute | solution.py:991
  830.3 6.1 collective-permute-done.64
  841.6 38.4 %all-reduce.8.cloned.1.call-done = bf16[1024,1024]{1,0:T(8,128)(2,1)} async-done(((bf16[1024,1024]{1,0:T(8,128)(2,1)}), bf16[1024,1024]{1,0:T(8,128)(2,1)}) %all-reduce.8.cloned.1.call-update) | async-done | bytes 2097168 | tf_op jit(solution)/shard_map/psum | solution.py:1316
  899.7 11.6 %collective-permute-done.70 = bf16[128,1024]{1,0:T(8,128)(2,1)S(1)} collective-permute-done((bf16[128,1024]{1,0:T(8,128)(2,1)S(1)}, bf16[128,1024]{1,0:T(8,128)(2,1)S(1)}, u32[]{:S(2)}, u32[]{:S(2)}) %collective-permute-start.70) | collective-permute-done | bytes 262176 | tf_op jit(solution)/shard_map/ppermute | solution.py:991
  (429 shorter events, 358.3 us)
Async XLA Ops:
  7.2 238.2 %all-gather.7.cloned.1.call-start = ((), (), s32[]{:S(2)}) async-start(), calls=%async_computation.3 | async-start | bytes 5242880 | tf_op jit(solution)/shard_map/all_gather | solution.py:1049
  57.1 199.7 %all-gather.9.cloned.1.call-start = ((), (), s32[]{:S(2)}) async-start(), calls=%async_computation.4 | async-start | bytes 5242880 | tf_op jit(solution)/shard_map/all_gather | solution.py:1049
  65.1 43.1 %collective-permute-start.10 = (bf16[1024,384]{1,0:T(8,128)(2,1)}, bf16[1024,384]{1,0:T(8,128)(2,1)S(1)}, u32[]{:S(2)}, u32[]{:S(2)}) collective-permute-start(bf16[1024,384]{1,0:T(8,128)(2,1)} %copy.51), channel_id=1, source_target_pairs={{0,1},{1,0},{2,3},{3,2},{4,6},{5,7},{6,4},{7,5},{8,9},{9,8},{10,11... | collective-permute-start | bytes 2359304 | tf_op jit(solution)/shard_map/ppermute | solution.py:985
  65.4 42.8 %collective-permute-start.9 = (bf16[1024,384]{1,0:T(8,128)(2,1)}, bf16[1024,384]{1,0:T(8,128)(2,1)}, u32[]{:S(2)}, u32[]{:S(2)}) collective-permute-start(bf16[1024,384]{1,0:T(8,128)(2,1)} %copy.51), channel_id=1, source_target_pairs={{0,2},{1,3},{2,0},{3,1},{4,5},{5,4},{6,7},{7,6},{8,10},{9,11},{10,... | collective-permute-start | bytes 2359304 | tf_op jit(solution)/shard_map/ppermute | solution.py:988
  69.8 38.4 %collective-permute-start.12 = (bf16[1,128,1024]{2,1,0:T(8,128)(2,1)}, bf16[1,128,1024]{2,1,0:T(8,128)(2,1)}, u32[]{:S(2)}, u32[]{:S(2)}) collective-permute-start(bf16[1,128,1024]{2,1,0:T(8,128)(2,1)} %get-tuple-element.285), channel_id=1, source_target_pairs={{0,1},{1,0},{2,3},{3,2},{4,6},{5,7},{6,4},{7,5},{8,9},{9,8},{10,11... | collective-permute-start | bytes 786440 | tf_op jit(solution)/shard_map/ppermute | solution.py:985
  70.9 37.4 %collective-permute-start.13 = (bf16[1,128,1024]{2,1,0:T(8,128)(2,1)}, bf16[1,128,1024]{2,1,0:T(8,128)(2,1)}, u32[]{:S(2)}, u32[]{:S(2)}) collective-permute-start(bf16[1,128,1024]{2,1,0:T(8,128)(2,1)} %get-tuple-element.286), channel_id=1, source_target_pairs={{0,2},{1,3},{2,0},{3,1},{4,5},{5,4},{6,7},{7,6},{8,10},{9,11},{10,... | collective-permute-start | bytes 786440 | tf_op jit(solution)/shard_map/ppermute | solution.py:988
  73.4 42.6 %collective-permute-start.14 = (bf16[1,128,1024]{2,1,0:T(8,128)(2,1)}, bf16[1,128,1024]{2,1,0:T(8,128)(2,1)S(1)}, u32[]{:S(2)}, u32[]{:S(2)}) collective-permute-start(bf16[1,128,1024]{2,1,0:T(8,128)(2,1)} %get-tuple-element.287), channel_id=1, source_target_pairs={{0,3},{1,2},{2,1},{3,0},{4,7},{5,6},{6,5},{7,4},{8,11},{9,10},{10,... | collective-permute-start | bytes 786440 | tf_op jit(solution)/shard_map/ppermute | solution.py:961
  116.7 214.8 %all-gather.11.cloned.1.call-start = ((), (), s32[]{:S(2)}) async-start(), calls=%async_computation.5 | async-start | bytes 5242880 | tf_op jit(solution)/shard_map/all_gather | solution.py:1049
  120.2 55.6 %collective-permute-start.7 = (bf16[384,1024]{1,0:T(8,128)(2,1)S(1)}, bf16[384,1024]{1,0:T(8,128)(2,1)S(1)}, u32[]{:S(2)}, u32[]{:S(2)}) collective-permute-start(bf16[384,1024]{1,0:T(8,128)(2,1)S(1)} %pad_maximum_fusion.12.refs_0_), channel_id=1, source_target_pairs={{0,2},{1,3},{2,0},{3,1},{4,5},{5,4},{6,7},{7,6},{8,10},{9,11},{10,... | collective-permute-start | bytes 2359304 | tf_op jit(solution)/shard_map/ppermute | solution.py:988
  120.3 55.5 %collective-permute-start.8 = (bf16[384,1024]{1,0:T(8,128)(2,1)S(1)}, bf16[384,1024]{1,0:T(8,128)(2,1)S(1)}, u32[]{:S(2)}, u32[]{:S(2)}) collective-permute-start(bf16[384,1024]{1,0:T(8,128)(2,1)S(1)} %pad_maximum_fusion.12.refs_0_), channel_id=1, source_target_pairs={{0,1},{1,0},{2,3},{3,2},{4,6},{5,7},{6,4},{7,5},{8,9},{9,8},{10,11... | collective-permute-start | bytes 2359304 | tf_op jit(solution)/shard_map/ppermute | solution.py:985
  121.9 44.5 %collective-permute-start.11 = (bf16[1024,384]{1,0:T(8,128)(2,1)}, bf16[1024,384]{1,0:T(8,128)(2,1)}, u32[]{:S(2)}, u32[]{:S(2)}) collective-permute-start(bf16[1024,384]{1,0:T(8,128)(2,1)} %collective-permute-done.9.refs_1_), channel_id=1, source_target_pairs={{0,1},{1,0},{2,3},{3,2},{4,6},{5,7},{6,4},{7,5},{8,9},{9,8},{10,11... | collective-permute-start | bytes 2359304 | tf_op jit(solution)/shard_map/ppermute | solution.py:985
  175.8 36.0 %collective-permute-start.16 = (bf16[384,1024]{1,0:T(8,128)(2,1)S(1)}, bf16[384,1024]{1,0:T(8,128)(2,1)S(1)}, u32[]{:S(2)}, u32[]{:S(2)}) collective-permute-start(bf16[384,1024]{1,0:T(8,128)(2,1)S(1)} %collective-permute-done.7.refs_1_), channel_id=1, source_target_pairs={{0,1},{1,0},{2,3},{3,2},{4,6},{5,7},{6,4},{7,5},{8,9},{9,8},{10,11... | collective-permute-start | bytes 2359304 | tf_op jit(solution)/shard_map/ppermute | solution.py:985
  176.3 41.8 %collective-permute-start.17 = (bf16[1024,384]{1,0:T(8,128)(2,1)S(1)}, bf16[1024,384]{1,0:T(8,128)(2,1)}, u32[]{:S(2)}, u32[]{:S(2)}) collective-permute-start(bf16[1024,384]{1,0:T(8,128)(2,1)S(1)} %pad_maximum_fusion.13.refs_0_), channel_id=1, source_target_pairs={{0,2},{1,3},{2,0},{3,1},{4,5},{5,4},{6,7},{7,6},{8,10},{9,11},{10,... | collective-permute-start | bytes 2359304 | tf_op jit(solution)/shard_map/ppermute | solution.py:988
  176.3 44.5 %collective-permute-start.18 = (bf16[1024,384]{1,0:T(8,128)(2,1)S(1)}, bf16[1024,384]{1,0:T(8,128)(2,1)S(1)}, u32[]{:S(2)}, u32[]{:S(2)}) collective-permute-start(bf16[1024,384]{1,0:T(8,128)(2,1)S(1)} %pad_maximum_fusion.13.refs_0_), channel_id=1, source_target_pairs={{0,1},{1,0},{2,3},{3,2},{4,6},{5,7},{6,4},{7,5},{8,9},{9,8},{10,11... | collective-permute-start | bytes 2359304 | tf_op jit(solution)/shard_map/ppermute | solution.py:985
  227.1 38.7 %collective-permute-start.20 = (bf16[1024,384]{1,0:T(8,128)(2,1)}, bf16[1024,384]{1,0:T(8,128)(2,1)S(1)}, u32[]{:S(2)}, u32[]{:S(2)}) collective-permute-start(bf16[1024,384]{1,0:T(8,128)(2,1)} %collective-permute-done.17.refs_1_), channel_id=1, source_target_pairs={{0,1},{1,0},{2,3},{3,2},{4,6},{5,7},{6,4},{7,5},{8,9},{9,8},{10,11... | collective-permute-start | bytes 2359304 | tf_op jit(solution)/shard_map/ppermute | solution.py:985
  228.3 394.7 %all-reduce.4.cloned.1.call-start = ((), (), s32[]{:S(2)}) async-start(), calls=%async_computation | async-start | bytes 4194304 | tf_op jit(solution)/shard_map/psum | solution.py:1252
  278.0 31.8 %collective-permute-start.23 = (bf16[512,1024]{1,0:T(8,128)(2,1)S(1)}, bf16[512,1024]{1,0:T(8,128)(2,1)S(1)}, u32[]{:S(2)}, u32[]{:S(2)}) collective-permute-start(bf16[512,1024]{1,0:T(8,128)(2,1)S(1)} %copy-done.9), channel_id=1, source_target_pairs={{0,2},{1,3},{2,0},{3,1},{4,5},{5,4},{6,7},{7,6},{8,10},{9,11},{10,... | collective-permute-start | bytes 3145736 | tf_op jit(solution)/shard_map/ppermute | solution.py:988
  279.2 30.6 %collective-permute-start.24 = (bf16[512,1024]{1,0:T(8,128)(2,1)S(1)}, bf16[512,1024]{1,0:T(8,128)(2,1)S(1)}, u32[]{:S(2)}, u32[]{:S(2)}) collective-permute-start(bf16[512,1024]{1,0:T(8,128)(2,1)S(1)} %copy-done.9), channel_id=1, source_target_pairs={{0,1},{1,0},{2,3},{3,2},{4,6},{5,7},{6,4},{7,5},{8,9},{9,8},{10,11... | collective-permute-start | bytes 3145736 | tf_op jit(solution)/shard_map/ppermute | solution.py:985
  316.9 26.2 %collective-permute-start.26 = (bf16[512,1024]{1,0:T(8,128)(2,1)S(1)}, bf16[512,1024]{1,0:T(8,128)(2,1)S(1)}, u32[]{:S(2)}, u32[]{:S(2)}) collective-permute-start(bf16[512,1024]{1,0:T(8,128)(2,1)S(1)} %collective-permute-done.23.refs_1_), channel_id=1, source_target_pairs={{0,1},{1,0},{2,3},{3,2},{4,6},{5,7},{6,4},{7,5},{8,9},{9,8},{10,11... | collective-permute-start | bytes 3145736 | tf_op jit(solution)/shard_map/ppermute | solution.py:985
  376.8 25.4 %collective-permute-start.32 = (bf16[1024,1024]{1,0:T(8,128)(2,1)}, bf16[1024,1024]{1,0:T(8,128)(2,1)S(1)}, u32[]{:S(2)}, u32[]{:S(2)}) collective-permute-start(bf16[1024,1024]{1,0:T(8,128)(2,1)} %weight_grads.14), channel_id=1, source_target_pairs={{0,1},{1,0},{2,3},{3,2},{4,6},{5,7},{6,4},{7,5},{8,9},{9,8},{10,11... | collective-permute-start | bytes 6291464 | tf_op jit(solution)/shard_map/ppermute | solution.py:985
  403.4 31.0 %collective-permute-start.34 = (bf16[1024,1024]{1,0:T(8,128)(2,1)}, bf16[1024,1024]{1,0:T(8,128)(2,1)S(1)}, u32[]{:S(2)}, u32[]{:S(2)}) collective-permute-start(bf16[1024,1024]{1,0:T(8,128)(2,1)} %weight_grads.15), channel_id=1, source_target_pairs={{0,1},{1,0},{2,3},{3,2},{4,6},{5,7},{6,4},{7,5},{8,9},{9,8},{10,11... | collective-permute-start | bytes 6291464 | tf_op jit(solution)/shard_map/ppermute | solution.py:985
  419.1 42.6 %collective-permute-start.35 = (bf16[512,1024]{1,0:T(8,128)(2,1)}, bf16[512,1024]{1,0:T(8,128)(2,1)S(1)}, u32[]{:S(2)}, u32[]{:S(2)}) collective-permute-start(bf16[512,1024]{1,0:T(8,128)(2,1)} %get-tuple-element.557), channel_id=1, source_target_pairs={{0,2},{1,3},{2,0},{3,1},{4,5},{5,4},{6,7},{7,6},{8,10},{9,11},{10,... | collective-permute-start | bytes 3145736 | tf_op jit(solution)/shard_map/ppermute | solution.py:988
  436.4 25.4 %collective-permute-start.36 = (bf16[512,1024]{1,0:T(8,128)(2,1)}, bf16[512,1024]{1,0:T(8,128)(2,1)S(1)}, u32[]{:S(2)}, u32[]{:S(2)}) collective-permute-start(bf16[512,1024]{1,0:T(8,128)(2,1)} %get-tuple-element.558), channel_id=1, source_target_pairs={{0,2},{1,3},{2,0},{3,1},{4,5},{5,4},{6,7},{7,6},{8,10},{9,11},{10,... | collective-permute-start | bytes 3145736 | tf_op jit(solution)/shard_map/ppermute | solution.py:988
  477.4 38.6 %collective-permute-start.40 = (bf16[1024,1024]{1,0:T(8,128)(2,1)}, bf16[1024,1024]{1,0:T(8,128)(2,1)S(1)}, u32[]{:S(2)}, u32[]{:S(2)}) collective-permute-start(bf16[1024,1024]{1,0:T(8,128)(2,1)} %product_columns_back.8.refs_1_), channel_id=1, source_target_pairs={{0,4},{4,0},{1,5},{5,1},{2,6},{6,2},{3,7},{7,3},{8,12},{12,8},{9,1... | collective-permute-start | bytes 6291464 | tf_op jit(solution)/shard_map/ppermute | solution.py:942
  491.8 25.4 %collective-permute-start.39 = (bf16[1024,1024]{1,0:T(8,128)(2,1)}, bf16[1024,1024]{1,0:T(8,128)(2,1)S(1)}, u32[]{:S(2)}, u32[]{:S(2)}) collective-permute-start(bf16[1024,1024]{1,0:T(8,128)(2,1)} %weight_grads.18), channel_id=1, source_target_pairs={{0,1},{1,0},{2,3},{3,2},{4,6},{5,7},{6,4},{7,5},{8,9},{9,8},{10,11... | collective-permute-start | bytes 6291464 | tf_op jit(solution)/shard_map/ppermute | solution.py:985
  518.6 25.5 %collective-permute-start.38 = (bf16[1024,1024]{1,0:T(8,128)(2,1)}, bf16[1024,1024]{1,0:T(8,128)(2,1)}, u32[]{:S(2)}, u32[]{:S(2)}) collective-permute-start(bf16[1024,1024]{1,0:T(8,128)(2,1)} %weight_grads.19), channel_id=1, source_target_pairs={{0,1},{1,0},{2,3},{3,2},{4,6},{5,7},{6,4},{7,5},{8,9},{9,8},{10,11... | collective-permute-start | bytes 6291464 | tf_op jit(solution)/shard_map/ppermute | solution.py:985
  519.6 211.6 %all-reduce.6.cloned.1.call-start = ((), (), s32[]{:S(2)}) async-start(), calls=%async_computation.1 | async-start | bytes 4194304 | tf_op jit(solution)/shard_map/psum | solution.py:1300
  553.7 69.2 %collective-permute-start.42 = (bf16[1024,1024]{1,0:T(8,128)(2,1)}, bf16[1024,1024]{1,0:T(8,128)(2,1)}, u32[]{:S(2)}, u32[]{:S(2)}) collective-permute-start(bf16[1024,1024]{1,0:T(8,128)(2,1)} %weight_grads.21), channel_id=1, source_target_pairs={{0,1},{1,0},{2,3},{3,2},{4,6},{5,7},{6,4},{7,5},{8,9},{9,8},{10,11... | collective-permute-start | bytes 6291464 | tf_op jit(solution)/shard_map/ppermute | solution.py:985
  556.7 25.6 %collective-permute-start.43 = (bf16[512,1024]{1,0:T(8,128)(2,1)}, bf16[512,1024]{1,0:T(8,128)(2,1)S(1)}, u32[]{:S(2)}, u32[]{:S(2)}) collective-permute-start(bf16[512,1024]{1,0:T(8,128)(2,1)} %get-tuple-element.553), channel_id=1, source_target_pairs={{0,2},{1,3},{2,0},{3,1},{4,5},{5,4},{6,7},{7,6},{8,10},{9,11},{10,... | collective-permute-start | bytes 3145736 | tf_op jit(solution)/shard_map/ppermute | solution.py:988
  557.9 45.1 %collective-permute-start.44 = (bf16[512,1024]{1,0:T(8,128)(2,1)S(1)}, bf16[512,1024]{1,0:T(8,128)(2,1)S(1)}, u32[]{:S(2)}, u32[]{:S(2)}) collective-permute-start(bf16[512,1024]{1,0:T(8,128)(2,1)S(1)} %get-tuple-element.554), channel_id=1, source_target_pairs={{0,2},{1,3},{2,0},{3,1},{4,5},{5,4},{6,7},{7,6},{8,10},{9,11},{10,... | collective-permute-start | bytes 3145736 | tf_op jit(solution)/shard_map/ppermute | solution.py:988
  632.9 36.4 %collective-permute-start.45 = (bf16[1024,1024]{1,0:T(8,128)(2,1)}, bf16[1024,1024]{1,0:T(8,128)(2,1)S(1)}, u32[]{:S(2)}, u32[]{:S(2)}) collective-permute-start(bf16[1024,1024]{1,0:T(8,128)(2,1)} %weight_grads.24), channel_id=1, source_target_pairs={{0,1},{1,0},{2,3},{3,2},{4,6},{5,7},{6,4},{7,5},{8,9},{9,8},{10,11... | collective-permute-start | bytes 6291464 | tf_op jit(solution)/shard_map/ppermute | solution.py:985
  633.9 246.1 %all-reduce.8.cloned.1.call-start = ((), (), s32[]{:S(2)}) async-start(), calls=%async_computation.2 | async-start | bytes 4194304 | tf_op jit(solution)/shard_map/psum | solution.py:1316
  634.0 94.9 %collective-permute-start.49 = (bf16[512,1024]{1,0:T(8,128)(2,1)}, bf16[512,1024]{1,0:T(8,128)(2,1)S(1)}, u32[]{:S(2)}, u32[]{:S(2)}) collective-permute-start(bf16[512,1024]{1,0:T(8,128)(2,1)} %get-tuple-element.550), channel_id=1, source_target_pairs={{0,2},{1,3},{2,0},{3,1},{4,5},{5,4},{6,7},{7,6},{8,10},{9,11},{10,... | collective-permute-start | bytes 3145736 | tf_op jit(solution)/shard_map/ppermute | solution.py:988
  671.2 57.7 %collective-permute-start.50 = (bf16[512,1024]{1,0:T(8,128)(2,1)}, bf16[512,1024]{1,0:T(8,128)(2,1)S(1)}, u32[]{:S(2)}, u32[]{:S(2)}) collective-permute-start(bf16[512,1024]{1,0:T(8,128)(2,1)} %get-tuple-element.548), channel_id=1, source_target_pairs={{0,2},{1,3},{2,0},{3,1},{4,5},{5,4},{6,7},{7,6},{8,10},{9,11},{10,... | collective-permute-start | bytes 3145736 | tf_op jit(solution)/shard_map/ppermute | solution.py:988
  674.1 23.2 %collective-permute-start.48 = (bf16[1,128,1024]{2,1,0:T(8,128)(2,1)S(1)}, bf16[1,128,1024]{2,1,0:T(8,128)(2,1)S(1)}, u32[]{:S(2)}, u32[]{:S(2)}) collective-permute-start(bf16[1,128,1024]{2,1,0:T(8,128)(2,1)S(1)} %get-tuple-element.447), channel_id=1, source_target_pairs={{0,3},{1,2},{2,1},{3,0},{4,7},{5,6},{6,5},{7,4},{8,11},{9,10},{10,... | collective-permute-start | bytes 786440 | tf_op jit(solution)/shard_map/ppermute | solution.py:961
  739.3 26.9 %collective-permute-start.52 = (bf16[1024,1024]{1,0:T(8,128)(2,1)}, bf16[1024,1024]{1,0:T(8,128)(2,1)}, u32[]{:S(2)}, u32[]{:S(2)}) collective-permute-start(bf16[1024,1024]{1,0:T(8,128)(2,1)} %weight_grads.26), channel_id=1, source_target_pairs={{0,1},{1,0},{2,3},{3,2},{4,6},{5,7},{6,4},{7,5},{8,9},{9,8},{10,11... | collective-permute-start | bytes 6291464 | tf_op jit(solution)/shard_map/ppermute | solution.py:985
  743.5 37.6 %collective-permute-start.54 = (bf16[1024,1024]{1,0:T(8,128)(2,1)S(1)}, bf16[1024,1024]{1,0:T(8,128)(2,1)}, u32[]{:S(2)}, u32[]{:S(2)}) collective-permute-start(bf16[1024,1024]{1,0:T(8,128)(2,1)S(1)} %copy-done.13), channel_id=1, source_target_pairs={{0,4},{4,0},{1,5},{5,1},{2,6},{6,2},{3,7},{7,3},{8,12},{12,8},{9,1... | collective-permute-start | bytes 6291464 | tf_op jit(solution)/shard_map/ppermute | solution.py:942
  745.9 26.6 %collective-permute-start.72 = (bf16[1024,512]{1,0:T(8,128)(2,1)}, bf16[1024,512]{1,0:T(8,128)(2,1)}, u32[]{:S(2)}, u32[]{:S(2)}) collective-permute-start(bf16[1024,512]{1,0:T(8,128)(2,1)} %constant_dynamic-slice_fusion.2), channel_id=1, source_target_pairs={{0,4},{4,0},{1,5},{5,1},{2,6},{6,2},{3,7},{7,3},{8,12},{12,8},{9,1... | collective-permute-start | bytes 3145736 | tf_op jit(solution)/shard_map/ppermute | solution.py:942
  791.3 47.7 %collective-permute-start.65 = (bf16[128,1024]{1,0:T(8,128)(2,1)}, bf16[128,1024]{1,0:T(8,128)(2,1)}, u32[]{:S(2)}, u32[]{:S(2)}) collective-permute-start(bf16[128,1024]{1,0:T(8,128)(2,1)} %get-tuple-element.575), channel_id=1, source_target_pairs={{0,24},{8,16},{16,8},{24,0},{1,25},{9,17},{17,9},{25,1},{2,26},{10... | collective-permute-start | bytes 786440 | tf_op jit(solution)/shard_map/ppermute | solution.py:991
  792.5 47.5 %collective-permute-start.66 = (bf16[128,1024]{1,0:T(8,128)(2,1)}, bf16[128,1024]{1,0:T(8,128)(2,1)}, u32[]{:S(2)}, u32[]{:S(2)}) collective-permute-start(bf16[128,1024]{1,0:T(8,128)(2,1)} %get-tuple-element.574), channel_id=1, source_target_pairs={{0,16},{8,24},{16,0},{24,8},{1,17},{9,25},{17,1},{25,9},{2,18},{10... | collective-permute-start | bytes 786440 | tf_op jit(solution)/shard_map/ppermute | solution.py:991
  793.6 46.7 %collective-permute-start.67 = (bf16[128,1024]{1,0:T(8,128)(2,1)}, bf16[128,1024]{1,0:T(8,128)(2,1)}, u32[]{:S(2)}, u32[]{:S(2)}) collective-permute-start(bf16[128,1024]{1,0:T(8,128)(2,1)} %get-tuple-element.573), channel_id=1, source_target_pairs={{0,8},{8,0},{16,24},{24,16},{1,9},{9,1},{17,25},{25,17},{2,10},{10... | collective-permute-start | bytes 786440 | tf_op jit(solution)/shard_map/ppermute | solution.py:991
  799.4 84.2 %collective-permute-start.58 = (bf16[1,128,1024]{2,1,0:T(8,128)(2,1)S(1)}, bf16[1,128,1024]{2,1,0:T(8,128)(2,1)}, u32[]{:S(2)}, u32[]{:S(2)}) collective-permute-start(bf16[1,128,1024]{2,1,0:T(8,128)(2,1)S(1)} %get-tuple-element.486), channel_id=1, source_target_pairs={{0,1},{1,0},{2,3},{3,2},{4,6},{5,7},{6,4},{7,5},{8,9},{9,8},{10,11... | collective-permute-start | bytes 786440 | tf_op jit(solution)/shard_map/ppermute | solution.py:985
  801.0 29.2 %collective-permute-start.63 = (f32[14,512]{1,0:T(8,128)S(1)}, f32[14,512]{1,0:T(8,128)S(1)}, u32[]{:S(2)}, u32[]{:S(2)}) collective-permute-start(f32[14,512]{1,0:T(8,128)S(1)} %add.252), channel_id=1, source_target_pairs={{0,8},{8,0},{16,24},{24,16},{1,9},{9,1},{17,25},{25,17},{2,10},{10... | collective-permute-start | bytes 86024 | tf_op jit(solution)/shard_map/ppermute | solution.py:991
  836.4 49.3 %collective-permute-start.59 = (bf16[1,128,1024]{2,1,0:T(8,128)(2,1)S(1)}, bf16[1,128,1024]{2,1,0:T(8,128)(2,1)S(1)}, u32[]{:S(2)}, u32[]{:S(2)}) collective-permute-start(bf16[1,128,1024]{2,1,0:T(8,128)(2,1)S(1)} %get-tuple-element.487), channel_id=1, source_target_pairs={{0,2},{1,3},{2,0},{3,1},{4,5},{5,4},{6,7},{7,6},{8,10},{9,11},{10,... | collective-permute-start | bytes 786440 | tf_op jit(solution)/shard_map/ppermute | solution.py:988
  838.9 48.7 %collective-permute-start.60 = (bf16[1,128,1024]{2,1,0:T(8,128)(2,1)S(1)}, bf16[1,128,1024]{2,1,0:T(8,128)(2,1)}, u32[]{:S(2)}, u32[]{:S(2)}) collective-permute-start(bf16[1,128,1024]{2,1,0:T(8,128)(2,1)S(1)} %get-tuple-element.488), channel_id=1, source_target_pairs={{0,3},{1,2},{2,1},{3,0},{4,7},{5,6},{6,5},{7,4},{8,11},{9,10},{10,... | collective-permute-start | bytes 786440 | tf_op jit(solution)/shard_map/ppermute | solution.py:961
  840.0 49.8 %collective-permute-start.55 = (bf16[1,128,1024]{2,1,0:T(8,128)(2,1)S(1)}, bf16[1,128,1024]{2,1,0:T(8,128)(2,1)S(1)}, u32[]{:S(2)}, u32[]{:S(2)}) collective-permute-start(bf16[1,128,1024]{2,1,0:T(8,128)(2,1)S(1)} %get-tuple-element.480), channel_id=1, source_target_pairs={{0,1},{1,0},{2,3},{3,2},{4,6},{5,7},{6,4},{7,5},{8,9},{9,8},{10,11... | collective-permute-start | bytes 786440 | tf_op jit(solution)/shard_map/ppermute | solution.py:985
  840.3 49.8 %collective-permute-start.56 = (bf16[1,128,1024]{2,1,0:T(8,128)(2,1)S(1)}, bf16[1,128,1024]{2,1,0:T(8,128)(2,1)S(1)}, u32[]{:S(2)}, u32[]{:S(2)}) collective-permute-start(bf16[1,128,1024]{2,1,0:T(8,128)(2,1)S(1)} %get-tuple-element.481), channel_id=1, source_target_pairs={{0,2},{1,3},{2,0},{3,1},{4,5},{5,4},{6,7},{7,6},{8,10},{9,11},{10,... | collective-permute-start | bytes 786440 | tf_op jit(solution)/shard_map/ppermute | solution.py:988
  890.1 34.2 %collective-permute-start.73 = (bf16[1024,512]{1,0:T(8,128)(2,1)}, bf16[1024,512]{1,0:T(8,128)(2,1)}, u32[]{:S(2)}, u32[]{:S(2)}) collective-permute-start(bf16[1024,512]{1,0:T(8,128)(2,1)} %constant_dynamic-slice_fusion.1), channel_id=1, source_target_pairs={{0,4},{4,0},{1,5},{5,1},{2,6},{6,2},{3,7},{7,3},{8,12},{12,8},{9,1... | collective-permute-start | bytes 3145736 | tf_op jit(solution)/shard_map/ppermute | solution.py:942
  (101 other events, 935.5 us)
Sparse Core Ops, SparseCore 0:
  57.2 79.3 all-gather.6
  138.5 73.3 all-gather.8
  228.4 52.7 all-gather.10
  519.8 84.5 all-reduce.3
  634.1 84.3 all-reduce.5
  772.6 107.3 all-reduce.7

commit v4 on v2

--- a/solution.py
+++ b/solution.py
@@ -975,11 +975,16 @@
     def both_cores(self, rows):
         return self.ordered(rows, self.other(rows), self.core)
 
-    def from_slot(self, rows):
+    def from_start(self, rows):
         half = rows.shape[0] // 2
         own = lax.dynamic_slice_in_dim(rows, self.core * half, half, 0)
-        rows = self.swap_rows(own.reshape(4, half // 4, -1))
-        return rows.reshape(4, half // 4, -1)
+        return self.swap_start(own.reshape(4, half // 4, -1))
+
+    def from_end(self, parts):
+        return self.swap_end(parts).reshape((4,) + parts[0].shape[1:])
+
+    def from_slot(self, rows):
+        return self.from_end(self.from_start(rows))
 
     def send_near(self, block):
         return lax.ppermute(block, CROSS, self.first)
@@ -1093,6 +1098,7 @@
     launch(1, swapped)
     x_source = chip.both_cores(swapped)
     sent_target = chip.swap_start(pin(target, swapped))
+    w_enc_up = all_groups(pin(own_columns(enc_up), swapped))
     source_ids = lax.dynamic_index_in_dim(source_segments, chip.place, 0, keepdims=False)
     target_ids = lax.dynamic_index_in_dim(target_segments, chip.place, 0, keepdims=False)
     ids = jnp.arange(LANES, dtype=jnp.int32)[None] % HEAD_DIM
@@ -1108,17 +1114,16 @@
     mixed_a, total_a = attend_self(qkv_a, (source_query, source_key), False)
     mixed_a, sent_target = tie((relay(1, mixed_a), sent_target))
     x_target = chip.both_cores(chip.swap_end(sent_target))
-    w_enc_up = all_groups(pin(own_columns(enc_up), mixed_a))
+    w_enc_down = all_groups(pin(own_rows(enc_down), mixed_a))
     rows_c = norm_rows(pin(x_target, target_query, target_key), *dec(0))
     rows_c = arrived(1, rows_c)
     qkv_c = piece_product("columns", rows_c, pieces[1], 0, bundles[1].shape[1])
     qkv_c = relay(2, qkv_c)
-    w_enc_down = all_groups(pin(own_rows(enc_down), qkv_c))
+    w_dec_up = all_groups(pin(own_columns(dec_up), qkv_c))
     mixed_c, total_c = attend_self(qkv_c, (target_query, target_key), True)
     proj_rows = bundles[2].shape[0] // 3
     mixed_c, mixed_a = tie((arrived(2, mixed_c), mixed_a))
     launch(3, mixed_c)
-    w_dec_up = all_groups(pin(own_columns(dec_up), mixed_c))
     own_a, other_a = part_rows(mixed_a, pieces[2], 0, proj_rows)
     own_c, other_c = part_rows(mixed_c, pieces[2], proj_rows, 2 * proj_rows)
     other_a, other_c = tie((other_a, other_c, own_a, own_c))[:2]
@@ -1303,24 +1308,26 @@
     own_c = piece_product("columns_back", d_qkv_c, pieces[1], 0, 3 * head_width)
     own_c, keep_c = keep_half(own_c, near_c, *pairs_c)
     low_hidden, decoded = tie((low_hidden, decoded, own_c))[:2]
-    decoded = chip.from_slot(decoded)
+    sent_decoded = chip.from_start(decoded)
     d_mixed = piece_product("rows_back", low_hidden, pieces[2], 0, proj_rows)
-    d_mixed, side_c = here(d_mixed, to_side, *keep_c)
-    d_mixed, decoded = tie((d_mixed, decoded))
     d_qkv_a = self_back(d_mixed, qkv_a, (source_query, source_key), False, total_a, mixed_a)
     pairs_a = ((mixed_a, low_hidden), (d_qkv_a, rows_a))
     d_qkv_a, near_a = send_half(d_qkv_a, *pairs_a)
-    d_qkv_a, (_, total_xc) = here(d_qkv_a, sum_line, side_x, side_c)
-    d_qkv_a, sum_b, total_xc = tie((d_qkv_a, sum_b, total_xc))
+    d_qkv_a, side_c = here(d_qkv_a, to_side, *keep_c)
+    own_a = piece_product("columns_back", d_qkv_a, pieces[0], 0, 3 * head_width)
+    own_a, (_, total_xc) = here(own_a, sum_line, side_x, side_c)
+    own_a, sum_b, total_xc, sent_decoded, near_a = tie(
+        (own_a, sum_b, total_xc, sent_decoded, near_a)
+    )
+    decoded = chip.from_end(sent_decoded)
     sum_xc = lax.psum(total_xc, "dp")
-    own_a, other_a = part_back(d_qkv_a, pieces[0], 0, 3 * head_width)
-    other_c = chip.other(pin(own_c, own_a))
+    other_a, other_c = chip.other(own_a), chip.other(pin(own_c, own_a))
     own_a, keep_a = keep_half(own_a, near_a, *pairs_a)
+    own_a, side_a = here(own_a, to_side, *keep_a)
     source_grad, gain_e0, shift_e0 = norm_back_rows(
         x_source, own_a, other_a, enc(0)[0], d_hidden, [BF16]
     )
     own_c = pin(own_c, source_grad)
-    own_c, side_a = here(own_c, to_side, *keep_a)
     target_grad, gain_d0, shift_d0 = norm_back_rows(
         x_target, own_c, other_c, dec(0)[0], d_self, [BF16]
     )
@@ -1328,7 +1335,6 @@
     source_grad = chip.from_slot(pin(source_grad, gain_d0))
     target_grad = chip.from_slot(pin(target_grad, gain_d0))
     line_a, sum_xc = tie((line_a, sum_xc))
-    sum_f, sum_b = tie((sum_f, sum_b, gain_d0))[:2]
 
     norms = jnp.concatenate(
         [

time: 977 us -> 932 us (0.954)
  waiting for transfers between devices: 286 us -> 236 us
  local copies, waits for them, and re-layouts: 55.9 us -> 67.8 us
  starting transfers between devices: 83.7 us -> 72.2 us
    ppermute x8, waiting for transfers between devices: 55.6 us -> 30.3 us  [along(): return lax.ppermute(block, 'dp', swap_pairs(4, bit))]
    all_gather x3, waiting for transfers between devices: 17.1 us -> 0.02 us  [all_groups(): return [order, lax.all_gather(own, 'tensor', axis=0)]]
    ppermute x19, waiting for transfers between devices: 67.8 us -> 55.1 us  [send_side(): return lax.ppermute(block, CROSS, self.second)]
  transfers between devices with their start and end apart: 81 -> 81, of which waited for: 37 -> 31; matrix products, arithmetic and copies ran while one was open for 9% -> 11% of each run, Pallas kernels for 43% -> 46%
where the time goes in v4:
time: 932 us; the launch traced here: 923 us
  Pallas kernels  459 us (49%)
  waiting for transfers between devices  236 us (25%)
  starting transfers between devices  72.2 us (8%)
  other arithmetic  71.2 us (8%)
  local copies, waits for them, and re-layouts  67.8 us (7%)
  between operations  15.5 us (2%)
    pallas_call x22, Pallas kernels, piece_product(): pl.pallas_call(functools.partial(piece_kernel, kind, low, high, 1 if stac...  165 us
    ppermute x24, waiting for transfers between devices, send_near(): return lax.ppermute(block, CROSS, self.first)  94.3 us
    pallas_call x13, Pallas kernels, row_call(): pl.pallas_call(kernel, grid=(rows // ROW_BLOCK,), in_specs=[block] * len(...  91.5 us
    pallas_call x14, Pallas kernels, weight_grads(): pl.pallas_call(functools.partial(weight_kernel, len(pairs)), grid=(2,), i...  84 us
    pallas_call x3, Pallas kernels, chip_attend_back(): pl.pallas_call(functools.partial(chip_attend_back_kernel, causal, fused),...  65.4 us
    ppermute x19, waiting for transfers between devices, send_side(): return lax.ppermute(block, CROSS, self.second)  55.1 us
    pallas_call x3, Pallas kernels, chip_attend(): pl.pallas_call(functools.partial(chip_attend_kernel, causal), grid=(count...  53.5 us
    psum x1, waiting for transfers between devices, chip_local(): sum_xc = lax.psum(total_xc, 'dp')  31.8 us
  transfers between devices with their start and end apart: 81, of which 31 were waited for; matrix products, arithmetic and copies ran while one was open for 11% of the time, Pallas kernels for 46%

profile of v4, /device:TPU:9, one launch (start us, length us, event | category | flops | bytes accessed | tf_op | source)
XLA Modules:
  0.0 922.5 jit_solution(2259765539326994880)
XLA Ops:
  14.5 14.7 %collective-permute-done.refs_1_ = bf16[1024,384]{1,0:T(8,128)(2,1)} collective-permute-done((bf16[1024,384]{1,0:T(8,128)(2,1)}, bf16[1024,384]{1,0:T(8,128)(2,1)}, u32[]{:S(2)}, u32[]{:S(2)}) %collective-permute-start) | collective-permute-done | bytes 786464 | tf_op jit(solution)/shard_map/ppermute | solution.py:993
  51.3 6.4 collective-permute-done.2.refs_3_
  84.1 8.1 product_columns.4.q_ref.k_ref.v_ref.refs_0_.refs_1_.refs_2_
  92.2 18.8 %attend.3 = (bf16[1024,512]{1,0:T(8,128)(2,1)}, f32[4,2,1024]{2,1,0:T(2,128)}) custom-call(bf16[1024,1536]{1,0:T(8,128)(2,1)} %product_columns.4.q_ref.k_ref.v_ref.refs_0_.refs_1_.refs_2_, bf16[1024,1536]{1,0:T(8,128)(2,1)} %product_columns.4.q_ref.k_ref.v_ref.refs_0_.refs_1_.refs_2_, ...), custom_call_target="tpu_custom_call" | custom-call | flops 1048576 | bytes 65536 | tf_op jit(solution)/shard_map/attend/pallas_call | solution.py:721
  111.1 7.6 collective-permute-done.14
  130.2 33.5 %collective-permute-done.11.refs_3_ = bf16[1024,384]{1,0:T(8,128)(2,1)} collective-permute-done((bf16[1024,384]{1,0:T(8,128)(2,1)}, bf16[1024,384]{1,0:T(8,128)(2,1)}, u32[]{:S(2)}, u32[]{:S(2)}) %collective-permute-start.11) | collective-permute-done | bytes 786464 | tf_op jit(solution)/shard_map/ppermute | solution.py:990
  165.9 8.0 product_columns.5.q_ref.k_ref.v_ref.refs_0_.refs_1_.refs_2_
  174.3 15.9 %attend.4 = (bf16[1024,512]{1,0:T(8,128)(2,1)}, f32[4,2,1024]{2,1,0:T(2,128)}) custom-call(bf16[1024,1536]{1,0:T(8,128)(2,1)} %product_columns.5.q_ref.k_ref.v_ref.refs_0_.refs_1_.refs_2_, bf16[1024,1536]{1,0:T(8,128)(2,1)} %product_columns.5.q_ref.k_ref.v_ref.refs_0_.refs_1_.refs_2_, ...), custom_call_target="tpu_custom_call" | custom-call | flops 1048576 | bytes 65536 | tf_op jit(solution)/shard_map/attend/pallas_call | solution.py:721
  190.2 11.7 %collective-permute-done.16.refs_3_ = bf16[384,1024]{1,0:T(8,128)(2,1)S(1)} collective-permute-done((bf16[384,1024]{1,0:T(8,128)(2,1)S(1)}, bf16[384,1024]{1,0:T(8,128)(2,1)S(1)}, u32[]{:S(2)}, u32[]{:S(2)}) %collective-permute-start.16) | collective-permute-done | bytes 786464 | tf_op jit(solution)/shard_map/ppermute | solution.py:990
  224.9 6.3 add_norm.4
  231.2 11.5 %product_gelu.2 = (bf16[1024,2048]{1,0:T(8,128)(2,1)}, bf16[1024,2048]{1,0:T(8,128)(2,1)}) custom-call(bf16[1024,1024]{1,0:T(8,128)(2,1)} %get-tuple-element.395.x_ref.refs_1_, s32[4]{0:T(128)} %add_xor_fusion.refs_0_, bf16[4,1024,512]{2,1,0:T(8,128)(2,1)} %bitcast.94), custom_call_target="tpu_custom_call" | custom-call | flops 1048576 | bytes 65536 | tf_op jit(solution)/shard_map/product_gelu/pallas_call | solution.py:881
  242.8 9.1 product_rows.7.own_ref
  257.8 6.3 add_norm.6
  264.2 16.1 %collective-permute-done.21.refs_3_ = bf16[1024,384]{1,0:T(8,128)(2,1)S(1)} collective-permute-done((bf16[1024,384]{1,0:T(8,128)(2,1)S(1)}, bf16[1024,384]{1,0:T(8,128)(2,1)S(1)}, u32[]{:S(2)}, u32[]{:S(2)}) %collective-permute-start.21) | collective-permute-done | bytes 786464 | tf_op jit(solution)/shard_map/ppermute | solution.py:990
  293.1 18.8 %attend.5 = (bf16[1024,512]{1,0:T(8,128)(2,1)}, f32[4,2,1024]{2,1,0:T(2,128)}) custom-call(bf16[1024,512]{1,0:T(8,128)(2,1)} %product_columns.6.q_ref.refs_0_, bf16[1024,1024]{1,0:T(8,128)(2,1)} %product_columns.7.k_ref.v_ref.refs_1_.refs_2_, bf16[1024,1024]{1,0:T(8,128)(2,1)} %product_columns.7.k_ref.v_ref.refs_1_.refs_2_, ...), custom_call_target="tpu_custom_call" | custom-call | flops 1048576 | bytes 65536 | tf_op jit(solution)/shard_map/attend/pallas_call | solution.py:721
  311.9 6.2 product_rows.8.own_ref
  325.0 6.6 add_norm.7
  335.2 11.4 %product_gelu.3 = (bf16[1024,2048]{1,0:T(8,128)(2,1)}, bf16[1024,2048]{1,0:T(8,128)(2,1)}) custom-call(bf16[1024,1024]{1,0:T(8,128)(2,1)} %get-tuple-element.369.x_ref.refs_1_, s32[4]{0:T(128)} %add_xor_fusion.refs_0_, bf16[4,1024,512]{2,1,0:T(8,128)(2,1)} %bitcast.96), custom_call_target="tpu_custom_call" | custom-call | flops 1048576 | bytes 65536 | tf_op jit(solution)/shard_map/product_gelu/pallas_call | solution.py:881
  347.7 8.5 product_rows.9.own_ref
  365.9 9.1 last_norm.1
  381.7 9.2 product_rows_back_slope.2.refs_0_.x_ref
  396.4 8.6 product_columns_back.6.refs_1_
  423.3 8.5 norm_back.6
  441.0 23.8 %attend_back.3 = (bf16[1024,512]{1,0:T(8,128)(2,1)}, bf16[1024,1024]{1,0:T(8,128)(2,1)}) custom-call(bf16[1024,512]{1,0:T(8,128)(2,1)} %product_columns.6.q_ref.refs_0_, bf16[1024,1024]{1,0:T(8,128)(2,1)} %product_columns.7.k_ref.v_ref.refs_1_.refs_2_, bf16[1024,1024]{1,0:T(8,128)(2,1)} %product_columns.7.k_ref.v_ref.refs_1_.refs_2_, ...), custom_call_target="tpu_custom_call" | custom-call | flops 1048576 | bytes 65536 | tf_op jit(solution)/shard_map/attend_back/pallas_call | solution.py:811
  483.4 7.6 norm_back.7
  496.5 9.3 %product_rows_back_slope.3.refs_0_.x_ref = bf16[1024,2048]{1,0:T(8,128)(2,1)} custom-call(bf16[1024,1024]{1,0:T(8,128)(2,1)} %get-tuple-element.416.refs_1_.x_ref, s32[4]{0:T(128)} %add_xor_fusion.refs_0_, bf16[4,512,1024]{2,1,0:T(8,128)(2,1)} %bitcast.93, bf16[1024,2048]{1,0:T(8,128)(2,1)} %get-tuple-element.392.refs_2_), custom_call_target="tpu_custom_call" | custom-call | flops 1048576 | bytes 65536 | tf_op jit(solution)/shard_map/product_rows_back_slope/pallas_call | solution.py:881
  511.3 8.6 product_columns_back.9.refs_1_
  534.7 8.7 norm_back.8
  551.3 7.1 weight_grads.21
  561.9 7.0 weight_grads.22
  568.9 8.8 norm_back.9
  585.9 21.9 %collective-permute-done.44 = bf16[512,1024]{1,0:T(8,128)(2,1)S(1)} collective-permute-done((bf16[512,1024]{1,0:T(8,128)(2,1)S(1)}, bf16[512,1024]{1,0:T(8,128)(2,1)S(1)}, u32[]{:S(2)}, u32[]{:S(2)}) %collective-permute-start.44) | collective-permute-done | bytes 1048608 | tf_op jit(solution)/shard_map/ppermute | solution.py:993
  610.1 17.6 %attend_back.4.refs_1_.x_ref = bf16[1024,1536]{1,0:T(8,128)(2,1)} custom-call(bf16[1024,1536]{1,0:T(8,128)(2,1)} %product_columns.5.q_ref.k_ref.v_ref.refs_0_.refs_1_.refs_2_, bf16[1024,1536]{1,0:T(8,128)(2,1)} %product_columns.5.q_ref.k_ref.v_ref.refs_0_.refs_1_.refs_2_, bf16[1024,1536]{1,0:T(8,128)(2,1)} %product_columns.5.q_ref.k_ref.v_ref.refs_0_.refs_1_.refs_2_, ...), custom_call_target="tpu_custom_call" | custom-call | flops 1048576 | bytes 65536 | tf_op jit(solution)/shard_map/attend_back/pallas_call | solution.py:811
  631.2 6.2 weight_grads.24
  637.9 8.0 product_columns_back.10.refs_1_
  645.9 6.2 weight_grads.25
  657.7 24.0 %attend_back.5.refs_1_.x_ref = bf16[1024,1536]{1,0:T(8,128)(2,1)} custom-call(bf16[1024,1536]{1,0:T(8,128)(2,1)} %product_columns.4.q_ref.k_ref.v_ref.refs_0_.refs_1_.refs_2_, bf16[1024,1536]{1,0:T(8,128)(2,1)} %product_columns.4.q_ref.k_ref.v_ref.refs_0_.refs_1_.refs_2_, bf16[1024,1536]{1,0:T(8,128)(2,1)} %product_columns.4.q_ref.k_ref.v_ref.refs_0_.refs_1_.refs_2_, ...), custom_call_target="tpu_custom_call" | custom-call | flops 1048576 | bytes 65536 | tf_op jit(solution)/shard_map/attend_back/pallas_call | solution.py:811
  681.7 6.3 weight_grads.26
  697.9 8.2 product_columns_back.11.refs_1_
  706.8 11.8 %collective-permute-done.47 = bf16[512,1024]{1,0:T(8,128)(2,1)S(1)} collective-permute-done((bf16[512,1024]{1,0:T(8,128)(2,1)}, bf16[512,1024]{1,0:T(8,128)(2,1)S(1)}, u32[]{:S(2)}, u32[]{:S(2)}) %collective-permute-start.47) | collective-permute-done | bytes 1048608 | tf_op jit(solution)/shard_map/ppermute | solution.py:993
  723.3 9.8 %collective-permute-done.48 = bf16[1,128,1024]{2,1,0:T(8,128)(2,1)} collective-permute-done((bf16[1,128,1024]{2,1,0:T(8,128)(2,1)}, bf16[1,128,1024]{2,1,0:T(8,128)(2,1)}, u32[]{:S(2)}, u32[]{:S(2)}) %collective-permute-start.48) | collective-permute-done | bytes 262176 | tf_op jit(solution)/shard_map/ppermute | solution.py:990
  746.4 6.2 weight_grads.27
  772.0 7.2 norm_back.10
  779.2 7.5 norm_back.11
  799.8 16.6 %collective-permute-done.63 = f32[14,512]{1,0:T(8,128)S(1)} collective-permute-done((f32[14,512]{1,0:T(8,128)S(1)}, f32[14,512]{1,0:T(8,128)S(1)}, u32[]{:S(2)}, u32[]{:S(2)}) %collective-permute-start.63) | collective-permute-done | bytes 28704 | tf_op jit(solution)/shard_map/ppermute | solution.py:996
  826.5 31.8 %all-reduce.8.cloned.1.call-done = bf16[1024,1024]{1,0:T(8,128)(2,1)} async-done(((bf16[1024,1024]{1,0:T(8,128)(2,1)}), bf16[1024,1024]{1,0:T(8,128)(2,1)}) %all-reduce.8.cloned.1.call-update) | async-done | bytes 2097168 | tf_op jit(solution)/shard_map/psum | solution.py:1323
  865.3 6.4 collective-permute-done.68
  874.1 7.9 collective-permute-start.73
  (429 shorter events, 361.6 us)
Async XLA Ops:
  7.2 224.0 %all-gather.7.cloned.1.call-start = ((), (), s32[]{:S(2)}) async-start(), calls=%async_computation.3 | async-start | bytes 5242880 | tf_op jit(solution)/shard_map/all_gather | solution.py:1054
  57.7 185.1 %all-gather.9.cloned.1.call-start = ((), (), s32[]{:S(2)}) async-start(), calls=%async_computation.4 | async-start | bytes 5242880 | tf_op jit(solution)/shard_map/all_gather | solution.py:1054
  68.1 42.9 %collective-permute-start.10 = (bf16[1024,384]{1,0:T(8,128)(2,1)}, bf16[1024,384]{1,0:T(8,128)(2,1)}, u32[]{:S(2)}, u32[]{:S(2)}) collective-permute-start(bf16[1024,384]{1,0:T(8,128)(2,1)} %copy.51), channel_id=1, source_target_pairs={{0,1},{1,0},{2,3},{3,2},{4,6},{5,7},{6,4},{7,5},{8,9},{9,8},{10,11... | collective-permute-start | bytes 2359304 | tf_op jit(solution)/shard_map/ppermute | solution.py:990
  68.8 42.3 %collective-permute-start.9 = (bf16[1024,384]{1,0:T(8,128)(2,1)}, bf16[1024,384]{1,0:T(8,128)(2,1)}, u32[]{:S(2)}, u32[]{:S(2)}) collective-permute-start(bf16[1024,384]{1,0:T(8,128)(2,1)} %copy.51), channel_id=1, source_target_pairs={{0,2},{1,3},{2,0},{3,1},{4,5},{5,4},{6,7},{7,6},{8,10},{9,11},{10,... | collective-permute-start | bytes 2359304 | tf_op jit(solution)/shard_map/ppermute | solution.py:993
  72.9 38.2 %collective-permute-start.12 = (bf16[1,128,1024]{2,1,0:T(8,128)(2,1)S(1)}, bf16[1,128,1024]{2,1,0:T(8,128)(2,1)S(1)}, u32[]{:S(2)}, u32[]{:S(2)}) collective-permute-start(bf16[1,128,1024]{2,1,0:T(8,128)(2,1)S(1)} %get-tuple-element.288), channel_id=1, source_target_pairs={{0,1},{1,0},{2,3},{3,2},{4,6},{5,7},{6,4},{7,5},{8,9},{9,8},{10,11... | collective-permute-start | bytes 786440 | tf_op jit(solution)/shard_map/ppermute | solution.py:990
  74.2 36.9 %collective-permute-start.13 = (bf16[1,128,1024]{2,1,0:T(8,128)(2,1)S(1)}, bf16[1,128,1024]{2,1,0:T(8,128)(2,1)S(1)}, u32[]{:S(2)}, u32[]{:S(2)}) collective-permute-start(bf16[1,128,1024]{2,1,0:T(8,128)(2,1)S(1)} %get-tuple-element.289), channel_id=1, source_target_pairs={{0,2},{1,3},{2,0},{3,1},{4,5},{5,4},{6,7},{7,6},{8,10},{9,11},{10,... | collective-permute-start | bytes 786440 | tf_op jit(solution)/shard_map/ppermute | solution.py:993
  76.5 42.2 %collective-permute-start.14 = (bf16[1,128,1024]{2,1,0:T(8,128)(2,1)S(1)}, bf16[1,128,1024]{2,1,0:T(8,128)(2,1)S(1)}, u32[]{:S(2)}, u32[]{:S(2)}) collective-permute-start(bf16[1,128,1024]{2,1,0:T(8,128)(2,1)S(1)} %get-tuple-element.290), channel_id=1, source_target_pairs={{0,3},{1,2},{2,1},{3,0},{4,7},{5,6},{6,5},{7,4},{8,11},{9,10},{10,... | collective-permute-start | bytes 786440 | tf_op jit(solution)/shard_map/ppermute | solution.py:961
  118.7 216.5 %all-gather.11.cloned.1.call-start = ((), (), s32[]{:S(2)}) async-start(), calls=%async_computation.5 | async-start | bytes 5242880 | tf_op jit(solution)/shard_map/all_gather | solution.py:1054
  120.8 53.2 %collective-permute-start.7 = (bf16[384,1024]{1,0:T(8,128)(2,1)S(1)}, bf16[384,1024]{1,0:T(8,128)(2,1)S(1)}, u32[]{:S(2)}, u32[]{:S(2)}) collective-permute-start(bf16[384,1024]{1,0:T(8,128)(2,1)S(1)} %pad_maximum_fusion.13.refs_0_), channel_id=1, source_target_pairs={{0,2},{1,3},{2,0},{3,1},{4,5},{5,4},{6,7},{7,6},{8,10},{9,11},{10,... | collective-permute-start | bytes 2359304 | tf_op jit(solution)/shard_map/ppermute | solution.py:993
  121.3 52.7 %collective-permute-start.8 = (bf16[384,1024]{1,0:T(8,128)(2,1)S(1)}, bf16[384,1024]{1,0:T(8,128)(2,1)S(1)}, u32[]{:S(2)}, u32[]{:S(2)}) collective-permute-start(bf16[384,1024]{1,0:T(8,128)(2,1)S(1)} %pad_maximum_fusion.13.refs_0_), channel_id=1, source_target_pairs={{0,1},{1,0},{2,3},{3,2},{4,6},{5,7},{6,4},{7,5},{8,9},{9,8},{10,11... | collective-permute-start | bytes 2359304 | tf_op jit(solution)/shard_map/ppermute | solution.py:990
  121.4 42.2 %collective-permute-start.11 = (bf16[1024,384]{1,0:T(8,128)(2,1)}, bf16[1024,384]{1,0:T(8,128)(2,1)}, u32[]{:S(2)}, u32[]{:S(2)}) collective-permute-start(bf16[1024,384]{1,0:T(8,128)(2,1)} %collective-permute-done.9.refs_1_), channel_id=1, source_target_pairs={{0,1},{1,0},{2,3},{3,2},{4,6},{5,7},{6,4},{7,5},{8,9},{9,8},{10,11... | collective-permute-start | bytes 2359304 | tf_op jit(solution)/shard_map/ppermute | solution.py:990
  174.0 28.0 %collective-permute-start.16 = (bf16[384,1024]{1,0:T(8,128)(2,1)S(1)}, bf16[384,1024]{1,0:T(8,128)(2,1)S(1)}, u32[]{:S(2)}, u32[]{:S(2)}) collective-permute-start(bf16[384,1024]{1,0:T(8,128)(2,1)S(1)} %collective-permute-done.7.refs_1_), channel_id=1, source_target_pairs={{0,1},{1,0},{2,3},{3,2},{4,6},{5,7},{6,4},{7,5},{8,9},{9,8},{10,11... | collective-permute-start | bytes 2359304 | tf_op jit(solution)/shard_map/ppermute | solution.py:990
  215.2 27.5 %collective-permute-start.17 = (bf16[1024,384]{1,0:T(8,128)(2,1)S(1)}, bf16[1024,384]{1,0:T(8,128)(2,1)S(1)}, u32[]{:S(2)}, u32[]{:S(2)}) collective-permute-start(bf16[1024,384]{1,0:T(8,128)(2,1)S(1)} %pad_maximum_fusion.12.refs_0_), channel_id=1, source_target_pairs={{0,2},{1,3},{2,0},{3,1},{4,5},{5,4},{6,7},{7,6},{8,10},{9,11},{10,... | collective-permute-start | bytes 2359304 | tf_op jit(solution)/shard_map/ppermute | solution.py:993
  216.2 26.5 %collective-permute-start.18 = (bf16[1024,384]{1,0:T(8,128)(2,1)S(1)}, bf16[1024,384]{1,0:T(8,128)(2,1)S(1)}, u32[]{:S(2)}, u32[]{:S(2)}) collective-permute-start(bf16[1024,384]{1,0:T(8,128)(2,1)S(1)} %pad_maximum_fusion.12.refs_0_), channel_id=1, source_target_pairs={{0,1},{1,0},{2,3},{3,2},{4,6},{5,7},{6,4},{7,5},{8,9},{9,8},{10,11... | collective-permute-start | bytes 2359304 | tf_op jit(solution)/shard_map/ppermute | solution.py:990
  217.9 409.8 %all-reduce.4.cloned.1.call-start = ((), (), s32[]{:S(2)}) async-start(), calls=%async_computation | async-start | bytes 4194304 | tf_op jit(solution)/shard_map/psum | solution.py:1256
  252.5 27.7 %collective-permute-start.21 = (bf16[1024,384]{1,0:T(8,128)(2,1)S(1)}, bf16[1024,384]{1,0:T(8,128)(2,1)S(1)}, u32[]{:S(2)}, u32[]{:S(2)}) collective-permute-start(bf16[1024,384]{1,0:T(8,128)(2,1)S(1)} %collective-permute-done.17.refs_1_), channel_id=1, source_target_pairs={{0,1},{1,0},{2,3},{3,2},{4,6},{5,7},{6,4},{7,5},{8,9},{9,8},{10,11... | collective-permute-start | bytes 2359304 | tf_op jit(solution)/shard_map/ppermute | solution.py:990
  280.2 31.7 %collective-permute-start.23 = (bf16[512,1024]{1,0:T(8,128)(2,1)S(1)}, bf16[512,1024]{1,0:T(8,128)(2,1)S(1)}, u32[]{:S(2)}, u32[]{:S(2)}) collective-permute-start(bf16[512,1024]{1,0:T(8,128)(2,1)S(1)} %constant_dynamic-slice_fusion.43.refs_0_), channel_id=1, source_target_pairs={{0,2},{1,3},{2,0},{3,1},{4,5},{5,4},{6,7},{7,6},{8,10},{9,11},{10,... | collective-permute-start | bytes 3145736 | tf_op jit(solution)/shard_map/ppermute | solution.py:993
  281.4 30.5 %collective-permute-start.24 = (bf16[512,1024]{1,0:T(8,128)(2,1)S(1)}, bf16[512,1024]{1,0:T(8,128)(2,1)S(1)}, u32[]{:S(2)}, u32[]{:S(2)}) collective-permute-start(bf16[512,1024]{1,0:T(8,128)(2,1)S(1)} %constant_dynamic-slice_fusion.43.refs_0_), channel_id=1, source_target_pairs={{0,1},{1,0},{2,3},{3,2},{4,6},{5,7},{6,4},{7,5},{8,9},{9,8},{10,11... | collective-permute-start | bytes 3145736 | tf_op jit(solution)/shard_map/ppermute | solution.py:990
  319.7 27.0 %collective-permute-start.26 = (bf16[512,1024]{1,0:T(8,128)(2,1)S(1)}, bf16[512,1024]{1,0:T(8,128)(2,1)S(1)}, u32[]{:S(2)}, u32[]{:S(2)}) collective-permute-start(bf16[512,1024]{1,0:T(8,128)(2,1)S(1)} %collective-permute-done.23.refs_1_), channel_id=1, source_target_pairs={{0,1},{1,0},{2,3},{3,2},{4,6},{5,7},{6,4},{7,5},{8,9},{9,8},{10,11... | collective-permute-start | bytes 3145736 | tf_op jit(solution)/shard_map/ppermute | solution.py:990
  380.5 25.4 %collective-permute-start.32 = (bf16[1024,1024]{1,0:T(8,128)(2,1)}, bf16[1024,1024]{1,0:T(8,128)(2,1)S(1)}, u32[]{:S(2)}, u32[]{:S(2)}) collective-permute-start(bf16[1024,1024]{1,0:T(8,128)(2,1)} %weight_grads.14), channel_id=1, source_target_pairs={{0,1},{1,0},{2,3},{3,2},{4,6},{5,7},{6,4},{7,5},{8,9},{9,8},{10,11... | collective-permute-start | bytes 6291464 | tf_op jit(solution)/shard_map/ppermute | solution.py:990
  407.1 31.4 %collective-permute-start.34 = (bf16[1024,1024]{1,0:T(8,128)(2,1)}, bf16[1024,1024]{1,0:T(8,128)(2,1)S(1)}, u32[]{:S(2)}, u32[]{:S(2)}) collective-permute-start(bf16[1024,1024]{1,0:T(8,128)(2,1)} %weight_grads.15), channel_id=1, source_target_pairs={{0,1},{1,0},{2,3},{3,2},{4,6},{5,7},{6,4},{7,5},{8,9},{9,8},{10,11... | collective-permute-start | bytes 6291464 | tf_op jit(solution)/shard_map/ppermute | solution.py:990
  423.3 41.6 %collective-permute-start.35 = (bf16[512,1024]{1,0:T(8,128)(2,1)}, bf16[512,1024]{1,0:T(8,128)(2,1)S(1)}, u32[]{:S(2)}, u32[]{:S(2)}) collective-permute-start(bf16[512,1024]{1,0:T(8,128)(2,1)} %get-tuple-element.563), channel_id=1, source_target_pairs={{0,2},{1,3},{2,0},{3,1},{4,5},{5,4},{6,7},{7,6},{8,10},{9,11},{10,... | collective-permute-start | bytes 3145736 | tf_op jit(solution)/shard_map/ppermute | solution.py:993
  482.0 37.9 %collective-permute-start.40 = (bf16[1024,1024]{1,0:T(8,128)(2,1)}, bf16[1024,1024]{1,0:T(8,128)(2,1)S(1)}, u32[]{:S(2)}, u32[]{:S(2)}) collective-permute-start(bf16[1024,1024]{1,0:T(8,128)(2,1)} %product_columns_back.8.refs_1_), channel_id=1, source_target_pairs={{0,4},{4,0},{1,5},{5,1},{2,6},{6,2},{3,7},{7,3},{8,12},{12,8},{9,1... | collective-permute-start | bytes 6291464 | tf_op jit(solution)/shard_map/ppermute | solution.py:942
  496.5 25.4 %collective-permute-start.39 = (bf16[1024,1024]{1,0:T(8,128)(2,1)}, bf16[1024,1024]{1,0:T(8,128)(2,1)S(1)}, u32[]{:S(2)}, u32[]{:S(2)}) collective-permute-start(bf16[1024,1024]{1,0:T(8,128)(2,1)} %weight_grads.18), channel_id=1, source_target_pairs={{0,1},{1,0},{2,3},{3,2},{4,6},{5,7},{6,4},{7,5},{8,9},{9,8},{10,11... | collective-permute-start | bytes 6291464 | tf_op jit(solution)/shard_map/ppermute | solution.py:990
  523.2 25.5 %collective-permute-start.38 = (bf16[1024,1024]{1,0:T(8,128)(2,1)}, bf16[1024,1024]{1,0:T(8,128)(2,1)}, u32[]{:S(2)}, u32[]{:S(2)}) collective-permute-start(bf16[1024,1024]{1,0:T(8,128)(2,1)} %weight_grads.19), channel_id=1, source_target_pairs={{0,1},{1,0},{2,3},{3,2},{4,6},{5,7},{6,4},{7,5},{8,9},{9,8},{10,11... | collective-permute-start | bytes 6291464 | tf_op jit(solution)/shard_map/ppermute | solution.py:990
  523.3 209.9 %all-reduce.6.cloned.1.call-start = ((), (), s32[]{:S(2)}) async-start(), calls=%async_computation.1 | async-start | bytes 4194304 | tf_op jit(solution)/shard_map/psum | solution.py:1304
  558.4 69.2 %collective-permute-start.42 = (bf16[1024,1024]{1,0:T(8,128)(2,1)}, bf16[1024,1024]{1,0:T(8,128)(2,1)}, u32[]{:S(2)}, u32[]{:S(2)}) collective-permute-start(bf16[1024,1024]{1,0:T(8,128)(2,1)} %weight_grads.21), channel_id=1, source_target_pairs={{0,1},{1,0},{2,3},{3,2},{4,6},{5,7},{6,4},{7,5},{8,9},{9,8},{10,11... | collective-permute-start | bytes 6291464 | tf_op jit(solution)/shard_map/ppermute | solution.py:990
  560.4 25.4 %collective-permute-start.43 = (bf16[512,1024]{1,0:T(8,128)(2,1)}, bf16[512,1024]{1,0:T(8,128)(2,1)S(1)}, u32[]{:S(2)}, u32[]{:S(2)}) collective-permute-start(bf16[512,1024]{1,0:T(8,128)(2,1)} %get-tuple-element.559), channel_id=1, source_target_pairs={{0,2},{1,3},{2,0},{3,1},{4,5},{5,4},{6,7},{7,6},{8,10},{9,11},{10,... | collective-permute-start | bytes 3145736 | tf_op jit(solution)/shard_map/ppermute | solution.py:993
  561.0 46.7 %collective-permute-start.44 = (bf16[512,1024]{1,0:T(8,128)(2,1)S(1)}, bf16[512,1024]{1,0:T(8,128)(2,1)S(1)}, u32[]{:S(2)}, u32[]{:S(2)}) collective-permute-start(bf16[512,1024]{1,0:T(8,128)(2,1)S(1)} %get-tuple-element.560), channel_id=1, source_target_pairs={{0,2},{1,3},{2,0},{3,1},{4,5},{5,4},{6,7},{7,6},{8,10},{9,11},{10,... | collective-permute-start | bytes 3145736 | tf_op jit(solution)/shard_map/ppermute | solution.py:993
  637.4 51.8 %collective-permute-start.46 = (bf16[1024,1024]{1,0:T(8,128)(2,1)}, bf16[1024,1024]{1,0:T(8,128)(2,1)}, u32[]{:S(2)}, u32[]{:S(2)}) collective-permute-start(bf16[1024,1024]{1,0:T(8,128)(2,1)} %weight_grads.24), channel_id=1, source_target_pairs={{0,1},{1,0},{2,3},{3,2},{4,6},{5,7},{6,4},{7,5},{8,9},{9,8},{10,11... | collective-permute-start | bytes 6291464 | tf_op jit(solution)/shard_map/ppermute | solution.py:990
  637.4 220.9 %all-reduce.8.cloned.1.call-start = ((), (), s32[]{:S(2)}) async-start(), calls=%async_computation.2 | async-start | bytes 4194304 | tf_op jit(solution)/shard_map/psum | solution.py:1323
  637.5 68.6 %collective-permute-start.45 = (bf16[512,1024]{1,0:T(8,128)(2,1)}, bf16[512,1024]{1,0:T(8,128)(2,1)}, u32[]{:S(2)}, u32[]{:S(2)}) collective-permute-start(bf16[512,1024]{1,0:T(8,128)(2,1)} %get-tuple-element.557), channel_id=1, source_target_pairs={{0,2},{1,3},{2,0},{3,1},{4,5},{5,4},{6,7},{7,6},{8,10},{9,11},{10,... | collective-permute-start | bytes 3145736 | tf_op jit(solution)/shard_map/ppermute | solution.py:993
  687.9 45.2 %collective-permute-start.51 = (bf16[1024,1024]{1,0:T(8,128)(2,1)}, bf16[1024,1024]{1,0:T(8,128)(2,1)}, u32[]{:S(2)}, u32[]{:S(2)}) collective-permute-start(bf16[1024,1024]{1,0:T(8,128)(2,1)} %weight_grads.26), channel_id=1, source_target_pairs={{0,1},{1,0},{2,3},{3,2},{4,6},{5,7},{6,4},{7,5},{8,9},{9,8},{10,11... | collective-permute-start | bytes 6291464 | tf_op jit(solution)/shard_map/ppermute | solution.py:990
  693.1 25.6 %collective-permute-start.47 = (bf16[512,1024]{1,0:T(8,128)(2,1)}, bf16[512,1024]{1,0:T(8,128)(2,1)S(1)}, u32[]{:S(2)}, u32[]{:S(2)}) collective-permute-start(bf16[512,1024]{1,0:T(8,128)(2,1)} %get-tuple-element.555), channel_id=1, source_target_pairs={{0,2},{1,3},{2,0},{3,1},{4,5},{5,4},{6,7},{7,6},{8,10},{9,11},{10,... | collective-permute-start | bytes 3145736 | tf_op jit(solution)/shard_map/ppermute | solution.py:993
  696.8 43.3 %collective-permute-start.74 = (bf16[1024,512]{1,0:T(8,128)(2,1)}, bf16[1024,512]{1,0:T(8,128)(2,1)}, u32[]{:S(2)}, u32[]{:S(2)}) collective-permute-start(bf16[1024,512]{1,0:T(8,128)(2,1)} %constant_dynamic-slice_fusion), channel_id=1, source_target_pairs={{0,4},{4,0},{1,5},{5,1},{2,6},{6,2},{3,7},{7,3},{8,12},{12,8},{9,1... | collective-permute-start | bytes 3145736 | tf_op jit(solution)/shard_map/ppermute | solution.py:942
  697.9 35.2 %collective-permute-start.48 = (bf16[1,128,1024]{2,1,0:T(8,128)(2,1)}, bf16[1,128,1024]{2,1,0:T(8,128)(2,1)}, u32[]{:S(2)}, u32[]{:S(2)}) collective-permute-start(bf16[1,128,1024]{2,1,0:T(8,128)(2,1)} %get-tuple-element.457), channel_id=1, source_target_pairs={{0,1},{1,0},{2,3},{3,2},{4,6},{5,7},{6,4},{7,5},{8,9},{9,8},{10,11... | collective-permute-start | bytes 786440 | tf_op jit(solution)/shard_map/ppermute | solution.py:990
  706.1 27.0 %collective-permute-start.49 = (bf16[1,128,1024]{2,1,0:T(8,128)(2,1)}, bf16[1,128,1024]{2,1,0:T(8,128)(2,1)}, u32[]{:S(2)}, u32[]{:S(2)}) collective-permute-start(bf16[1,128,1024]{2,1,0:T(8,128)(2,1)} %get-tuple-element.458), channel_id=1, source_target_pairs={{0,2},{1,3},{2,0},{3,1},{4,5},{5,4},{6,7},{7,6},{8,10},{9,11},{10,... | collective-permute-start | bytes 786440 | tf_op jit(solution)/shard_map/ppermute | solution.py:993
  733.2 38.8 %collective-permute-start.52 = (bf16[1024,1024]{1,0:T(8,128)(2,1)}, bf16[1024,1024]{1,0:T(8,128)(2,1)}, u32[]{:S(2)}, u32[]{:S(2)}) collective-permute-start(bf16[1024,1024]{1,0:T(8,128)(2,1)} %product_columns_back.11.refs_1_), channel_id=1, source_target_pairs={{0,4},{4,0},{1,5},{5,1},{2,6},{6,2},{3,7},{7,3},{8,12},{12,8},{9,1... | collective-permute-start | bytes 6291464 | tf_op jit(solution)/shard_map/ppermute | solution.py:942
  737.3 41.9 %collective-permute-start.54 = (bf16[1024,1024]{1,0:T(8,128)(2,1)S(1)}, bf16[1024,1024]{1,0:T(8,128)(2,1)}, u32[]{:S(2)}, u32[]{:S(2)}) collective-permute-start(bf16[1024,1024]{1,0:T(8,128)(2,1)S(1)} %copy-done.12), channel_id=1, source_target_pairs={{0,4},{4,0},{1,5},{5,1},{2,6},{6,2},{3,7},{7,3},{8,12},{12,8},{9,1... | collective-permute-start | bytes 6291464 | tf_op jit(solution)/shard_map/ppermute | solution.py:942
  757.0 29.8 %collective-permute-start.53 = (bf16[512,1024]{1,0:T(8,128)(2,1)}, bf16[512,1024]{1,0:T(8,128)(2,1)}, u32[]{:S(2)}, u32[]{:S(2)}) collective-permute-start(bf16[512,1024]{1,0:T(8,128)(2,1)} %get-tuple-element.552), channel_id=1, source_target_pairs={{0,2},{1,3},{2,0},{3,1},{4,5},{5,4},{6,7},{7,6},{8,10},{9,11},{10,... | collective-permute-start | bytes 3145736 | tf_op jit(solution)/shard_map/ppermute | solution.py:993
  789.2 34.0 %collective-permute-start.65 = (bf16[128,1024]{1,0:T(8,128)(2,1)}, bf16[128,1024]{1,0:T(8,128)(2,1)S(1)}, u32[]{:S(2)}, u32[]{:S(2)}) collective-permute-start(bf16[128,1024]{1,0:T(8,128)(2,1)} %get-tuple-element.581), channel_id=1, source_target_pairs={{0,24},{8,16},{16,8},{24,0},{1,25},{9,17},{17,9},{25,1},{2,26},{10... | collective-permute-start | bytes 786440 | tf_op jit(solution)/shard_map/ppermute | solution.py:996
  790.6 34.4 %collective-permute-start.66 = (bf16[128,1024]{1,0:T(8,128)(2,1)}, bf16[128,1024]{1,0:T(8,128)(2,1)S(1)}, u32[]{:S(2)}, u32[]{:S(2)}) collective-permute-start(bf16[128,1024]{1,0:T(8,128)(2,1)} %get-tuple-element.580), channel_id=1, source_target_pairs={{0,16},{8,24},{16,0},{24,8},{1,17},{9,25},{17,1},{25,9},{2,18},{10... | collective-permute-start | bytes 786440 | tf_op jit(solution)/shard_map/ppermute | solution.py:996
  791.6 33.8 %collective-permute-start.67 = (bf16[128,1024]{1,0:T(8,128)(2,1)}, bf16[128,1024]{1,0:T(8,128)(2,1)S(1)}, u32[]{:S(2)}, u32[]{:S(2)}) collective-permute-start(bf16[128,1024]{1,0:T(8,128)(2,1)} %get-tuple-element.579), channel_id=1, source_target_pairs={{0,8},{8,0},{16,24},{24,16},{1,9},{9,1},{17,25},{25,17},{2,10},{10... | collective-permute-start | bytes 786440 | tf_op jit(solution)/shard_map/ppermute | solution.py:996
  797.2 62.6 %collective-permute-start.55 = (bf16[1,128,1024]{2,1,0:T(8,128)(2,1)}, bf16[1,128,1024]{2,1,0:T(8,128)(2,1)}, u32[]{:S(2)}, u32[]{:S(2)}) collective-permute-start(bf16[1,128,1024]{2,1,0:T(8,128)(2,1)} %get-tuple-element.486), channel_id=1, source_target_pairs={{0,1},{1,0},{2,3},{3,2},{4,6},{5,7},{6,4},{7,5},{8,9},{9,8},{10,11... | collective-permute-start | bytes 786440 | tf_op jit(solution)/shard_map/ppermute | solution.py:990
  821.5 40.2 %collective-permute-start.56 = (bf16[1,128,1024]{2,1,0:T(8,128)(2,1)}, bf16[1,128,1024]{2,1,0:T(8,128)(2,1)}, u32[]{:S(2)}, u32[]{:S(2)}) collective-permute-start(bf16[1,128,1024]{2,1,0:T(8,128)(2,1)} %get-tuple-element.487), channel_id=1, source_target_pairs={{0,2},{1,3},{2,0},{3,1},{4,5},{5,4},{6,7},{7,6},{8,10},{9,11},{10,... | collective-permute-start | bytes 786440 | tf_op jit(solution)/shard_map/ppermute | solution.py:993
  823.2 39.5 %collective-permute-start.57 = (bf16[1,128,1024]{2,1,0:T(8,128)(2,1)}, bf16[1,128,1024]{2,1,0:T(8,128)(2,1)}, u32[]{:S(2)}, u32[]{:S(2)}) collective-permute-start(bf16[1,128,1024]{2,1,0:T(8,128)(2,1)} %get-tuple-element.488), channel_id=1, source_target_pairs={{0,3},{1,2},{2,1},{3,0},{4,7},{5,6},{6,5},{7,4},{8,11},{9,10},{10,... | collective-permute-start | bytes 786440 | tf_op jit(solution)/shard_map/ppermute | solution.py:961
  825.0 62.6 %collective-permute-start.58 = (bf16[1,128,1024]{2,1,0:T(8,128)(2,1)}, bf16[1,128,1024]{2,1,0:T(8,128)(2,1)}, u32[]{:S(2)}, u32[]{:S(2)}) collective-permute-start(bf16[1,128,1024]{2,1,0:T(8,128)(2,1)} %get-tuple-element.492), channel_id=1, source_target_pairs={{0,1},{1,0},{2,3},{3,2},{4,6},{5,7},{6,4},{7,5},{8,9},{9,8},{10,11... | collective-permute-start | bytes 786440 | tf_op jit(solution)/shard_map/ppermute | solution.py:990
  825.4 62.2 %collective-permute-start.59 = (bf16[1,128,1024]{2,1,0:T(8,128)(2,1)S(1)}, bf16[1,128,1024]{2,1,0:T(8,128)(2,1)}, u32[]{:S(2)}, u32[]{:S(2)}) collective-permute-start(bf16[1,128,1024]{2,1,0:T(8,128)(2,1)S(1)} %get-tuple-element.493), channel_id=1, source_target_pairs={{0,2},{1,3},{2,0},{3,1},{4,5},{5,4},{6,7},{7,6},{8,10},{9,11},{10,... | collective-permute-start | bytes 786440 | tf_op jit(solution)/shard_map/ppermute | solution.py:993
  (99 other events, 853.5 us)
Sparse Core Ops, SparseCore 0:
  57.9 80.7 all-gather.6
  141.1 65.2 all-gather.8
  218.0 69.0 all-gather.10
  523.4 84.8 all-reduce.3
  637.5 84.6 all-reduce.5
  758.5 99.8 all-reduce.7

commit v5 on v4

--- a/solution.py
+++ b/solution.py
@@ -1333,8 +1333,9 @@
     )
     gain_d0, line_a = here(gain_d0, to_line, side_a)
     source_grad = chip.from_slot(pin(source_grad, gain_d0))
-    target_grad = chip.from_slot(pin(target_grad, gain_d0))
-    line_a, sum_xc = tie((line_a, sum_xc))
+    sent_grad = chip.from_start(pin(target_grad, gain_d0))
+    sent_grad, sum_xc = tie((sent_grad, sum_xc))
+    target_grad = chip.from_end(sent_grad)
 
     norms = jnp.concatenate(
         [

time: 932 us -> 943 us (1.012)
  waiting for transfers between devices: 236 us -> 251 us
    ppermute x8, waiting for transfers between devices: 30.3 us -> 49.8 us  [along(): return lax.ppermute(block, 'dp', swap_pairs(4, bit))]
    psum x1, waiting for transfers between devices: 31.8 us -> 22.2 us  [chip_local(): sum_xc = lax.psum(total_xc, 'dp')]
  transfers between devices with their start and end apart: 81 -> 81, of which waited for: 31 -> 32; matrix products, arithmetic and copies ran while one was open for 11% -> 11% of each run, Pallas kernels for 46% -> 46%
where the time goes in v5:
time: 943 us; the launch traced here: 928 us
  Pallas kernels  460 us (49%)
  waiting for transfers between devices  251 us (27%)
  other arithmetic  69.6 us (7%)
  local copies, waits for them, and re-layouts  68.4 us (7%)
  starting transfers between devices  64.8 us (7%)
  between operations  15.6 us (2%)
    pallas_call x22, Pallas kernels, piece_product(): pl.pallas_call(functools.partial(piece_kernel, kind, low, high, 1 if stac...  165 us
    ppermute x24, waiting for transfers between devices, send_near(): return lax.ppermute(block, CROSS, self.first)  93.3 us
    pallas_call x13, Pallas kernels, row_call(): pl.pallas_call(kernel, grid=(rows // ROW_BLOCK,), in_specs=[block] * len(...  91.5 us
    pallas_call x14, Pallas kernels, weight_grads(): pl.pallas_call(functools.partial(weight_kernel, len(pairs)), grid=(2,), i...  83.9 us
    pallas_call x3, Pallas kernels, chip_attend_back(): pl.pallas_call(functools.partial(chip_attend_back_kernel, causal, fused),...  65.7 us
    ppermute x19, waiting for transfers between devices, send_side(): return lax.ppermute(block, CROSS, self.second)  54.2 us
    pallas_call x3, Pallas kernels, chip_attend(): pl.pallas_call(functools.partial(chip_attend_kernel, causal), grid=(count...  53.6 us
    ppermute x8, waiting for transfers between devices, along(): return lax.ppermute(block, 'dp', swap_pairs(4, bit))  49.8 us
  transfers between devices with their start and end apart: 81, of which 32 were waited for; matrix products, arithmetic and copies ran while one was open for 11% of the time, Pallas kernels for 46%

profile of v5, /device:TPU:9, one launch (start us, length us, event | category | flops | bytes accessed | tf_op | source)
XLA Modules:
  0.0 928.5 jit_solution(18432142946392307783)
XLA Ops:
  14.5 14.7 %collective-permute-done.refs_1_ = bf16[1024,384]{1,0:T(8,128)(2,1)} collective-permute-done((bf16[1024,384]{1,0:T(8,128)(2,1)}, bf16[1024,384]{1,0:T(8,128)(2,1)}, u32[]{:S(2)}, u32[]{:S(2)}) %collective-permute-start) | collective-permute-done | bytes 786464 | tf_op jit(solution)/shard_map/ppermute | solution.py:993
  51.3 6.4 collective-permute-done.2.refs_3_
  84.1 8.1 product_columns.4.q_ref.k_ref.v_ref.refs_0_.refs_1_.refs_2_
  92.2 18.8 %attend.3 = (bf16[1024,512]{1,0:T(8,128)(2,1)}, f32[4,2,1024]{2,1,0:T(2,128)}) custom-call(bf16[1024,1536]{1,0:T(8,128)(2,1)} %product_columns.4.q_ref.k_ref.v_ref.refs_0_.refs_1_.refs_2_, bf16[1024,1536]{1,0:T(8,128)(2,1)} %product_columns.4.q_ref.k_ref.v_ref.refs_0_.refs_1_.refs_2_, ...), custom_call_target="tpu_custom_call" | custom-call | flops 1048576 | bytes 65536 | tf_op jit(solution)/shard_map/attend/pallas_call | solution.py:721
  111.1 7.7 collective-permute-done.14
  130.2 33.5 %collective-permute-done.11.refs_3_ = bf16[1024,384]{1,0:T(8,128)(2,1)} collective-permute-done((bf16[1024,384]{1,0:T(8,128)(2,1)}, bf16[1024,384]{1,0:T(8,128)(2,1)}, u32[]{:S(2)}, u32[]{:S(2)}) %collective-permute-start.11) | collective-permute-done | bytes 786464 | tf_op jit(solution)/shard_map/ppermute | solution.py:990
  165.9 8.0 product_columns.5.q_ref.k_ref.v_ref.refs_0_.refs_1_.refs_2_
  174.3 15.9 %attend.4 = (bf16[1024,512]{1,0:T(8,128)(2,1)}, f32[4,2,1024]{2,1,0:T(2,128)}) custom-call(bf16[1024,1536]{1,0:T(8,128)(2,1)} %product_columns.5.q_ref.k_ref.v_ref.refs_0_.refs_1_.refs_2_, bf16[1024,1536]{1,0:T(8,128)(2,1)} %product_columns.5.q_ref.k_ref.v_ref.refs_0_.refs_1_.refs_2_, ...), custom_call_target="tpu_custom_call" | custom-call | flops 1048576 | bytes 65536 | tf_op jit(solution)/shard_map/attend/pallas_call | solution.py:721
  190.3 11.7 %collective-permute-done.16.refs_3_ = bf16[384,1024]{1,0:T(8,128)(2,1)S(1)} collective-permute-done((bf16[384,1024]{1,0:T(8,128)(2,1)S(1)}, bf16[384,1024]{1,0:T(8,128)(2,1)S(1)}, u32[]{:S(2)}, u32[]{:S(2)}) %collective-permute-start.16) | collective-permute-done | bytes 786464 | tf_op jit(solution)/shard_map/ppermute | solution.py:990
  225.0 6.3 add_norm.4
  231.3 11.5 %product_gelu.2 = (bf16[1024,2048]{1,0:T(8,128)(2,1)}, bf16[1024,2048]{1,0:T(8,128)(2,1)}) custom-call(bf16[1024,1024]{1,0:T(8,128)(2,1)} %get-tuple-element.395.x_ref.refs_1_, s32[4]{0:T(128)} %add_xor_fusion.refs_0_, bf16[4,1024,512]{2,1,0:T(8,128)(2,1)} %bitcast.94), custom_call_target="tpu_custom_call" | custom-call | flops 1048576 | bytes 65536 | tf_op jit(solution)/shard_map/product_gelu/pallas_call | solution.py:881
  242.8 9.1 product_rows.7.own_ref
  257.8 6.4 add_norm.6
  264.2 16.1 %collective-permute-done.21.refs_3_ = bf16[1024,384]{1,0:T(8,128)(2,1)S(1)} collective-permute-done((bf16[1024,384]{1,0:T(8,128)(2,1)S(1)}, bf16[1024,384]{1,0:T(8,128)(2,1)S(1)}, u32[]{:S(2)}, u32[]{:S(2)}) %collective-permute-start.21) | collective-permute-done | bytes 786464 | tf_op jit(solution)/shard_map/ppermute | solution.py:990
  293.0 18.8 %attend.5 = (bf16[1024,512]{1,0:T(8,128)(2,1)}, f32[4,2,1024]{2,1,0:T(2,128)}) custom-call(bf16[1024,512]{1,0:T(8,128)(2,1)} %product_columns.6.q_ref.refs_0_, bf16[1024,1024]{1,0:T(8,128)(2,1)} %product_columns.7.k_ref.v_ref.refs_1_.refs_2_, bf16[1024,1024]{1,0:T(8,128)(2,1)} %product_columns.7.k_ref.v_ref.refs_1_.refs_2_, ...), custom_call_target="tpu_custom_call" | custom-call | flops 1048576 | bytes 65536 | tf_op jit(solution)/shard_map/attend/pallas_call | solution.py:721
  311.9 6.2 product_rows.8.own_ref
  325.0 6.6 add_norm.7
  335.2 11.4 %product_gelu.3 = (bf16[1024,2048]{1,0:T(8,128)(2,1)}, bf16[1024,2048]{1,0:T(8,128)(2,1)}) custom-call(bf16[1024,1024]{1,0:T(8,128)(2,1)} %get-tuple-element.369.x_ref.refs_1_, s32[4]{0:T(128)} %add_xor_fusion.refs_0_, bf16[4,1024,512]{2,1,0:T(8,128)(2,1)} %bitcast.96), custom_call_target="tpu_custom_call" | custom-call | flops 1048576 | bytes 65536 | tf_op jit(solution)/shard_map/product_gelu/pallas_call | solution.py:881
  347.7 8.5 product_rows.9.own_ref
  365.9 9.0 last_norm.1
  381.6 9.2 product_rows_back_slope.2.refs_0_.x_ref
  396.3 8.6 product_columns_back.6.refs_1_
  413.8 5.9 weight_grads.17
  423.2 8.5 norm_back.6
  441.1 23.8 %attend_back.3 = (bf16[1024,512]{1,0:T(8,128)(2,1)}, bf16[1024,1024]{1,0:T(8,128)(2,1)}) custom-call(bf16[1024,512]{1,0:T(8,128)(2,1)} %product_columns.6.q_ref.refs_0_, bf16[1024,1024]{1,0:T(8,128)(2,1)} %product_columns.7.k_ref.v_ref.refs_1_.refs_2_, bf16[1024,1024]{1,0:T(8,128)(2,1)} %product_columns.7.k_ref.v_ref.refs_1_.refs_2_, ...), custom_call_target="tpu_custom_call" | custom-call | flops 1048576 | bytes 65536 | tf_op jit(solution)/shard_map/attend_back/pallas_call | solution.py:811
  483.3 7.6 norm_back.7
  496.4 9.3 %product_rows_back_slope.3.refs_0_.x_ref = bf16[1024,2048]{1,0:T(8,128)(2,1)} custom-call(bf16[1024,1024]{1,0:T(8,128)(2,1)} %get-tuple-element.416.refs_1_.x_ref, s32[4]{0:T(128)} %add_xor_fusion.refs_0_, bf16[4,512,1024]{2,1,0:T(8,128)(2,1)} %bitcast.93, bf16[1024,2048]{1,0:T(8,128)(2,1)} %get-tuple-element.392.refs_2_), custom_call_target="tpu_custom_call" | custom-call | flops 1048576 | bytes 65536 | tf_op jit(solution)/shard_map/product_rows_back_slope/pallas_call | solution.py:881
  511.2 8.6 product_columns_back.9.refs_1_
  534.6 8.7 norm_back.8
  551.2 7.1 weight_grads.21
  561.8 7.0 weight_grads.22
  568.8 8.8 norm_back.9
  585.8 21.9 %collective-permute-done.44 = bf16[512,1024]{1,0:T(8,128)(2,1)S(1)} collective-permute-done((bf16[512,1024]{1,0:T(8,128)(2,1)S(1)}, bf16[512,1024]{1,0:T(8,128)(2,1)S(1)}, u32[]{:S(2)}, u32[]{:S(2)}) %collective-permute-start.44) | collective-permute-done | bytes 1048608 | tf_op jit(solution)/shard_map/ppermute | solution.py:993
  610.0 17.7 %attend_back.4.refs_1_.x_ref = bf16[1024,1536]{1,0:T(8,128)(2,1)} custom-call(bf16[1024,1536]{1,0:T(8,128)(2,1)} %product_columns.5.q_ref.k_ref.v_ref.refs_0_.refs_1_.refs_2_, bf16[1024,1536]{1,0:T(8,128)(2,1)} %product_columns.5.q_ref.k_ref.v_ref.refs_0_.refs_1_.refs_2_, bf16[1024,1536]{1,0:T(8,128)(2,1)} %product_columns.5.q_ref.k_ref.v_ref.refs_0_.refs_1_.refs_2_, ...), custom_call_target="tpu_custom_call" | custom-call | flops 1048576 | bytes 65536 | tf_op jit(solution)/shard_map/attend_back/pallas_call | solution.py:811
  631.2 6.1 weight_grads.24
  637.9 8.0 product_columns_back.10.refs_1_
  645.9 6.2 weight_grads.25
  657.6 24.1 %attend_back.5.refs_1_.x_ref = bf16[1024,1536]{1,0:T(8,128)(2,1)} custom-call(bf16[1024,1536]{1,0:T(8,128)(2,1)} %product_columns.4.q_ref.k_ref.v_ref.refs_0_.refs_1_.refs_2_, bf16[1024,1536]{1,0:T(8,128)(2,1)} %product_columns.4.q_ref.k_ref.v_ref.refs_0_.refs_1_.refs_2_, bf16[1024,1536]{1,0:T(8,128)(2,1)} %product_columns.4.q_ref.k_ref.v_ref.refs_0_.refs_1_.refs_2_, ...), custom_call_target="tpu_custom_call" | custom-call | flops 1048576 | bytes 65536 | tf_op jit(solution)/shard_map/attend_back/pallas_call | solution.py:811
  681.7 6.3 weight_grads.26
  697.9 8.2 product_columns_back.11.refs_1_
  706.9 11.7 %collective-permute-done.47 = bf16[512,1024]{1,0:T(8,128)(2,1)S(1)} collective-permute-done((bf16[512,1024]{1,0:T(8,128)(2,1)}, bf16[512,1024]{1,0:T(8,128)(2,1)S(1)}, u32[]{:S(2)}, u32[]{:S(2)}) %collective-permute-start.47) | collective-permute-done | bytes 1048608 | tf_op jit(solution)/shard_map/ppermute | solution.py:993
  723.3 9.8 %collective-permute-done.48 = bf16[1,128,1024]{2,1,0:T(8,128)(2,1)} collective-permute-done((bf16[1,128,1024]{2,1,0:T(8,128)(2,1)}, bf16[1,128,1024]{2,1,0:T(8,128)(2,1)}, u32[]{:S(2)}, u32[]{:S(2)}) %collective-permute-start.48) | collective-permute-done | bytes 262176 | tf_op jit(solution)/shard_map/ppermute | solution.py:990
  741.9 6.2 weight_grads.27
  768.2 7.2 norm_back.10
  775.4 7.5 norm_back.11
  790.7 25.6 %collective-permute-done.65 = bf16[128,1024]{1,0:T(8,128)(2,1)S(1)} collective-permute-done((bf16[128,1024]{1,0:T(8,128)(2,1)S(1)}, bf16[128,1024]{1,0:T(8,128)(2,1)S(1)}, u32[]{:S(2)}, u32[]{:S(2)}) %collective-permute-start.65) | collective-permute-done | bytes 262176 | tf_op jit(solution)/shard_map/ppermute | solution.py:996
  832.9 16.2 %collective-permute-done.63 = f32[14,512]{1,0:T(8,128)S(1)} collective-permute-done((f32[14,512]{1,0:T(8,128)S(1)}, f32[14,512]{1,0:T(8,128)S(1)}, u32[]{:S(2)}, u32[]{:S(2)}) %collective-permute-start.63) | collective-permute-done | bytes 28704 | tf_op jit(solution)/shard_map/ppermute | solution.py:996
  860.8 22.2 %all-reduce.8.cloned.1.call-done = bf16[1024,1024]{1,0:T(8,128)(2,1)} async-done(((bf16[1024,1024]{1,0:T(8,128)(2,1)}), bf16[1024,1024]{1,0:T(8,128)(2,1)}) %all-reduce.8.cloned.1.call-update) | async-done | bytes 2097168 | tf_op jit(solution)/shard_map/psum | solution.py:1323
  (437 shorter events, 360.1 us)
Async XLA Ops:
  7.2 224.1 %all-gather.7.cloned.1.call-start = ((), (), s32[]{:S(2)}) async-start(), calls=%async_computation.3 | async-start | bytes 5242880 | tf_op jit(solution)/shard_map/all_gather | solution.py:1054
  57.7 185.1 %all-gather.9.cloned.1.call-start = ((), (), s32[]{:S(2)}) async-start(), calls=%async_computation.4 | async-start | bytes 5242880 | tf_op jit(solution)/shard_map/all_gather | solution.py:1054
  68.1 42.9 %collective-permute-start.10 = (bf16[1024,384]{1,0:T(8,128)(2,1)}, bf16[1024,384]{1,0:T(8,128)(2,1)}, u32[]{:S(2)}, u32[]{:S(2)}) collective-permute-start(bf16[1024,384]{1,0:T(8,128)(2,1)} %copy.51), channel_id=1, source_target_pairs={{0,1},{1,0},{2,3},{3,2},{4,6},{5,7},{6,4},{7,5},{8,9},{9,8},{10,11... | collective-permute-start | bytes 2359304 | tf_op jit(solution)/shard_map/ppermute | solution.py:990
  68.8 42.3 %collective-permute-start.9 = (bf16[1024,384]{1,0:T(8,128)(2,1)}, bf16[1024,384]{1,0:T(8,128)(2,1)}, u32[]{:S(2)}, u32[]{:S(2)}) collective-permute-start(bf16[1024,384]{1,0:T(8,128)(2,1)} %copy.51), channel_id=1, source_target_pairs={{0,2},{1,3},{2,0},{3,1},{4,5},{5,4},{6,7},{7,6},{8,10},{9,11},{10,... | collective-permute-start | bytes 2359304 | tf_op jit(solution)/shard_map/ppermute | solution.py:993
  72.9 38.2 %collective-permute-start.12 = (bf16[1,128,1024]{2,1,0:T(8,128)(2,1)S(1)}, bf16[1,128,1024]{2,1,0:T(8,128)(2,1)S(1)}, u32[]{:S(2)}, u32[]{:S(2)}) collective-permute-start(bf16[1,128,1024]{2,1,0:T(8,128)(2,1)S(1)} %get-tuple-element.288), channel_id=1, source_target_pairs={{0,1},{1,0},{2,3},{3,2},{4,6},{5,7},{6,4},{7,5},{8,9},{9,8},{10,11... | collective-permute-start | bytes 786440 | tf_op jit(solution)/shard_map/ppermute | solution.py:990
  74.2 36.9 %collective-permute-start.13 = (bf16[1,128,1024]{2,1,0:T(8,128)(2,1)S(1)}, bf16[1,128,1024]{2,1,0:T(8,128)(2,1)S(1)}, u32[]{:S(2)}, u32[]{:S(2)}) collective-permute-start(bf16[1,128,1024]{2,1,0:T(8,128)(2,1)S(1)} %get-tuple-element.289), channel_id=1, source_target_pairs={{0,2},{1,3},{2,0},{3,1},{4,5},{5,4},{6,7},{7,6},{8,10},{9,11},{10,... | collective-permute-start | bytes 786440 | tf_op jit(solution)/shard_map/ppermute | solution.py:993
  76.5 42.2 %collective-permute-start.14 = (bf16[1,128,1024]{2,1,0:T(8,128)(2,1)S(1)}, bf16[1,128,1024]{2,1,0:T(8,128)(2,1)S(1)}, u32[]{:S(2)}, u32[]{:S(2)}) collective-permute-start(bf16[1,128,1024]{2,1,0:T(8,128)(2,1)S(1)} %get-tuple-element.290), channel_id=1, source_target_pairs={{0,3},{1,2},{2,1},{3,0},{4,7},{5,6},{6,5},{7,4},{8,11},{9,10},{10,... | collective-permute-start | bytes 786440 | tf_op jit(solution)/shard_map/ppermute | solution.py:961
  118.7 216.4 %all-gather.11.cloned.1.call-start = ((), (), s32[]{:S(2)}) async-start(), calls=%async_computation.5 | async-start | bytes 5242880 | tf_op jit(solution)/shard_map/all_gather | solution.py:1054
  120.8 53.2 %collective-permute-start.7 = (bf16[384,1024]{1,0:T(8,128)(2,1)S(1)}, bf16[384,1024]{1,0:T(8,128)(2,1)S(1)}, u32[]{:S(2)}, u32[]{:S(2)}) collective-permute-start(bf16[384,1024]{1,0:T(8,128)(2,1)S(1)} %pad_maximum_fusion.13.refs_0_), channel_id=1, source_target_pairs={{0,2},{1,3},{2,0},{3,1},{4,5},{5,4},{6,7},{7,6},{8,10},{9,11},{10,... | collective-permute-start | bytes 2359304 | tf_op jit(solution)/shard_map/ppermute | solution.py:993
  121.3 52.7 %collective-permute-start.8 = (bf16[384,1024]{1,0:T(8,128)(2,1)S(1)}, bf16[384,1024]{1,0:T(8,128)(2,1)S(1)}, u32[]{:S(2)}, u32[]{:S(2)}) collective-permute-start(bf16[384,1024]{1,0:T(8,128)(2,1)S(1)} %pad_maximum_fusion.13.refs_0_), channel_id=1, source_target_pairs={{0,1},{1,0},{2,3},{3,2},{4,6},{5,7},{6,4},{7,5},{8,9},{9,8},{10,11... | collective-permute-start | bytes 2359304 | tf_op jit(solution)/shard_map/ppermute | solution.py:990
  121.4 42.2 %collective-permute-start.11 = (bf16[1024,384]{1,0:T(8,128)(2,1)}, bf16[1024,384]{1,0:T(8,128)(2,1)}, u32[]{:S(2)}, u32[]{:S(2)}) collective-permute-start(bf16[1024,384]{1,0:T(8,128)(2,1)} %collective-permute-done.9.refs_1_), channel_id=1, source_target_pairs={{0,1},{1,0},{2,3},{3,2},{4,6},{5,7},{6,4},{7,5},{8,9},{9,8},{10,11... | collective-permute-start | bytes 2359304 | tf_op jit(solution)/shard_map/ppermute | solution.py:990
  174.0 28.0 %collective-permute-start.16 = (bf16[384,1024]{1,0:T(8,128)(2,1)S(1)}, bf16[384,1024]{1,0:T(8,128)(2,1)S(1)}, u32[]{:S(2)}, u32[]{:S(2)}) collective-permute-start(bf16[384,1024]{1,0:T(8,128)(2,1)S(1)} %collective-permute-done.7.refs_1_), channel_id=1, source_target_pairs={{0,1},{1,0},{2,3},{3,2},{4,6},{5,7},{6,4},{7,5},{8,9},{9,8},{10,11... | collective-permute-start | bytes 2359304 | tf_op jit(solution)/shard_map/ppermute | solution.py:990
  215.3 27.5 %collective-permute-start.17 = (bf16[1024,384]{1,0:T(8,128)(2,1)S(1)}, bf16[1024,384]{1,0:T(8,128)(2,1)S(1)}, u32[]{:S(2)}, u32[]{:S(2)}) collective-permute-start(bf16[1024,384]{1,0:T(8,128)(2,1)S(1)} %pad_maximum_fusion.12.refs_0_), channel_id=1, source_target_pairs={{0,2},{1,3},{2,0},{3,1},{4,5},{5,4},{6,7},{7,6},{8,10},{9,11},{10,... | collective-permute-start | bytes 2359304 | tf_op jit(solution)/shard_map/ppermute | solution.py:993
  216.3 26.5 %collective-permute-start.18 = (bf16[1024,384]{1,0:T(8,128)(2,1)S(1)}, bf16[1024,384]{1,0:T(8,128)(2,1)S(1)}, u32[]{:S(2)}, u32[]{:S(2)}) collective-permute-start(bf16[1024,384]{1,0:T(8,128)(2,1)S(1)} %pad_maximum_fusion.12.refs_0_), channel_id=1, source_target_pairs={{0,1},{1,0},{2,3},{3,2},{4,6},{5,7},{6,4},{7,5},{8,9},{9,8},{10,11... | collective-permute-start | bytes 2359304 | tf_op jit(solution)/shard_map/ppermute | solution.py:990
  217.9 409.8 %all-reduce.4.cloned.1.call-start = ((), (), s32[]{:S(2)}) async-start(), calls=%async_computation | async-start | bytes 4194304 | tf_op jit(solution)/shard_map/psum | solution.py:1256
  252.5 27.8 %collective-permute-start.21 = (bf16[1024,384]{1,0:T(8,128)(2,1)S(1)}, bf16[1024,384]{1,0:T(8,128)(2,1)S(1)}, u32[]{:S(2)}, u32[]{:S(2)}) collective-permute-start(bf16[1024,384]{1,0:T(8,128)(2,1)S(1)} %collective-permute-done.17.refs_1_), channel_id=1, source_target_pairs={{0,1},{1,0},{2,3},{3,2},{4,6},{5,7},{6,4},{7,5},{8,9},{9,8},{10,11... | collective-permute-start | bytes 2359304 | tf_op jit(solution)/shard_map/ppermute | solution.py:990
  280.3 31.6 %collective-permute-start.23 = (bf16[512,1024]{1,0:T(8,128)(2,1)S(1)}, bf16[512,1024]{1,0:T(8,128)(2,1)S(1)}, u32[]{:S(2)}, u32[]{:S(2)}) collective-permute-start(bf16[512,1024]{1,0:T(8,128)(2,1)S(1)} %constant_dynamic-slice_fusion.43.refs_0_), channel_id=1, source_target_pairs={{0,2},{1,3},{2,0},{3,1},{4,5},{5,4},{6,7},{7,6},{8,10},{9,11},{10,... | collective-permute-start | bytes 3145736 | tf_op jit(solution)/shard_map/ppermute | solution.py:993
  281.5 30.4 %collective-permute-start.24 = (bf16[512,1024]{1,0:T(8,128)(2,1)S(1)}, bf16[512,1024]{1,0:T(8,128)(2,1)S(1)}, u32[]{:S(2)}, u32[]{:S(2)}) collective-permute-start(bf16[512,1024]{1,0:T(8,128)(2,1)S(1)} %constant_dynamic-slice_fusion.43.refs_0_), channel_id=1, source_target_pairs={{0,1},{1,0},{2,3},{3,2},{4,6},{5,7},{6,4},{7,5},{8,9},{9,8},{10,11... | collective-permute-start | bytes 3145736 | tf_op jit(solution)/shard_map/ppermute | solution.py:990
  319.6 27.0 %collective-permute-start.26 = (bf16[512,1024]{1,0:T(8,128)(2,1)S(1)}, bf16[512,1024]{1,0:T(8,128)(2,1)S(1)}, u32[]{:S(2)}, u32[]{:S(2)}) collective-permute-start(bf16[512,1024]{1,0:T(8,128)(2,1)S(1)} %collective-permute-done.23.refs_1_), channel_id=1, source_target_pairs={{0,1},{1,0},{2,3},{3,2},{4,6},{5,7},{6,4},{7,5},{8,9},{9,8},{10,11... | collective-permute-start | bytes 3145736 | tf_op jit(solution)/shard_map/ppermute | solution.py:990
  380.4 25.4 %collective-permute-start.32 = (bf16[1024,1024]{1,0:T(8,128)(2,1)}, bf16[1024,1024]{1,0:T(8,128)(2,1)S(1)}, u32[]{:S(2)}, u32[]{:S(2)}) collective-permute-start(bf16[1024,1024]{1,0:T(8,128)(2,1)} %weight_grads.14), channel_id=1, source_target_pairs={{0,1},{1,0},{2,3},{3,2},{4,6},{5,7},{6,4},{7,5},{8,9},{9,8},{10,11... | collective-permute-start | bytes 6291464 | tf_op jit(solution)/shard_map/ppermute | solution.py:990
  407.0 31.4 %collective-permute-start.34 = (bf16[1024,1024]{1,0:T(8,128)(2,1)}, bf16[1024,1024]{1,0:T(8,128)(2,1)S(1)}, u32[]{:S(2)}, u32[]{:S(2)}) collective-permute-start(bf16[1024,1024]{1,0:T(8,128)(2,1)} %weight_grads.15), channel_id=1, source_target_pairs={{0,1},{1,0},{2,3},{3,2},{4,6},{5,7},{6,4},{7,5},{8,9},{9,8},{10,11... | collective-permute-start | bytes 6291464 | tf_op jit(solution)/shard_map/ppermute | solution.py:990
  423.2 41.7 %collective-permute-start.35 = (bf16[512,1024]{1,0:T(8,128)(2,1)}, bf16[512,1024]{1,0:T(8,128)(2,1)S(1)}, u32[]{:S(2)}, u32[]{:S(2)}) collective-permute-start(bf16[512,1024]{1,0:T(8,128)(2,1)} %get-tuple-element.565), channel_id=1, source_target_pairs={{0,2},{1,3},{2,0},{3,1},{4,5},{5,4},{6,7},{7,6},{8,10},{9,11},{10,... | collective-permute-start | bytes 3145736 | tf_op jit(solution)/shard_map/ppermute | solution.py:993
  481.9 37.9 %collective-permute-start.40 = (bf16[1024,1024]{1,0:T(8,128)(2,1)}, bf16[1024,1024]{1,0:T(8,128)(2,1)S(1)}, u32[]{:S(2)}, u32[]{:S(2)}) collective-permute-start(bf16[1024,1024]{1,0:T(8,128)(2,1)} %product_columns_back.8.refs_1_), channel_id=1, source_target_pairs={{0,4},{4,0},{1,5},{5,1},{2,6},{6,2},{3,7},{7,3},{8,12},{12,8},{9,1... | collective-permute-start | bytes 6291464 | tf_op jit(solution)/shard_map/ppermute | solution.py:942
  523.1 25.5 %collective-permute-start.38 = (bf16[1024,1024]{1,0:T(8,128)(2,1)}, bf16[1024,1024]{1,0:T(8,128)(2,1)}, u32[]{:S(2)}, u32[]{:S(2)}) collective-permute-start(bf16[1024,1024]{1,0:T(8,128)(2,1)} %weight_grads.19), channel_id=1, source_target_pairs={{0,1},{1,0},{2,3},{3,2},{4,6},{5,7},{6,4},{7,5},{8,9},{9,8},{10,11... | collective-permute-start | bytes 6291464 | tf_op jit(solution)/shard_map/ppermute | solution.py:990
  523.2 210.0 %all-reduce.6.cloned.1.call-start = ((), (), s32[]{:S(2)}) async-start(), calls=%async_computation.1 | async-start | bytes 4194304 | tf_op jit(solution)/shard_map/psum | solution.py:1304
  558.3 69.4 %collective-permute-start.42 = (bf16[1024,1024]{1,0:T(8,128)(2,1)}, bf16[1024,1024]{1,0:T(8,128)(2,1)}, u32[]{:S(2)}, u32[]{:S(2)}) collective-permute-start(bf16[1024,1024]{1,0:T(8,128)(2,1)} %weight_grads.21), channel_id=1, source_target_pairs={{0,1},{1,0},{2,3},{3,2},{4,6},{5,7},{6,4},{7,5},{8,9},{9,8},{10,11... | collective-permute-start | bytes 6291464 | tf_op jit(solution)/shard_map/ppermute | solution.py:990
  560.3 25.4 %collective-permute-start.43 = (bf16[512,1024]{1,0:T(8,128)(2,1)}, bf16[512,1024]{1,0:T(8,128)(2,1)S(1)}, u32[]{:S(2)}, u32[]{:S(2)}) collective-permute-start(bf16[512,1024]{1,0:T(8,128)(2,1)} %get-tuple-element.561), channel_id=1, source_target_pairs={{0,2},{1,3},{2,0},{3,1},{4,5},{5,4},{6,7},{7,6},{8,10},{9,11},{10,... | collective-permute-start | bytes 3145736 | tf_op jit(solution)/shard_map/ppermute | solution.py:993
  561.0 46.6 %collective-permute-start.44 = (bf16[512,1024]{1,0:T(8,128)(2,1)S(1)}, bf16[512,1024]{1,0:T(8,128)(2,1)S(1)}, u32[]{:S(2)}, u32[]{:S(2)}) collective-permute-start(bf16[512,1024]{1,0:T(8,128)(2,1)S(1)} %get-tuple-element.562), channel_id=1, source_target_pairs={{0,2},{1,3},{2,0},{3,1},{4,5},{5,4},{6,7},{7,6},{8,10},{9,11},{10,... | collective-permute-start | bytes 3145736 | tf_op jit(solution)/shard_map/ppermute | solution.py:993
  637.4 51.9 %collective-permute-start.46 = (bf16[1024,1024]{1,0:T(8,128)(2,1)}, bf16[1024,1024]{1,0:T(8,128)(2,1)}, u32[]{:S(2)}, u32[]{:S(2)}) collective-permute-start(bf16[1024,1024]{1,0:T(8,128)(2,1)} %weight_grads.24), channel_id=1, source_target_pairs={{0,1},{1,0},{2,3},{3,2},{4,6},{5,7},{6,4},{7,5},{8,9},{9,8},{10,11... | collective-permute-start | bytes 6291464 | tf_op jit(solution)/shard_map/ppermute | solution.py:990
  637.4 245.6 %all-reduce.8.cloned.1.call-start = ((), (), s32[]{:S(2)}) async-start(), calls=%async_computation.2 | async-start | bytes 4194304 | tf_op jit(solution)/shard_map/psum | solution.py:1323
  637.4 68.7 %collective-permute-start.45 = (bf16[512,1024]{1,0:T(8,128)(2,1)}, bf16[512,1024]{1,0:T(8,128)(2,1)}, u32[]{:S(2)}, u32[]{:S(2)}) collective-permute-start(bf16[512,1024]{1,0:T(8,128)(2,1)} %get-tuple-element.559), channel_id=1, source_target_pairs={{0,2},{1,3},{2,0},{3,1},{4,5},{5,4},{6,7},{7,6},{8,10},{9,11},{10,... | collective-permute-start | bytes 3145736 | tf_op jit(solution)/shard_map/ppermute | solution.py:993
  688.0 45.2 %collective-permute-start.51 = (bf16[1024,1024]{1,0:T(8,128)(2,1)}, bf16[1024,1024]{1,0:T(8,128)(2,1)}, u32[]{:S(2)}, u32[]{:S(2)}) collective-permute-start(bf16[1024,1024]{1,0:T(8,128)(2,1)} %weight_grads.26), channel_id=1, source_target_pairs={{0,1},{1,0},{2,3},{3,2},{4,6},{5,7},{6,4},{7,5},{8,9},{9,8},{10,11... | collective-permute-start | bytes 6291464 | tf_op jit(solution)/shard_map/ppermute | solution.py:990
  693.1 25.6 %collective-permute-start.47 = (bf16[512,1024]{1,0:T(8,128)(2,1)}, bf16[512,1024]{1,0:T(8,128)(2,1)S(1)}, u32[]{:S(2)}, u32[]{:S(2)}) collective-permute-start(bf16[512,1024]{1,0:T(8,128)(2,1)} %get-tuple-element.557), channel_id=1, source_target_pairs={{0,2},{1,3},{2,0},{3,1},{4,5},{5,4},{6,7},{7,6},{8,10},{9,11},{10,... | collective-permute-start | bytes 3145736 | tf_op jit(solution)/shard_map/ppermute | solution.py:993
  696.9 43.4 %collective-permute-start.74 = (bf16[1024,512]{1,0:T(8,128)(2,1)}, bf16[1024,512]{1,0:T(8,128)(2,1)}, u32[]{:S(2)}, u32[]{:S(2)}) collective-permute-start(bf16[1024,512]{1,0:T(8,128)(2,1)} %constant_dynamic-slice_fusion), channel_id=1, source_target_pairs={{0,4},{4,0},{1,5},{5,1},{2,6},{6,2},{3,7},{7,3},{8,12},{12,8},{9,1... | collective-permute-start | bytes 3145736 | tf_op jit(solution)/shard_map/ppermute | solution.py:942
  697.9 35.3 %collective-permute-start.48 = (bf16[1,128,1024]{2,1,0:T(8,128)(2,1)}, bf16[1,128,1024]{2,1,0:T(8,128)(2,1)}, u32[]{:S(2)}, u32[]{:S(2)}) collective-permute-start(bf16[1,128,1024]{2,1,0:T(8,128)(2,1)} %get-tuple-element.457), channel_id=1, source_target_pairs={{0,1},{1,0},{2,3},{3,2},{4,6},{5,7},{6,4},{7,5},{8,9},{9,8},{10,11... | collective-permute-start | bytes 786440 | tf_op jit(solution)/shard_map/ppermute | solution.py:990
  706.1 27.0 %collective-permute-start.49 = (bf16[1,128,1024]{2,1,0:T(8,128)(2,1)}, bf16[1,128,1024]{2,1,0:T(8,128)(2,1)}, u32[]{:S(2)}, u32[]{:S(2)}) collective-permute-start(bf16[1,128,1024]{2,1,0:T(8,128)(2,1)} %get-tuple-element.458), channel_id=1, source_target_pairs={{0,2},{1,3},{2,0},{3,1},{4,5},{5,4},{6,7},{7,6},{8,10},{9,11},{10,... | collective-permute-start | bytes 786440 | tf_op jit(solution)/shard_map/ppermute | solution.py:993
  733.2 35.0 %collective-permute-start.52 = (bf16[1024,1024]{1,0:T(8,128)(2,1)}, bf16[1024,1024]{1,0:T(8,128)(2,1)}, u32[]{:S(2)}, u32[]{:S(2)}) collective-permute-start(bf16[1024,1024]{1,0:T(8,128)(2,1)} %product_columns_back.11.refs_1_), channel_id=1, source_target_pairs={{0,4},{4,0},{1,5},{5,1},{2,6},{6,2},{3,7},{7,3},{8,12},{12,8},{9,1... | collective-permute-start | bytes 6291464 | tf_op jit(solution)/shard_map/ppermute | solution.py:942
  737.3 38.1 %collective-permute-start.54 = (bf16[1024,1024]{1,0:T(8,128)(2,1)S(1)}, bf16[1024,1024]{1,0:T(8,128)(2,1)}, u32[]{:S(2)}, u32[]{:S(2)}) collective-permute-start(bf16[1024,1024]{1,0:T(8,128)(2,1)S(1)} %copy-done.12), channel_id=1, source_target_pairs={{0,4},{4,0},{1,5},{5,1},{2,6},{6,2},{3,7},{7,3},{8,12},{12,8},{9,1... | collective-permute-start | bytes 6291464 | tf_op jit(solution)/shard_map/ppermute | solution.py:942
  752.6 30.4 %collective-permute-start.53 = (bf16[512,1024]{1,0:T(8,128)(2,1)}, bf16[512,1024]{1,0:T(8,128)(2,1)}, u32[]{:S(2)}, u32[]{:S(2)}) collective-permute-start(bf16[512,1024]{1,0:T(8,128)(2,1)} %get-tuple-element.554), channel_id=1, source_target_pairs={{0,2},{1,3},{2,0},{3,1},{4,5},{5,4},{6,7},{7,6},{8,10},{9,11},{10,... | collective-permute-start | bytes 3145736 | tf_op jit(solution)/shard_map/ppermute | solution.py:993
  784.4 31.8 %collective-permute-start.65 = (bf16[128,1024]{1,0:T(8,128)(2,1)S(1)}, bf16[128,1024]{1,0:T(8,128)(2,1)S(1)}, u32[]{:S(2)}, u32[]{:S(2)}) collective-permute-start(bf16[128,1024]{1,0:T(8,128)(2,1)S(1)} %get-tuple-element.581), channel_id=1, source_target_pairs={{0,24},{8,16},{16,8},{24,0},{1,25},{9,17},{17,9},{25,1},{2,26},{10... | collective-permute-start | bytes 786440 | tf_op jit(solution)/shard_map/ppermute | solution.py:996
  785.9 34.5 %collective-permute-start.66 = (bf16[128,1024]{1,0:T(8,128)(2,1)S(1)}, bf16[128,1024]{1,0:T(8,128)(2,1)S(1)}, u32[]{:S(2)}, u32[]{:S(2)}) collective-permute-start(bf16[128,1024]{1,0:T(8,128)(2,1)S(1)} %get-tuple-element.583), channel_id=1, source_target_pairs={{0,16},{8,24},{16,0},{24,8},{1,17},{9,25},{17,1},{25,9},{2,18},{10... | collective-permute-start | bytes 786440 | tf_op jit(solution)/shard_map/ppermute | solution.py:996
  787.0 33.3 %collective-permute-start.67 = (bf16[128,1024]{1,0:T(8,128)(2,1)S(1)}, bf16[128,1024]{1,0:T(8,128)(2,1)S(1)}, u32[]{:S(2)}, u32[]{:S(2)}) collective-permute-start(bf16[128,1024]{1,0:T(8,128)(2,1)S(1)} %get-tuple-element.582), channel_id=1, source_target_pairs={{0,8},{8,0},{16,24},{24,16},{1,9},{9,1},{17,25},{25,17},{2,10},{10... | collective-permute-start | bytes 786440 | tf_op jit(solution)/shard_map/ppermute | solution.py:996
  821.5 63.8 %collective-permute-start.68 = (bf16[128,1024]{1,0:T(8,128)(2,1)S(1)}, bf16[128,1024]{1,0:T(8,128)(2,1)}, u32[]{:S(2)}, u32[]{:S(2)}) collective-permute-start(bf16[128,1024]{1,0:T(8,128)(2,1)S(1)} %add_convert_fusion.20), channel_id=1, source_target_pairs={{0,8},{8,0},{16,24},{24,16},{1,9},{9,1},{17,25},{25,17},{2,10},{10... | collective-permute-start | bytes 786440 | tf_op jit(solution)/shard_map/ppermute | solution.py:996
  824.8 63.4 %collective-permute-start.69 = (bf16[128,1024]{1,0:T(8,128)(2,1)S(1)}, bf16[128,1024]{1,0:T(8,128)(2,1)S(1)}, u32[]{:S(2)}, u32[]{:S(2)}) collective-permute-start(bf16[128,1024]{1,0:T(8,128)(2,1)S(1)} %add_convert_fusion.20), channel_id=1, source_target_pairs={{0,16},{8,24},{16,0},{24,8},{1,17},{9,25},{17,1},{25,9},{2,18},{10... | collective-permute-start | bytes 786440 | tf_op jit(solution)/shard_map/ppermute | solution.py:996
  829.5 25.6 %collective-permute-start.58 = (bf16[1,128,1024]{2,1,0:T(8,128)(2,1)S(1)}, bf16[1,128,1024]{2,1,0:T(8,128)(2,1)S(1)}, u32[]{:S(2)}, u32[]{:S(2)}) collective-permute-start(bf16[1,128,1024]{2,1,0:T(8,128)(2,1)S(1)} %get-tuple-element.492), channel_id=1, source_target_pairs={{0,1},{1,0},{2,3},{3,2},{4,6},{5,7},{6,4},{7,5},{8,9},{9,8},{10,11... | collective-permute-start | bytes 786440 | tf_op jit(solution)/shard_map/ppermute | solution.py:990
  855.1 33.8 %collective-permute-start.70 = (bf16[128,1024]{1,0:T(8,128)(2,1)S(1)}, bf16[128,1024]{1,0:T(8,128)(2,1)S(1)}, u32[]{:S(2)}, u32[]{:S(2)}) collective-permute-start(bf16[128,1024]{1,0:T(8,128)(2,1)S(1)} %add_convert_fusion.20), channel_id=1, source_target_pairs={{0,24},{8,16},{16,8},{24,0},{1,25},{9,17},{17,9},{25,1},{2,26},{10... | collective-permute-start | bytes 786440 | tf_op jit(solution)/shard_map/ppermute | solution.py:996
  855.1 36.0 %collective-permute-start.55 = (bf16[1,128,1024]{2,1,0:T(8,128)(2,1)}, bf16[1,128,1024]{2,1,0:T(8,128)(2,1)}, u32[]{:S(2)}, u32[]{:S(2)}) collective-permute-start(bf16[1,128,1024]{2,1,0:T(8,128)(2,1)} %get-tuple-element.486), channel_id=1, source_target_pairs={{0,1},{1,0},{2,3},{3,2},{4,6},{5,7},{6,4},{7,5},{8,9},{9,8},{10,11... | collective-permute-start | bytes 786440 | tf_op jit(solution)/shard_map/ppermute | solution.py:990
  860.5 30.6 %collective-permute-start.56 = (bf16[1,128,1024]{2,1,0:T(8,128)(2,1)S(1)}, bf16[1,128,1024]{2,1,0:T(8,128)(2,1)}, u32[]{:S(2)}, u32[]{:S(2)}) collective-permute-start(bf16[1,128,1024]{2,1,0:T(8,128)(2,1)S(1)} %get-tuple-element.487), channel_id=1, source_target_pairs={{0,2},{1,3},{2,0},{3,1},{4,5},{5,4},{6,7},{7,6},{8,10},{9,11},{10,... | collective-permute-start | bytes 786440 | tf_op jit(solution)/shard_map/ppermute | solution.py:993
  (103 other events, 1317.2 us)
Sparse Core Ops, SparseCore 0:
  57.9 80.7 all-gather.6
  141.1 65.2 all-gather.8
  218.0 69.1 all-gather.10
  523.3 84.8 all-reduce.3
  637.5 84.6 all-reduce.5
  758.5 124.4 all-reduce.7

commit v6 on v4

--- a/solution.py
+++ b/solution.py
@@ -1324,6 +1324,7 @@
     other_a, other_c = chip.other(own_a), chip.other(pin(own_c, own_a))
     own_a, keep_a = keep_half(own_a, near_a, *pairs_a)
     own_a, side_a = here(own_a, to_side, *keep_a)
+    sum_f, sum_b = tie((sum_f, sum_b, own_a))[:2]
     source_grad, gain_e0, shift_e0 = norm_back_rows(
         x_source, own_a, other_a, enc(0)[0], d_hidden, [BF16]
     )

time: 932 us -> 925 us (level)
    unnamed x138 -> x142, local copies, waits for them, and re-layouts: 17.9 us -> 19.2 us
  transfers between devices with their start and end apart: 81 -> 81, of which waited for: 31 -> 31; matrix products, arithmetic and copies ran while one was open for 11% -> 10% of each run, Pallas kernels for 46% -> 46%
where the time goes in v6:
time: 925 us; the launch traced here: 916 us
  Pallas kernels  459 us (50%)
  waiting for transfers between devices  230 us (25%)
  starting transfers between devices  72.2 us (8%)
  other arithmetic  71 us (8%)
  local copies, waits for them, and re-layouts  67.9 us (7%)
  between operations  15.5 us (2%)
    pallas_call x22, Pallas kernels, piece_product(): pl.pallas_call(functools.partial(piece_kernel, kind, low, high, 1 if stac...  165 us
    ppermute x24, waiting for transfers between devices, send_near(): return lax.ppermute(block, CROSS, self.first)  94 us
    pallas_call x13, Pallas kernels, row_call(): pl.pallas_call(kernel, grid=(rows // ROW_BLOCK,), in_specs=[block] * len(...  91.5 us
    pallas_call x14, Pallas kernels, weight_grads(): pl.pallas_call(functools.partial(weight_kernel, len(pairs)), grid=(2,), i...  83.9 us
    pallas_call x3, Pallas kernels, chip_attend_back(): pl.pallas_call(functools.partial(chip_attend_back_kernel, causal, fused),...  65.4 us
    ppermute x19, waiting for transfers between devices, send_side(): return lax.ppermute(block, CROSS, self.second)  54.5 us
    pallas_call x3, Pallas kernels, chip_attend(): pl.pallas_call(functools.partial(chip_attend_kernel, causal), grid=(count...  53.5 us
    ppermute x8, waiting for transfers between devices, along(): return lax.ppermute(block, 'dp', swap_pairs(4, bit))  30.2 us
  transfers between devices with their start and end apart: 81, of which 31 were waited for; matrix products, arithmetic and copies ran while one was open for 10% of the time, Pallas kernels for 46%

profile of v6, /device:TPU:9, one launch (start us, length us, event | category | flops | bytes accessed | tf_op | source)
XLA Modules:
  0.0 915.9 jit_solution(3674099175568685725)
XLA Ops:
  14.5 14.7 %collective-permute-done.refs_1_ = bf16[1024,384]{1,0:T(8,128)(2,1)} collective-permute-done((bf16[1024,384]{1,0:T(8,128)(2,1)}, bf16[1024,384]{1,0:T(8,128)(2,1)}, u32[]{:S(2)}, u32[]{:S(2)}) %collective-permute-start) | collective-permute-done | bytes 786464 | tf_op jit(solution)/shard_map/ppermute | solution.py:993
  51.3 6.4 collective-permute-done.2.refs_3_
  84.1 8.1 product_columns.4.q_ref.k_ref.v_ref.refs_0_.refs_1_.refs_2_
  92.2 18.8 %attend.3 = (bf16[1024,512]{1,0:T(8,128)(2,1)}, f32[4,2,1024]{2,1,0:T(2,128)}) custom-call(bf16[1024,1536]{1,0:T(8,128)(2,1)} %product_columns.4.q_ref.k_ref.v_ref.refs_0_.refs_1_.refs_2_, bf16[1024,1536]{1,0:T(8,128)(2,1)} %product_columns.4.q_ref.k_ref.v_ref.refs_0_.refs_1_.refs_2_, ...), custom_call_target="tpu_custom_call" | custom-call | flops 1048576 | bytes 65536 | tf_op jit(solution)/shard_map/attend/pallas_call | solution.py:721
  111.1 7.6 collective-permute-done.14
  130.2 33.5 %collective-permute-done.11.refs_3_ = bf16[1024,384]{1,0:T(8,128)(2,1)} collective-permute-done((bf16[1024,384]{1,0:T(8,128)(2,1)}, bf16[1024,384]{1,0:T(8,128)(2,1)}, u32[]{:S(2)}, u32[]{:S(2)}) %collective-permute-start.11) | collective-permute-done | bytes 786464 | tf_op jit(solution)/shard_map/ppermute | solution.py:990
  165.9 8.0 product_columns.5.q_ref.k_ref.v_ref.refs_0_.refs_1_.refs_2_
  174.3 15.9 %attend.4 = (bf16[1024,512]{1,0:T(8,128)(2,1)}, f32[4,2,1024]{2,1,0:T(2,128)}) custom-call(bf16[1024,1536]{1,0:T(8,128)(2,1)} %product_columns.5.q_ref.k_ref.v_ref.refs_0_.refs_1_.refs_2_, bf16[1024,1536]{1,0:T(8,128)(2,1)} %product_columns.5.q_ref.k_ref.v_ref.refs_0_.refs_1_.refs_2_, ...), custom_call_target="tpu_custom_call" | custom-call | flops 1048576 | bytes 65536 | tf_op jit(solution)/shard_map/attend/pallas_call | solution.py:721
  190.2 11.7 %collective-permute-done.16.refs_3_ = bf16[384,1024]{1,0:T(8,128)(2,1)S(1)} collective-permute-done((bf16[384,1024]{1,0:T(8,128)(2,1)S(1)}, bf16[384,1024]{1,0:T(8,128)(2,1)S(1)}, u32[]{:S(2)}, u32[]{:S(2)}) %collective-permute-start.16) | collective-permute-done | bytes 786464 | tf_op jit(solution)/shard_map/ppermute | solution.py:990
  224.9 6.3 add_norm.4
  231.2 11.5 %product_gelu.2 = (bf16[1024,2048]{1,0:T(8,128)(2,1)}, bf16[1024,2048]{1,0:T(8,128)(2,1)}) custom-call(bf16[1024,1024]{1,0:T(8,128)(2,1)} %get-tuple-element.397.x_ref.refs_1_, s32[4]{0:T(128)} %add_xor_fusion.refs_0_, bf16[4,1024,512]{2,1,0:T(8,128)(2,1)} %bitcast.94), custom_call_target="tpu_custom_call" | custom-call | flops 1048576 | bytes 65536 | tf_op jit(solution)/shard_map/product_gelu/pallas_call | solution.py:881
  242.8 9.1 product_rows.7.own_ref
  257.8 6.3 add_norm.6
  264.2 16.1 %collective-permute-done.21.refs_3_ = bf16[1024,384]{1,0:T(8,128)(2,1)S(1)} collective-permute-done((bf16[1024,384]{1,0:T(8,128)(2,1)S(1)}, bf16[1024,384]{1,0:T(8,128)(2,1)S(1)}, u32[]{:S(2)}, u32[]{:S(2)}) %collective-permute-start.21) | collective-permute-done | bytes 786464 | tf_op jit(solution)/shard_map/ppermute | solution.py:990
  293.1 18.8 %attend.5 = (bf16[1024,512]{1,0:T(8,128)(2,1)}, f32[4,2,1024]{2,1,0:T(2,128)}) custom-call(bf16[1024,512]{1,0:T(8,128)(2,1)} %product_columns.6.q_ref.refs_0_, bf16[1024,1024]{1,0:T(8,128)(2,1)} %product_columns.7.k_ref.v_ref.refs_1_.refs_2_, bf16[1024,1024]{1,0:T(8,128)(2,1)} %product_columns.7.k_ref.v_ref.refs_1_.refs_2_, ...), custom_call_target="tpu_custom_call" | custom-call | flops 1048576 | bytes 65536 | tf_op jit(solution)/shard_map/attend/pallas_call | solution.py:721
  311.9 6.2 product_rows.8.own_ref
  325.0 6.6 add_norm.7
  335.2 11.4 %product_gelu.3 = (bf16[1024,2048]{1,0:T(8,128)(2,1)}, bf16[1024,2048]{1,0:T(8,128)(2,1)}) custom-call(bf16[1024,1024]{1,0:T(8,128)(2,1)} %get-tuple-element.371.x_ref.refs_1_, s32[4]{0:T(128)} %add_xor_fusion.refs_0_, bf16[4,1024,512]{2,1,0:T(8,128)(2,1)} %bitcast.96), custom_call_target="tpu_custom_call" | custom-call | flops 1048576 | bytes 65536 | tf_op jit(solution)/shard_map/product_gelu/pallas_call | solution.py:881
  347.7 8.5 product_rows.9.own_ref
  365.9 9.1 last_norm.1
  381.7 9.2 %product_rows_back_slope.2.refs_0_.x_ref = bf16[1024,2048]{1,0:T(8,128)(2,1)} custom-call(bf16[1024,1024]{1,0:T(8,128)(2,1)} %get-tuple-element.379.refs_1_.x_ref, bf16[512,1024]{1,0:T(8,128)(2,1)} %copy-done.10, bf16[512,1024]{1,0:T(8,128)(2,1)} %copy-done.18, bf16[512,1024]{1,0:T(8,128)(2,1)} %copy-done.19, bf16[512,1024]{1,0:T(8,128)(2,1)} %copy-done.20, ...), custom_call_target="tpu_custom_call" | custom-call | flops 1048576 | bytes 65536 | tf_op jit(solution)/shard_map/product_rows_back_slope/pallas_call | solution.py:881
  396.4 8.6 product_columns_back.6.refs_1_
  423.3 8.5 norm_back.6
  441.0 23.8 %attend_back.3 = (bf16[1024,512]{1,0:T(8,128)(2,1)}, bf16[1024,1024]{1,0:T(8,128)(2,1)}) custom-call(bf16[1024,512]{1,0:T(8,128)(2,1)} %product_columns.6.q_ref.refs_0_, bf16[1024,1024]{1,0:T(8,128)(2,1)} %product_columns.7.k_ref.v_ref.refs_1_.refs_2_, bf16[1024,1024]{1,0:T(8,128)(2,1)} %product_columns.7.k_ref.v_ref.refs_1_.refs_2_, ...), custom_call_target="tpu_custom_call" | custom-call | flops 1048576 | bytes 65536 | tf_op jit(solution)/shard_map/attend_back/pallas_call | solution.py:811
  483.4 7.6 norm_back.7
  496.5 9.3 %product_rows_back_slope.3.refs_0_.x_ref = bf16[1024,2048]{1,0:T(8,128)(2,1)} custom-call(bf16[1024,1024]{1,0:T(8,128)(2,1)} %get-tuple-element.418.refs_1_.x_ref, s32[4]{0:T(128)} %add_xor_fusion.refs_0_, bf16[4,512,1024]{2,1,0:T(8,128)(2,1)} %bitcast.93, bf16[1024,2048]{1,0:T(8,128)(2,1)} %get-tuple-element.394.refs_2_), custom_call_target="tpu_custom_call" | custom-call | flops 1048576 | bytes 65536 | tf_op jit(solution)/shard_map/product_rows_back_slope/pallas_call | solution.py:881
  511.3 8.6 product_columns_back.9.refs_1_
  534.7 8.7 norm_back.8
  551.3 7.1 weight_grads.21
  561.9 7.0 weight_grads.22
  568.9 8.8 norm_back.9
  585.9 21.9 %collective-permute-done.44 = bf16[512,1024]{1,0:T(8,128)(2,1)S(1)} collective-permute-done((bf16[512,1024]{1,0:T(8,128)(2,1)S(1)}, bf16[512,1024]{1,0:T(8,128)(2,1)S(1)}, u32[]{:S(2)}, u32[]{:S(2)}) %collective-permute-start.44) | collective-permute-done | bytes 1048608 | tf_op jit(solution)/shard_map/ppermute | solution.py:993
  610.1 17.6 %attend_back.4.refs_1_.x_ref = bf16[1024,1536]{1,0:T(8,128)(2,1)} custom-call(bf16[1024,1536]{1,0:T(8,128)(2,1)} %product_columns.5.q_ref.k_ref.v_ref.refs_0_.refs_1_.refs_2_, bf16[1024,1536]{1,0:T(8,128)(2,1)} %product_columns.5.q_ref.k_ref.v_ref.refs_0_.refs_1_.refs_2_, bf16[1024,1536]{1,0:T(8,128)(2,1)} %product_columns.5.q_ref.k_ref.v_ref.refs_0_.refs_1_.refs_2_, ...), custom_call_target="tpu_custom_call" | custom-call | flops 1048576 | bytes 65536 | tf_op jit(solution)/shard_map/attend_back/pallas_call | solution.py:811
  631.2 6.2 weight_grads.24
  637.9 8.0 product_columns_back.10.refs_1_
  645.9 6.2 weight_grads.25
  657.6 24.0 %attend_back.5.refs_1_.x_ref = bf16[1024,1536]{1,0:T(8,128)(2,1)} custom-call(bf16[1024,1536]{1,0:T(8,128)(2,1)} %product_columns.4.q_ref.k_ref.v_ref.refs_0_.refs_1_.refs_2_, bf16[1024,1536]{1,0:T(8,128)(2,1)} %product_columns.4.q_ref.k_ref.v_ref.refs_0_.refs_1_.refs_2_, bf16[1024,1536]{1,0:T(8,128)(2,1)} %product_columns.4.q_ref.k_ref.v_ref.refs_0_.refs_1_.refs_2_, ...), custom_call_target="tpu_custom_call" | custom-call | flops 1048576 | bytes 65536 | tf_op jit(solution)/shard_map/attend_back/pallas_call | solution.py:811
  681.6 6.3 weight_grads.26
  696.9 8.3 product_columns_back.11.refs_1_
  707.5 11.1 %collective-permute-done.47 = bf16[512,1024]{1,0:T(8,128)(2,1)} collective-permute-done((bf16[512,1024]{1,0:T(8,128)(2,1)}, bf16[512,1024]{1,0:T(8,128)(2,1)}, u32[]{:S(2)}, u32[]{:S(2)}) %collective-permute-start.47) | collective-permute-done | bytes 1048608 | tf_op jit(solution)/shard_map/ppermute | solution.py:993
  723.4 9.6 %collective-permute-done.48 = bf16[1,128,1024]{2,1,0:T(8,128)(2,1)} collective-permute-done((bf16[1,128,1024]{2,1,0:T(8,128)(2,1)}, bf16[1,128,1024]{2,1,0:T(8,128)(2,1)}, u32[]{:S(2)}, u32[]{:S(2)}) %collective-permute-start.48) | collective-permute-done | bytes 262176 | tf_op jit(solution)/shard_map/ppermute | solution.py:990
  771.7 7.2 norm_back.10
  779.0 7.5 norm_back.11
  799.5 11.6 %collective-permute-done.63 = f32[14,512]{1,0:T(8,128)S(1)} collective-permute-done((f32[14,512]{1,0:T(8,128)S(1)}, f32[14,512]{1,0:T(8,128)S(1)}, u32[]{:S(2)}, u32[]{:S(2)}) %collective-permute-start.63) | collective-permute-done | bytes 28704 | tf_op jit(solution)/shard_map/ppermute | solution.py:996
  812.7 6.9 collective-permute-done.64
  824.2 26.3 %all-reduce.8.cloned.1.call-done = bf16[1024,1024]{1,0:T(8,128)(2,1)} async-done(((bf16[1024,1024]{1,0:T(8,128)(2,1)}), bf16[1024,1024]{1,0:T(8,128)(2,1)}) %all-reduce.8.cloned.1.call-update) | async-done | bytes 2097168 | tf_op jit(solution)/shard_map/psum | solution.py:1323
  858.7 6.3 collective-permute-done.68
  867.3 6.8 collective-permute-start.73
  (433 shorter events, 366.7 us)
Async XLA Ops:
  7.2 224.0 %all-gather.7.cloned.1.call-start = ((), (), s32[]{:S(2)}) async-start(), calls=%async_computation.3 | async-start | bytes 5242880 | tf_op jit(solution)/shard_map/all_gather | solution.py:1054
  57.7 185.1 %all-gather.9.cloned.1.call-start = ((), (), s32[]{:S(2)}) async-start(), calls=%async_computation.4 | async-start | bytes 5242880 | tf_op jit(solution)/shard_map/all_gather | solution.py:1054
  68.1 42.9 %collective-permute-start.10 = (bf16[1024,384]{1,0:T(8,128)(2,1)}, bf16[1024,384]{1,0:T(8,128)(2,1)}, u32[]{:S(2)}, u32[]{:S(2)}) collective-permute-start(bf16[1024,384]{1,0:T(8,128)(2,1)} %copy.51), channel_id=1, source_target_pairs={{0,1},{1,0},{2,3},{3,2},{4,6},{5,7},{6,4},{7,5},{8,9},{9,8},{10,11... | collective-permute-start | bytes 2359304 | tf_op jit(solution)/shard_map/ppermute | solution.py:990
  68.8 42.3 %collective-permute-start.9 = (bf16[1024,384]{1,0:T(8,128)(2,1)}, bf16[1024,384]{1,0:T(8,128)(2,1)}, u32[]{:S(2)}, u32[]{:S(2)}) collective-permute-start(bf16[1024,384]{1,0:T(8,128)(2,1)} %copy.51), channel_id=1, source_target_pairs={{0,2},{1,3},{2,0},{3,1},{4,5},{5,4},{6,7},{7,6},{8,10},{9,11},{10,... | collective-permute-start | bytes 2359304 | tf_op jit(solution)/shard_map/ppermute | solution.py:993
  72.9 38.2 %collective-permute-start.12 = (bf16[1,128,1024]{2,1,0:T(8,128)(2,1)S(1)}, bf16[1,128,1024]{2,1,0:T(8,128)(2,1)S(1)}, u32[]{:S(2)}, u32[]{:S(2)}) collective-permute-start(bf16[1,128,1024]{2,1,0:T(8,128)(2,1)S(1)} %get-tuple-element.290), channel_id=1, source_target_pairs={{0,1},{1,0},{2,3},{3,2},{4,6},{5,7},{6,4},{7,5},{8,9},{9,8},{10,11... | collective-permute-start | bytes 786440 | tf_op jit(solution)/shard_map/ppermute | solution.py:990
  74.2 36.9 %collective-permute-start.13 = (bf16[1,128,1024]{2,1,0:T(8,128)(2,1)S(1)}, bf16[1,128,1024]{2,1,0:T(8,128)(2,1)S(1)}, u32[]{:S(2)}, u32[]{:S(2)}) collective-permute-start(bf16[1,128,1024]{2,1,0:T(8,128)(2,1)S(1)} %get-tuple-element.291), channel_id=1, source_target_pairs={{0,2},{1,3},{2,0},{3,1},{4,5},{5,4},{6,7},{7,6},{8,10},{9,11},{10,... | collective-permute-start | bytes 786440 | tf_op jit(solution)/shard_map/ppermute | solution.py:993
  76.5 42.2 %collective-permute-start.14 = (bf16[1,128,1024]{2,1,0:T(8,128)(2,1)S(1)}, bf16[1,128,1024]{2,1,0:T(8,128)(2,1)S(1)}, u32[]{:S(2)}, u32[]{:S(2)}) collective-permute-start(bf16[1,128,1024]{2,1,0:T(8,128)(2,1)S(1)} %get-tuple-element.292), channel_id=1, source_target_pairs={{0,3},{1,2},{2,1},{3,0},{4,7},{5,6},{6,5},{7,4},{8,11},{9,10},{10,... | collective-permute-start | bytes 786440 | tf_op jit(solution)/shard_map/ppermute | solution.py:961
  118.7 216.5 %all-gather.11.cloned.1.call-start = ((), (), s32[]{:S(2)}) async-start(), calls=%async_computation.5 | async-start | bytes 5242880 | tf_op jit(solution)/shard_map/all_gather | solution.py:1054
  120.8 53.2 %collective-permute-start.7 = (bf16[384,1024]{1,0:T(8,128)(2,1)S(1)}, bf16[384,1024]{1,0:T(8,128)(2,1)S(1)}, u32[]{:S(2)}, u32[]{:S(2)}) collective-permute-start(bf16[384,1024]{1,0:T(8,128)(2,1)S(1)} %pad_maximum_fusion.13.refs_0_), channel_id=1, source_target_pairs={{0,2},{1,3},{2,0},{3,1},{4,5},{5,4},{6,7},{7,6},{8,10},{9,11},{10,... | collective-permute-start | bytes 2359304 | tf_op jit(solution)/shard_map/ppermute | solution.py:993
  121.3 52.7 %collective-permute-start.8 = (bf16[384,1024]{1,0:T(8,128)(2,1)S(1)}, bf16[384,1024]{1,0:T(8,128)(2,1)S(1)}, u32[]{:S(2)}, u32[]{:S(2)}) collective-permute-start(bf16[384,1024]{1,0:T(8,128)(2,1)S(1)} %pad_maximum_fusion.13.refs_0_), channel_id=1, source_target_pairs={{0,1},{1,0},{2,3},{3,2},{4,6},{5,7},{6,4},{7,5},{8,9},{9,8},{10,11... | collective-permute-start | bytes 2359304 | tf_op jit(solution)/shard_map/ppermute | solution.py:990
  121.4 42.2 %collective-permute-start.11 = (bf16[1024,384]{1,0:T(8,128)(2,1)}, bf16[1024,384]{1,0:T(8,128)(2,1)}, u32[]{:S(2)}, u32[]{:S(2)}) collective-permute-start(bf16[1024,384]{1,0:T(8,128)(2,1)} %collective-permute-done.9.refs_1_), channel_id=1, source_target_pairs={{0,1},{1,0},{2,3},{3,2},{4,6},{5,7},{6,4},{7,5},{8,9},{9,8},{10,11... | collective-permute-start | bytes 2359304 | tf_op jit(solution)/shard_map/ppermute | solution.py:990
  174.0 28.0 %collective-permute-start.16 = (bf16[384,1024]{1,0:T(8,128)(2,1)S(1)}, bf16[384,1024]{1,0:T(8,128)(2,1)S(1)}, u32[]{:S(2)}, u32[]{:S(2)}) collective-permute-start(bf16[384,1024]{1,0:T(8,128)(2,1)S(1)} %collective-permute-done.7.refs_1_), channel_id=1, source_target_pairs={{0,1},{1,0},{2,3},{3,2},{4,6},{5,7},{6,4},{7,5},{8,9},{9,8},{10,11... | collective-permute-start | bytes 2359304 | tf_op jit(solution)/shard_map/ppermute | solution.py:990
  215.2 27.5 %collective-permute-start.17 = (bf16[1024,384]{1,0:T(8,128)(2,1)S(1)}, bf16[1024,384]{1,0:T(8,128)(2,1)S(1)}, u32[]{:S(2)}, u32[]{:S(2)}) collective-permute-start(bf16[1024,384]{1,0:T(8,128)(2,1)S(1)} %pad_maximum_fusion.12.refs_0_), channel_id=1, source_target_pairs={{0,2},{1,3},{2,0},{3,1},{4,5},{5,4},{6,7},{7,6},{8,10},{9,11},{10,... | collective-permute-start | bytes 2359304 | tf_op jit(solution)/shard_map/ppermute | solution.py:993
  216.2 26.5 %collective-permute-start.18 = (bf16[1024,384]{1,0:T(8,128)(2,1)S(1)}, bf16[1024,384]{1,0:T(8,128)(2,1)S(1)}, u32[]{:S(2)}, u32[]{:S(2)}) collective-permute-start(bf16[1024,384]{1,0:T(8,128)(2,1)S(1)} %pad_maximum_fusion.12.refs_0_), channel_id=1, source_target_pairs={{0,1},{1,0},{2,3},{3,2},{4,6},{5,7},{6,4},{7,5},{8,9},{9,8},{10,11... | collective-permute-start | bytes 2359304 | tf_op jit(solution)/shard_map/ppermute | solution.py:990
  217.9 409.8 %all-reduce.4.cloned.1.call-start = ((), (), s32[]{:S(2)}) async-start(), calls=%async_computation | async-start | bytes 4194304 | tf_op jit(solution)/shard_map/psum | solution.py:1256
  252.5 27.7 %collective-permute-start.21 = (bf16[1024,384]{1,0:T(8,128)(2,1)S(1)}, bf16[1024,384]{1,0:T(8,128)(2,1)S(1)}, u32[]{:S(2)}, u32[]{:S(2)}) collective-permute-start(bf16[1024,384]{1,0:T(8,128)(2,1)S(1)} %collective-permute-done.17.refs_1_), channel_id=1, source_target_pairs={{0,1},{1,0},{2,3},{3,2},{4,6},{5,7},{6,4},{7,5},{8,9},{9,8},{10,11... | collective-permute-start | bytes 2359304 | tf_op jit(solution)/shard_map/ppermute | solution.py:990
  280.2 31.7 %collective-permute-start.23 = (bf16[512,1024]{1,0:T(8,128)(2,1)S(1)}, bf16[512,1024]{1,0:T(8,128)(2,1)S(1)}, u32[]{:S(2)}, u32[]{:S(2)}) collective-permute-start(bf16[512,1024]{1,0:T(8,128)(2,1)S(1)} %constant_dynamic-slice_fusion.43.refs_0_), channel_id=1, source_target_pairs={{0,2},{1,3},{2,0},{3,1},{4,5},{5,4},{6,7},{7,6},{8,10},{9,11},{10,... | collective-permute-start | bytes 3145736 | tf_op jit(solution)/shard_map/ppermute | solution.py:993
  281.4 30.5 %collective-permute-start.24 = (bf16[512,1024]{1,0:T(8,128)(2,1)S(1)}, bf16[512,1024]{1,0:T(8,128)(2,1)S(1)}, u32[]{:S(2)}, u32[]{:S(2)}) collective-permute-start(bf16[512,1024]{1,0:T(8,128)(2,1)S(1)} %constant_dynamic-slice_fusion.43.refs_0_), channel_id=1, source_target_pairs={{0,1},{1,0},{2,3},{3,2},{4,6},{5,7},{6,4},{7,5},{8,9},{9,8},{10,11... | collective-permute-start | bytes 3145736 | tf_op jit(solution)/shard_map/ppermute | solution.py:990
  319.7 27.0 %collective-permute-start.26 = (bf16[512,1024]{1,0:T(8,128)(2,1)S(1)}, bf16[512,1024]{1,0:T(8,128)(2,1)S(1)}, u32[]{:S(2)}, u32[]{:S(2)}) collective-permute-start(bf16[512,1024]{1,0:T(8,128)(2,1)S(1)} %collective-permute-done.23.refs_1_), channel_id=1, source_target_pairs={{0,1},{1,0},{2,3},{3,2},{4,6},{5,7},{6,4},{7,5},{8,9},{9,8},{10,11... | collective-permute-start | bytes 3145736 | tf_op jit(solution)/shard_map/ppermute | solution.py:990
  380.5 25.4 %collective-permute-start.32 = (bf16[1024,1024]{1,0:T(8,128)(2,1)}, bf16[1024,1024]{1,0:T(8,128)(2,1)S(1)}, u32[]{:S(2)}, u32[]{:S(2)}) collective-permute-start(bf16[1024,1024]{1,0:T(8,128)(2,1)} %weight_grads.14), channel_id=1, source_target_pairs={{0,1},{1,0},{2,3},{3,2},{4,6},{5,7},{6,4},{7,5},{8,9},{9,8},{10,11... | collective-permute-start | bytes 6291464 | tf_op jit(solution)/shard_map/ppermute | solution.py:990
  407.1 31.4 %collective-permute-start.34 = (bf16[1024,1024]{1,0:T(8,128)(2,1)}, bf16[1024,1024]{1,0:T(8,128)(2,1)S(1)}, u32[]{:S(2)}, u32[]{:S(2)}) collective-permute-start(bf16[1024,1024]{1,0:T(8,128)(2,1)} %weight_grads.15), channel_id=1, source_target_pairs={{0,1},{1,0},{2,3},{3,2},{4,6},{5,7},{6,4},{7,5},{8,9},{9,8},{10,11... | collective-permute-start | bytes 6291464 | tf_op jit(solution)/shard_map/ppermute | solution.py:990
  423.3 41.6 %collective-permute-start.35 = (bf16[512,1024]{1,0:T(8,128)(2,1)}, bf16[512,1024]{1,0:T(8,128)(2,1)S(1)}, u32[]{:S(2)}, u32[]{:S(2)}) collective-permute-start(bf16[512,1024]{1,0:T(8,128)(2,1)} %get-tuple-element.567), channel_id=1, source_target_pairs={{0,2},{1,3},{2,0},{3,1},{4,5},{5,4},{6,7},{7,6},{8,10},{9,11},{10,... | collective-permute-start | bytes 3145736 | tf_op jit(solution)/shard_map/ppermute | solution.py:993
  482.0 37.9 %collective-permute-start.40 = (bf16[1024,1024]{1,0:T(8,128)(2,1)}, bf16[1024,1024]{1,0:T(8,128)(2,1)S(1)}, u32[]{:S(2)}, u32[]{:S(2)}) collective-permute-start(bf16[1024,1024]{1,0:T(8,128)(2,1)} %product_columns_back.8.refs_1_), channel_id=1, source_target_pairs={{0,4},{4,0},{1,5},{5,1},{2,6},{6,2},{3,7},{7,3},{8,12},{12,8},{9,1... | collective-permute-start | bytes 6291464 | tf_op jit(solution)/shard_map/ppermute | solution.py:942
  496.5 25.4 %collective-permute-start.39 = (bf16[1024,1024]{1,0:T(8,128)(2,1)}, bf16[1024,1024]{1,0:T(8,128)(2,1)S(1)}, u32[]{:S(2)}, u32[]{:S(2)}) collective-permute-start(bf16[1024,1024]{1,0:T(8,128)(2,1)} %weight_grads.18), channel_id=1, source_target_pairs={{0,1},{1,0},{2,3},{3,2},{4,6},{5,7},{6,4},{7,5},{8,9},{9,8},{10,11... | collective-permute-start | bytes 6291464 | tf_op jit(solution)/shard_map/ppermute | solution.py:990
  523.2 25.5 %collective-permute-start.38 = (bf16[1024,1024]{1,0:T(8,128)(2,1)}, bf16[1024,1024]{1,0:T(8,128)(2,1)}, u32[]{:S(2)}, u32[]{:S(2)}) collective-permute-start(bf16[1024,1024]{1,0:T(8,128)(2,1)} %weight_grads.19), channel_id=1, source_target_pairs={{0,1},{1,0},{2,3},{3,2},{4,6},{5,7},{6,4},{7,5},{8,9},{9,8},{10,11... | collective-permute-start | bytes 6291464 | tf_op jit(solution)/shard_map/ppermute | solution.py:990
  523.3 209.8 %all-reduce.6.cloned.1.call-start = ((), (), s32[]{:S(2)}) async-start(), calls=%async_computation.1 | async-start | bytes 4194304 | tf_op jit(solution)/shard_map/psum | solution.py:1304
  558.4 69.2 %collective-permute-start.42 = (bf16[1024,1024]{1,0:T(8,128)(2,1)}, bf16[1024,1024]{1,0:T(8,128)(2,1)}, u32[]{:S(2)}, u32[]{:S(2)}) collective-permute-start(bf16[1024,1024]{1,0:T(8,128)(2,1)} %weight_grads.21), channel_id=1, source_target_pairs={{0,1},{1,0},{2,3},{3,2},{4,6},{5,7},{6,4},{7,5},{8,9},{9,8},{10,11... | collective-permute-start | bytes 6291464 | tf_op jit(solution)/shard_map/ppermute | solution.py:990
  560.4 25.4 %collective-permute-start.43 = (bf16[512,1024]{1,0:T(8,128)(2,1)}, bf16[512,1024]{1,0:T(8,128)(2,1)S(1)}, u32[]{:S(2)}, u32[]{:S(2)}) collective-permute-start(bf16[512,1024]{1,0:T(8,128)(2,1)} %get-tuple-element.563), channel_id=1, source_target_pairs={{0,2},{1,3},{2,0},{3,1},{4,5},{5,4},{6,7},{7,6},{8,10},{9,11},{10,... | collective-permute-start | bytes 3145736 | tf_op jit(solution)/shard_map/ppermute | solution.py:993
  561.0 46.7 %collective-permute-start.44 = (bf16[512,1024]{1,0:T(8,128)(2,1)S(1)}, bf16[512,1024]{1,0:T(8,128)(2,1)S(1)}, u32[]{:S(2)}, u32[]{:S(2)}) collective-permute-start(bf16[512,1024]{1,0:T(8,128)(2,1)S(1)} %get-tuple-element.564), channel_id=1, source_target_pairs={{0,2},{1,3},{2,0},{3,1},{4,5},{5,4},{6,7},{7,6},{8,10},{9,11},{10,... | collective-permute-start | bytes 3145736 | tf_op jit(solution)/shard_map/ppermute | solution.py:993
  637.3 51.8 %collective-permute-start.46 = (bf16[1024,1024]{1,0:T(8,128)(2,1)}, bf16[1024,1024]{1,0:T(8,128)(2,1)}, u32[]{:S(2)}, u32[]{:S(2)}) collective-permute-start(bf16[1024,1024]{1,0:T(8,128)(2,1)} %weight_grads.24), channel_id=1, source_target_pairs={{0,1},{1,0},{2,3},{3,2},{4,6},{5,7},{6,4},{7,5},{8,9},{9,8},{10,11... | collective-permute-start | bytes 6291464 | tf_op jit(solution)/shard_map/ppermute | solution.py:990
  637.4 213.2 %all-reduce.8.cloned.1.call-start = ((), (), s32[]{:S(2)}) async-start(), calls=%async_computation.2 | async-start | bytes 4194304 | tf_op jit(solution)/shard_map/psum | solution.py:1323
  637.4 67.8 %collective-permute-start.45 = (bf16[512,1024]{1,0:T(8,128)(2,1)}, bf16[512,1024]{1,0:T(8,128)(2,1)}, u32[]{:S(2)}, u32[]{:S(2)}) collective-permute-start(bf16[512,1024]{1,0:T(8,128)(2,1)} %get-tuple-element.561), channel_id=1, source_target_pairs={{0,2},{1,3},{2,0},{3,1},{4,5},{5,4},{6,7},{7,6},{8,10},{9,11},{10,... | collective-permute-start | bytes 3145736 | tf_op jit(solution)/shard_map/ppermute | solution.py:993
  687.9 45.2 %collective-permute-start.51 = (bf16[1024,1024]{1,0:T(8,128)(2,1)}, bf16[1024,1024]{1,0:T(8,128)(2,1)}, u32[]{:S(2)}, u32[]{:S(2)}) collective-permute-start(bf16[1024,1024]{1,0:T(8,128)(2,1)} %weight_grads.26), channel_id=1, source_target_pairs={{0,1},{1,0},{2,3},{3,2},{4,6},{5,7},{6,4},{7,5},{8,9},{9,8},{10,11... | collective-permute-start | bytes 6291464 | tf_op jit(solution)/shard_map/ppermute | solution.py:990
  693.0 25.6 %collective-permute-start.47 = (bf16[512,1024]{1,0:T(8,128)(2,1)}, bf16[512,1024]{1,0:T(8,128)(2,1)}, u32[]{:S(2)}, u32[]{:S(2)}) collective-permute-start(bf16[512,1024]{1,0:T(8,128)(2,1)} %get-tuple-element.559), channel_id=1, source_target_pairs={{0,2},{1,3},{2,0},{3,1},{4,5},{5,4},{6,7},{7,6},{8,10},{9,11},{10,... | collective-permute-start | bytes 3145736 | tf_op jit(solution)/shard_map/ppermute | solution.py:993
  696.5 36.5 %collective-permute-start.48 = (bf16[1,128,1024]{2,1,0:T(8,128)(2,1)}, bf16[1,128,1024]{2,1,0:T(8,128)(2,1)}, u32[]{:S(2)}, u32[]{:S(2)}) collective-permute-start(bf16[1,128,1024]{2,1,0:T(8,128)(2,1)} %get-tuple-element.459), channel_id=1, source_target_pairs={{0,1},{1,0},{2,3},{3,2},{4,6},{5,7},{6,4},{7,5},{8,9},{9,8},{10,11... | collective-permute-start | bytes 786440 | tf_op jit(solution)/shard_map/ppermute | solution.py:990
  696.6 36.4 %collective-permute-start.49 = (bf16[1,128,1024]{2,1,0:T(8,128)(2,1)}, bf16[1,128,1024]{2,1,0:T(8,128)(2,1)}, u32[]{:S(2)}, u32[]{:S(2)}) collective-permute-start(bf16[1,128,1024]{2,1,0:T(8,128)(2,1)} %get-tuple-element.460), channel_id=1, source_target_pairs={{0,2},{1,3},{2,0},{3,1},{4,5},{5,4},{6,7},{7,6},{8,10},{9,11},{10,... | collective-permute-start | bytes 786440 | tf_op jit(solution)/shard_map/ppermute | solution.py:993
  705.2 27.8 %collective-permute-start.50 = (bf16[1,128,1024]{2,1,0:T(8,128)(2,1)}, bf16[1,128,1024]{2,1,0:T(8,128)(2,1)}, u32[]{:S(2)}, u32[]{:S(2)}) collective-permute-start(bf16[1,128,1024]{2,1,0:T(8,128)(2,1)} %get-tuple-element.461), channel_id=1, source_target_pairs={{0,3},{1,2},{2,1},{3,0},{4,7},{5,6},{6,5},{7,4},{8,11},{9,10},{10,... | collective-permute-start | bytes 786440 | tf_op jit(solution)/shard_map/ppermute | solution.py:961
  751.0 27.9 %collective-permute-start.54 = (bf16[1024,1024]{1,0:T(8,128)(2,1)S(1)}, bf16[1024,1024]{1,0:T(8,128)(2,1)}, u32[]{:S(2)}, u32[]{:S(2)}) collective-permute-start(bf16[1024,1024]{1,0:T(8,128)(2,1)S(1)} %copy-done.12), channel_id=1, source_target_pairs={{0,4},{4,0},{1,5},{5,1},{2,6},{6,2},{3,7},{7,3},{8,12},{12,8},{9,1... | collective-permute-start | bytes 6291464 | tf_op jit(solution)/shard_map/ppermute | solution.py:942
  751.5 35.0 %collective-permute-start.53 = (bf16[512,1024]{1,0:T(8,128)(2,1)}, bf16[512,1024]{1,0:T(8,128)(2,1)}, u32[]{:S(2)}, u32[]{:S(2)}) collective-permute-start(bf16[512,1024]{1,0:T(8,128)(2,1)} %get-tuple-element.556), channel_id=1, source_target_pairs={{0,2},{1,3},{2,0},{3,1},{4,5},{5,4},{6,7},{7,6},{8,10},{9,11},{10,... | collective-permute-start | bytes 3145736 | tf_op jit(solution)/shard_map/ppermute | solution.py:993
  789.0 31.3 %collective-permute-start.65 = (bf16[128,1024]{1,0:T(8,128)(2,1)}, bf16[128,1024]{1,0:T(8,128)(2,1)S(1)}, u32[]{:S(2)}, u32[]{:S(2)}) collective-permute-start(bf16[128,1024]{1,0:T(8,128)(2,1)} %get-tuple-element.585), channel_id=1, source_target_pairs={{0,24},{8,16},{16,8},{24,0},{1,25},{9,17},{17,9},{25,1},{2,26},{10... | collective-permute-start | bytes 786440 | tf_op jit(solution)/shard_map/ppermute | solution.py:996
  790.3 31.6 %collective-permute-start.66 = (bf16[128,1024]{1,0:T(8,128)(2,1)}, bf16[128,1024]{1,0:T(8,128)(2,1)S(1)}, u32[]{:S(2)}, u32[]{:S(2)}) collective-permute-start(bf16[128,1024]{1,0:T(8,128)(2,1)} %get-tuple-element.584), channel_id=1, source_target_pairs={{0,16},{8,24},{16,0},{24,8},{1,17},{9,25},{17,1},{25,9},{2,18},{10... | collective-permute-start | bytes 786440 | tf_op jit(solution)/shard_map/ppermute | solution.py:996
  791.3 32.2 %collective-permute-start.67 = (bf16[128,1024]{1,0:T(8,128)(2,1)}, bf16[128,1024]{1,0:T(8,128)(2,1)S(1)}, u32[]{:S(2)}, u32[]{:S(2)}) collective-permute-start(bf16[128,1024]{1,0:T(8,128)(2,1)} %get-tuple-element.583), channel_id=1, source_target_pairs={{0,8},{8,0},{16,24},{24,16},{1,9},{9,1},{17,25},{25,17},{2,10},{10... | collective-permute-start | bytes 786440 | tf_op jit(solution)/shard_map/ppermute | solution.py:996
  796.9 55.1 %collective-permute-start.55 = (bf16[1,128,1024]{2,1,0:T(8,128)(2,1)}, bf16[1,128,1024]{2,1,0:T(8,128)(2,1)}, u32[]{:S(2)}, u32[]{:S(2)}) collective-permute-start(bf16[1,128,1024]{2,1,0:T(8,128)(2,1)} %get-tuple-element.488), channel_id=1, source_target_pairs={{0,1},{1,0},{2,3},{3,2},{4,6},{5,7},{6,4},{7,5},{8,9},{9,8},{10,11... | collective-permute-start | bytes 786440 | tf_op jit(solution)/shard_map/ppermute | solution.py:990
  819.6 35.5 %collective-permute-start.56 = (bf16[1,128,1024]{2,1,0:T(8,128)(2,1)}, bf16[1,128,1024]{2,1,0:T(8,128)(2,1)}, u32[]{:S(2)}, u32[]{:S(2)}) collective-permute-start(bf16[1,128,1024]{2,1,0:T(8,128)(2,1)} %get-tuple-element.489), channel_id=1, source_target_pairs={{0,2},{1,3},{2,0},{3,1},{4,5},{5,4},{6,7},{7,6},{8,10},{9,11},{10,... | collective-permute-start | bytes 786440 | tf_op jit(solution)/shard_map/ppermute | solution.py:993
  820.2 35.2 %collective-permute-start.57 = (bf16[1,128,1024]{2,1,0:T(8,128)(2,1)}, bf16[1,128,1024]{2,1,0:T(8,128)(2,1)}, u32[]{:S(2)}, u32[]{:S(2)}) collective-permute-start(bf16[1,128,1024]{2,1,0:T(8,128)(2,1)} %get-tuple-element.490), channel_id=1, source_target_pairs={{0,3},{1,2},{2,1},{3,0},{4,7},{5,6},{6,5},{7,4},{8,11},{9,10},{10,... | collective-permute-start | bytes 786440 | tf_op jit(solution)/shard_map/ppermute | solution.py:961
  821.9 59.1 %collective-permute-start.58 = (bf16[1,128,1024]{2,1,0:T(8,128)(2,1)}, bf16[1,128,1024]{2,1,0:T(8,128)(2,1)}, u32[]{:S(2)}, u32[]{:S(2)}) collective-permute-start(bf16[1,128,1024]{2,1,0:T(8,128)(2,1)} %get-tuple-element.494), channel_id=1, source_target_pairs={{0,1},{1,0},{2,3},{3,2},{4,6},{5,7},{6,4},{7,5},{8,9},{9,8},{10,11... | collective-permute-start | bytes 786440 | tf_op jit(solution)/shard_map/ppermute | solution.py:990
  823.5 57.5 %collective-permute-start.59 = (bf16[1,128,1024]{2,1,0:T(8,128)(2,1)S(1)}, bf16[1,128,1024]{2,1,0:T(8,128)(2,1)}, u32[]{:S(2)}, u32[]{:S(2)}) collective-permute-start(bf16[1,128,1024]{2,1,0:T(8,128)(2,1)S(1)} %get-tuple-element.495), channel_id=1, source_target_pairs={{0,2},{1,3},{2,0},{3,1},{4,5},{5,4},{6,7},{7,6},{8,10},{9,11},{10,... | collective-permute-start | bytes 786440 | tf_op jit(solution)/shard_map/ppermute | solution.py:993
  867.3 24.8 %collective-permute-start.73 = (bf16[1024,512]{1,0:T(8,128)(2,1)}, bf16[1024,512]{1,0:T(8,128)(2,1)}, u32[]{:S(2)}, u32[]{:S(2)}) collective-permute-start(bf16[1024,512]{1,0:T(8,128)(2,1)} %constant_dynamic-slice_fusion.1), channel_id=1, source_target_pairs={{0,4},{4,0},{1,5},{5,1},{2,6},{6,2},{3,7},{7,3},{8,12},{12,8},{9,1... | collective-permute-start | bytes 3145736 | tf_op jit(solution)/shard_map/ppermute | solution.py:942
  (101 other events, 826.0 us)
Sparse Core Ops, SparseCore 0:
  57.9 80.7 all-gather.6
  141.1 65.2 all-gather.8
  218.0 69.0 all-gather.10
  523.4 84.8 all-reduce.3
  637.5 84.6 all-reduce.5
  753.0 97.5 all-reduce.7
